TPU v7x, 32 devices: a whole 2x2x4 slice. The times are simulated.
32 devices in a mesh: crop: 4 (over y, x), row: 4 (over z), col: 2 (over core).
Axes of the slice: x: 2, y: 2, z: 4, core: 2. Of those that a mesh axis runs over, the one named last changes fastest.
Arguments:
- pair_acts: bfloat16 [4, 512, 512, 128], P('crop', 'row', 'col'), may hold values from -6 to 6
- residue_mask: int32 [4, 512], P('crop'), may hold values 0 or 1
- dist_bins: int32 [4, 512, 512], P('crop', 'row', 'col'), may hold values from 0 to 63
- w_in: float32 [128, 640], replicated, may hold values from -0.5 to 0.5
- w_out: float32 [128, 128], replicated, may hold values from -0.5 to 0.5
- w_t1: float32 [128, 512], replicated, may hold values from -0.5 to 0.5
- w_t2: float32 [512, 128], replicated, may hold values from -0.25 to 0.25
- w_dist: float32 [128, 64], replicated, may hold values from -0.5 to 0.5
- norm_params: float32 [6, 128], replicated, may hold values from -0.6 to 1.45
- dist_bias: float32 [64], replicated, may hold values from -3 to 3
- m_in: float32 [128, 640], replicated, may hold values from -2.2888184e-05 to 2.2888184e-05
- m_out: float32 [128, 128], replicated, may hold values from -2.2888184e-05 to 2.2888184e-05
- m_t1: float32 [128, 512], replicated, may hold values from -2.2888184e-05 to 2.2888184e-05
- m_t2: float32 [512, 128], replicated, may hold values from -2.2888184e-05 to 2.2888184e-05
- m_dist: float32 [128, 64], replicated, may hold values from -2.2888184e-05 to 2.2888184e-05
- m_norm: float32 [6, 128], replicated, may hold values from -7.6293945e-05 to 7.6293945e-05
- m_bias: float32 [64], replicated, may hold values from -7.6293945e-05 to 7.6293945e-05
- v_in: float32 [128, 640], replicated, may hold values from 1.6778523e-12 to 6.711409e-12
- v_out: float32 [128, 128], replicated, may hold values from 1.6778523e-12 to 6.711409e-12
- v_t1: float32 [128, 512], replicated, may hold values from 1.6778523e-12 to 6.711409e-12
- v_t2: float32 [512, 128], replicated, may hold values from 1.6778523e-12 to 6.711409e-12
- v_dist: float32 [128, 64], replicated, may hold values from 1.6778523e-12 to 6.711409e-12
- v_norm: float32 [6, 128], replicated, may hold values from 1.510067e-11 to 6.040268e-11
- v_bias: float32 [64], replicated, may hold values from 1.510067e-11 to 6.040268e-11
Outputs:
- new_w_in: float32 [128, 640], replicated
- new_w_out: float32 [128, 128], replicated
- new_w_t1: float32 [128, 512], replicated
- new_w_t2: float32 [512, 128], replicated
- new_w_dist: float32 [128, 64], replicated
- new_norm: float32 [6, 128], replicated
- new_bias: float32 [64], replicated
- new_m_in: float32 [128, 640], replicated
- new_m_out: float32 [128, 128], replicated
- new_m_t1: float32 [128, 512], replicated
- new_m_t2: float32 [512, 128], replicated
- new_m_dist: float32 [128, 64], replicated
- new_m_norm: float32 [6, 128], replicated
- new_m_bias: float32 [64], replicated
- new_v_in: float32 [128, 640], replicated
- new_v_out: float32 [128, 128], replicated
- new_v_t1: float32 [128, 512], replicated
- new_v_t2: float32 [512, 128], replicated
- new_v_dist: float32 [128, 64], replicated
- new_v_norm: float32 [6, 128], replicated
- new_v_bias: float32 [64], replicated
- loss_sum: float32 [], replicated
- pair_total: float32 [], replicated
- grad_norm: float32 [], replicated
All inputs are finite; a program needn't handle non-finite values. No bound on the sum of `residue_mask` on one device may be relied on, other than what follows from the above.
Results may differ from a plain program's by a relative error of at most 0.006.
Values may be sent and summed in bfloat16 or wider, within the bound.
A program may use at most 640 MiB of HBM per device.

v0:
```python
import jax
import jax.numpy as jnp
from jax import lax
from jax.sharding import PartitionSpec as P

STEP = 10


NORM_EPS = 1e-05
CLIP_NORM = 0.02
LEARN_RATE = 0.03
GAIN_RATE = 0.3
BETA_ONE = 0.9
BETA_TWO = 0.999
ADAM_EPS = 1e-08
WEIGHT_DECAY = 0.01


def standardize(values):
    center = values - jnp.mean(values, -1, keepdims=True)
    rstd = lax.rsqrt(jnp.mean(center * center, -1, keepdims=True) + NORM_EPS)
    return (center * rstd, rstd)


def standard_back(grad, normed, rstd):
    return rstd * (
        grad
        - jnp.mean(grad, -1, keepdims=True)
        - normed * jnp.mean(grad * normed, -1, keepdims=True)
    )


def linear(values, weight):
    return jnp.einsum("ijc,cd->ijd", values, weight, preferred_element_type=jnp.float32)


def weight_grad(values, grad):
    return jnp.einsum("ijc,ijd->cd", values, grad, preferred_element_type=jnp.float32)


def transposed(grad, weight):
    return jnp.einsum("ijd,cd->ijc", grad, weight, preferred_element_type=jnp.float32)


def adamw_update(weight, first, second, grad, scale, rate):
    clipped = grad * scale
    first_new = BETA_ONE * first + (1.0 - BETA_ONE) * clipped
    second_new = BETA_TWO * second + (1.0 - BETA_TWO) * clipped * clipped
    first_hat = first_new / (1.0 - BETA_ONE**STEP)
    second_hat = second_new / (1.0 - BETA_TWO**STEP)
    stepped = weight - rate * (
        first_hat / (jnp.sqrt(second_hat) + ADAM_EPS) + WEIGHT_DECAY * weight
    )
    return (stepped, first_new, second_new)


def on_device(
    pair_acts,
    residue_mask,
    dist_bins,
    w_in,
    w_out,
    w_t1,
    w_t2,
    w_dist,
    norm_params,
    dist_bias,
    m_in,
    m_out,
    m_t1,
    m_t2,
    m_dist,
    m_norm,
    m_bias,
    v_in,
    v_out,
    v_t1,
    v_t2,
    v_dist,
    v_norm,
    v_bias,
):
    tile_rows = pair_acts.shape[1]
    tile_cols = pair_acts.shape[2]
    width = w_out.shape[0]
    row_first = lax.axis_index("row") * tile_rows
    col_first = lax.axis_index("col") * tile_cols
    mask_vals = residue_mask[0].astype(jnp.float32)
    row_mask = lax.dynamic_slice_in_dim(mask_vals, row_first, tile_rows)
    col_mask = lax.dynamic_slice_in_dim(mask_vals, col_first, tile_cols)
    pair_mask = row_mask[:, None] * col_mask[None, :]
    mask_cube = pair_mask[..., None]
    pair_total = lax.psum(jnp.sum(pair_mask), ("crop", "row", "col"))
    low_in, low_out, low_t1, low_t2, low_dist = [
        weight.astype(jnp.bfloat16) for weight in (w_in, w_out, w_t1, w_t2, w_dist)
    ]
    acts = pair_acts[0].astype(jnp.float32)
    normed_one, rstd_one = standardize(acts)
    pair_norm = (normed_one * norm_params[0] + norm_params[1]).astype(jnp.bfloat16)
    projected = linear(pair_norm, low_in)
    left_proj = projected[..., :width]
    left_sig = jax.nn.sigmoid(projected[..., width : 2 * width])
    right_proj = projected[..., 2 * width : 3 * width]
    right_sig = jax.nn.sigmoid(projected[..., 3 * width : 4 * width])
    gate_sig = jax.nn.sigmoid(projected[..., 4 * width :])
    left_vals = (mask_cube * left_sig * left_proj).astype(jnp.bfloat16)
    right_vals = (mask_cube * right_sig * right_proj).astype(jnp.bfloat16)
    strips = lax.all_gather(right_vals, "row", axis=0, tiled=True)
    piece = strips
    triangle = jnp.transpose(
        lax.psum_scatter(
            jnp.einsum("jkc,ikc->jic", piece, left_vals, preferred_element_type=jnp.float32),
            "col",
            scatter_dimension=0,
            tiled=True,
        ),
        (1, 0, 2),
    )
    normed_two, rstd_two = standardize(triangle)
    tri_norm = (normed_two * norm_params[2] + norm_params[3]).astype(jnp.bfloat16)
    out_proj = linear(tri_norm, low_out)
    updated = acts + gate_sig * out_proj
    normed_three, rstd_three = standardize(updated)
    trans_in = (normed_three * norm_params[4] + norm_params[5]).astype(jnp.bfloat16)
    pre_act = linear(trans_in, low_t1)
    hidden = jax.nn.silu(pre_act).astype(jnp.bfloat16)
    final = updated + linear(hidden, low_t2)
    final_low = final.astype(jnp.bfloat16)
    logits = linear(final_low, low_dist) + dist_bias
    log_total = jax.nn.logsumexp(logits, -1)
    onehot = (dist_bins[0][..., None] == jnp.arange(w_dist.shape[1])).astype(jnp.float32)
    loss_local = jnp.sum(pair_mask * (log_total - jnp.sum(logits * onehot, -1)))
    d_logits = (mask_cube * (jnp.exp(logits - log_total[..., None]) - onehot) / pair_total).astype(
        jnp.bfloat16
    )
    grad_dist = weight_grad(final_low, d_logits)
    grad_bias = jnp.sum(d_logits.astype(jnp.float32), (0, 1))
    d_final = transposed(d_logits, low_dist)
    d_trans = d_final.astype(jnp.bfloat16)
    grad_t2 = weight_grad(hidden, d_trans)
    d_hidden = transposed(d_trans, low_t2)
    sig_pre = jax.nn.sigmoid(pre_act)
    d_pre = (d_hidden * sig_pre * (1.0 + pre_act * (1.0 - sig_pre))).astype(jnp.bfloat16)
    grad_t1 = weight_grad(trans_in, d_pre)
    d_trans_in = transposed(d_pre, low_t1)
    d_updated = d_final + standard_back(d_trans_in * norm_params[4], normed_three, rstd_three)
    d_out = (d_updated * gate_sig).astype(jnp.bfloat16)
    d_out_gate = d_updated * out_proj * gate_sig * (1.0 - gate_sig)
    grad_out = weight_grad(tri_norm, d_out)
    d_tri_norm = transposed(d_out, low_out)
    d_triangle = standard_back(d_tri_norm * norm_params[2], normed_two, rstd_two).astype(
        jnp.bfloat16
    )
    d_rows = lax.all_gather(d_triangle, "col", axis=1, tiled=True)
    d_left = jnp.einsum("ijc,jkc->ikc", d_rows, strips, preferred_element_type=jnp.float32)
    piece = d_rows
    d_right = lax.psum_scatter(
        jnp.einsum("ijc,ikc->jkc", piece, left_vals, preferred_element_type=jnp.float32).astype(
            jnp.bfloat16
        ),
        "row",
        scatter_dimension=0,
        tiled=True,
    ).astype(jnp.float32)
    d_proj = jnp.concatenate(
        [
            d_left * mask_cube * left_sig,
            d_left * mask_cube * left_proj * left_sig * (1.0 - left_sig),
            d_right * mask_cube * right_sig,
            d_right * mask_cube * right_proj * right_sig * (1.0 - right_sig),
            d_out_gate,
        ],
        -1,
    ).astype(jnp.bfloat16)
    grad_in = weight_grad(pair_norm, d_proj)
    d_pair_norm = transposed(d_proj, low_in)
    grad_norms = jnp.stack(
        [
            jnp.sum(d_pair_norm * normed_one, (0, 1)),
            jnp.sum(d_pair_norm, (0, 1)),
            jnp.sum(d_tri_norm * normed_two, (0, 1)),
            jnp.sum(d_tri_norm, (0, 1)),
            jnp.sum(d_trans_in * normed_three, (0, 1)),
            jnp.sum(d_trans_in, (0, 1)),
        ]
    )
    summed = lax.psum(
        (grad_in, grad_out, grad_t1, grad_t2, grad_dist, grad_norms, grad_bias, loss_local),
        ("crop", "row", "col"),
    )
    grads = summed[:7]
    squares = jnp.zeros((), jnp.float32)
    for grad in grads:
        squares = squares + jnp.sum(grad * grad)
    grad_norm = jnp.sqrt(squares)
    scale = CLIP_NORM / jnp.maximum(grad_norm, CLIP_NORM)
    params = (w_in, w_out, w_t1, w_t2, w_dist, norm_params, dist_bias)
    firsts = (m_in, m_out, m_t1, m_t2, m_dist, m_norm, m_bias)
    seconds = (v_in, v_out, v_t1, v_t2, v_dist, v_norm, v_bias)
    rates = (LEARN_RATE, LEARN_RATE, LEARN_RATE, LEARN_RATE, LEARN_RATE, GAIN_RATE, GAIN_RATE)
    results = [
        adamw_update(
            params[index], firsts[index], seconds[index], grads[index], scale, rates[index]
        )
        for index in range(7)
    ]
    return (
        results[0][0],
        results[1][0],
        results[2][0],
        results[3][0],
        results[4][0],
        results[5][0],
        results[6][0],
        results[0][1],
        results[1][1],
        results[2][1],
        results[3][1],
        results[4][1],
        results[5][1],
        results[6][1],
        results[0][2],
        results[1][2],
        results[2][2],
        results[3][2],
        results[4][2],
        results[5][2],
        results[6][2],
        summed[7],
        pair_total,
        grad_norm,
    )


def solution(mesh):
    in_specs = (
        P("crop", "row", "col", None),
        P("crop", None),
        P("crop", "row", "col"),
        P(),
        P(),
        P(),
        P(),
        P(),
        P(),
        P(),
        P(),
        P(),
        P(),
        P(),
        P(),
        P(),
        P(),
        P(),
        P(),
        P(),
        P(),
        P(),
        P(),
        P(),
    )
    out_specs = (
        P(),
        P(),
        P(),
        P(),
        P(),
        P(),
        P(),
        P(),
        P(),
        P(),
        P(),
        P(),
        P(),
        P(),
        P(),
        P(),
        P(),
        P(),
        P(),
        P(),
        P(),
        P(),
        P(),
        P(),
    )
    return jax.shard_map(
        on_device, mesh=mesh, in_specs=in_specs, out_specs=out_specs, check_vma=False
    )
```

profile of v0, /device:TPU:0, one launch (start us, length us, event | category | flops | bytes accessed | tf_op | source)
XLA Modules:
  0.0 2073.9 jit_solution(8481462081027518702)
XLA Ops:
  26.0 31.5 %fusion.31 = f32[128,256,640]{2,1,0:T(8,128)} fusion(bf16[1,128,256,128]{3,2,1,0:T(8,128)(2,1)} %param.24, f32[128]{0:T(128)S(1)} %get-tuple-element.75, f32[128]{0:T(128)S(1)} %get-tuple-element.76, f32[128,256]{1,0:T(8,128)S(1)} %add_rsqrt_fusion.2, f32[128,256]{1,0:T(8,128)S(1)} %broadcast_multiply_fusion.7, f32[128,640]{1,0:T(8,128)S(1)} %copy-done.20), kind=kOutput, calls=%fused_computation.72 | convolution fusion | flops 5393956864 | bytes 92865536 | tf_op jit(solution)/shard_map/ijc,cd->ijd/dot_general | solution.py:34
  57.6 28.7 %multiply_convert_fusion.9 = (bf16[128,256,128]{2,1,0:T(8,128)(2,1)}, bf16[128,256,128]{2,1,0:T(8,128)(2,1)}) fusion(f32[128,256,640]{2,1,0:T(8,128)} %fusion.31, f32[128,256]{1,0:T(8,128)S(1)} %broadcast_multiply_fusion), kind=kLoop, calls=%fused_computation.49 | loop fusion | flops 50331648 | bytes 84017152 | tf_op jit(solution)/shard_map/convert_element_type | solution.py:106
  99.6 551.0 %all-gather.3.cloned.1.call-done = bf16[512,256,128]{2,1,0:T(8,128)(2,1)} async-done(((bf16[128,256,128]{2,1,0:T(8,128)(2,1)}), bf16[512,256,128]{2,1,0:T(8,128)(2,1)}) %all-gather.3.cloned.1.call-update) | async-done | bytes 33554448 | tf_op jit(solution)/shard_map/all_gather | solution.py:108
  650.6 47.3 %copy.78 = bf16[512,256,128]{0,1,2:T(8,128)(2,1)} copy(bf16[512,256,128]{2,1,0:T(8,128)(2,1)} %all-gather.3.cloned.1.call-done) | data formatting | bytes 67108864 | tf_op jit(solution)/shard_map/all_gather | solution.py:108
  697.9 26.9 %convolution_bitcast_fusion = f32[512,128,128]{0,1,2:T(8,128)} fusion(bf16[128,256,128]{0,1,2:T(8,128)(2,1)} %copy.80, bf16[512,256,128]{0,1,2:T(8,128)(2,1)} %copy.78), kind=kOutput, calls=%fused_computation.55 | convolution fusion | flops 4294967296 | bytes 75497472 | tf_op jit(solution)/shard_map/jkc,ikc->jic/dot_general | solution.py:112
  725.2 43.2 %reduce-scatter.5.cloned.1.call-done = f32[256,128,128]{0,1,2:T(8,128)} async-done(((f32[512,128,128]{0,1,2:T(8,128)}), f32[256,128,128]{0,1,2:T(8,128)}) %reduce-scatter.5.cloned.1.call-update) | async-done | bytes 16777232 | tf_op jit(solution)/shard_map/reduce_scatter | solution.py:111
  793.8 29.3 %fusion.86 = (f32[128,256]{1,0:T(8,128)S(1)}, f32[128,256,128]{2,1,0:T(8,128)}, f32[128,256,128]{2,1,0:T(8,128)}) fusion(f32[128,256,640]{2,1,0:T(8,128)} %fusion.31, bf16[1,128,256,128]{3,2,1,0:T(8,128)(2,1)} %param.24, f32[128,128]{1,0:T(8,128)S(1)} %copy-done.38, bf16[128,256,128]{1,0,2:T(8,128)(2,1)} %add_convert_fusion.2), kind=kOutput, calls=%fused_computation.166 | convolution fusion | flops 1103085568 | bytes 67305472 | tf_op jit(solution)/shard_map/ijc,cd->ijd/dot_general | solution.py:34
  834.7 32.2 %multiply_convert_fusion.1 = (bf16[128,256,512]{2,1,0:T(8,128)(2,1)}, f32[128,256,512]{2,1,0:T(8,128)}) fusion(f32[128,512]{1,0:T(8,128)S(1)} %copy-done.28, f32[128,256,128]{2,1,0:T(8,128)S(1)} %copy-done, f32[128]{0:T(128)S(1)} %copy-done.52, f32[128]{0:T(128)S(1)} %copy-done.48, f32[128,256]{1,0:T(8,128)S(1)} %add_rsqrt_fusion, ...), kind=kOutput, calls=%fused_computation.1 | convolution fusion | flops 4399890432 | bytes 117965824 | tf_op jit(solution)/shard_map/ijc,cd->ijd/dot_general | solution.py:34
  866.9 31.8 %add_convert_fusion = bf16[128,256,128]{2,1,0:T(8,128)(2,1)} fusion(f32[128,256,128]{2,1,0:T(8,128)} %get-tuple-element.69, bf16[128,256,512]{2,1,0:T(8,128)(2,1)} %get-tuple-element.79, f32[512,128]{1,0:T(8,128)S(1)} %copy-done.26), kind=kOutput, calls=%fused_computation.44 | convolution fusion | flops 4303421440 | bytes 58982400 | tf_op jit(solution)/shard_map/ijc,cd->ijd/dot_general | solution.py:34
  914.1 40.8 %psum.63 = f32[]{:T(128)} all-reduce(f32[]{:T(128)} %get-tuple-element.35), channel_id=1, replica_groups=mesh['crop'=4,'row'=4,'col'=2] {'crop','row','col'}, use_global_device_ids=true, to_apply=%region_10.11 | all-reduce | flops 1 | bytes 8 | tf_op jit(solution)/shard_map/psum | solution.py:93
  989.3 43.8 %multiply_convert_fusion = bf16[128,256,512]{2,1,0:T(8,128)(2,1)} fusion(f32[128,256,512]{2,1,0:T(8,128)} %get-tuple-element.80, f32[128,256,128]{1,2,0:T(8,128)} %fusion.68, f32[512,128]{1,0:T(8,128)S(1)} %copy-done.26), kind=kOutput, calls=%fused_computation | convolution fusion | flops 4450222080 | bytes 117702656 | tf_op jit(solution)/shard_map/ijd,cd->ijc/dot_general | solution.py:42
  1033.1 27.7 %fusion.89 = (f32[128]{0:T(128)}, f32[128,256,128]{1,2,0:T(8,128)}) fusion(bf16[128,256,512]{2,1,0:T(8,128)(2,1)} %multiply_convert_fusion, f32[128,512]{1,0:T(8,128)S(1)} %copy-done.29), kind=kOutput, calls=%fused_computation.168 | convolution fusion | flops 4299227136 | bytes 50594304 | tf_op jit(solution)/shard_map/ijd,cd->ijc/dot_general | solution.py:42
  1078.3 21.5 %multiply_reduce_fusion = (f32[128]{0:T(128)}, f32[128,256]{1,0:T(8,128)S(1)}, f32[128,256]{1,0:T(8,128)S(1)}) fusion(f32[128,256,128]{2,1,0:T(8,128)} %copy.75, f32[128,256,128]{2,1,0:T(8,128)} %get-tuple-element.69, f32[128,256]{1,0:T(8,128)S(1)} %copy-done.13, f32[128,256]{1,0:T(8,128)S(1)} %copy-done.11, f32[128]{0:T(128)S(1)} %copy-done.49), kind=kLoop, calls=%fused_computation.31 | loop fusion | flops 33488768 | bytes 34079744 | tf_op jit(solution)/shard_map/reduce_sum | solution.py:183
  1099.9 23.0 %multiply_convert_fusion.8 = bf16[128,256,128]{2,1,0:T(8,128)(2,1)S(1)} fusion(f32[128,256,128]{2,1,0:T(8,128)} %copy.76, f32[128,256,128]{2,1,0:T(8,128)} %get-tuple-element.69, f32[128,256,128]{2,1,0:T(8,128)} %copy.75, f32[128,256]{1,0:T(8,128)S(1)} %get-tuple-element.87, f32[128,256]{1,0:T(8,128)S(1)} %get-tuple-element.88, f32[128]{0:T(128)S(1)} %copy-done.49, ...), kind=kLoop, calls=%fused_computation.41 | loop fusion | flops 54525952 | bytes 76022272 | tf_op jit(solution)/shard_map/convert_element_type | solution.py:147
  1175.8 29.4 %all-gather.5.cloned.1.call-done = bf16[128,512,128]{1,0,2:T(8,128)(2,1)} async-done(((bf16[128,256,128]{1,0,2:T(8,128)(2,1)}), bf16[128,512,128]{1,0,2:T(8,128)(2,1)}) %all-gather.5.cloned.1.call-update) | async-done | bytes 16777232 | tf_op jit(solution)/shard_map/all_gather | solution.py:154
  1205.1 23.3 %convert_bitcast_fusion = bf16[512,256,128]{0,1,2:T(8,128)(2,1)} fusion(bf16[128,256,128]{0,1,2:T(8,128)(2,1)} %copy.80, bf16[128,512,128]{1,0,2:T(8,128)(2,1)} %all-gather.5.cloned.1.call-done), kind=kOutput, calls=%fused_computation.3 | convolution fusion | flops 4311744512 | bytes 58720256 | tf_op jit(solution)/shard_map/ijc,ikc->jkc/dot_general | solution.py:158
  1228.4 47.7 %copy.81 = bf16[512,256,128]{2,1,0:T(8,128)(2,1)} copy(bf16[512,256,128]{0,1,2:T(8,128)(2,1)} %convert_bitcast_fusion) | data formatting | bytes 67108864 | tf_op jit(solution)/shard_map/convert_element_type | solution.py:158
  1315.1 22.6 %convolution_bitcast_fusion.1 = f32[128,512]{1,0:T(8,128)} fusion(bf16[128,256,512]{2,1,0:T(8,128)(2,1)} %multiply_convert_fusion, f32[128,256,128]{2,1,0:T(8,128)} %get-tuple-element.69, f32[128]{0:T(128)S(1)} %copy-done.53, f32[128]{0:T(128)S(1)} %copy-done.49, f32[128,256]{1,0:T(8,128)S(1)} %copy-done.13, f32[128,256]{1,0:T(8,128)S(1)} %copy-done.11), kind=kOutput, calls=%fused_computation.78 | convolution fusion | flops 4315938816 | bytes 50856960 | tf_op jit(solution)/shard_map/ijc,ijd->cd/dot_general | solution.py:38
  1337.7 25.3 %fusion.90 = f32[128,256,128]{2,1,0:T(8,128)} fusion(bf16[512,256,128]{0,1,2:T(8,128)(2,1)} %copy.78, bf16[128,512,128]{1,0,2:T(8,128)(2,1)} %all-gather.5.cloned.1.call-done), kind=kOutput, calls=%fused_computation.169 | convolution fusion | flops 4294967296 | bytes 67108864 | tf_op jit(solution)/shard_map/ijc,jkc->ikc/dot_general | solution.py:155
  1415.2 414.3 %reduce-scatter.7.cloned.1.call-done = bf16[128,256,128]{2,1,0:T(8,128)(2,1)} async-done(((bf16[512,256,128]{2,1,0:T(8,128)(2,1)}), bf16[128,256,128]{2,1,0:T(8,128)(2,1)}) %reduce-scatter.7.cloned.1.call-update) | async-done | bytes 8388624
  1865.1 24.8 %fusion.24 = bf16[128,256,640]{2,1,0:T(8,128)(2,1)} fusion(bf16[128,256,640]{2,1,0:T(8,128)(2,1)} %fusion.23, f32[128,256,128]{2,1,0:T(8,128)} %get-tuple-element.78, f32[128,256,128]{2,1,0:T(8,128)} %copy.76, f32[128,256,128]{2,1,0:T(8,128)S(1)} %bitcast.152, f32[128,256,128]{2,1,0:T(8,128)} %copy.75, f32[128,256]{1,0:T(8,128)S(1)} %copy-done.23, ...), kind=kLoop, calls=%fused_computation.60 | loop fusion | flops 67108864 | bytes 92799488 | tf_op jit(solution)/shard_map/concatenate | solution.py:165
  1890.0 23.7 %fusion.36 = f32[128,640]{1,0:T(8,128)} fusion(bf16[128,256,640]{2,1,0:T(8,128)(2,1)} %fusion.24, bf16[1,128,256,128]{3,2,1,0:T(8,128)(2,1)} %param.24, f32[128]{0:T(128)S(1)} %copy-done.62, f32[128]{0:T(128)S(1)} %copy-done.64, f32[128,256]{1,0:T(8,128)S(1)} %copy-done.32, f32[128,256]{1,0:T(8,128)S(1)} %copy-done.19), kind=kOutput, calls=%fused_computation.76 | convolution fusion | flops 5393874944 | bytes 50922496 | tf_op jit(solution)/shard_map/ijc,ijd->cd/dot_general | solution.py:38
  1931.9 41.7 %all-reduce.1 = (f32[128,64]{0,1:T(8,128)S(1)}, f32[6,128]{1,0:T(8,128)S(1)}, f32[64]{0:T(128)S(1)}, f32[]{:T(128)}) all-reduce(f32[128,64]{0,1:T(8,128)S(1)} %copy-done.45, f32[6,128]{1,0:T(8,128)S(1)} %stack.27, f32[64]{0:T(128)S(1)} %copy-done.72, ...), channel_id=1, replica_groups=mesh['crop'=4,'row'=4,'col'=2] {'crop','row','col'}, use_global_device_ids=true, to_apply=%region_24.25 | all-reduce | flops 9025 | bytes 72200 | tf_op jit(solution)/shard_map/psum | solution.py:187
  1975.5 69.9 %all-reduce.5.cloned.1.call-done = (f32[128,640]{1,0:T(8,128)}, f32[128,128]{1,0:T(8,128)}, f32[128,512]{1,0:T(8,128)}, f32[512,128]{1,0:T(8,128)}) async-done(((f32[128,640]{1,0:T(8,128)}, f32[128,128]{1,0:T(8,128)}, f32[128,512]{1,0:T(8,128)}, f32[512,128]{1,0:T(8,128)}), (f32[128,640]{1,0:T(8,128)}, f32[128,128]{1,0:T(8,128)}, f32[128,512]{1,0:T(8,128)}, ...) | async-done | bytes 917520 | tf_op jit(solution)/shard_map/psum | solution.py:187
  (228 shorter events, 351.6 us)
Async XLA Ops:
  7.2 643.4 %all-gather.3.cloned.1.call-start = ((), (), s32[]{:S(2)}) async-start(), calls=%async_computation.2 | async-start | bytes 41943040 | tf_op jit(solution)/shard_map/all_gather | solution.py:108
  9.4 773.4 %copy-start.59 = (f32[128]{0:T(128)}, f32[128]{0:T(128)S(1)}, u32[]{:S(2)}) copy-start(f32[128]{0:T(128)S(1)} %get-tuple-element.74) | copy-start | bytes 1540
  86.4 682.1 %reduce-scatter.5.cloned.1.call-start = ((), (), s32[]{:S(2)}) async-start(), calls=%async_computation.3 | async-start | bytes 50331648 | tf_op jit(solution)/shard_map/reduce_scatter | solution.py:111
  724.9 480.2 %all-gather.5.cloned.1.call-start = ((), (), s32[]{:S(2)}) async-start(), calls=%async_computation.4 | async-start | bytes 25165824 | tf_op jit(solution)/shard_map/all_gather | solution.py:154
  1175.7 653.8 %reduce-scatter.7.cloned.1.call-start = ((), (), s32[]{:S(2)}) async-start(), calls=%async_computation.5 | async-start | bytes 41943040
  1276.1 769.3 %all-reduce.5.cloned.1.call-start = ((), (), s32[]{:S(2)}) async-start(), calls=%async_computation.6 | async-start | bytes 1835008 | tf_op jit(solution)/shard_map/psum | solution.py:187
  1913.7 142.6 %copy-start.55 = (f32[64]{0:T(128)S(1)}, f32[64]{0:T(128)}, u32[]{:S(2)}) copy-start(f32[64]{0:T(128)} %param.33) | copy-start | bytes 772
  1913.8 143.1 %copy-start.56 = (f32[6,128]{1,0:T(8,128)S(1)}, f32[6,128]{1,0:T(8,128)}, u32[]{:S(2)}) copy-start(f32[6,128]{1,0:T(8,128)} %param.32) | copy-start | bytes 9220
  1913.8 143.1 %copy-start.65 = (f32[6,128]{1,0:T(8,128)S(1)}, f32[6,128]{1,0:T(8,128)}, u32[]{:S(2)}) copy-start(f32[6,128]{1,0:T(8,128)} %param.39) | copy-start | bytes 9220
  1913.8 143.1 %copy-start.66 = (f32[6,128]{1,0:T(8,128)S(1)}, f32[6,128]{1,0:T(8,128)}, u32[]{:S(2)}) copy-start(f32[6,128]{1,0:T(8,128)} %param.46) | copy-start | bytes 9220
  1913.8 143.7 %copy-start.37 = (f32[128,64]{0,1:T(8,128)S(1)}, f32[128,64]{0,1:T(8,128)}, u32[]{:S(2)}) copy-start(f32[128,64]{0,1:T(8,128)} %param.31) | copy-start | bytes 98308
  1913.8 143.7 %copy-start.50 = (f32[128,64]{0,1:T(8,128)S(1)}, f32[128,64]{0,1:T(8,128)}, u32[]{:S(2)}) copy-start(f32[128,64]{0,1:T(8,128)} %param.38) | copy-start | bytes 98308
  1913.8 143.7 %copy-start.51 = (f32[128,64]{0,1:T(8,128)S(1)}, f32[128,64]{0,1:T(8,128)}, u32[]{:S(2)}) copy-start(f32[128,64]{0,1:T(8,128)} %param.45) | copy-start | bytes 98308
  1913.8 144.4 %copy-start.40 = (f32[128,128]{1,0:T(8,128)S(1)}, f32[128,128]{1,0:T(8,128)}, u32[]{:S(2)}) copy-start(f32[128,128]{1,0:T(8,128)} %param.28) | copy-start | bytes 196612
  1913.9 144.4 %copy-start.46 = (f32[128,128]{1,0:T(8,128)S(1)}, f32[128,128]{1,0:T(8,128)}, u32[]{:S(2)}) copy-start(f32[128,128]{1,0:T(8,128)} %param.35) | copy-start | bytes 196612
  1913.9 144.4 %copy-start.47 = (f32[128,128]{1,0:T(8,128)S(1)}, f32[128,128]{1,0:T(8,128)}, u32[]{:S(2)}) copy-start(f32[128,128]{1,0:T(8,128)} %param.42) | copy-start | bytes 196612
  1913.9 145.9 %copy-start.27 = (f32[512,128]{1,0:T(8,128)S(1)}, f32[512,128]{1,0:T(8,128)}, u32[]{:S(2)}) copy-start(f32[512,128]{1,0:T(8,128)} %param.30) | copy-start | bytes 786436
  1913.9 145.9 %copy-start.41 = (f32[512,128]{1,0:T(8,128)S(1)}, f32[512,128]{1,0:T(8,128)}, u32[]{:S(2)}) copy-start(f32[512,128]{1,0:T(8,128)} %param.37) | copy-start | bytes 786436
  1913.9 145.9 %copy-start.42 = (f32[512,128]{1,0:T(8,128)S(1)}, f32[512,128]{1,0:T(8,128)}, u32[]{:S(2)}) copy-start(f32[512,128]{1,0:T(8,128)} %param.44) | copy-start | bytes 786436
  1913.9 147.8 %copy-start.30 = (f32[128,512]{1,0:T(8,128)S(1)}, f32[128,512]{1,0:T(8,128)}, u32[]{:S(2)}) copy-start(f32[128,512]{1,0:T(8,128)} %param.29) | copy-start | bytes 786436
  1913.9 147.8 %copy-start.43 = (f32[128,512]{1,0:T(8,128)S(1)}, f32[128,512]{1,0:T(8,128)}, u32[]{:S(2)}) copy-start(f32[128,512]{1,0:T(8,128)} %param.36) | copy-start | bytes 786436
  1913.9 147.8 %copy-start.44 = (f32[128,512]{1,0:T(8,128)S(1)}, f32[128,512]{1,0:T(8,128)}, u32[]{:S(2)}) copy-start(f32[128,512]{1,0:T(8,128)} %param.43) | copy-start | bytes 786436
  1914.0 149.8 %copy-start.34 = (f32[128,640]{1,0:T(8,128)S(1)}, f32[128,640]{1,0:T(8,128)}, u32[]{:S(2)}) copy-start(f32[128,640]{1,0:T(8,128)} %param.34) | copy-start | bytes 983044
  1914.0 149.7 %copy-start.35 = (f32[128,640]{1,0:T(8,128)S(1)}, f32[128,640]{1,0:T(8,128)}, u32[]{:S(2)}) copy-start(f32[128,640]{1,0:T(8,128)} %param.41) | copy-start | bytes 983044
  (61 other events, 1636.4 us)
Sparse Core Ops, SparseCore 0:
  86.5 564.0 all-gather.2
  725.0 43.3 reduce-scatter.4
  1175.8 29.2 all-gather.4
  1276.2 553.2 reduce-scatter.6
  1913.8 131.5 all-reduce.4
where the time goes:
time: 2090 us; the launch traced here: 2070 us
  waiting for transfers between devices  1110 us (53%)
  matrix products  398 us (19%)
  other arithmetic  274 us (13%)
  local copies, waits for them, and re-layouts  190 us (9%)
  blocking collectives  82.5 us (4%)
  between operations  21 us (1%)
    all_gather x1, waiting for transfers between devices, on_device(): strips = lax.all_gather(right_vals, 'row', axis=0, tiled=True)  551 us
    unnamed x6, waiting for transfers between devices  414 us
    dot_general x5, matrix products, linear(): jnp.einsum('ijc,cd->ijd', values, weight, preferred_element_type=jnp.floa...  131 us
    dot_general x5, matrix products, transposed(): jnp.einsum('ijd,cd->ijc', grad, weight, preferred_element_type=jnp.float32)  106 us
    dot_general x5, matrix products, weight_grad(): jnp.einsum('ijc,ijd->cd', values, grad, preferred_element_type=jnp.float32)  85.3 us
    psum x1, waiting for transfers between devices, on_device(): lax.psum((grad_in, grad_out, grad_t1, grad_t2, grad_dist, grad_norms, gra...  69.9 us
    unnamed x5, other arithmetic  68 us
    dot_general x3, local copies, waits for them, and re-layouts, transposed(): jnp.einsum('ijd,cd->ijc', grad, weight, preferred_element_type=jnp.float32)  52.6 us
  transfers between devices with their start and end apart: 5, of which 5 were waited for; matrix products, arithmetic and copies ran while one was open for 8% of the time, Pallas kernels for 0%

commit v1 on v0

--- a/solution.py
+++ b/solution.py
@@ -1,6 +1,10 @@
+import functools
+
 import jax
 import jax.numpy as jnp
 from jax import lax
+from jax.experimental import pallas as pl
+from jax.experimental.pallas import tpu as pltpu
 from jax.sharding import PartitionSpec as P
 
 STEP = 10
@@ -54,7 +58,7 @@
     return (stepped, first_new, second_new)
 
 
-def on_device(
+def on_device_general(
     pair_acts,
     residue_mask,
     dist_bins,
@@ -232,59 +236,594 @@
     )
 
 
+F32 = jnp.float32
+BF16 = jnp.bfloat16
+NT = (((1,), (1,)), ((), ()))
+NN = (((1,), (0,)), ((), ()))
+TN = (((0,), (0,)), ((), ()))
+VMEM_LIMIT = 56 * 1024 * 1024
+
+
+def dot(left, right, dims=NN):
+    return lax.dot_general(left, right, dims, preferred_element_type=F32)
+
+
+def sigmoid(values):
+    return 0.5 * jnp.tanh(0.5 * values) + 0.5
+
+
+def column_stats(values):
+    center = values - jnp.mean(values, 0, keepdims=True)
+    rstd = lax.rsqrt(jnp.mean(center * center, 0, keepdims=True) + NORM_EPS)
+    return center * rstd, rstd
+
+
+def column_back(grad, normed, rstd):
+    return rstd * (
+        grad
+        - jnp.mean(grad, 0, keepdims=True)
+        - normed * jnp.mean(grad * normed, 0, keepdims=True)
+    )
+
+
+def widen(param, lanes):
+    return jnp.concatenate([param] * (lanes // param.shape[1]), 1)
+
+
+def spread_rows(scratch, block):
+    channels, rows, lanes = block.shape
+    for part in range(lanes // 128):
+        scratch[part] = (
+            block[:, :, 128 * part : 128 * part + 128].astype(F32).reshape(channels * rows, 128)
+        )
+
+
+def take_row(scratch, row, channels, rows):
+    parts = [
+        scratch[part, pl.ds(row, channels, stride=rows), :] for part in range(scratch.shape[0])
+    ]
+    return parts[0] if len(parts) == 1 else jnp.concatenate(parts, 1)
+
+
+def put_row(scratch, row, values, rows):
+    for part in range(scratch.shape[0]):
+        scratch[part, pl.ds(row, values.shape[0], stride=rows), :] = values[
+            :, 128 * part : 128 * part + 128
+        ]
+
+
+def gather_rows(scratch, out_ref):
+    channels, rows, _ = out_ref.shape
+    for part in range(scratch.shape[0]):
+        out_ref[:, :, 128 * part : 128 * part + 128] = (
+            scratch[part].reshape(channels, rows, 128).astype(out_ref.dtype)
+        )
+
+
+def call(kernel, grid, scalars, ins, outs, scratch, flops, name):
+    moved = sum(a.size * a.dtype.itemsize for a, _, _ in ins)
+    moved += sum(jnp.dtype(t).itemsize * functools.reduce(lambda x, y: x * y, s) for s, t, _, _ in outs)
+    return pl.pallas_call(
+        kernel,
+        grid_spec=pltpu.PrefetchScalarGridSpec(
+            num_scalar_prefetch=len(scalars),
+            grid=grid,
+            in_specs=[pl.BlockSpec(block, index) for _, block, index in ins],
+            out_specs=[pl.BlockSpec(block, index) for _, _, block, index in outs],
+            scratch_shapes=scratch,
+        ),
+        out_shape=[jax.ShapeDtypeStruct(shape, dtype) for shape, dtype, _, _ in outs],
+        compiler_params=pltpu.CompilerParams(vmem_limit_bytes=VMEM_LIMIT),
+        cost_estimate=pl.CostEstimate(flops=int(flops), bytes_accessed=int(moved), transcendentals=0),
+        name=name,
+    )(*scalars, *[a for a, _, _ in ins])
+
+
+ROWS = 16
+
+
+def project_kernel(row_mask, acts_ref, w_ref, ln_ref, col_ref, a_ref, b_ref, acts_s, a_s, b_s):
+    first = pl.program_id(0) * ROWS
+    width = a_ref.shape[0]
+    spread_rows(acts_s, acts_ref[...])
+
+    def one(row, carry):
+        values = take_row(acts_s, row, acts_ref.shape[0], ROWS)
+        lanes = values.shape[1]
+        normed, _ = column_stats(values)
+        low = (normed * widen(ln_ref[0], lanes) + widen(ln_ref[1], lanes)).astype(BF16)
+        proj = dot(w_ref[...], low)
+        mask = col_ref[...] * row_mask[first + row]
+        put_row(a_s, row, proj[:width] * sigmoid(proj[width : 2 * width]) * mask, ROWS)
+        put_row(b_s, row, proj[2 * width : 3 * width] * sigmoid(proj[3 * width :]) * mask, ROWS)
+        return carry
+
+    lax.fori_loop(0, ROWS, one, 0, unroll=4)
+    gather_rows(a_s, a_ref)
+    gather_rows(b_s, b_ref)
+
+
+def fixed(*zeros):
+    return lambda i, *_: zeros
+
+
+def project(acts, w_proj, ln_wide, row_mask, col_mask):
+    chans, rows, lanes = acts.shape
+    block = (chans, ROWS, lanes)
+    mid = lambda i, *_: (0, i, 0)
+    out = ((chans, rows, lanes), BF16, block, mid)
+    staged = pltpu.VMEM((lanes // 128, chans * ROWS, 128), F32)
+    return call(
+        project_kernel,
+        (rows // ROWS,),
+        [row_mask],
+        [
+            (acts, block, mid),
+            (w_proj, w_proj.shape, fixed(0, 0)),
+            (ln_wide, ln_wide.shape, fixed(0, 0, 0)),
+            (col_mask, col_mask.shape, fixed(0, 0)),
+        ],
+        [out, out],
+        [staged, staged, staged],
+        2 * rows * lanes * w_proj.size * 4,
+        "project",
+    )
+
+
+CHANS = 8
+
+
+def triangle_kernel(flag, a0, a1, b0, b1, keep_ref, send_ref):
+    kept_first = flag[0] == 0
+    for chan in range(CHANS):
+        rows = jnp.concatenate([a0[chan], a1[chan]], 0)
+        one, two = dot(b0[chan], rows, NT), dot(b1[chan], rows, NT)
+        keep_ref[chan] = jnp.where(kept_first, one, two)
+        send_ref[chan] = jnp.where(kept_first, two, one).astype(BF16)
+
+
+def triangle(which, a, b):
+    chans, half, lanes = a[0].shape
+    lead = lambda i, *_: (i, 0, 0)
+    block = (CHANS, half, lanes)
+    out = (chans, half, 2 * half)
+    return call(
+        triangle_kernel,
+        (chans // CHANS,),
+        [which],
+        [(v, block, lead) for v in (*a, *b)],
+        [(out, F32, (CHANS, half, 2 * half), lead), (out, BF16, (CHANS, half, 2 * half), lead)],
+        [],
+        2 * chans * half * 2 * half * 2 * lanes * 4,
+        "triangle",
+    )
+
+
+GROUP = 2
+
+
+def pair_kernel(
+    place, x_keep, x_recv, acts_ref, code_ref, scale_ref, ln_ref, w_outT, w_out, w_ogT, w_t1T, w_t1,
+    w_t2T, w_t2, w_distT, w_dist, bias_ref,
+    dx_ref, g_t1, g_t2, g_out, g_og, g_dist, g_norm, g_bias, loss_ref,
+    x_s, acts_s, dx_s,
+):
+    chans = acts_ref.shape[0]
+    lanes = 128 * GROUP
+
+    @pl.when(pl.program_id(0) == 0)
+    def _():
+        for ref in (g_t1, g_t2, g_out, g_og, g_dist, g_norm, g_bias, loss_ref):
+            ref[...] = jnp.zeros_like(ref)
+
+    x_s[0] = (x_keep[...] + x_recv[...].astype(F32)).reshape(chans * ROWS, 128)
+    spread_rows(acts_s, acts_ref[...])
+    inverse = scale_ref[0:1, :]
+    param = [widen(ln_ref[index], lanes) for index in range(6)]
+    bins = w_distT.shape[0]
+    bin_index = lax.broadcasted_iota(jnp.int32, (bins, lanes), 0)
+
+    def fold(values):
+        return sum(values[:, 128 * part : 128 * part + 128] for part in range(GROUP))
+
+    def group(step, carry):
+        first = step * GROUP
+        cat = lambda pieces: jnp.concatenate(pieces, 1)
+        x = cat([take_row(x_s, first + u, chans, ROWS) for u in range(GROUP)])
+        acts = cat([take_row(acts_s, first + u, chans, ROWS) for u in range(GROUP)])
+        code = cat([code_ref[pl.ds(first + u, 1), :] for u in range(GROUP)])
+        normed_two, rstd_two = column_stats(x)
+        tri = (normed_two * param[2] + param[3]).astype(BF16)
+        out = dot(w_outT[...], tri)
+        normed_one, _ = column_stats(acts)
+        low = (normed_one * param[0] + param[1]).astype(BF16)
+        gate = sigmoid(dot(w_ogT[...], low))
+        z1 = acts + gate * out
+        normed_three, rstd_three = column_stats(z1)
+        trans = (normed_three * param[4] + param[5]).astype(BF16)
+        pre = dot(w_t1T[...], trans)
+        sig = sigmoid(pre)
+        act = pre * sig
+        hidden = act.astype(BF16)
+        slope = sig * (1.0 + (pre - act))
+        final = (z1 + dot(w_t2T[...], hidden)).astype(BF16)
+        logits = dot(w_distT[...], final) + widen(bias_ref[...], lanes)
+        top = jnp.max(logits, 0, keepdims=True)
+        powers = jnp.exp(logits - top)
+        total = jnp.sum(powers, 0, keepdims=True)
+        present = (code >= 0).astype(F32)
+        hot = bin_index == code
+        picked = jnp.sum(jnp.where(hot, logits, 0.0), 0, keepdims=True)
+        loss_ref[...] += fold(present * (jnp.log(total) + top) - picked)
+        weight = present * widen(inverse, lanes)
+        d_logits = (
+            powers * (weight / total) - jnp.where(hot, widen(inverse, lanes), 0.0)
+        ).astype(BF16)
+        g_dist[...] += dot(d_logits, final, NT)
+        g_bias[...] += fold(d_logits.astype(F32))
+        d_final = dot(w_dist[...], d_logits)
+        d_trans = d_final.astype(BF16)
+        g_t2[...] += dot(hidden, d_trans, NT)
+        d_pre = (dot(w_t2[...], d_trans) * slope).astype(BF16)
+        g_t1[...] += dot(d_pre, trans, NT)
+        d_tn = dot(w_t1[...], d_pre)
+        g_norm[2] += fold(d_tn * normed_three)
+        g_norm[3] += fold(d_tn)
+        d_z1 = d_final + column_back(d_tn * param[4], normed_three, rstd_three)
+        d_gated = d_z1 * gate
+        d_out = d_gated.astype(BF16)
+        d_og = (d_gated * out * (1.0 - gate)).astype(BF16)
+        g_out[...] += dot(d_out, tri, NT)
+        g_og[...] += dot(d_og, jnp.concatenate([low, normed_one.astype(BF16)], 0), NT)
+        g_norm[4] += fold(d_og.astype(F32))
+        d_xn = dot(w_out[...], d_out)
+        g_norm[0] += fold(d_xn * normed_two)
+        g_norm[1] += fold(d_xn)
+        d_x = column_back(d_xn * param[2], normed_two, rstd_two)
+        for u in range(GROUP):
+            put_row(dx_s, first + u, d_x[:, 128 * u : 128 * u + 128], ROWS)
+        return carry
+
+    lax.fori_loop(0, ROWS // GROUP, group, 0)
+    gather_rows(dx_s, dx_ref)
+
+
+def pair_block(place, x_keep, x_recv, acts_kj, code, scale, ln_wide, weights, bias):
+    chans, rows, lanes = x_keep.shape
+    block = (chans, ROWS, lanes)
+    mid = lambda i, *_: (0, i, 0)
+
+    def where(i, spot):
+        return 8 * ((i // 2) ^ spot[0]) + 2 * spot[1] + i % 2
+
+    full = [(w, w.shape, fixed(*([0] * w.ndim))) for w in (scale, ln_wide, *weights, bias)]
+    sums = [(512, 128), (512, 128), (128, 128), (128, 256), (64, 128), (5, 128, 128), (64, 128), (1, 128)]
+    return call(
+        pair_kernel,
+        (rows // ROWS,),
+        [place],
+        [
+            (x_keep, block, mid),
+            (x_recv, block, mid),
+            (acts_kj, block, lambda i, spot: (0, where(i, spot), 0)),
+            (code, (ROWS, lanes), lambda i, spot: (where(i, spot), 0)),
+        ]
+        + full,
+        [((chans, rows, lanes), BF16, block, mid)]
+        + [(s, F32, s, fixed(*([0] * len(s)))) for s in sums],
+        [pltpu.VMEM((1, chans * ROWS, 128), F32)] * 3,
+        rows * lanes * 35e9 / 32768 * 4,
+        "pair",
+    )
+
+
+def right_back_kernel(flag, dx_own, dx_other, a0, a1, out0, out1):
+    own_first = flag[0] == 0
+    for chan in range(CHANS):
+        rows = jnp.concatenate([a0[chan], a1[chan]], 0)
+        own, other = dx_own[chan], dx_other[chan]
+        both = jnp.concatenate(
+            [jnp.where(own_first, own, other), jnp.where(own_first, other, own)], 0
+        )
+        grads = dot(both, rows).astype(BF16)
+        half = out0.shape[1]
+        out0[chan] = grads[:half]
+        out1[chan] = grads[half:]
+
+
+def right_back(which, dx_own, dx_other, a):
+    chans, half, lanes = a[0].shape
+    lead = lambda i, *_: (i, 0, 0)
+    out = ((chans, half, lanes), BF16, (CHANS, half, lanes), lead)
+    return call(
+        right_back_kernel,
+        (chans // CHANS,),
+        [which],
+        [(v, (CHANS, half, 2 * half), lead) for v in (dx_own, dx_other)]
+        + [(v, (CHANS, half, lanes), lead) for v in a],
+        [out, out],
+        [],
+        2 * chans * 4 * half * half * lanes * 4,
+        "right_back",
+    )
+
+
+def left_back_kernel(flag, *refs):
+    owns, others, firsts, seconds = refs[:4], refs[4:8], refs[8:12], refs[12:16]
+    out0, out1 = refs[16:]
+    half = out0.shape[1]
+    for chan in range(CHANS):
+        total = None
+        for pair in range(2):
+            own_first = flag[0] == pair
+            grads, values = [], []
+            for q in (2 * pair, 2 * pair + 1):
+                own, other = owns[q][chan], others[q][chan]
+                grads += [jnp.where(own_first, own, other), jnp.where(own_first, other, own)]
+                values += [firsts[q][chan], seconds[q][chan]]
+            term = dot(jnp.concatenate(grads, 0), jnp.concatenate(values, 0), TN)
+            total = term if total is None else total + term
+        total = total.astype(BF16)
+        out0[chan] = total[:half]
+        out1[chan] = total[half:]
+
+
+def left_back(which, owns, others, firsts, seconds):
+    chans, half, lanes = firsts[0].shape
+    lead = lambda i, *_: (i, 0, 0)
+    out = ((chans, half, lanes), BF16, (CHANS, half, lanes), lead)
+    return call(
+        left_back_kernel,
+        (chans // CHANS,),
+        [which],
+        [(v, (CHANS, half, 2 * half), lead) for v in (*owns, *others)]
+        + [(v, (CHANS, half, lanes), lead) for v in (*firsts, *seconds)],
+        [out, out],
+        [],
+        2 * chans * 16 * half * half * lanes * 4,
+        "left_back",
+    )
+
+
+def input_back_kernel(row_mask, acts_ref, w_ref, ln_ref, col_ref, *rest):
+    grads, (g_ref, sum_ref), (acts_s, grad_s) = rest[:-4], rest[-4:-2], rest[-2:]
+    first = pl.program_id(0) * ROWS
+    chans = acts_ref.shape[0]
+    width = grads[0].shape[0]
+
+    @pl.when(pl.program_id(0) == 0)
+    def _():
+        g_ref[...] = jnp.zeros_like(g_ref)
+        sum_ref[...] = jnp.zeros_like(sum_ref)
+
+    spread_rows(acts_s, acts_ref[...])
+    total = grads[0][...].astype(F32)
+    for ref in grads[1:]:
+        total = total + ref[...].astype(F32)
+    spread_rows(grad_s, total)
+
+    def one(row, carry):
+        values = take_row(acts_s, row, chans, ROWS)
+        lanes = values.shape[1]
+        normed, _ = column_stats(values)
+        low = (normed * widen(ln_ref[0], lanes) + widen(ln_ref[1], lanes)).astype(BF16)
+        proj = dot(w_ref[...], low)
+        gate = sigmoid(proj[width:])
+        d_value = take_row(grad_s, row, width, ROWS) * (col_ref[...] * row_mask[first + row]) * gate
+        d_gate = d_value * proj[:width] * (1.0 - gate)
+        d_proj = jnp.concatenate([d_value.astype(BF16), d_gate.astype(BF16)], 0)
+        g_ref[...] += dot(d_proj, jnp.concatenate([low, normed.astype(BF16)], 0), NT)
+        wide = d_proj.astype(F32)
+        sum_ref[...] += sum(wide[:, 128 * u : 128 * u + 128] for u in range(lanes // 128))
+        return carry
+
+    lax.fori_loop(0, ROWS, one, 0, unroll=4)
+
+
+def input_back(acts, w_part, ln_wide, row_mask, col_mask, grads):
+    chans, rows, lanes = acts.shape
+    block = (chans, ROWS, lanes)
+    mid = lambda i, *_: (0, i, 0)
+    staged = pltpu.VMEM((lanes // 128, chans * ROWS, 128), F32)
+    depth = w_part.shape[0]
+    return call(
+        input_back_kernel,
+        (rows // ROWS,),
+        [row_mask],
+        [
+            (acts, block, mid),
+            (w_part, w_part.shape, fixed(0, 0)),
+            (ln_wide, ln_wide.shape, fixed(0, 0, 0)),
+            (col_mask, col_mask.shape, fixed(0, 0)),
+        ]
+        + [(v, block, mid) for v in grads],
+        [((depth, 2 * chans), F32, (depth, 2 * chans), fixed(0, 0)), ((depth, 128), F32, (depth, 128), fixed(0, 0))],
+        [staged, staged],
+        2 * rows * lanes * w_part.size * 3 * 4,
+        "input_back",
+    )
+
+
+def on_device_planes(
+    pair_acts, residue_mask, dist_bins, w_in, w_out, w_t1, w_t2, w_dist, norm_params, dist_bias, *moments
+):
+    firsts, seconds = moments[:7], moments[7:]
+    spot = lax.axis_index("crop")
+    level = lax.axis_index("row")
+    side = lax.axis_index("col")
+    rows, cols, chans = pair_acts.shape[1:]
+    width = w_out.shape[0]
+    sub = rows // 4
+
+    def over_x(v):
+        return lax.ppermute(v, "crop", [(g, g ^ 1) for g in range(4)])
+
+    def over_y(v):
+        return lax.ppermute(v, "crop", [(g, g ^ 2) for g in range(4)])
+
+    def over_core(v):
+        return lax.ppermute(v, "col", [(0, 1), (1, 0)])
+
+    def to_plane(v, label):
+        start = (spot ^ level ^ label) * sub
+        piece = lax.dynamic_slice_in_dim(v, start, sub, v.ndim - 2)
+        one = [(c * 4 + z, (c ^ label ^ z) * 4 + z) for c in range(4) for z in range(4)]
+        two = [(g * 4 + z, g * 4 + (g ^ label ^ z)) for g in range(4) for z in range(4)]
+        return lax.ppermute(lax.ppermute(piece, ("crop", "row"), one), ("crop", "row"), two)
+
+    all_masks = lax.all_gather(residue_mask[0], "crop", axis=0).astype(F32)
+    pair_total = jnp.sum(jnp.square(jnp.sum(all_masks, -1)))
+    mask_vals = lax.dynamic_index_in_dim(all_masks, level, 0, keepdims=False)
+    acts_major = jnp.transpose(pair_acts[0], (2, 0, 1))
+    pieces = [to_plane(acts_major, label) for label in range(4)]
+    acts = [jnp.concatenate(pieces[2 * h : 2 * h + 2], 1) for h in range(2)]
+    acts_kj = jnp.swapaxes(jnp.concatenate(acts, 1), 1, 2)
+    bins = jnp.concatenate([to_plane(dist_bins[0], label) for label in range(4)], 0)
+    row_mask = jnp.concatenate(
+        [
+            lax.dynamic_slice_in_dim(mask_vals, rows * (spot ^ level ^ label) + sub * spot, sub)
+            for label in range(4)
+        ]
+    )
+    col_mask = lax.dynamic_slice_in_dim(mask_vals, cols * side, cols)
+    code = jnp.where((col_mask[:, None] * row_mask[None, :]) > 0, bins.T, -1)
+
+    low_in, low_out, low_t1, low_t2, low_dist = [
+        weight.astype(BF16) for weight in (w_in, w_out, w_t1, w_t2, w_dist)
+    ]
+    ln_wide = jnp.broadcast_to(norm_params[:, :, None], (*norm_params.shape, 128))
+    bias_wide = jnp.broadcast_to(dist_bias[:, None], (dist_bias.shape[0], 128))
+    scale_wide = jnp.full((8, 128), 1.0 / pair_total, F32)
+    col_row = col_mask[None, :]
+    half_mask = [row_mask[: 2 * sub], row_mask[2 * sub :]]
+    in_T = low_in.T
+
+    a, b_own = [], []
+    for h in range(2):
+        left, right = project(acts[h], in_T[: 4 * width], ln_wide, half_mask[h], col_row)
+        a.append(left)
+        b_own.append(right)
+    b_x = [over_x(v) for v in b_own]
+    b_y = [over_y(v) for v in b_own]
+    b_d = [over_y(b_x[0]), over_x(b_y[1])]
+    blocks = [b_own, b_x, b_y, b_d]
+
+    weights = (
+        low_out.T, low_out, in_T[4 * width :], low_t1.T, low_t1, low_t2.T, low_t2, low_dist.T, low_dist,
+    )
+    dx_own, dx_other, sums, flags = [], [], None, []
+    keeps, sends = [], []
+    for q in range(4):
+        owner = spot ^ q
+        flags.append((side ^ (owner // 2) ^ (level // 2)).astype(jnp.int32)[None])
+        keep, send = triangle(flags[q], a, blocks[q])
+        keeps.append(keep)
+        sends.append(over_core(send))
+    for q in range(4):
+        owner = spot ^ q
+        place = jnp.stack([(owner ^ level) & 1, owner]).astype(jnp.int32)
+        d_x, *parts = pair_block(
+            place, keeps[q], sends[q], acts_kj, code, scale_wide, ln_wide, weights, bias_wide
+        )
+        dx_own.append(d_x)
+        dx_other.append(over_core(d_x))
+        sums = parts if sums is None else [u + v for u, v in zip(sums, parts)]
+    back = [right_back(flags[q], dx_own[q], dx_other[q], a) for q in range(4)]
+    own0 = [back[0][0], over_y(back[2][0])]
+    x0 = (back[1][0].astype(F32) + over_y(back[3][0]).astype(F32)).astype(BF16)
+    own0.append(over_x(x0))
+    own1 = [back[0][1], over_x(back[1][1])]
+    y1 = (back[2][1].astype(F32) + over_x(back[3][1]).astype(F32)).astype(BF16)
+    own1.append(over_y(y1))
+    d_left = left_back(
+        flags[0], dx_own, dx_other, [v[0] for v in blocks], [v[1] for v in blocks]
+    )
+    left_sums = [
+        input_back(acts[h], in_T[: 2 * width], ln_wide, half_mask[h], col_row, [d_left[h]])
+        for h in range(2)
+    ]
+    right_sums = [
+        input_back(acts[h], in_T[2 * width : 4 * width], ln_wide, half_mask[h], col_row, own)
+        for h, own in enumerate((own0, own1))
+    ]
+
+    g_t1, g_t2, g_out, g_og, g_dist, g_norm, g_bias, loss = sums
+    outer = jnp.concatenate(
+        [
+            left_sums[0][0] + left_sums[1][0],
+            right_sums[0][0] + right_sums[1][0],
+            g_og,
+        ],
+        0,
+    )
+    norm_sums = jnp.sum(g_norm, -1)
+    totals = jnp.concatenate(
+        [
+            jnp.sum(left_sums[0][1] + left_sums[1][1], -1),
+            jnp.sum(right_sums[0][1] + right_sums[1][1], -1),
+            norm_sums[4],
+        ]
+    )
+    wide_in = in_T.astype(F32)
+    grad_norms = jnp.concatenate(
+        [
+            jnp.sum(wide_in * outer[:, chans:], 0)[None],
+            jnp.sum(wide_in * totals[:, None], 0)[None],
+            norm_sums[:4],
+        ],
+        0,
+    )
+    summed = lax.psum(
+        (
+            outer[:, :chans],
+            g_out,
+            g_t1,
+            g_t2,
+            g_dist,
+            grad_norms,
+            jnp.sum(g_bias, -1),
+            jnp.sum(loss),
+        ),
+        ("crop", "row", "col"),
+    )
+    grads = (
+        summed[0].T,
+        summed[1].T,
+        summed[2].T,
+        summed[3],
+        summed[4].T,
+        summed[5],
+        summed[6],
+    )
+    squares = jnp.zeros((), F32)
+    for grad in grads:
+        squares = squares + jnp.sum(grad * grad)
+    grad_norm = jnp.sqrt(squares)
+    scale = CLIP_NORM / jnp.maximum(grad_norm, CLIP_NORM)
+    params = (w_in, w_out, w_t1, w_t2, w_dist, norm_params, dist_bias)
+    rates = (LEARN_RATE,) * 5 + (GAIN_RATE,) * 2
+    results = [
+        adamw_update(*terms, scale, rate)
+        for *terms, rate in zip(params, firsts, seconds, grads, rates)
+    ]
+    return (
+        *[r[0] for r in results],
+        *[r[1] for r in results],
+        *[r[2] for r in results],
+        summed[7],
+        pair_total,
+        grad_norm,
+    )
+
+
 def solution(mesh):
+    planes = mesh.shape["crop"] == 4 and mesh.shape["row"] == 4 and mesh.shape["col"] == 2
+    body = on_device_planes if planes else on_device_general
     in_specs = (
         P("crop", "row", "col", None),
         P("crop", None),
         P("crop", "row", "col"),
-        P(),
-        P(),
-        P(),
-        P(),
-        P(),
-        P(),
-        P(),
-        P(),
-        P(),
-        P(),
-        P(),
-        P(),
-        P(),
-        P(),
-        P(),
-        P(),
-        P(),
-        P(),
-        P(),
-        P(),
-        P(),
-    )
-    out_specs = (
-        P(),
-        P(),
-        P(),
-        P(),
-        P(),
-        P(),
-        P(),
-        P(),
-        P(),
-        P(),
-        P(),
-        P(),
-        P(),
-        P(),
-        P(),
-        P(),
-        P(),
-        P(),
-        P(),
-        P(),
-        P(),
-        P(),
-        P(),
-        P(),
-    )
+    ) + (P(),) * 21
     return jax.shard_map(
-        on_device, mesh=mesh, in_specs=in_specs, out_specs=out_specs, check_vma=False
-    )
+        body, mesh=mesh, in_specs=in_specs, out_specs=(P(),) * 24, check_vma=False
+    )

time: 2090 us -> 1410 us (0.67)
  waiting for transfers between devices: 1110 us -> 465 us
  Pallas kernels: 0 us -> 531 us
  matrix products: 398 us -> 0 us
  other arithmetic: 274 us -> 47 us
  starting transfers between devices: 0.46 us -> 208 us
  local copies, waits for them, and re-layouts: 190 us -> 67.6 us
    all_gather x2 -> x0, waiting for transfers between devices: 580 us -> none  [the longest x1 551 us: on_device(): strips = lax.all_gather(right_vals, 'row', axis=0, tiled=True)]
    pallas_call x0 -> x19, Pallas kernels: none -> 531 us  [call(): pl.pallas_call(kernel, grid_spec=pltpu.PrefetchScalarGridSpec(num_scalar_...]
    unnamed x6 -> x1, waiting for transfers between devices: 414 us -> 0.02 us
    dot_general x18 -> x0, matrix products: 398 us -> none  [the longest x5 131 us: linear(): jnp.einsum('ijc,cd->ijd', values, weight, preferred_element_type=jnp.floa...]
    ppermute x0 -> x36, waiting for transfers between devices: none -> 377 us  [the longest x6 167 us: over_y(): return lax.ppermute(v, 'crop', [(g, g ^ 2) for g in range(4)])]
    ppermute x0 -> x36, starting transfers between devices: none -> 208 us  [the longest x6 79.3 us: over_x(): return lax.ppermute(v, 'crop', [(g, g ^ 1) for g in range(4)])]
    reduce_sum x17 -> x14, other arithmetic: 97.8 us -> 11.7 us  [the longest x7 8.24 us: on_device_planes(): squares = squares + jnp.sum(grad * grad)]
    dot_general x4 -> x0, local copies, waits for them, and re-layouts: 70.3 us -> none  [the longest x3 52.6 us: transposed(): jnp.einsum('ijd,cd->ijc', grad, weight, preferred_element_type=jnp.float32)]
  transfers between devices with their start and end apart: 5 -> 37, of which waited for: 5 -> 10; matrix products, arithmetic and copies ran while one was open for 8% -> 5% of each run, Pallas kernels for 0% -> 36%
where the time goes in v1:
time: 1410 us; the launch traced here: 1400 us
  Pallas kernels  531 us (38%)
  waiting for transfers between devices  465 us (33%)
  starting transfers between devices  208 us (15%)
  local copies, waits for them, and re-layouts  67.6 us (5%)
  blocking collectives  62.1 us (4%)
  other arithmetic  47 us (3%)
  between operations  21.9 us (2%)
    pallas_call x19, Pallas kernels, call(): pl.pallas_call(kernel, grid_spec=pltpu.PrefetchScalarGridSpec(num_scalar_...  531 us
    ppermute x6, waiting for transfers between devices, over_y(): return lax.ppermute(v, 'crop', [(g, g ^ 2) for g in range(4)])  167 us
    ppermute x8, waiting for transfers between devices, to_plane(): lax.ppermute(piece, ('crop', 'row'), one)  121 us
    psum x1, waiting for transfers between devices, on_device_planes(): lax.psum((outer[:, :chans], g_out, g_t1, g_t2, g_dist, grad_norms, jnp.su...  88 us
    ppermute x6, starting transfers between devices, over_x(): return lax.ppermute(v, 'crop', [(g, g ^ 1) for g in range(4)])  79.3 us
    ppermute x8, waiting for transfers between devices, to_plane(): lax.ppermute(lax.ppermute(piece, ('crop', 'row'), one), ('crop', 'row'),...  63.8 us
    ppermute x8, starting transfers between devices, to_plane(): lax.ppermute(lax.ppermute(piece, ('crop', 'row'), one), ('crop', 'row'),...  45.5 us
    ppermute x6, starting transfers between devices, over_y(): return lax.ppermute(v, 'crop', [(g, g ^ 2) for g in range(4)])  44 us
  transfers between devices with their start and end apart: 37, of which 10 were waited for; matrix products, arithmetic and copies ran while one was open for 5% of the time, Pallas kernels for 36%

profile of v1, /device:TPU:0, one launch (start us, length us, event | category | flops | bytes accessed | tf_op | source)
XLA Modules:
  0.0 1403.0 jit_solution(6685412764227700526)
XLA Ops:
  57.8 56.2 %collective-permute-done.4 = bf16[128,32,256]{2,1,0:T(8,128)(2,1)} collective-permute-done((bf16[128,32,256]{2,1,0:T(8,128)(2,1)}, bf16[128,32,256]{2,1,0:T(8,128)(2,1)}, u32[]{:S(2)}, u32[]{:S(2)}) %collective-permute-start.4) | collective-permute-done | bytes 2097184 | tf_op jit(solution)/shard_map/ppermute | solution.py:672
  140.4 22.0 %all-gather = s32[4,1,512]{2,1,0:T(1,128)S(1)} all-gather(s32[1,1,512]{2,1,0:T(1,128)S(1)} %bitcast.100), channel_id=1, replica_groups=mesh['crop'=4,'row'=4,'col'=2] {'crop'}, dimensions={0}, use_global_device_ids=true | all-gather | bytes 10240 | tf_op jit(solution)/shard_map/all_gather | solution.py:674
  165.3 45.4 %collective-permute-done.5 = bf16[128,32,256]{2,1,0:T(8,128)(2,1)S(1)} collective-permute-done((bf16[128,32,256]{2,1,0:T(8,128)(2,1)}, bf16[128,32,256]{2,1,0:T(8,128)(2,1)S(1)}, u32[]{:S(2)}, u32[]{:S(2)}) %collective-permute-start.5) | collective-permute-done | bytes 2097184 | tf_op jit(solution)/shard_map/ppermute | solution.py:672
  214.9 20.4 %project.3 = (bf16[128,64,256]{2,1,0:T(8,128)(2,1)}, bf16[128,64,256]{2,1,0:T(8,128)(2,1)}) custom-call(f32[64]{0:T(128)} %pad_maximum_fusion.4.row_mask, bf16[128,64,256]{2,1,0:T(8,128)(2,1)} %copy-done.11, bf16[512,128]{1,0:T(8,128)(2,1)} %slice.40.w_ref, f32[6,128,128]{2,1,0:T(8,128)} %broadcast_in_dim.41.ln_ref, f32[1,256]{1,0:T(1,128)} %fusion.30.col_ref), custom_call_target="tpu_custom_call" | custom-call | flops 8589934592 | bytes 13108224 | tf_op jit(solution)/shard_map/project/pallas_call | solution.py:306
  259.5 20.6 %project.2 = (bf16[128,64,256]{2,1,0:T(8,128)(2,1)}, bf16[128,64,256]{2,1,0:T(8,128)(2,1)}) custom-call(f32[64]{0:T(128)} %pad_maximum_fusion.3.row_mask, bf16[128,64,256]{2,1,0:T(8,128)(2,1)} %copy-done.12, bf16[512,128]{1,0:T(8,128)(2,1)} %slice.40.w_ref, f32[6,128,128]{2,1,0:T(8,128)} %broadcast_in_dim.41.ln_ref, f32[1,256]{1,0:T(1,128)} %fusion.30.col_ref), custom_call_target="tpu_custom_call" | custom-call | flops 8589934592 | bytes 13108224 | tf_op jit(solution)/shard_map/project/pallas_call | solution.py:306
  280.1 26.8 %collective-permute-start.17 = (bf16[128,64,256]{2,1,0:T(8,128)(2,1)}, bf16[128,64,256]{2,1,0:T(8,128)(2,1)}, u32[]{:S(2)}, u32[]{:S(2)}) collective-permute-start(bf16[128,64,256]{2,1,0:T(8,128)(2,1)} %get-tuple-element.92.b0.refs_8_), channel_id=1, source_target_pairs={{0,8},{8,0},{16,24},{24,16},{1,9},{9,1},{17,25},{25,17},{2,10},{10... | collective-permute-start | bytes 12582920 | tf_op jit(solution)/shard_map/ppermute | solution.py:659
  306.9 21.1 %collective-permute-done.21.b1.refs_14_ = bf16[128,64,256]{2,1,0:T(8,128)(2,1)} collective-permute-done((bf16[128,64,256]{2,1,0:T(8,128)(2,1)}, bf16[128,64,256]{2,1,0:T(8,128)(2,1)}, u32[]{:S(2)}, u32[]{:S(2)}) %collective-permute-start.21) | collective-permute-done | bytes 4194336 | tf_op jit(solution)/shard_map/ppermute | solution.py:662
  328.0 45.4 %collective-permute-start.24 = (bf16[128,64,256]{2,1,0:T(8,128)(2,1)}, bf16[128,64,256]{2,1,0:T(8,128)(2,1)}, u32[]{:S(2)}, u32[]{:S(2)}) collective-permute-start(bf16[128,64,256]{2,1,0:T(8,128)(2,1)} %collective-permute-done.21.b1.refs_14_), channel_id=1, source_target_pairs={{0,8},{8,0},{16,24},{24,16},{1,9},{9,1},{17,25},{25,17},{2,10},{10... | collective-permute-start | bytes 12582920 | tf_op jit(solution)/shard_map/ppermute | solution.py:659
  373.4 25.1 %collective-permute-done.17.b0.refs_9_ = bf16[128,64,256]{2,1,0:T(8,128)(2,1)} collective-permute-done((bf16[128,64,256]{2,1,0:T(8,128)(2,1)}, bf16[128,64,256]{2,1,0:T(8,128)(2,1)}, u32[]{:S(2)}, u32[]{:S(2)}) %collective-permute-start.17) | collective-permute-done | bytes 4194336 | tf_op jit(solution)/shard_map/ppermute | solution.py:659
  398.6 39.3 %collective-permute-start.23 = (bf16[128,64,256]{2,1,0:T(8,128)(2,1)}, bf16[128,64,256]{2,1,0:T(8,128)(2,1)}, u32[]{:S(2)}, u32[]{:S(2)}) collective-permute-start(bf16[128,64,256]{2,1,0:T(8,128)(2,1)} %collective-permute-done.17.b0.refs_9_), channel_id=1, source_target_pairs={{0,16},{8,24},{16,0},{24,8},{1,17},{9,25},{17,1},{25,9},{2,18},{10... | collective-permute-start | bytes 12582920 | tf_op jit(solution)/shard_map/ppermute | solution.py:662
  468.0 23.2 %collective-permute-done.11 = s32[32,256]{0,1:T(8,128)} collective-permute-done((s32[32,256]{0,1:T(8,128)S(1)}, s32[32,256]{0,1:T(8,128)}, u32[]{:S(2)}, u32[]{:S(2)}) %collective-permute-start.11) | collective-permute-done | bytes 32800 | tf_op jit(solution)/shard_map/ppermute | solution.py:672
  491.8 41.5 %collective-permute-done.13 = s32[32,256]{0,1:T(8,128)} collective-permute-done((s32[32,256]{0,1:T(8,128)S(1)}, s32[32,256]{0,1:T(8,128)}, u32[]{:S(2)}, u32[]{:S(2)}) %collective-permute-start.13) | collective-permute-done | bytes 32800 | tf_op jit(solution)/shard_map/ppermute | solution.py:672
  604.9 65.5 %pair.4 = (bf16[128,64,128]{2,1,0:T(8,128)(2,1)}, f32[512,128]{1,0:T(8,128)}, f32[512,128]{1,0:T(8,128)}, f32[128,128]{1,0:T(8,128)}, f32[128,256]{1,0:T(8,128)}...) custom-call(s32[2]{0:T(128)} %pad_add_fusion.place, ...), custom_call_target="tpu_custom_call" | custom-call | flops 35000000512 | bytes 19108352 | tf_op jit(solution)/shard_map/pair/pallas_call | solution.py:306
  705.5 65.5 %pair.7 = (bf16[128,64,128]{2,1,0:T(8,128)(2,1)}, f32[512,128]{1,0:T(8,128)}, f32[512,128]{1,0:T(8,128)}, f32[128,128]{1,0:T(8,128)}, f32[128,256]{1,0:T(8,128)}...) custom-call(s32[2]{0:T(128)} %pad_add_fusion.3.place, ...), custom_call_target="tpu_custom_call" | custom-call | flops 35000000512 | bytes 19108352 | tf_op jit(solution)/shard_map/pair/pallas_call | solution.py:306
  771.2 65.6 %pair.5 = (bf16[128,64,128]{2,1,0:T(8,128)(2,1)}, f32[512,128]{1,0:T(8,128)}, f32[512,128]{1,0:T(8,128)}, f32[128,128]{1,0:T(8,128)}, f32[128,256]{1,0:T(8,128)}...) custom-call(s32[2]{0:T(128)} %pad_add_fusion.1.place, ...), custom_call_target="tpu_custom_call" | custom-call | flops 35000000512 | bytes 19108352 | tf_op jit(solution)/shard_map/pair/pallas_call | solution.py:306
  855.4 65.7 %pair.6 = (bf16[128,64,128]{2,1,0:T(8,128)(2,1)}, f32[512,128]{1,0:T(8,128)}, f32[512,128]{1,0:T(8,128)}, f32[128,128]{1,0:T(8,128)}, f32[128,256]{1,0:T(8,128)}...) custom-call(s32[2]{0:T(128)} %pad_add_fusion.2.place, ...), custom_call_target="tpu_custom_call" | custom-call | flops 35000000512 | bytes 19108352 | tf_op jit(solution)/shard_map/pair/pallas_call | solution.py:306
  979.3 35.6 %collective-permute-done.31 = bf16[128,64,256]{2,1,0:T(8,128)(2,1)} collective-permute-done((bf16[128,64,256]{2,1,0:T(8,128)(2,1)}, bf16[128,64,256]{2,1,0:T(8,128)(2,1)}, u32[]{:S(2)}, u32[]{:S(2)}) %collective-permute-start.31) | collective-permute-done | bytes 4194336 | tf_op jit(solution)/shard_map/ppermute | solution.py:662
  1020.2 23.8 %left_back.1 = (bf16[128,64,256]{2,1,0:T(8,128)(2,1)}, bf16[128,64,256]{2,1,0:T(8,128)(2,1)}) custom-call(s32[1]{0:T(128)} %bitcast.9.flag, bf16[128,64,128]{2,1,0:T(8,128)(2,1)} %get-tuple-element.96.refs_0_.dx_own, bf16[128,64,128]{2,1,0:T(8,128)(2,1)} %get-tuple-element.99.refs_1_.dx_own, bf16[128,64,128]{2,1,0:T(8,128)(2,1)} %get-tuple-element.102.refs_2_.dx_own, ...), custom_call_target="tpu_custom_call" | custom-call | flops 17179869184 | bytes 58720256 | tf_op jit(solution)/shard_map/left_back/pallas_call | solution.py:306
  1063.2 19.2 %input_back.4 = (f32[256,256]{1,0:T(8,128)}, f32[256,128]{1,0:T(8,128)}) custom-call(f32[64]{0:T(128)} %pad_maximum_fusion.3.row_mask, bf16[128,64,256]{2,1,0:T(8,128)(2,1)} %copy-done.12, bf16[256,128]{1,0:T(8,128)(2,1)} %get-tuple-element.240.w_ref, f32[6,128,128]{2,1,0:T(8,128)} %broadcast_in_dim.41.ln_ref, f32[1,256]{1,0:T(1,128)} %fusion.30.col_ref, ...), custom_call_target="tpu_custom_call" | custom-call | flops 12884901888 | bytes 9241600 | tf_op jit(solution)/shard_map/input_back/pallas_call | solution.py:306
  1083.4 110.8 %collective-permute-done.35.rest_2_ = bf16[128,64,256]{2,1,0:T(8,128)(2,1)} collective-permute-done((bf16[128,64,256]{2,1,0:T(8,128)(2,1)}, bf16[128,64,256]{2,1,0:T(8,128)(2,1)}, u32[]{:S(2)}, u32[]{:S(2)}) %collective-permute-start.35) | collective-permute-done | bytes 4194336 | tf_op jit(solution)/shard_map/ppermute | solution.py:662
  1194.2 20.6 %input_back.7 = (f32[256,256]{1,0:T(8,128)}, f32[256,128]{1,0:T(8,128)}) custom-call(f32[64]{0:T(128)} %pad_maximum_fusion.4.row_mask, bf16[128,64,256]{2,1,0:T(8,128)(2,1)} %copy-done.11, bf16[256,128]{1,0:T(8,128)(2,1)} %get-tuple-element.241.w_ref, f32[6,128,128]{2,1,0:T(8,128)} %broadcast_in_dim.41.ln_ref, f32[1,256]{1,0:T(1,128)} %fusion.30.col_ref, ...), custom_call_target="tpu_custom_call" | custom-call | flops 12884901888 | bytes 17630208 | tf_op jit(solution)/shard_map/input_back/pallas_call | solution.py:306
  1214.9 20.8 %input_back.6 = (f32[256,256]{1,0:T(8,128)}, f32[256,128]{1,0:T(8,128)}) custom-call(f32[64]{0:T(128)} %pad_maximum_fusion.3.row_mask, bf16[128,64,256]{2,1,0:T(8,128)(2,1)} %copy-done.12, bf16[256,128]{1,0:T(8,128)(2,1)} %get-tuple-element.241.w_ref, f32[6,128,128]{2,1,0:T(8,128)} %broadcast_in_dim.41.ln_ref, f32[1,256]{1,0:T(1,128)} %fusion.30.col_ref, ...), custom_call_target="tpu_custom_call" | custom-call | flops 12884901888 | bytes 17630208 | tf_op jit(solution)/shard_map/input_back/pallas_call | solution.py:306
  1238.7 40.2 %all-reduce = (f32[64,128]{1,0:T(8,128)S(1)}, f32[6,128]{1,0:T(8,128)S(1)}, f32[64]{0:T(128)S(1)}, f32[]{:T(128)}) all-reduce(f32[64,128]{1,0:T(8,128)S(1)} %get-tuple-element.253, f32[6,128]{1,0:T(8,128)S(1)} %pad_maximum_fusion.2, f32[64]{0:T(128)S(1)} %get-tuple-element.252, ...), channel_id=1, replica_groups=mesh['crop'=4,'row'=4,'col'=2] {'crop','row','col'}, use_global_device_ids=true, to_apply=%region_10.11 | all-reduce | flops 9025 | bytes 72200 | tf_op jit(solution)/shard_map/psum | solution.py:776
  1280.7 88.0 %all-reduce.4.cloned.1.call-done = (f32[640,128]{1,0:T(8,128)}, f32[128,128]{1,0:T(8,128)}, f32[512,128]{1,0:T(8,128)}, f32[512,128]{1,0:T(8,128)}) async-done(((f32[640,128]{1,0:T(8,128)}, f32[128,128]{1,0:T(8,128)}, f32[512,128]{1,0:T(8,128)}, f32[512,128]{1,0:T(8,128)}), (f32[640,128]{1,0:T(8,128)}, f32[128,128]{1,0:T(8,128)}, f32[512,128]{1,0:T(8,128)}, ...) | async-done | bytes 917520 | tf_op jit(solution)/shard_map/psum | solution.py:776
  (328 shorter events, 372.7 us)
Async XLA Ops:
  7.2 1361.5 %all-reduce.4.cloned.1.call-start = ((), (), s32[]{:S(2)}) async-start(), calls=%async_computation | async-start | bytes 1835008 | tf_op jit(solution)/shard_map/psum | solution.py:776
  18.2 95.7 %collective-permute-start.4 = (bf16[128,32,256]{2,1,0:T(8,128)(2,1)}, bf16[128,32,256]{2,1,0:T(8,128)(2,1)}, u32[]{:S(2)}, u32[]{:S(2)}) collective-permute-start(bf16[128,32,256]{2,1,0:T(8,128)(2,1)} %bitcast.92), channel_id=1, source_target_pairs={{0,16},{2,26},{4,4},{6,14},{8,24},{10,18},{12,12},{14,6},{16,0},{1... | collective-permute-start | bytes 6291464 | tf_op jit(solution)/shard_map/ppermute | solution.py:672
  113.9 96.7 %collective-permute-start.5 = (bf16[128,32,256]{2,1,0:T(8,128)(2,1)}, bf16[128,32,256]{2,1,0:T(8,128)(2,1)S(1)}, u32[]{:S(2)}, u32[]{:S(2)}) collective-permute-start(bf16[128,32,256]{2,1,0:T(8,128)(2,1)} %collective-permute-done.4), channel_id=1, source_target_pairs={{0,4},{2,6},{4,0},{6,2},{8,14},{10,12},{12,10},{14,8},{16,16},{18,... | collective-permute-start | bytes 6291464 | tf_op jit(solution)/shard_map/ppermute | solution.py:672
  115.8 95.1 %collective-permute-start.7 = (bf16[128,32,256]{2,1,0:T(8,128)(2,1)}, bf16[128,32,256]{2,1,0:T(8,128)(2,1)}, u32[]{:S(2)}, u32[]{:S(2)}) collective-permute-start(bf16[128,32,256]{2,1,0:T(8,128)(2,1)} %collective-permute-done.6), channel_id=1, source_target_pairs={{0,6},{2,4},{4,2},{6,0},{8,12},{10,14},{12,8},{14,10},{16,18},{18,... | collective-permute-start | bytes 6291464 | tf_op jit(solution)/shard_map/ppermute | solution.py:672
  117.8 117.5 %collective-permute-start.1 = (bf16[128,32,256]{2,1,0:T(8,128)(2,1)}, bf16[128,32,256]{2,1,0:T(8,128)(2,1)}, u32[]{:S(2)}, u32[]{:S(2)}) collective-permute-start(bf16[128,32,256]{2,1,0:T(8,128)(2,1)} %collective-permute-done), channel_id=1, source_target_pairs={{0,0},{2,2},{4,4},{6,6},{8,10},{10,8},{12,14},{14,12},{16,20},{18,... | collective-permute-start | bytes 6291464 | tf_op jit(solution)/shard_map/ppermute | solution.py:672
  135.0 120.6 %collective-permute-start.3 = (bf16[128,32,256]{2,1,0:T(8,128)(2,1)}, bf16[128,32,256]{2,1,0:T(8,128)(2,1)}, u32[]{:S(2)}, u32[]{:S(2)}) collective-permute-start(bf16[128,32,256]{2,1,0:T(8,128)(2,1)} %collective-permute-done.2), channel_id=1, source_target_pairs={{0,2},{2,0},{4,6},{6,4},{8,8},{10,10},{12,12},{14,14},{16,22},{18,... | collective-permute-start | bytes 6291464 | tf_op jit(solution)/shard_map/ppermute | solution.py:672
  235.3 92.7 %collective-permute-start.21 = (bf16[128,64,256]{2,1,0:T(8,128)(2,1)}, bf16[128,64,256]{2,1,0:T(8,128)(2,1)}, u32[]{:S(2)}, u32[]{:S(2)}) collective-permute-start(bf16[128,64,256]{2,1,0:T(8,128)(2,1)} %get-tuple-element.93.b1.refs_12_), channel_id=1, source_target_pairs={{0,16},{8,24},{16,0},{24,8},{1,17},{9,25},{17,1},{25,9},{2,18},{10... | collective-permute-start | bytes 12582920 | tf_op jit(solution)/shard_map/ppermute | solution.py:662
  280.1 118.5 %collective-permute-start.17 = (bf16[128,64,256]{2,1,0:T(8,128)(2,1)}, bf16[128,64,256]{2,1,0:T(8,128)(2,1)}, u32[]{:S(2)}, u32[]{:S(2)}) collective-permute-start(bf16[128,64,256]{2,1,0:T(8,128)(2,1)} %get-tuple-element.92.b0.refs_8_), channel_id=1, source_target_pairs={{0,8},{8,0},{16,24},{24,16},{1,9},{9,1},{17,25},{25,17},{2,10},{10... | collective-permute-start | bytes 12582920 | tf_op jit(solution)/shard_map/ppermute | solution.py:659
  328.0 259.2 %collective-permute-start.24 = (bf16[128,64,256]{2,1,0:T(8,128)(2,1)}, bf16[128,64,256]{2,1,0:T(8,128)(2,1)}, u32[]{:S(2)}, u32[]{:S(2)}) collective-permute-start(bf16[128,64,256]{2,1,0:T(8,128)(2,1)} %collective-permute-done.21.b1.refs_14_), channel_id=1, source_target_pairs={{0,8},{8,0},{16,24},{24,16},{1,9},{9,1},{17,25},{25,17},{2,10},{10... | collective-permute-start | bytes 12582920 | tf_op jit(solution)/shard_map/ppermute | solution.py:659
  398.6 188.6 %collective-permute-start.23 = (bf16[128,64,256]{2,1,0:T(8,128)(2,1)}, bf16[128,64,256]{2,1,0:T(8,128)(2,1)}, u32[]{:S(2)}, u32[]{:S(2)}) collective-permute-start(bf16[128,64,256]{2,1,0:T(8,128)(2,1)} %collective-permute-done.17.b0.refs_9_), channel_id=1, source_target_pairs={{0,16},{8,24},{16,0},{24,8},{1,17},{9,25},{17,1},{25,9},{2,18},{10... | collective-permute-start | bytes 12582920 | tf_op jit(solution)/shard_map/ppermute | solution.py:662
  443.4 89.9 %collective-permute-start.13 = (s32[32,256]{0,1:T(8,128)S(1)}, s32[32,256]{0,1:T(8,128)}, u32[]{:S(2)}, u32[]{:S(2)}) collective-permute-start(s32[32,256]{0,1:T(8,128)S(1)} %bitcast.93), channel_id=1, source_target_pairs={{0,16},{2,26},{4,4},{6,14},{8,24},{10,18},{12,12},{14,6},{16,0},{1... | collective-permute-start | bytes 98312 | tf_op jit(solution)/shard_map/ppermute | solution.py:672
  491.3 112.3 %collective-permute-start.8 = (bf16[128,64,128]{2,1,0:T(8,128)(2,1)}, bf16[128,64,128]{2,1,0:T(8,128)(2,1)}, u32[]{:S(2)}, u32[]{:S(2)}) collective-permute-start(bf16[128,64,128]{2,1,0:T(8,128)(2,1)} %get-tuple-element.95), channel_id=1, source_target_pairs={{0,1},{1,0},{2,3},{3,2},{4,5},{5,4},{6,7},{7,6},{8,9},{9,8},{10,11... | collective-permute-start | bytes 6291464 | tf_op jit(solution)/shard_map/ppermute | solution.py:665
  562.5 108.5 %collective-permute-start.18 = (bf16[128,64,256]{2,1,0:T(8,128)(2,1)}, bf16[128,64,256]{2,1,0:T(8,128)(2,1)}, u32[]{:S(2)}, u32[]{:S(2)}) collective-permute-start(bf16[128,64,256]{2,1,0:T(8,128)(2,1)} %get-tuple-element.93.b1.refs_12_), channel_id=1, source_target_pairs={{0,8},{8,0},{16,24},{24,16},{1,9},{9,1},{17,25},{25,17},{2,10},{10... | collective-permute-start | bytes 12582920 | tf_op jit(solution)/shard_map/ppermute | solution.py:659
  566.2 121.2 %collective-permute-start.20 = (bf16[128,64,256]{2,1,0:T(8,128)(2,1)}, bf16[128,64,256]{2,1,0:T(8,128)(2,1)}, u32[]{:S(2)}, u32[]{:S(2)}) collective-permute-start(bf16[128,64,256]{2,1,0:T(8,128)(2,1)} %get-tuple-element.92.b0.refs_8_), channel_id=1, source_target_pairs={{0,16},{8,24},{16,0},{24,8},{1,17},{9,25},{17,1},{25,9},{2,18},{10... | collective-permute-start | bytes 12582920 | tf_op jit(solution)/shard_map/ppermute | solution.py:662
  603.6 100.6 %collective-permute-start.25 = (bf16[128,64,128]{2,1,0:T(8,128)(2,1)}, bf16[128,64,128]{2,1,0:T(8,128)(2,1)S(1)}, u32[]{:S(2)}, u32[]{:S(2)}) collective-permute-start(bf16[128,64,128]{2,1,0:T(8,128)(2,1)} %get-tuple-element.104), channel_id=1, source_target_pairs={{0,1},{1,0},{2,3},{3,2},{4,5},{5,4},{6,7},{7,6},{8,9},{9,8},{10,11... | collective-permute-start | bytes 6291464 | tf_op jit(solution)/shard_map/ppermute | solution.py:665
  670.4 252.5 %collective-permute-start.26 = (bf16[128,64,128]{2,1,0:T(8,128)(2,1)}, bf16[128,64,128]{2,1,0:T(8,128)(2,1)}, u32[]{:S(2)}, u32[]{:S(2)}) collective-permute-start(bf16[128,64,128]{2,1,0:T(8,128)(2,1)} %get-tuple-element.96.refs_0_.dx_own), channel_id=1, source_target_pairs={{0,1},{1,0},{2,3},{3,2},{4,5},{5,4},{6,7},{7,6},{8,9},{9,8},{10,11... | collective-permute-start | bytes 6291464 | tf_op jit(solution)/shard_map/ppermute | solution.py:665
  703.7 150.2 %collective-permute-start.22 = (bf16[128,64,128]{2,1,0:T(8,128)(2,1)}, bf16[128,64,128]{2,1,0:T(8,128)(2,1)S(1)}, u32[]{:S(2)}, u32[]{:S(2)}) collective-permute-start(bf16[128,64,128]{2,1,0:T(8,128)(2,1)} %get-tuple-element.101), channel_id=1, source_target_pairs={{0,1},{1,0},{2,3},{3,2},{4,5},{5,4},{6,7},{7,6},{8,9},{9,8},{10,11... | collective-permute-start | bytes 6291464 | tf_op jit(solution)/shard_map/ppermute | solution.py:665
  836.8 100.7 %collective-permute-start.27 = (bf16[128,64,128]{2,1,0:T(8,128)(2,1)}, bf16[128,64,128]{2,1,0:T(8,128)(2,1)}, u32[]{:S(2)}, u32[]{:S(2)}) collective-permute-start(bf16[128,64,128]{2,1,0:T(8,128)(2,1)} %get-tuple-element.99.refs_1_.dx_own), channel_id=1, source_target_pairs={{0,1},{1,0},{2,3},{3,2},{4,5},{5,4},{6,7},{7,6},{8,9},{9,8},{10,11... | collective-permute-start | bytes 6291464 | tf_op jit(solution)/shard_map/ppermute | solution.py:665
  853.1 119.9 %collective-permute-start.34 = (bf16[128,64,256]{2,1,0:T(8,128)(2,1)}, bf16[128,64,256]{2,1,0:T(8,128)(2,1)}, u32[]{:S(2)}, u32[]{:S(2)}) collective-permute-start(bf16[128,64,256]{2,1,0:T(8,128)(2,1)} %get-tuple-element.118), channel_id=1, source_target_pairs={{0,8},{8,0},{16,24},{24,16},{1,9},{9,1},{17,25},{25,17},{2,10},{10... | collective-permute-start | bytes 12582920 | tf_op jit(solution)/shard_map/ppermute | solution.py:659
  921.1 93.8 %collective-permute-start.31 = (bf16[128,64,256]{2,1,0:T(8,128)(2,1)}, bf16[128,64,256]{2,1,0:T(8,128)(2,1)}, u32[]{:S(2)}, u32[]{:S(2)}) collective-permute-start(bf16[128,64,256]{2,1,0:T(8,128)(2,1)} %get-tuple-element.113), channel_id=1, source_target_pairs={{0,16},{8,24},{16,0},{24,8},{1,17},{9,25},{17,1},{25,9},{2,18},{10... | collective-permute-start | bytes 12582920 | tf_op jit(solution)/shard_map/ppermute | solution.py:662
  952.5 131.0 %collective-permute-start.33 = (bf16[128,64,256]{2,1,0:T(8,128)(2,1)}, bf16[128,64,256]{2,1,0:T(8,128)(2,1)}, u32[]{:S(2)}, u32[]{:S(2)}) collective-permute-start(bf16[128,64,256]{2,1,0:T(8,128)(2,1)} %get-tuple-element.116), channel_id=1, source_target_pairs={{0,8},{8,0},{16,24},{24,16},{1,9},{9,1},{17,25},{25,17},{2,10},{10... | collective-permute-start | bytes 12582920 | tf_op jit(solution)/shard_map/ppermute | solution.py:659
  968.3 246.6 %collective-permute-start.30 = (bf16[128,64,256]{2,1,0:T(8,128)(2,1)}, bf16[128,64,256]{2,1,0:T(8,128)(2,1)}, u32[]{:S(2)}, u32[]{:S(2)}) collective-permute-start(bf16[128,64,256]{2,1,0:T(8,128)(2,1)} %get-tuple-element.111), channel_id=1, source_target_pairs={{0,16},{8,24},{16,0},{24,8},{1,17},{9,25},{17,1},{25,9},{2,18},{10... | collective-permute-start | bytes 12582920 | tf_op jit(solution)/shard_map/ppermute | solution.py:662
  979.3 215.0 %collective-permute-start.35 = (bf16[128,64,256]{2,1,0:T(8,128)(2,1)}, bf16[128,64,256]{2,1,0:T(8,128)(2,1)}, u32[]{:S(2)}, u32[]{:S(2)}) collective-permute-start(bf16[128,64,256]{2,1,0:T(8,128)(2,1)} %add_convert_fusion), channel_id=1, source_target_pairs={{0,16},{8,24},{16,0},{24,8},{1,17},{9,25},{17,1},{25,9},{2,18},{10... | collective-permute-start | bytes 12582920 | tf_op jit(solution)/shard_map/ppermute | solution.py:662
  1019.0 195.9 %collective-permute-start.32 = (bf16[128,64,256]{2,1,0:T(8,128)(2,1)S(1)}, bf16[128,64,256]{2,1,0:T(8,128)(2,1)}, u32[]{:S(2)}, u32[]{:S(2)}) collective-permute-start(bf16[128,64,256]{2,1,0:T(8,128)(2,1)S(1)} %add_convert_fusion.1), channel_id=1, source_target_pairs={{0,8},{8,0},{16,24},{24,16},{1,9},{9,1},{17,25},{25,17},{2,10},{10... | collective-permute-start | bytes 12582920 | tf_op jit(solution)/shard_map/ppermute | solution.py:659
  (93 other events, 3801.1 us)
Sparse Core Ops, SparseCore 0:
  1238.8 129.8 all-reduce.3

commit v2 on v1

v2 whole, which is shorter than its diff:
```python
import functools

import jax
import jax.numpy as jnp
from jax import lax
from jax.experimental import pallas as pl
from jax.experimental.pallas import tpu as pltpu
from jax.sharding import PartitionSpec as P

STEP = 10


NORM_EPS = 1e-05
CLIP_NORM = 0.02
LEARN_RATE = 0.03
GAIN_RATE = 0.3
BETA_ONE = 0.9
BETA_TWO = 0.999
ADAM_EPS = 1e-08
WEIGHT_DECAY = 0.01


def standardize(values):
    center = values - jnp.mean(values, -1, keepdims=True)
    rstd = lax.rsqrt(jnp.mean(center * center, -1, keepdims=True) + NORM_EPS)
    return (center * rstd, rstd)


def standard_back(grad, normed, rstd):
    return rstd * (
        grad
        - jnp.mean(grad, -1, keepdims=True)
        - normed * jnp.mean(grad * normed, -1, keepdims=True)
    )


def linear(values, weight):
    return jnp.einsum("ijc,cd->ijd", values, weight, preferred_element_type=jnp.float32)


def weight_grad(values, grad):
    return jnp.einsum("ijc,ijd->cd", values, grad, preferred_element_type=jnp.float32)


def transposed(grad, weight):
    return jnp.einsum("ijd,cd->ijc", grad, weight, preferred_element_type=jnp.float32)


def adamw_update(weight, first, second, grad, scale, rate):
    clipped = grad * scale
    first_new = BETA_ONE * first + (1.0 - BETA_ONE) * clipped
    second_new = BETA_TWO * second + (1.0 - BETA_TWO) * clipped * clipped
    first_hat = first_new / (1.0 - BETA_ONE**STEP)
    second_hat = second_new / (1.0 - BETA_TWO**STEP)
    stepped = weight - rate * (
        first_hat / (jnp.sqrt(second_hat) + ADAM_EPS) + WEIGHT_DECAY * weight
    )
    return (stepped, first_new, second_new)


def on_device_general(
    pair_acts,
    residue_mask,
    dist_bins,
    w_in,
    w_out,
    w_t1,
    w_t2,
    w_dist,
    norm_params,
    dist_bias,
    m_in,
    m_out,
    m_t1,
    m_t2,
    m_dist,
    m_norm,
    m_bias,
    v_in,
    v_out,
    v_t1,
    v_t2,
    v_dist,
    v_norm,
    v_bias,
):
    tile_rows = pair_acts.shape[1]
    tile_cols = pair_acts.shape[2]
    width = w_out.shape[0]
    row_first = lax.axis_index("row") * tile_rows
    col_first = lax.axis_index("col") * tile_cols
    mask_vals = residue_mask[0].astype(jnp.float32)
    row_mask = lax.dynamic_slice_in_dim(mask_vals, row_first, tile_rows)
    col_mask = lax.dynamic_slice_in_dim(mask_vals, col_first, tile_cols)
    pair_mask = row_mask[:, None] * col_mask[None, :]
    mask_cube = pair_mask[..., None]
    pair_total = lax.psum(jnp.sum(pair_mask), ("crop", "row", "col"))
    low_in, low_out, low_t1, low_t2, low_dist = [
        weight.astype(jnp.bfloat16) for weight in (w_in, w_out, w_t1, w_t2, w_dist)
    ]
    acts = pair_acts[0].astype(jnp.float32)
    normed_one, rstd_one = standardize(acts)
    pair_norm = (normed_one * norm_params[0] + norm_params[1]).astype(jnp.bfloat16)
    projected = linear(pair_norm, low_in)
    left_proj = projected[..., :width]
    left_sig = jax.nn.sigmoid(projected[..., width : 2 * width])
    right_proj = projected[..., 2 * width : 3 * width]
    right_sig = jax.nn.sigmoid(projected[..., 3 * width : 4 * width])
    gate_sig = jax.nn.sigmoid(projected[..., 4 * width :])
    left_vals = (mask_cube * left_sig * left_proj).astype(jnp.bfloat16)
    right_vals = (mask_cube * right_sig * right_proj).astype(jnp.bfloat16)
    strips = lax.all_gather(right_vals, "row", axis=0, tiled=True)
    piece = strips
    triangle = jnp.transpose(
        lax.psum_scatter(
            jnp.einsum("jkc,ikc->jic", piece, left_vals, preferred_element_type=jnp.float32),
            "col",
            scatter_dimension=0,
            tiled=True,
        ),
        (1, 0, 2),
    )
    normed_two, rstd_two = standardize(triangle)
    tri_norm = (normed_two * norm_params[2] + norm_params[3]).astype(jnp.bfloat16)
    out_proj = linear(tri_norm, low_out)
    updated = acts + gate_sig * out_proj
    normed_three, rstd_three = standardize(updated)
    trans_in = (normed_three * norm_params[4] + norm_params[5]).astype(jnp.bfloat16)
    pre_act = linear(trans_in, low_t1)
    hidden = jax.nn.silu(pre_act).astype(jnp.bfloat16)
    final = updated + linear(hidden, low_t2)
    final_low = final.astype(jnp.bfloat16)
    logits = linear(final_low, low_dist) + dist_bias
    log_total = jax.nn.logsumexp(logits, -1)
    onehot = (dist_bins[0][..., None] == jnp.arange(w_dist.shape[1])).astype(jnp.float32)
    loss_local = jnp.sum(pair_mask * (log_total - jnp.sum(logits * onehot, -1)))
    d_logits = (mask_cube * (jnp.exp(logits - log_total[..., None]) - onehot) / pair_total).astype(
        jnp.bfloat16
    )
    grad_dist = weight_grad(final_low, d_logits)
    grad_bias = jnp.sum(d_logits.astype(jnp.float32), (0, 1))
    d_final = transposed(d_logits, low_dist)
    d_trans = d_final.astype(jnp.bfloat16)
    grad_t2 = weight_grad(hidden, d_trans)
    d_hidden = transposed(d_trans, low_t2)
    sig_pre = jax.nn.sigmoid(pre_act)
    d_pre = (d_hidden * sig_pre * (1.0 + pre_act * (1.0 - sig_pre))).astype(jnp.bfloat16)
    grad_t1 = weight_grad(trans_in, d_pre)
    d_trans_in = transposed(d_pre, low_t1)
    d_updated = d_final + standard_back(d_trans_in * norm_params[4], normed_three, rstd_three)
    d_out = (d_updated * gate_sig).astype(jnp.bfloat16)
    d_out_gate = d_updated * out_proj * gate_sig * (1.0 - gate_sig)
    grad_out = weight_grad(tri_norm, d_out)
    d_tri_norm = transposed(d_out, low_out)
    d_triangle = standard_back(d_tri_norm * norm_params[2], normed_two, rstd_two).astype(
        jnp.bfloat16
    )
    d_rows = lax.all_gather(d_triangle, "col", axis=1, tiled=True)
    d_left = jnp.einsum("ijc,jkc->ikc", d_rows, strips, preferred_element_type=jnp.float32)
    piece = d_rows
    d_right = lax.psum_scatter(
        jnp.einsum("ijc,ikc->jkc", piece, left_vals, preferred_element_type=jnp.float32).astype(
            jnp.bfloat16
        ),
        "row",
        scatter_dimension=0,
        tiled=True,
    ).astype(jnp.float32)
    d_proj = jnp.concatenate(
        [
            d_left * mask_cube * left_sig,
            d_left * mask_cube * left_proj * left_sig * (1.0 - left_sig),
            d_right * mask_cube * right_sig,
            d_right * mask_cube * right_proj * right_sig * (1.0 - right_sig),
            d_out_gate,
        ],
        -1,
    ).astype(jnp.bfloat16)
    grad_in = weight_grad(pair_norm, d_proj)
    d_pair_norm = transposed(d_proj, low_in)
    grad_norms = jnp.stack(
        [
            jnp.sum(d_pair_norm * normed_one, (0, 1)),
            jnp.sum(d_pair_norm, (0, 1)),
            jnp.sum(d_tri_norm * normed_two, (0, 1)),
            jnp.sum(d_tri_norm, (0, 1)),
            jnp.sum(d_trans_in * normed_three, (0, 1)),
            jnp.sum(d_trans_in, (0, 1)),
        ]
    )
    summed = lax.psum(
        (grad_in, grad_out, grad_t1, grad_t2, grad_dist, grad_norms, grad_bias, loss_local),
        ("crop", "row", "col"),
    )
    grads = summed[:7]
    squares = jnp.zeros((), jnp.float32)
    for grad in grads:
        squares = squares + jnp.sum(grad * grad)
    grad_norm = jnp.sqrt(squares)
    scale = CLIP_NORM / jnp.maximum(grad_norm, CLIP_NORM)
    params = (w_in, w_out, w_t1, w_t2, w_dist, norm_params, dist_bias)
    firsts = (m_in, m_out, m_t1, m_t2, m_dist, m_norm, m_bias)
    seconds = (v_in, v_out, v_t1, v_t2, v_dist, v_norm, v_bias)
    rates = (LEARN_RATE, LEARN_RATE, LEARN_RATE, LEARN_RATE, LEARN_RATE, GAIN_RATE, GAIN_RATE)
    results = [
        adamw_update(
            params[index], firsts[index], seconds[index], grads[index], scale, rates[index]
        )
        for index in range(7)
    ]
    return (
        results[0][0],
        results[1][0],
        results[2][0],
        results[3][0],
        results[4][0],
        results[5][0],
        results[6][0],
        results[0][1],
        results[1][1],
        results[2][1],
        results[3][1],
        results[4][1],
        results[5][1],
        results[6][1],
        results[0][2],
        results[1][2],
        results[2][2],
        results[3][2],
        results[4][2],
        results[5][2],
        results[6][2],
        summed[7],
        pair_total,
        grad_norm,
    )


F32 = jnp.float32
BF16 = jnp.bfloat16
NT = (((1,), (1,)), ((), ()))
NN = (((1,), (0,)), ((), ()))
TN = (((0,), (0,)), ((), ()))
MICRO = 1e3
VMEM_LIMIT = 56 * 1024 * 1024


def dot(left, right, dims=NN):
    return lax.dot_general(left, right, dims, preferred_element_type=F32)


def sigmoid(values):
    return 0.5 * jnp.tanh(0.5 * values) + 0.5


def column_stats(values):
    center = values - jnp.mean(values, 0, keepdims=True)
    rstd = lax.rsqrt(jnp.mean(center * center, 0, keepdims=True) + NORM_EPS)
    return center * rstd, rstd


def column_back(grad, normed, rstd):
    return rstd * (
        grad
        - jnp.mean(grad, 0, keepdims=True)
        - normed * jnp.mean(grad * normed, 0, keepdims=True)
    )


def widen(param, lanes):
    return jnp.concatenate([param] * (lanes // param.shape[1]), 1)


def spread_rows(scratch, block):
    scratch[...] = jnp.swapaxes(block, 0, 1).astype(scratch.dtype)


def take_rows(scratch, start, count):
    return jnp.concatenate([scratch[start + u] for u in range(count)], 1).astype(F32)


def put_rows(scratch, start, count, values):
    lanes = values.shape[1] // count
    for u in range(count):
        scratch[start + u] = values[:, u * lanes : (u + 1) * lanes].astype(scratch.dtype)


def gather_rows(scratch, out_ref):
    out_ref[...] = jnp.swapaxes(scratch[...], 0, 1)


def call(kernel, grid, scalars, ins, outs, scratch, flops, name, aliases=None):
    return pl.pallas_call(
        kernel,
        grid_spec=pltpu.PrefetchScalarGridSpec(
            num_scalar_prefetch=len(scalars),
            grid=grid,
            in_specs=[pl.BlockSpec(block, index) for _, block, index in ins],
            out_specs=[pl.BlockSpec(block, index) for _, _, block, index in outs],
            scratch_shapes=scratch,
        ),
        out_shape=[jax.ShapeDtypeStruct(shape, dtype) for shape, dtype, _, _ in outs],
        compiler_params=pltpu.CompilerParams(vmem_limit_bytes=VMEM_LIMIT),
        cost_estimate=pl.CostEstimate(flops=int(flops), bytes_accessed=1, transcendentals=0),
        name=name,
        input_output_aliases=aliases or {},
    )(*scalars, *[a for a, _, _ in ins])


def code_rows(code_s, start, count):
    return jnp.concatenate([code_s[pl.ds(start + u, 1), :] for u in range(count)], 1)


def present_rows(code_s, start, count):
    return jnp.where(code_rows(code_s, start, count) < 0.0, 0.0, 1.0)


ROWS = 16
PROJECT_GROUP = 8
INPUT_GROUP = 8


def project_kernel(acts_ref, code_ref, w_ref, ln_ref, a_ref, b_ref, acts_s, a_s, b_s, code_s):
    width = a_ref.shape[0]
    code_s[...] = code_ref[0].astype(F32)
    spread_rows(acts_s, acts_ref[...])

    def some(step, carry):
        start = step * PROJECT_GROUP
        values = take_rows(acts_s, start, PROJECT_GROUP)
        lanes = values.shape[1]
        normed, _ = column_stats(values)
        low = (normed * widen(ln_ref[0], lanes) + widen(ln_ref[1], lanes)).astype(BF16)
        proj = dot(w_ref[...], low)
        mask = present_rows(code_s, start, PROJECT_GROUP)
        left = proj[:width] * sigmoid(proj[width : 2 * width]) * mask
        right = proj[2 * width : 3 * width] * sigmoid(proj[3 * width :]) * mask
        put_rows(a_s, start, PROJECT_GROUP, left)
        put_rows(b_s, start, PROJECT_GROUP, right)
        return carry

    lax.fori_loop(0, ROWS // PROJECT_GROUP, some, 0)
    gather_rows(a_s, a_ref)
    gather_rows(b_s, b_ref)


def fixed(*zeros):
    return lambda i, *_: zeros


def project(acts, w_proj, ln_wide):
    chans, rows, lanes = acts.shape[0] - 1, acts.shape[1], acts.shape[2]
    block = (chans, ROWS, lanes)
    mid = lambda i, *_: (0, i, 0)
    out = ((chans, rows, lanes), BF16, block, mid)
    staged = pltpu.VMEM((ROWS, chans, lanes), BF16)
    return call(
        project_kernel,
        (rows // ROWS,),
        [],
        [
            (acts, block, mid),
            (acts, (1, ROWS, lanes), lambda i, *_: (chans, i, 0)),
            (w_proj, w_proj.shape, fixed(0, 0)),
            (ln_wide, ln_wide.shape, fixed(0, 0, 0)),
        ],
        [out, out],
        [staged, staged, staged, pltpu.VMEM((ROWS, lanes), F32)],
        15 * MICRO,
        "project",
    )


CHANS = 16


def ordered(flag, own, other):
    part = own.shape[0] // 2
    waves = []
    for wave in range(2):
        mine, rest = own[wave * part : (wave + 1) * part], other[wave * part : (wave + 1) * part]
        waves += [jnp.where(flag, mine, rest), jnp.where(flag, rest, mine)]
    return jnp.concatenate(waves, 0)


def triangle_kernel(flag, a0, a1, b0, b1, keep_ref, send_ref):
    kept_first = flag[0] == 0
    part = b0.shape[1] // 2
    for chan in range(CHANS):
        rows = jnp.concatenate([a0[chan], a1[chan]], 0)
        one, two = [
            dot(jnp.concatenate([b[chan, part * u : part * u + part] for b in (b0, b1)], 0), rows, NT)
            for u in range(2)
        ]
        keep_ref[chan] = jnp.where(kept_first, one, two)
        send_ref[chan] = jnp.where(kept_first, two, one).astype(BF16)


def triangle(which, a, b):
    chans, half, lanes = a[0].shape
    lead = lambda i, *_: (i, 0, 0)
    block = (CHANS, half, lanes)
    out = (chans, half, 2 * half)
    return call(
        triangle_kernel,
        (chans // CHANS,),
        [which],
        [(v, block, lead) for v in (*a, *b)],
        [(out, F32, (CHANS, half, 2 * half), lead), (out, BF16, (CHANS, half, 2 * half), lead)],
        [],
        14 * MICRO,
        "triangle",
    )


GROUP = 16


T1_ROW, T2_ROW, OUT_ROW, OG_ROW, DIST_ROW, NORM_ROW, BIAS_ROW, LOSS_ROW, SUM_ROWS = (
    0, 512, 1024, 1152, 1280, 1344, 1350, 1351, 1352,
)


def row_sums(values):
    return jnp.sum(jnp.transpose(values), 0, keepdims=True)


def pair_kernel(
    first_call, last_call,
    place, x_keep, x_recv, acts_ref, code_ref, ln_ref, w_outT, w_out, w_ogT, w_t1T, w_t1,
    w_t2T, w_t2, w_distT, w_dist, bias_ref, *rest,
):
    prior = () if first_call else rest[:2]
    dx_ref, sums, wide, x_s, acts_s, dx_s, code_s = rest[len(prior) :]
    chans = acts_ref.shape[0]
    lanes = 128 * GROUP
    bins = w_distT.shape[0]
    hidden_width = w_t1T.shape[0]

    @pl.when(pl.program_id(0) == 0)
    def _():
        if first_call:
            sums[...] = jnp.zeros_like(sums)
            wide[...] = jnp.zeros_like(wide)
        else:
            sums[...] = prior[0][...]
            wide[...] = prior[1][...]

    spread_rows(x_s, x_keep[...] + x_recv[...].astype(F32))
    spread_rows(acts_s, acts_ref[...])
    code_s[...] = code_ref[0].astype(F32)
    param = [widen(ln_ref[index], lanes) for index in range(6)]
    bin_index = lax.broadcasted_iota(jnp.int32, (bins, lanes), 0).astype(F32)

    def fold(values):
        return sum(values[:, 128 * part : 128 * part + 128] for part in range(GROUP))

    def add(row, values):
        sums[row : row + values.shape[0]] += values

    def group(step, carry):
        first = step * GROUP
        x = take_rows(x_s, first, GROUP)
        acts = take_rows(acts_s, first, GROUP)
        code = code_rows(code_s, first, GROUP)
        normed_two, rstd_two = column_stats(x)
        tri = (normed_two * param[2] + param[3]).astype(BF16)
        out = dot(w_outT[...], tri)
        normed_one, _ = column_stats(acts)
        low = (normed_one * param[0] + param[1]).astype(BF16)
        gate = sigmoid(dot(w_ogT[...], low))
        z1 = acts + gate * out
        normed_three, rstd_three = column_stats(z1)
        trans = (normed_three * param[4] + param[5]).astype(BF16)
        pre = dot(w_t1T[...], trans)
        sig = sigmoid(pre)
        act = pre * sig
        hidden = act.astype(BF16)
        slope = sig * (1.0 + (pre - act))
        final = (z1 + dot(w_t2T[...], hidden)).astype(BF16)
        logits = dot(w_distT[...], final) + widen(bias_ref[...], lanes)
        top = jnp.max(logits, 0, keepdims=True)
        powers = jnp.exp(logits - top)
        total = jnp.sum(powers, 0, keepdims=True)
        present = jnp.where(code < 0.0, 0.0, 1.0)
        hot = bin_index == code
        picked = jnp.sum(jnp.where(hot, logits, 0.0), 0, keepdims=True)
        sums[LOSS_ROW : LOSS_ROW + 1] += fold(present * (jnp.log(total) + top) - picked)
        d_logits = (powers * (present / total) - jnp.where(hot, 1.0, 0.0)).astype(BF16)
        add(DIST_ROW, dot(d_logits, final, NT))
        wide[5, :bins] += fold(d_logits.astype(F32))
        d_final = dot(w_dist[...], d_logits)
        d_trans = d_final.astype(BF16)
        add(T2_ROW, dot(hidden, d_trans, NT))
        d_pre = (dot(w_t2[...], d_trans) * slope).astype(BF16)
        add(T1_ROW, dot(d_pre, trans, NT))
        d_tn = dot(w_t1[...], d_pre)
        wide[2] += fold(d_tn * normed_three)
        wide[3] += fold(d_tn)
        d_z1 = d_final + column_back(d_tn * param[4], normed_three, rstd_three)
        d_gated = d_z1 * gate
        d_out = d_gated.astype(BF16)
        d_og = (d_gated * out * (1.0 - gate)).astype(BF16)
        add(OUT_ROW, dot(d_out, tri, NT))
        g_og = dot(d_og, jnp.concatenate([low, normed_one.astype(BF16)], 0), NT)
        add(OG_ROW, g_og[:, :chans])
        wide[6] += g_og[:, chans:]
        wide[4] += fold(d_og.astype(F32))
        d_xn = dot(w_out[...], d_out)
        wide[0] += fold(d_xn * normed_two)
        wide[1] += fold(d_xn)
        d_x = column_back(d_xn * param[2], normed_two, rstd_two)
        put_rows(dx_s, first, GROUP, d_x)
        return carry

    lax.fori_loop(0, ROWS // GROUP, group, 0)
    gather_rows(dx_s, dx_ref)

    if last_call:

        @pl.when(pl.program_id(0) == pl.num_programs(0) - 1)
        def _():
            gate_w = w_ogT[...].astype(F32)
            for index in range(4):
                add(NORM_ROW + index, row_sums(wide[index]))
            add(NORM_ROW + 4, jnp.sum(gate_w * wide[6], 0, keepdims=True))
            add(NORM_ROW + 5, jnp.sum(gate_w * jnp.sum(wide[4], 1, keepdims=True), 0, keepdims=True))
            add(BIAS_ROW, row_sums(wide[5]))


def pair_block(place, x_keep, x_recv, acts_kj, ln_wide, weights, bias, prior, last_call):
    chans, rows, lanes = x_keep.shape
    block = (chans, ROWS, lanes)
    mid = lambda i, *_: (0, i, 0)

    def where(i, spot):
        return 8 * ((i % 2) ^ spot[0]) + 2 * spot[1] + i // 2

    full = [(w, w.shape, fixed(*([0] * w.ndim))) for w in (ln_wide, *weights, bias, *prior)]
    shapes = [(SUM_ROWS, 128), (7, 128, 128)]
    return call(
        functools.partial(pair_kernel, not prior, last_call),
        (rows // ROWS,),
        [place],
        [
            (x_keep, block, mid),
            (x_recv, block, mid),
            (acts_kj, block, lambda i, spot: (0, where(i, spot), 0)),
            (acts_kj, (1, ROWS, lanes), lambda i, spot: (chans, where(i, spot), 0)),
        ]
        + full,
        [((chans, rows, lanes), BF16, block, mid)]
        + [(s, F32, s, fixed(*([0] * len(s)))) for s in shapes],
        [pltpu.VMEM((ROWS, chans, lanes), t) for t in (F32, BF16, BF16)] + [pltpu.VMEM((ROWS, lanes), F32)],
        35 * MICRO,
        "pair",
    )


def right_back_kernel(flag, dx_own, dx_other, a0, a1, out0, out1):
    own_first = flag[0] == 0
    for chan in range(CHANS):
        rows = jnp.concatenate([a0[chan], a1[chan]], 0)
        both = ordered(own_first, dx_own[chan], dx_other[chan])
        grads = dot(both, rows).astype(BF16)
        half = out0.shape[1]
        out0[chan] = grads[:half]
        out1[chan] = grads[half:]


def right_back(which, dx_own, dx_other, a):
    chans, half, lanes = a[0].shape
    lead = lambda i, *_: (i, 0, 0)
    out = ((chans, half, lanes), BF16, (CHANS, half, lanes), lead)
    return call(
        right_back_kernel,
        (chans // CHANS,),
        [which],
        [(v, (CHANS, half, 2 * half), lead) for v in (dx_own, dx_other)]
        + [(v, (CHANS, half, lanes), lead) for v in a],
        [out, out],
        [],
        12 * MICRO,
        "right_back",
    )


def left_back_kernel(flag, *refs):
    owns, others, firsts, seconds = refs[:4], refs[4:8], refs[8:12], refs[12:16]
    out0, out1 = refs[16:]
    half = out0.shape[1]
    for chan in range(CHANS):
        total = None
        for pair in range(2):
            own_first = flag[0] == pair
            grads, values = [], []
            for q in (2 * pair, 2 * pair + 1):
                grads.append(ordered(own_first, owns[q][chan], others[q][chan]))
                values += [firsts[q][chan], seconds[q][chan]]
            term = dot(jnp.concatenate(grads, 0), jnp.concatenate(values, 0), TN)
            total = term if total is None else total + term
        total = total.astype(BF16)
        out0[chan] = total[:half]
        out1[chan] = total[half:]


def left_back(which, owns, others, firsts, seconds):
    chans, half, lanes = firsts[0].shape
    lead = lambda i, *_: (i, 0, 0)
    out = ((chans, half, lanes), BF16, (CHANS, half, lanes), lead)
    return call(
        left_back_kernel,
        (chans // CHANS,),
        [which],
        [(v, (CHANS, half, 2 * half), lead) for v in (*owns, *others)]
        + [(v, (CHANS, half, lanes), lead) for v in (*firsts, *seconds)],
        [out, out],
        [],
        25 * MICRO,
        "left_back",
    )


SIDE_ROWS = 272


def input_back_kernel(count, first_call, last_call, acts_ref, code_ref, w_ref, ln_ref, *rest):
    grads, rest = rest[:count], rest[count:]
    prior = () if first_call else rest[:3]
    out_ref, g_ref, sum_ref, acts_s, grad_s, code_s = rest[len(prior) :]
    width = grads[0].shape[0]
    chans = acts_ref.shape[0]

    @pl.when(pl.program_id(0) == 0)
    def _():
        if first_call:
            out_ref[...] = jnp.zeros_like(out_ref)
            g_ref[...] = jnp.zeros_like(g_ref)
            sum_ref[...] = jnp.zeros_like(sum_ref)
        else:
            out_ref[...] = prior[0][...]
            g_ref[...] = prior[1][...]
            sum_ref[...] = prior[2][...]

    code_s[...] = code_ref[0].astype(F32)
    spread_rows(acts_s, acts_ref[...])
    total = grads[0][...].astype(F32)
    for ref in grads[1:]:
        total = total + ref[...].astype(F32)
    spread_rows(grad_s, total)

    def some(step, carry):
        start = step * INPUT_GROUP
        values = take_rows(acts_s, start, INPUT_GROUP)
        lanes = values.shape[1]
        normed, _ = column_stats(values)
        low = (normed * widen(ln_ref[0], lanes) + widen(ln_ref[1], lanes)).astype(BF16)
        proj = dot(w_ref[...], low)
        gate = sigmoid(proj[width:])
        mask = present_rows(code_s, start, INPUT_GROUP)
        d_value = take_rows(grad_s, start, INPUT_GROUP) * mask * gate
        d_gate = d_value * proj[:width] * (1.0 - gate)
        d_proj = jnp.concatenate([d_value.astype(BF16), d_gate.astype(BF16)], 0)
        g_all = dot(d_proj, jnp.concatenate([low, normed.astype(BF16)], 0), NT)
        out_ref[: 2 * width] += g_all[:, :chans]
        g_ref[...] += g_all[:, chans:]
        wide = d_proj.astype(F32)
        sum_ref[...] += sum(wide[:, 128 * u : 128 * u + 128] for u in range(lanes // 128))
        return carry

    lax.fori_loop(0, ROWS // INPUT_GROUP, some, 0)

    if last_call:

        @pl.when(pl.program_id(0) == pl.num_programs(0) - 1)
        def _():
            part = w_ref[...].astype(F32)
            gain = jnp.sum(part * g_ref[...], 0, keepdims=True)
            shift = jnp.sum(part * jnp.sum(sum_ref[...], 1, keepdims=True), 0, keepdims=True)
            out_ref[2 * width : 2 * width + 1] = gain
            out_ref[2 * width + 1 : 2 * width + 2] = shift


def input_back(acts, w_part, ln_wide, grads, prior, last_call):
    chans, rows, lanes = acts.shape[0] - 1, acts.shape[1], acts.shape[2]
    block = (chans, ROWS, lanes)
    mid = lambda i, *_: (0, i, 0)
    depth = w_part.shape[0]
    shapes = [(SIDE_ROWS, chans), (depth, chans), (depth, 128)]
    return call(
        functools.partial(input_back_kernel, len(grads), not prior, last_call),
        (rows // ROWS,),
        [],
        [
            (acts, block, mid),
            (acts, (1, ROWS, lanes), lambda i, *_: (chans, i, 0)),
            (w_part, w_part.shape, fixed(0, 0)),
            (ln_wide, ln_wide.shape, fixed(0, 0, 0)),
        ]
        + [(v, block, mid) for v in grads]
        + [(v, v.shape, fixed(0, 0)) for v in prior],
        [(s, F32, s, fixed(0, 0)) for s in shapes],
        [
            pltpu.VMEM((ROWS, chans, lanes), BF16),
            pltpu.VMEM((ROWS, chans, lanes), F32),
            pltpu.VMEM((ROWS, lanes), F32),
        ],
        16 * MICRO,
        "input_back",
    )


def reduce_kernel(part_ref, out_ref, half_s, crop_s, row_s, full_s, send, recv):
    side, spot, level = lax.axis_index("col"), lax.axis_index("crop"), lax.axis_index("row")
    sibling = {"col": 1 - side}
    others = [{"crop": lax.rem(spot + n, 4)} for n in range(1, 4)]
    others += [{"row": lax.rem(level + n, 4)} for n in range(1, 4)]
    barrier = pltpu.get_barrier_semaphore()
    for device in [sibling] + others:
        pl.semaphore_signal(barrier, inc=1, device_id=device, device_id_type=pl.DeviceIdType.MESH)
    pl.semaphore_wait(barrier, 7)

    def copy(source, target, index, device):
        return pltpu.make_async_remote_copy(
            src_ref=source, dst_ref=target, send_sem=send.at[index], recv_sem=recv.at[index],
            device_id=device, device_id_type=pl.DeviceIdType.MESH,
        )

    rows = half_s.shape[0]
    away = pl.multiple_of((1 - side) * rows, 8)
    here = pl.multiple_of(side * rows, 8)
    one = copy(part_ref.at[pl.ds(away, rows)], half_s, 0, sibling)
    one.start()
    one.wait()
    crop_s[spot] = part_ref[pl.ds(here, rows)] + half_s[...]
    sends = [copy(crop_s.at[spot], crop_s.at[spot], 1 + n, others[n]) for n in range(3)]
    for one in sends:
        one.start()
    for one in sends:
        one.wait()
    row_s[level] = crop_s[0] + crop_s[1] + crop_s[2] + crop_s[3]
    sends = [copy(row_s.at[level], row_s.at[level], 4 + n, others[3 + n]) for n in range(3)]
    for one in sends:
        one.start()
    for one in sends:
        one.wait()
    full_s[side] = row_s[0] + row_s[1] + row_s[2] + row_s[3]
    one = copy(full_s.at[side], full_s.at[side], 7, sibling)
    one.start()
    one.wait()
    out_ref[:rows] = full_s[0]
    out_ref[rows:] = full_s[1]


def reduce_all(part):
    rows, lanes = part.shape[0] // 2, part.shape[1]
    return pl.pallas_call(
        reduce_kernel,
        out_shape=jax.ShapeDtypeStruct(part.shape, F32),
        scratch_shapes=[
            pltpu.VMEM((rows, lanes), F32),
            pltpu.VMEM((4, rows, lanes), F32),
            pltpu.VMEM((4, rows, lanes), F32),
            pltpu.VMEM((2, rows, lanes), F32),
            pltpu.SemaphoreType.DMA((8,)),
            pltpu.SemaphoreType.DMA((8,)),
        ],
        compiler_params=pltpu.CompilerParams(collective_id=1, has_side_effects=True),
        name="reduce_all",
    )(part)


def flip(a, b):
    return 2 * lax.rem(a // 2 + b // 2, 2) + lax.rem(a + b, 2)


def swap_bits(a):
    return 2 * lax.rem(a, 2) + a // 2


def spread_kernel(acts_ref, wave0_ref, mid1_ref, mid0, plane_send, plane_recv, level_send, level_recv, local):
    side, spot, level = lax.axis_index("col"), lax.axis_index("crop"), lax.axis_index("row")
    chans = acts_ref.shape[0]
    cuts = [(0, chans // 2), (chans // 2, chans - chans // 2)]
    barrier = pltpu.get_barrier_semaphore()
    for n in range(1, 4):
        for device in ({"crop": lax.rem(spot + n, 4)}, {"row": lax.rem(level + n, 4)}):
            pl.semaphore_signal(barrier, inc=1, device_id=device, device_id_type=pl.DeviceIdType.MESH)
    pl.semaphore_wait(barrier, 6)

    def plane_copy(wave, cut, distance):
        first, count = cuts[cut] if wave == 0 else (0, chans)
        target = flip(spot, distance)
        rows = pl.ds(pl.multiple_of(32 * target + 16 * wave, 16), 16)
        source = acts_ref.at[pl.ds(first, count), rows]
        landing = (mid0 if wave == 0 else mid1_ref).at[distance, pl.ds(first, count)]
        index = 4 * cut + distance if wave == 0 else 8 + distance
        if distance == 0:
            return pltpu.make_async_copy(source, landing, plane_recv.at[index])
        return pltpu.make_async_remote_copy(
            src_ref=source, dst_ref=landing, send_sem=plane_send.at[index], recv_sem=plane_recv.at[index],
            device_id={"crop": target}, device_id_type=pl.DeviceIdType.MESH,
        )

    def level_copy(cut, label, distance):
        first, count = cuts[cut]
        source = mid0.at[distance, pl.ds(first, count)]
        landing = wave0_ref.at[pl.ds(first, count), pl.ds(16 * label, 16)]
        target = swap_bits(flip(spot, distance))
        index = 4 * cut + label
        remote = pltpu.make_async_remote_copy(
            src_ref=source, dst_ref=landing, send_sem=level_send.at[index], recv_sem=level_recv.at[index],
            device_id={"row": target}, device_id_type=pl.DeviceIdType.MESH,
        )
        return target, remote, pltpu.make_async_copy(source, landing, local.at[cut])

    def each_level(action):
        for cut in range(2):
            for label in range(4):
                for distance in range(4):

                    @pl.when(flip(level, label) == distance)
                    def _(cut=cut, label=label, distance=distance):
                        action(cut, label, distance)

    plane = [plane_copy(0, cut, distance) for cut in range(2) for distance in range(4)]
    plane += [plane_copy(1, 0, distance) for distance in range(4)]
    for one in plane:
        one.start()

    def begin(cut, label, distance):
        one = plane[4 * cut + distance]
        one.wait() if distance == 0 else one.wait_recv()
        target, remote, stay = level_copy(cut, label, distance)

        @pl.when(target == level)
        def _():
            stay.start()

        @pl.when(target != level)
        def _():
            remote.start()

    def finish(cut, label, distance):
        target, remote, stay = level_copy(cut, label, distance)

        @pl.when(target == level)
        def _():
            stay.wait()

        @pl.when(target != level)
        def _():
            remote.wait()

    each_level(begin)
    for index, one in enumerate(plane):
        if index % 4 == 0:
            if index == 8:
                one.wait()
        else:
            one.wait_send()
            if index > 8:
                one.wait_recv()
    each_level(finish)


def spread(acts_major):
    chans, rows, lanes = acts_major.shape
    anywhere = pl.BlockSpec(memory_space=pl.ANY)
    return pl.pallas_call(
        spread_kernel,
        in_specs=[anywhere],
        out_specs=[anywhere, anywhere],
        out_shape=[
            jax.ShapeDtypeStruct((chans, rows // 2, lanes), BF16),
            jax.ShapeDtypeStruct((4, chans, rows // 8, lanes), BF16),
        ],
        scratch_shapes=[
            pltpu.VMEM((4, chans, rows // 8, lanes), BF16),
            pltpu.SemaphoreType.DMA((12,)),
            pltpu.SemaphoreType.DMA((12,)),
            pltpu.SemaphoreType.DMA((8,)),
            pltpu.SemaphoreType.DMA((8,)),
            pltpu.SemaphoreType.DMA((2,)),
        ],
        compiler_params=pltpu.CompilerParams(
            collective_id=2, has_side_effects=True, vmem_limit_bytes=VMEM_LIMIT
        ),
        name="spread",
    )(acts_major)


def update_kernel(early_ref, left_ref, right_ref, *refs):
    ins, outs = refs[:21], refs[21:]
    loss_ref, total_ref, norm_ref = outs[21:]
    total = early_ref[LOSS_ROW - 1, 127]
    inverse = 1.0 / total
    half = left_ref.shape[0] - 16
    grads = [
        jnp.concatenate(
            [
                jnp.transpose(left_ref[:half]),
                jnp.transpose(right_ref[:half]),
                jnp.transpose(early_ref[OG_ROW : OG_ROW + 128]),
            ],
            1,
        ),
        jnp.transpose(early_ref[OUT_ROW : OUT_ROW + 128]),
        jnp.transpose(early_ref[T1_ROW : T1_ROW + 512]),
        early_ref[T2_ROW : T2_ROW + 512],
        jnp.transpose(early_ref[DIST_ROW : DIST_ROW + 64]),
        jnp.concatenate(
            [
                left_ref[half : half + 2] + right_ref[half : half + 2] + early_ref[NORM_ROW + 4 : NORM_ROW + 6],
                early_ref[NORM_ROW : NORM_ROW + 4],
            ],
            0,
        ),
        early_ref[BIAS_ROW : BIAS_ROW + 1, :64],
    ]
    grads = [grad * inverse for grad in grads]
    squares = sum(jnp.sum(grad * grad, keepdims=True).reshape(1, 1) for grad in grads)
    grad_norm = jnp.sqrt(squares)
    scale = CLIP_NORM / jnp.maximum(grad_norm, CLIP_NORM)
    rates = (LEARN_RATE,) * 5 + (GAIN_RATE,) * 2
    for index in range(7):
        new = adamw_update(
            ins[index][...], ins[7 + index][...], ins[14 + index][...], grads[index], scale, rates[index]
        )
        for part in range(3):
            outs[7 * part + index][...] = new[part]
    norm_ref[...] = grad_norm
    loss_ref[...] = jnp.sum(early_ref[LOSS_ROW : LOSS_ROW + 1], keepdims=True).reshape(1, 1)
    total_ref[...] = jnp.full((1, 1), total, F32)


def update(early, left, right, params, firsts, seconds):
    flat = [v.reshape(1, -1) if v.ndim == 1 else v for v in (*params, *firsts, *seconds)]
    shapes = [v.shape for v in flat] + [(1, 1)] * 3
    outs = pl.pallas_call(
        update_kernel,
        out_shape=[jax.ShapeDtypeStruct(s, F32) for s in shapes],
        compiler_params=pltpu.CompilerParams(vmem_limit_bytes=VMEM_LIMIT),
        name="update",
    )(early, left, right, *flat)
    outs = [v.reshape(-1) if index in (6, 13, 20) else v for index, v in enumerate(outs)]
    return (*outs[:21], *[v[0, 0] for v in outs[21:]])


def after(value, *earlier):
    return lax.optimization_barrier((value, *earlier))[0]


def on_device_planes(
    pair_acts, residue_mask, dist_bins, w_in, w_out, w_t1, w_t2, w_dist, norm_params, dist_bias, *moments
):
    firsts, seconds = moments[:7], moments[7:]
    spot = lax.axis_index("crop")
    level = lax.axis_index("row")
    side = lax.axis_index("col")
    rows, cols, chans = pair_acts.shape[1:]
    width = w_out.shape[0]
    sub = rows // 4
    plane_of = (0, 2, 1, 3)
    crop = (level % 2) * 2 + level // 2

    def over_x(v):
        return lax.ppermute(v, "crop", [(g, g ^ 1) for g in range(4)])

    def over_y(v):
        return lax.ppermute(v, "crop", [(g, g ^ 2) for g in range(4)])

    def over_core(v):
        return lax.ppermute(v, "col", [(0, 1), (1, 0)])

    own_mask = residue_mask[0]
    row_own = lax.dynamic_slice_in_dim(own_mask, rows * level, rows)
    col_own = lax.dynamic_slice_in_dim(own_mask, cols * side, cols)
    code_own = jnp.where((row_own[:, None] * col_own[None, :]) > 0, dist_bins[0], -1).astype(BF16)
    acts_major = jnp.transpose(pair_acts[0], (2, 0, 1))

    acts_major = jnp.concatenate([acts_major, code_own[None]], 0)
    wave0, mid1 = spread(acts_major)

    def along_z(label):
        piece = lax.dynamic_index_in_dim(mid1, level ^ label, 0, keepdims=False)
        pairs = [(g * 4 + z, g * 4 + plane_of[g ^ label ^ z]) for g in range(4) for z in range(4)]
        stays = sum(((spot * 4 + level) == i).astype(jnp.int32) for i, j in pairs if i == j)
        moved = lax.ppermute(piece, ("crop", "row"), [(i, j) for i, j in pairs if i != j])
        return jnp.where(stays > 0, piece, moved)

    count = jnp.sum(own_mask).astype(F32)
    share = count * count / (lax.axis_size("row") * lax.axis_size("col"))
    low_in, low_out, low_t1, low_t2, low_dist = [
        weight.astype(BF16) for weight in (w_in, w_out, w_t1, w_t2, w_dist)
    ]
    ln_wide = jnp.broadcast_to(norm_params[:, :, None], (*norm_params.shape, 128))
    bias_wide = jnp.broadcast_to(dist_bias[:, None], (dist_bias.shape[0], 128))
    in_T = low_in.T

    pieces = [along_z(label) for label in range(4)]
    acts, a, b_own = [], [], []
    for h in range(2):
        acts.append(wave0 if h == 0 else jnp.concatenate([after(v, a[0]) for v in pieces], 1))
        left, right = project(acts[h], in_T[: 4 * width], ln_wide)
        a.append(left)
        b_own.append(right)
    b_x = [over_x(v) for v in b_own]
    b_y = [over_y(v) for v in b_own]
    b_d = [over_y(b_x[0]), over_x(b_y[1])]
    blocks = [b_own, b_x, b_y, b_d]

    weights = (
        low_out.T, low_out, in_T[4 * width :], low_t1.T, low_t1, low_t2.T, low_t2, low_dist.T, low_dist,
    )
    flags = [(side ^ ((spot ^ q) // 2) ^ (crop // 2)).astype(jnp.int32)[None] for q in range(4)]
    keeps, recvs, dx_own, dx_other, back = {}, {}, {}, {}, {}
    sums = []

    def forward(q, *earlier):
        keeps[q], send = triangle(flags[q], [after(v, *earlier) for v in a], blocks[q])
        recvs[q] = over_core(send)
        return send

    def middle(q, *earlier):
        owner = spot ^ q
        place = jnp.stack([(owner ^ crop) & 1, owner]).astype(jnp.int32)
        dx_own[q], *sums[:] = pair_block(
            after(place, *earlier), keeps[q], recvs[q], acts_kj, ln_wide, weights, bias_wide, list(sums), q == 3
        )
        dx_other[q] = over_core(dx_own[q])
        return dx_own[q]

    def backward(q, *earlier):
        back[q] = right_back(after(flags[q], *earlier), dx_own[q], dx_other[q], a)
        return back[q][0]

    done = forward(0, b_own[1], b_x[0], b_y[0])
    acts_kj = jnp.swapaxes(jnp.concatenate([after(v, done) for v in acts], 1), 1, 2)
    done = middle(0, acts_kj)
    done = forward(1, done)
    done = forward(2, done)
    done = middle(1, done)
    done = middle(2, done)
    done = backward(1, done)
    done = backward(2, done)
    done = forward(3, done)
    y0, x1 = over_y(back[2][0]), over_x(back[1][1])
    done = middle(3, done)
    done = backward(3, done, y0, x1)
    d0, d1 = over_y(back[3][0]), over_x(back[3][1])
    done = backward(0, done)
    d_left = left_back(
        after(flags[0], done),
        [dx_own[q] for q in range(4)],
        [dx_other[q] for q in range(4)],
        [v[0] for v in blocks],
        [v[1] for v in blocks],
    )
    x0 = (back[1][0].astype(F32) + d0.astype(F32)).astype(BF16)
    y1 = (back[2][1].astype(F32) + d1.astype(F32)).astype(BF16)
    own = [[back[0][0], y0, over_x(x0)], [back[0][1], x1, over_y(y1)]]
    left_w, right_w = in_T[: 2 * width], in_T[2 * width : 4 * width]
    left, right = [], []
    for h in range(2):
        left = input_back(acts[h], left_w, ln_wide, [d_left[h]], left, h == 1)
    everywhere = ("crop", "row", "col")
    early = sums[0].at[LOSS_ROW - 1, 127].set(share)
    early = lax.psum(early, everywhere)
    own[0][0] = after(own[0][0], left[0])
    for h in range(2):
        right = input_back(acts[h], right_w, ln_wide, own[h], right, h == 1)
    both = reduce_all(jnp.concatenate([left[0], after(right[0], early)], 0))
    params = (w_in, w_out, w_t1, w_t2, w_dist, norm_params, dist_bias)
    return update(early, both[:SIDE_ROWS], both[SIDE_ROWS:], params, firsts, seconds)


def solution(mesh):
    planes = mesh.shape["crop"] == 4 and mesh.shape["row"] == 4 and mesh.shape["col"] == 2
    body = on_device_planes if planes else on_device_general
    in_specs = (
        P("crop", "row", "col", None),
        P("crop", None),
        P("crop", "row", "col"),
    ) + (P(),) * 21
    return jax.shard_map(
        body, mesh=mesh, in_specs=in_specs, out_specs=(P(),) * 24, check_vma=False
    )
```

time: 1410 us -> 885 us (0.63)
  waiting for transfers between devices: 465 us -> 224 us
  starting transfers between devices: 208 us -> 64.7 us
  blocking collectives: 62.1 us -> 0 us
  Pallas kernels: 531 us -> 482 us
    pallas_call x19, Pallas kernels: 531 us -> 334 us  [call(): pl.pallas_call(kernel, grid_spec=pltpu.PrefetchScalarGridSpec(num_scalar_...]
    ppermute x16 -> x4, waiting for transfers between devices: 185 us -> 32.4 us  [along_z(): lax.ppermute(piece, ('crop', 'row'), [(i, j) for i, j in pairs if i != j])]
    pallas_call x0 -> x3, Pallas kernels: none -> 149 us  [the longest x1 116 us: spread(): pl.pallas_call(spread_kernel, in_specs=[anywhere], out_specs=[anywhere, a...]
    psum x1, waiting for transfers between devices: 88 us -> 9.33 us  [on_device_planes(): early = lax.psum(early, everywhere)]
    ppermute x16 -> x4, starting transfers between devices: 83.3 us -> 10.3 us  [along_z(): lax.ppermute(piece, ('crop', 'row'), [(i, j) for i, j in pairs if i != j])]
    ppermute x6, starting transfers between devices: 79.3 us -> 38.7 us  [over_x(): return lax.ppermute(v, 'crop', [(g, g ^ 1) for g in range(4)])]
    psum x1 -> x0, blocking collectives: 40.2 us -> none  [on_device_planes(): lax.psum((outer[:, :chans], g_out, g_t1, g_t2, g_dist, grad_norms, jnp.su...]
    ppermute x6, starting transfers between devices: 44 us -> 14.3 us  [over_y(): return lax.ppermute(v, 'crop', [(g, g ^ 2) for g in range(4)])]
  transfers between devices with their start and end apart: 37 -> 25, of which waited for: 10 -> 10; matrix products, arithmetic and copies ran while one was open for 5% -> 6% of each run, Pallas kernels for 36% -> 35%
where the time goes in v2:
time: 885 us; the launch traced here: 877 us
  Pallas kernels  482 us (54%)
  waiting for transfers between devices  224 us (25%)
  starting transfers between devices  64.7 us (7%)
  local copies, waits for them, and re-layouts  55.9 us (6%)
  other arithmetic  34.8 us (4%)
  between operations  15.4 us (2%)
    pallas_call x19, Pallas kernels, call(): pl.pallas_call(kernel, grid_spec=pltpu.PrefetchScalarGridSpec(num_scalar_...  334 us
    ppermute x6, waiting for transfers between devices, over_y(): return lax.ppermute(v, 'crop', [(g, g ^ 2) for g in range(4)])  146 us
    pallas_call x1, Pallas kernels, spread(): pl.pallas_call(spread_kernel, in_specs=[anywhere], out_specs=[anywhere, a...  116 us
    ppermute x6, starting transfers between devices, over_x(): return lax.ppermute(v, 'crop', [(g, g ^ 1) for g in range(4)])  38.7 us
    ppermute x6, waiting for transfers between devices, over_x(): return lax.ppermute(v, 'crop', [(g, g ^ 1) for g in range(4)])  34.8 us
    ppermute x4, waiting for transfers between devices, along_z(): lax.ppermute(piece, ('crop', 'row'), [(i, j) for i, j in pairs if i != j])  32.4 us
    unnamed x57, local copies, waits for them, and re-layouts  27.9 us
    pallas_call x1, Pallas kernels, reduce_all(): pl.pallas_call(reduce_kernel, out_shape=jax.ShapeDtypeStruct(part.shape,...  27.3 us
  transfers between devices with their start and end apart: 25, of which 10 were waited for; matrix products, arithmetic and copies ran while one was open for 6% of the time, Pallas kernels for 35%

profile of v2, /device:TPU:0, one launch (start us, length us, event | category | flops | bytes accessed | tf_op | source)
XLA Modules:
  0.0 877.4 jit_solution(17405778959149989128)
XLA Ops:
  8.6 12.6 %copy.48 = bf16[1,128,256,128]{2,1,3,0:T(8,128)(2,1)} copy(bf16[1,128,256,128]{3,2,1,0:T(8,128)(2,1)} %param.26) | data formatting | bytes 16777216 | tf_op args[0]
  28.8 116.4 %spread.1 = (bf16[129,64,256]{2,1,0:T(8,128)(2,1)}, bf16[4,129,16,256]{3,2,1,0:T(8,128)(2,1)}) custom-call(bf16[129,128,256]{2,1,0:T(8,128)(2,1)} %pad_maximum_fusion.acts_ref), custom_call_target="tpu_custom_call" | custom-call | tf_op jit(solution)/shard_map/spread/pallas_call | solution.py:870
  160.9 13.5 %project.2 = (bf16[128,64,256]{2,1,0:T(8,128)(2,1)}, bf16[128,64,256]{2,1,0:T(8,128)(2,1)}) custom-call(bf16[129,64,256]{2,1,0:T(8,128)(2,1)} %get-tuple-element.141.acts_ref.code_ref, bf16[129,64,256]{2,1,0:T(8,128)(2,1)} %get-tuple-element.141.acts_ref.code_ref, bf16[512,128]{1,0:T(8,128)(2,1)} %slice.44.w_ref, f32[6,128,128]{2,1,0:T(8,128)} %broadcast_in_dim.33.ln_ref), custom_call_target="tpu_custom_call" | custom-call | flops 15000 | bytes 1 | tf_op jit(solution)/shard_map/project/pallas_call | solution.py:293
  184.1 17.8 %collective-permute-done.2 = bf16[129,16,256]{2,1,0:T(8,128)(2,1)} collective-permute-done((bf16[129,16,256]{2,1,0:T(8,128)(2,1)S(1)}, bf16[129,16,256]{2,1,0:T(8,128)(2,1)}, u32[]{:S(2)}, u32[]{:S(2)}) %collective-permute-start.2) | collective-permute-done | bytes 1056800 | tf_op jit(solution)/shard_map/ppermute | solution.py:989
  203.2 14.6 %collective-permute-done.1 = bf16[129,16,256]{2,1,0:T(8,128)(2,1)} collective-permute-done((bf16[129,16,256]{2,1,0:T(8,128)(2,1)S(1)}, bf16[129,16,256]{2,1,0:T(8,128)(2,1)}, u32[]{:S(2)}, u32[]{:S(2)}) %collective-permute-start.1) | collective-permute-done | bytes 1056800 | tf_op jit(solution)/shard_map/ppermute | solution.py:989
  221.9 13.6 %project.3 = (bf16[128,64,256]{2,1,0:T(8,128)(2,1)}, bf16[128,64,256]{2,1,0:T(8,128)(2,1)}) custom-call(bf16[129,64,256]{2,1,0:T(8,128)(2,1)} %copy-done, bf16[129,64,256]{2,1,0:T(8,128)(2,1)} %copy-done, bf16[512,128]{1,0:T(8,128)(2,1)} %slice.44.w_ref, f32[6,128,128]{2,1,0:T(8,128)} %broadcast_in_dim.33.ln_ref), custom_call_target="tpu_custom_call" | custom-call | flops 15000 | bytes 1 | tf_op jit(solution)/shard_map/project/pallas_call | solution.py:293
  235.6 28.7 %collective-permute-start.7 = (bf16[128,64,256]{2,1,0:T(8,128)(2,1)}, bf16[128,64,256]{2,1,0:T(8,128)(2,1)}, u32[]{:S(2)}, u32[]{:S(2)}) collective-permute-start(bf16[128,64,256]{2,1,0:T(8,128)(2,1)} %get-tuple-element.135.b1.refs_12_), channel_id=1, source_target_pairs={{0,8},{8,0},{16,24},{24,16},{1,9},{9,1},{17,25},{25,17},{2,10},{10... | collective-permute-start | bytes 12582920 | tf_op jit(solution)/shard_map/ppermute | solution.py:968
  271.8 12.7 %triangle.4 = (f32[128,64,128]{2,1,0:T(8,128)}, bf16[128,64,128]{2,1,0:T(8,128)(2,1)}) custom-call(s32[1]{0:T(128)} %bitcast.16.flag, bf16[128,64,256]{2,1,0:T(8,128)(2,1)} %get-tuple-element.166.a0, bf16[128,64,256]{2,1,0:T(8,128)(2,1)} %get-tuple-element.167.a1, bf16[128,64,256]{2,1,0:T(8,128)(2,1)} %get-tuple-element.136.b0.refs_8_, ...), custom_call_target="tpu_custom_call" | custom-call | flops 14000 | bytes 1 | tf_op jit(solution)/shard_map/triangle/pallas_call | solution.py:293
  312.7 31.7 %pair.4 = (bf16[128,64,128]{2,1,0:T(8,128)(2,1)}, f32[1352,128]{1,0:T(8,128)}, f32[7,128,128]{2,1,0:T(8,128)}) custom-call(s32[2]{0:T(128)} %pad_add_fusion.3.place, f32[128,64,128]{2,1,0:T(8,128)} %get-tuple-element.144.x_keep, bf16[128,64,128]{2,1,0:T(8,128)(2,1)} %copy-done.8, bf16[129,256,128]{2,1,0:T(8,128)(2,1)} %copy.51.acts_ref.code_ref, ...), custom_call_target="tpu_custom_call" | custom-call | flops 35000 | bytes 1 | tf_op jit(solution)/shard_map/pair/pallas_call | solution.py:293
  344.4 13.2 %collective-permute-done.7.b1.refs_13_ = bf16[128,64,256]{2,1,0:T(8,128)(2,1)} collective-permute-done((bf16[128,64,256]{2,1,0:T(8,128)(2,1)}, bf16[128,64,256]{2,1,0:T(8,128)(2,1)}, u32[]{:S(2)}, u32[]{:S(2)}) %collective-permute-start.7) | collective-permute-done | bytes 4194336 | tf_op jit(solution)/shard_map/ppermute | solution.py:968
  357.6 12.6 %triangle.5 = (f32[128,64,128]{2,1,0:T(8,128)}, bf16[128,64,128]{2,1,0:T(8,128)(2,1)}) custom-call(s32[1]{0:T(128)} %bitcast.9.flag, bf16[128,64,256]{2,1,0:T(8,128)(2,1)} %get-tuple-element.166.a0, bf16[128,64,256]{2,1,0:T(8,128)(2,1)} %get-tuple-element.167.a1, bf16[128,64,256]{2,1,0:T(8,128)(2,1)} %collective-permute-done.4.b0.refs_9_, ...), custom_call_target="tpu_custom_call" | custom-call | flops 14000 | bytes 1 | tf_op jit(solution)/shard_map/triangle/pallas_call | solution.py:293
  370.2 12.8 %triangle.6 = (f32[128,64,128]{2,1,0:T(8,128)}, bf16[128,64,128]{2,1,0:T(8,128)(2,1)}) custom-call(s32[1]{0:T(128)} %bitcast.8.flag, bf16[128,64,256]{2,1,0:T(8,128)(2,1)} %get-tuple-element.166.a0, bf16[128,64,256]{2,1,0:T(8,128)(2,1)} %get-tuple-element.167.a1, bf16[128,64,256]{2,1,0:T(8,128)(2,1)} %collective-permute-done.5.b0.refs_10_, ...), custom_call_target="tpu_custom_call" | custom-call | flops 14000 | bytes 1 | tf_op jit(solution)/shard_map/triangle/pallas_call | solution.py:293
  390.4 32.3 %pair.5 = (bf16[128,64,128]{2,1,0:T(8,128)(2,1)}, f32[1352,128]{1,0:T(8,128)}, f32[7,128,128]{2,1,0:T(8,128)}) custom-call(s32[2]{0:T(128)} %pad_add_fusion.2.place, f32[128,64,128]{2,1,0:T(8,128)} %get-tuple-element.153.x_keep, bf16[128,64,128]{2,1,0:T(8,128)(2,1)} %copy-done.9, bf16[129,256,128]{2,1,0:T(8,128)(2,1)} %copy.51.acts_ref.code_ref, ...), custom_call_target="tpu_custom_call" | custom-call | flops 35000 | bytes 1 | tf_op jit(solution)/shard_map/pair/pallas_call | solution.py:293
  422.8 32.6 %pair.6 = (bf16[128,64,128]{2,1,0:T(8,128)(2,1)}, f32[1352,128]{1,0:T(8,128)}, f32[7,128,128]{2,1,0:T(8,128)}) custom-call(s32[2]{0:T(128)} %pad_add_fusion.1.place, f32[128,64,128]{2,1,0:T(8,128)} %get-tuple-element.158.x_keep, bf16[128,64,128]{2,1,0:T(8,128)(2,1)} %collective-permute-done.10.x_recv, bf16[129,256,128]{2,1,0:T(8,128)(2,1)} %copy.51.acts_ref.code_ref, ...), custom_call_target="tpu_custom_call" | custom-call | flops 35000 | bytes 1 | tf_op jit(solution)/shard_map/pair/pallas_call | solution.py:293
  497.4 32.6 %pair.7 = (bf16[128,64,128]{2,1,0:T(8,128)(2,1)}, f32[1352,128]{1,0:T(8,128)}, f32[7,128,128]{2,1,0:T(8,128)}) custom-call(s32[2]{0:T(128)} %pad_add_fusion.place, f32[128,64,128]{2,1,0:T(8,128)} %get-tuple-element.170.x_keep, bf16[128,64,128]{2,1,0:T(8,128)(2,1)} %copy-done.10, bf16[129,256,128]{2,1,0:T(8,128)(2,1)} %copy.51.acts_ref.code_ref, ...), custom_call_target="tpu_custom_call" | custom-call | flops 35000 | bytes 1 | tf_op jit(solution)/shard_map/pair/pallas_call | solution.py:293
  530.2 54.8 %collective-permute-done.16.rest_1_ = bf16[128,64,256]{2,1,0:T(8,128)(2,1)} collective-permute-done((bf16[128,64,256]{2,1,0:T(8,128)(2,1)}, bf16[128,64,256]{2,1,0:T(8,128)(2,1)}, u32[]{:S(2)}, u32[]{:S(2)}) %collective-permute-start.16) | collective-permute-done | bytes 4194336 | tf_op jit(solution)/shard_map/ppermute | solution.py:971
  600.5 89.2 %collective-permute-done.22 = bf16[128,64,256]{2,1,0:T(8,128)(2,1)S(1)} collective-permute-done((bf16[128,64,256]{2,1,0:T(8,128)(2,1)}, bf16[128,64,256]{2,1,0:T(8,128)(2,1)S(1)}, u32[]{:S(2)}, u32[]{:S(2)}) %collective-permute-start.22) | collective-permute-done | bytes 4194336 | tf_op jit(solution)/shard_map/ppermute | solution.py:971
  716.4 19.9 %left_back.1 = (bf16[128,64,256]{2,1,0:T(8,128)(2,1)}, bf16[128,64,256]{2,1,0:T(8,128)(2,1)}) custom-call(s32[1]{0:T(128)} %bitcast.16.flag, bf16[128,64,128]{2,1,0:T(8,128)(2,1)} %get-tuple-element.145.dx_own.refs_0_, bf16[128,64,128]{2,1,0:T(8,128)(2,1)} %get-tuple-element.156.dx_own.refs_1_, bf16[128,64,128]{2,1,0:T(8,128)(2,1)} %get-tuple-element.161.dx_own.refs_2_, ...), custom_call_target="tpu_custom_call" | custom-call | flops 25000 | bytes 1 | tf_op jit(solution)/shard_map/left_back/pallas_call | solution.py:293
  736.3 14.8 %input_back.4 = (f32[272,128]{1,0:T(8,128)}, f32[256,128]{1,0:T(8,128)}, f32[256,128]{1,0:T(8,128)}) custom-call(bf16[129,64,256]{2,1,0:T(8,128)(2,1)} %get-tuple-element.141.acts_ref.code_ref, bf16[129,64,256]{2,1,0:T(8,128)(2,1)} %get-tuple-element.141.acts_ref.code_ref, bf16[256,128]{1,0:T(8,128)(2,1)} %get-tuple-element.250.w_ref, ...), custom_call_target="tpu_custom_call" | custom-call | flops 16000 | bytes 1 | tf_op jit(solution)/shard_map/input_back/pallas_call | solution.py:293
  751.1 15.1 %input_back.5 = (f32[272,128]{1,0:T(8,128)}, f32[256,128]{1,0:T(8,128)}, f32[256,128]{1,0:T(8,128)}) custom-call(bf16[129,64,256]{2,1,0:T(8,128)(2,1)} %copy-done, bf16[129,64,256]{2,1,0:T(8,128)(2,1)} %copy-done, bf16[256,128]{1,0:T(8,128)(2,1)} %get-tuple-element.250.w_ref, f32[6,128,128]{2,1,0:T(8,128)} %broadcast_in_dim.33.ln_ref, ...), custom_call_target="tpu_custom_call" | custom-call | flops 16000 | bytes 1 | tf_op jit(solution)/shard_map/input_back/pallas_call | solution.py:293
  766.2 21.3 %collective-permute-done.23.rest_2_ = bf16[128,64,256]{2,1,0:T(8,128)(2,1)} collective-permute-done((bf16[128,64,256]{2,1,0:T(8,128)(2,1)}, bf16[128,64,256]{2,1,0:T(8,128)(2,1)}, u32[]{:S(2)}, u32[]{:S(2)}) %collective-permute-start.23) | collective-permute-done | bytes 4194336 | tf_op jit(solution)/shard_map/ppermute | solution.py:968
  787.6 16.3 %input_back.6 = (f32[272,128]{1,0:T(8,128)}, f32[256,128]{1,0:T(8,128)}, f32[256,128]{1,0:T(8,128)}) custom-call(bf16[129,64,256]{2,1,0:T(8,128)(2,1)} %get-tuple-element.141.acts_ref.code_ref, bf16[129,64,256]{2,1,0:T(8,128)(2,1)} %get-tuple-element.141.acts_ref.code_ref, bf16[256,128]{1,0:T(8,128)(2,1)} %get-tuple-element.251.w_ref, ...), custom_call_target="tpu_custom_call" | custom-call | flops 16000 | bytes 1 | tf_op jit(solution)/shard_map/input_back/pallas_call | solution.py:293
  803.9 16.9 %input_back.7 = (f32[272,128]{1,0:T(8,128)}, f32[256,128]{1,0:T(8,128)}, f32[256,128]{1,0:T(8,128)}) custom-call(bf16[129,64,256]{2,1,0:T(8,128)(2,1)} %copy-done, bf16[129,64,256]{2,1,0:T(8,128)(2,1)} %copy-done, bf16[256,128]{1,0:T(8,128)(2,1)} %get-tuple-element.251.w_ref, f32[6,128,128]{2,1,0:T(8,128)} %broadcast_in_dim.33.ln_ref, ...), custom_call_target="tpu_custom_call" | custom-call | flops 16000 | bytes 1 | tf_op jit(solution)/shard_map/input_back/pallas_call | solution.py:293
  831.8 27.3 %reduce_all.1 = f32[544,128]{1,0:T(8,128)} custom-call(f32[544,128]{1,0:T(8,128)} %pad_maximum_fusion.1.part_ref), custom_call_target="tpu_custom_call" | custom-call | tf_op jit(solution)/shard_map/reduce_all/pallas_call | solution.py:757
  (145 shorter events, 188.7 us)
Async XLA Ops:
  7.2 822.9 %all-reduce.2.cloned.1.call-start = ((), (), s32[]{:S(2)}) async-start(), calls=%async_computation | async-start | bytes 1384448 | tf_op jit(solution)/shard_map/psum | solution.py:1069
  148.9 32.2 %collective-permute-start.3 = (bf16[129,16,256]{2,1,0:T(8,128)(2,1)}, bf16[129,16,256]{2,1,0:T(8,128)(2,1)}, u32[]{:S(2)}, u32[]{:S(2)}) collective-permute-start(bf16[129,16,256]{2,1,0:T(8,128)(2,1)} %get-tuple-element.244), channel_id=1, source_target_pairs={{0,6},{6,0},{8,10},{10,14},{12,8},{14,12},{16,20},{18,16},{20,22},... | collective-permute-start | bytes 3170312 | tf_op jit(solution)/shard_map/ppermute | solution.py:989
  150.8 51.1 %collective-permute-start.2 = (bf16[129,16,256]{2,1,0:T(8,128)(2,1)S(1)}, bf16[129,16,256]{2,1,0:T(8,128)(2,1)}, u32[]{:S(2)}, u32[]{:S(2)}) collective-permute-start(bf16[129,16,256]{2,1,0:T(8,128)(2,1)S(1)} %get-tuple-element.245), channel_id=1, source_target_pairs={{0,2},{2,6},{4,0},{6,4},{8,14},{14,8},{18,20},{20,18},{24,28},{26,... | collective-permute-start | bytes 3170312 | tf_op jit(solution)/shard_map/ppermute | solution.py:989
  152.7 65.1 %collective-permute-start.1 = (bf16[129,16,256]{2,1,0:T(8,128)(2,1)S(1)}, bf16[129,16,256]{2,1,0:T(8,128)(2,1)}, u32[]{:S(2)}, u32[]{:S(2)}) collective-permute-start(bf16[129,16,256]{2,1,0:T(8,128)(2,1)S(1)} %get-tuple-element.246), channel_id=1, source_target_pairs={{0,4},{2,0},{4,6},{6,2},{10,12},{12,10},{16,22},{22,16},{24,26},{2... | collective-permute-start | bytes 3170312 | tf_op jit(solution)/shard_map/ppermute | solution.py:989
  174.3 95.7 %collective-permute-start.4 = (bf16[128,64,256]{2,1,0:T(8,128)(2,1)}, bf16[128,64,256]{2,1,0:T(8,128)(2,1)}, u32[]{:S(2)}, u32[]{:S(2)}) collective-permute-start(bf16[128,64,256]{2,1,0:T(8,128)(2,1)} %get-tuple-element.136.b0.refs_8_), channel_id=1, source_target_pairs={{0,8},{8,0},{16,24},{24,16},{1,9},{9,1},{17,25},{25,17},{2,10},{10... | collective-permute-start | bytes 12582920 | tf_op jit(solution)/shard_map/ppermute | solution.py:968
  178.2 93.5 %collective-permute-start.5 = (bf16[128,64,256]{2,1,0:T(8,128)(2,1)}, bf16[128,64,256]{2,1,0:T(8,128)(2,1)}, u32[]{:S(2)}, u32[]{:S(2)}) collective-permute-start(bf16[128,64,256]{2,1,0:T(8,128)(2,1)} %get-tuple-element.136.b0.refs_8_), channel_id=1, source_target_pairs={{0,16},{8,24},{16,0},{24,8},{1,17},{9,25},{17,1},{25,9},{2,18},{10... | collective-permute-start | bytes 12582920 | tf_op jit(solution)/shard_map/ppermute | solution.py:971
  181.1 38.1 %collective-permute-start = (bf16[129,16,256]{2,1,0:T(8,128)(2,1)S(1)}, bf16[129,16,256]{2,1,0:T(8,128)(2,1)}, u32[]{:S(2)}, u32[]{:S(2)}) collective-permute-start(bf16[129,16,256]{2,1,0:T(8,128)(2,1)S(1)} %get-tuple-element.247), channel_id=1, source_target_pairs={{2,4},{4,2},{8,12},{10,8},{12,14},{14,10},{16,18},{18,22},{20,16},... | collective-permute-start | bytes 3170312 | tf_op jit(solution)/shard_map/ppermute | solution.py:989
  235.6 122.0 %collective-permute-start.7 = (bf16[128,64,256]{2,1,0:T(8,128)(2,1)}, bf16[128,64,256]{2,1,0:T(8,128)(2,1)}, u32[]{:S(2)}, u32[]{:S(2)}) collective-permute-start(bf16[128,64,256]{2,1,0:T(8,128)(2,1)} %get-tuple-element.135.b1.refs_12_), channel_id=1, source_target_pairs={{0,8},{8,0},{16,24},{24,16},{1,9},{9,1},{17,25},{25,17},{2,10},{10... | collective-permute-start | bytes 12582920 | tf_op jit(solution)/shard_map/ppermute | solution.py:968
  264.2 106.0 %collective-permute-start.8 = (bf16[128,64,256]{2,1,0:T(8,128)(2,1)}, bf16[128,64,256]{2,1,0:T(8,128)(2,1)}, u32[]{:S(2)}, u32[]{:S(2)}) collective-permute-start(bf16[128,64,256]{2,1,0:T(8,128)(2,1)} %get-tuple-element.135.b1.refs_12_), channel_id=1, source_target_pairs={{0,16},{8,24},{16,0},{24,8},{1,17},{9,25},{17,1},{25,9},{2,18},{10... | collective-permute-start | bytes 12582920 | tf_op jit(solution)/shard_map/ppermute | solution.py:971
  284.4 26.9 %collective-permute-start.6 = (bf16[128,64,128]{2,1,0:T(8,128)(2,1)}, bf16[128,64,128]{2,1,0:T(8,128)(2,1)S(1)}, u32[]{:S(2)}, u32[]{:S(2)}) collective-permute-start(bf16[128,64,128]{2,1,0:T(8,128)(2,1)} %get-tuple-element.140), channel_id=1, source_target_pairs={{0,1},{1,0},{2,3},{3,2},{4,5},{5,4},{6,7},{7,6},{8,9},{9,8},{10,11... | collective-permute-start | bytes 6291464 | tf_op jit(solution)/shard_map/ppermute | solution.py:974
  370.2 18.9 %collective-permute-start.9 = (bf16[128,64,128]{2,1,0:T(8,128)(2,1)}, bf16[128,64,128]{2,1,0:T(8,128)(2,1)S(1)}, u32[]{:S(2)}, u32[]{:S(2)}) collective-permute-start(bf16[128,64,128]{2,1,0:T(8,128)(2,1)} %get-tuple-element.148), channel_id=1, source_target_pairs={{0,1},{1,0},{2,3},{3,2},{4,5},{5,4},{6,7},{7,6},{8,9},{9,8},{10,11... | collective-permute-start | bytes 6291464 | tf_op jit(solution)/shard_map/ppermute | solution.py:974
  383.0 39.8 %collective-permute-start.10 = (bf16[128,64,128]{2,1,0:T(8,128)(2,1)}, bf16[128,64,128]{2,1,0:T(8,128)(2,1)}, u32[]{:S(2)}, u32[]{:S(2)}) collective-permute-start(bf16[128,64,128]{2,1,0:T(8,128)(2,1)} %get-tuple-element.151), channel_id=1, source_target_pairs={{0,1},{1,0},{2,3},{3,2},{4,5},{5,4},{6,7},{7,6},{8,9},{9,8},{10,11... | collective-permute-start | bytes 6291464 | tf_op jit(solution)/shard_map/ppermute | solution.py:974
  383.5 95.6 %collective-permute-start.13 = (bf16[128,64,256]{2,1,0:T(8,128)(2,1)}, bf16[128,64,256]{2,1,0:T(8,128)(2,1)}, u32[]{:S(2)}, u32[]{:S(2)}) collective-permute-start(bf16[128,64,256]{2,1,0:T(8,128)(2,1)} %collective-permute-done.4.b0.refs_9_), channel_id=1, source_target_pairs={{0,16},{8,24},{16,0},{24,8},{1,17},{9,25},{17,1},{25,9},{2,18},{10... | collective-permute-start | bytes 12582920 | tf_op jit(solution)/shard_map/ppermute | solution.py:971
  386.2 92.9 %collective-permute-start.14 = (bf16[128,64,256]{2,1,0:T(8,128)(2,1)}, bf16[128,64,256]{2,1,0:T(8,128)(2,1)}, u32[]{:S(2)}, u32[]{:S(2)}) collective-permute-start(bf16[128,64,256]{2,1,0:T(8,128)(2,1)} %collective-permute-done.8.b1.refs_14_), channel_id=1, source_target_pairs={{0,8},{8,0},{16,24},{24,16},{1,9},{9,1},{17,25},{25,17},{2,10},{10... | collective-permute-start | bytes 12582920 | tf_op jit(solution)/shard_map/ppermute | solution.py:968
  422.7 33.2 %collective-permute-start.11 = (bf16[128,64,128]{2,1,0:T(8,128)(2,1)}, bf16[128,64,128]{2,1,0:T(8,128)(2,1)S(1)}, u32[]{:S(2)}, u32[]{:S(2)}) collective-permute-start(bf16[128,64,128]{2,1,0:T(8,128)(2,1)} %get-tuple-element.156.dx_own.refs_1_), channel_id=1, source_target_pairs={{0,1},{1,0},{2,3},{3,2},{4,5},{5,4},{6,7},{7,6},{8,9},{9,8},{10,11... | collective-permute-start | bytes 6291464 | tf_op jit(solution)/shard_map/ppermute | solution.py:974
  455.4 12.8 %collective-permute-start.12 = (bf16[128,64,128]{2,1,0:T(8,128)(2,1)}, bf16[128,64,128]{2,1,0:T(8,128)(2,1)}, u32[]{:S(2)}, u32[]{:S(2)}) collective-permute-start(bf16[128,64,128]{2,1,0:T(8,128)(2,1)} %get-tuple-element.161.dx_own.refs_2_), channel_id=1, source_target_pairs={{0,1},{1,0},{2,3},{3,2},{4,5},{5,4},{6,7},{7,6},{8,9},{9,8},{10,11... | collective-permute-start | bytes 6291464 | tf_op jit(solution)/shard_map/ppermute | solution.py:974
  491.8 93.3 %collective-permute-start.16 = (bf16[128,64,256]{2,1,0:T(8,128)(2,1)}, bf16[128,64,256]{2,1,0:T(8,128)(2,1)}, u32[]{:S(2)}, u32[]{:S(2)}) collective-permute-start(bf16[128,64,256]{2,1,0:T(8,128)(2,1)} %get-tuple-element.165), channel_id=1, source_target_pairs={{0,16},{8,24},{16,0},{24,8},{1,17},{9,25},{17,1},{25,9},{2,18},{10... | collective-permute-start | bytes 12582920 | tf_op jit(solution)/shard_map/ppermute | solution.py:971
  491.8 93.2 %collective-permute-start.17 = (bf16[128,64,256]{2,1,0:T(8,128)(2,1)}, bf16[128,64,256]{2,1,0:T(8,128)(2,1)}, u32[]{:S(2)}, u32[]{:S(2)}) collective-permute-start(bf16[128,64,256]{2,1,0:T(8,128)(2,1)} %get-tuple-element.175), channel_id=1, source_target_pairs={{0,8},{8,0},{16,24},{24,16},{1,9},{9,1},{17,25},{25,17},{2,10},{10... | collective-permute-start | bytes 12582920 | tf_op jit(solution)/shard_map/ppermute | solution.py:968
  530.0 55.0 %collective-permute-start.18 = (bf16[128,64,128]{2,1,0:T(8,128)(2,1)}, bf16[128,64,128]{2,1,0:T(8,128)(2,1)S(1)}, u32[]{:S(2)}, u32[]{:S(2)}) collective-permute-start(bf16[128,64,128]{2,1,0:T(8,128)(2,1)} %get-tuple-element.174.dx_own.refs_3_), channel_id=1, source_target_pairs={{0,1},{1,0},{2,3},{3,2},{4,5},{5,4},{6,7},{7,6},{8,9},{9,8},{10,11... | collective-permute-start | bytes 6291464 | tf_op jit(solution)/shard_map/ppermute | solution.py:974
  597.3 92.3 %collective-permute-start.22 = (bf16[128,64,256]{2,1,0:T(8,128)(2,1)}, bf16[128,64,256]{2,1,0:T(8,128)(2,1)S(1)}, u32[]{:S(2)}, u32[]{:S(2)}) collective-permute-start(bf16[128,64,256]{2,1,0:T(8,128)(2,1)} %get-tuple-element.177), channel_id=1, source_target_pairs={{0,16},{8,24},{16,0},{24,8},{1,17},{9,25},{17,1},{25,9},{2,18},{10... | collective-permute-start | bytes 12582920 | tf_op jit(solution)/shard_map/ppermute | solution.py:971
  599.1 95.9 %collective-permute-start.20 = (bf16[128,64,256]{2,1,0:T(8,128)(2,1)}, bf16[128,64,256]{2,1,0:T(8,128)(2,1)S(1)}, u32[]{:S(2)}, u32[]{:S(2)}) collective-permute-start(bf16[128,64,256]{2,1,0:T(8,128)(2,1)} %get-tuple-element.189), channel_id=1, source_target_pairs={{0,8},{8,0},{16,24},{24,16},{1,9},{9,1},{17,25},{25,17},{2,10},{10... | collective-permute-start | bytes 12582920 | tf_op jit(solution)/shard_map/ppermute | solution.py:968
  693.6 94.0 %collective-permute-start.23 = (bf16[128,64,256]{2,1,0:T(8,128)(2,1)}, bf16[128,64,256]{2,1,0:T(8,128)(2,1)}, u32[]{:S(2)}, u32[]{:S(2)}) collective-permute-start(bf16[128,64,256]{2,1,0:T(8,128)(2,1)} %add_convert_fusion), channel_id=1, source_target_pairs={{0,8},{8,0},{16,24},{24,16},{1,9},{9,1},{17,25},{25,17},{2,10},{10... | collective-permute-start | bytes 12582920 | tf_op jit(solution)/shard_map/ppermute | solution.py:968
  699.0 104.9 %collective-permute-start.21 = (bf16[128,64,256]{2,1,0:T(8,128)(2,1)}, bf16[128,64,256]{2,1,0:T(8,128)(2,1)}, u32[]{:S(2)}, u32[]{:S(2)}) collective-permute-start(bf16[128,64,256]{2,1,0:T(8,128)(2,1)} %add_convert_fusion.1), channel_id=1, source_target_pairs={{0,16},{8,24},{16,0},{24,8},{1,17},{9,25},{17,1},{25,9},{2,18},{10... | collective-permute-start | bytes 12582920 | tf_op jit(solution)/shard_map/ppermute | solution.py:971
  700.5 5.0 collective-permute-start.19
  (24 other events, 463.8 us)
Sparse Core Ops, SparseCore 0:
  703.5 126.6 all-reduce.1

commit v3 on v2

--- a/solution.py
+++ b/solution.py
@@ -557,32 +557,58 @@
     )
 
 
-def right_back_kernel(flag, dx_own, dx_other, a0, a1, out0, out1):
+def right_back_kernel(flag, *refs):
+    owns, others, firsts, seconds = refs[:4], refs[4:8], refs[8:12], refs[12:16]
+    out0, out1 = refs[16:]
+    half = out0.shape[1]
     own_first = flag[0] == 0
     for chan in range(CHANS):
-        rows = jnp.concatenate([a0[chan], a1[chan]], 0)
-        both = ordered(own_first, dx_own[chan], dx_other[chan])
-        grads = dot(both, rows).astype(BF16)
-        half = out0.shape[1]
-        out0[chan] = grads[:half]
-        out1[chan] = grads[half:]
-
-
-def right_back(which, dx_own, dx_other, a):
-    chans, half, lanes = a[0].shape
+        grads = jnp.concatenate(
+            [ordered(own_first, owns[q][chan], others[q][chan]) for q in range(4)], 1
+        )
+        values = jnp.concatenate([v[q][chan] for q in range(4) for v in (firsts, seconds)], 0)
+        total = dot(grads, values).astype(BF16)
+        out0[chan] = total[:half]
+        out1[chan] = total[half:]
+
+
+def right_back(which, owns, others, firsts, seconds):
+    chans, half, lanes = firsts[0].shape
     lead = lambda i, *_: (i, 0, 0)
     out = ((chans, half, lanes), BF16, (CHANS, half, lanes), lead)
     return call(
         right_back_kernel,
         (chans // CHANS,),
         [which],
-        [(v, (CHANS, half, 2 * half), lead) for v in (dx_own, dx_other)]
-        + [(v, (CHANS, half, lanes), lead) for v in a],
+        [(v, (CHANS, half, 2 * half), lead) for v in (*owns, *others)]
+        + [(v, (CHANS, half, lanes), lead) for v in (*firsts, *seconds)],
         [out, out],
         [],
+        25 * MICRO,
+        "right_back",
+    )
+
+
+def turn_kernel(first, second, out_ref):
+    for chan in range(first.shape[0]):
+        out_ref[chan] = jnp.transpose(jnp.concatenate([first[chan], second[chan]], 0))
+
+
+def turn(first, second):
+    chans, half, lanes = first.shape
+    lead = lambda i, *_: (i, 0, 0)
+    count = next(n for n in (43, 16, 8, 4, 2, 1) if chans % n == 0)
+    block = (count, half, lanes)
+    return call(
+        turn_kernel,
+        (chans // count,),
+        [],
+        [(first, block, lead), (second, block, lead)],
+        [((chans, lanes, 2 * half), BF16, (count, lanes, 2 * half), lead)],
+        [],
         12 * MICRO,
-        "right_back",
-    )
+        "turn",
+    )[0]
 
 
 def left_back_kernel(flag, *refs):
@@ -710,64 +736,79 @@
     )
 
 
-def reduce_kernel(part_ref, out_ref, half_s, crop_s, row_s, full_s, send, recv):
+def reduce_kernel(pair_ref, left_ref, right_ref, out_ref, full_s, core_s, crop_s, row_s, send, recv):
     side, spot, level = lax.axis_index("col"), lax.axis_index("crop"), lax.axis_index("row")
+    mesh_id = pl.DeviceIdType.MESH
     sibling = {"col": 1 - side}
-    others = [{"crop": lax.rem(spot + n, 4)} for n in range(1, 4)]
-    others += [{"row": lax.rem(level + n, 4)} for n in range(1, 4)]
+    crops = [{"crop": lax.rem(spot + n, 4)} for n in range(1, 4)]
+    levels = [{"row": lax.rem(level + n, 4)} for n in range(1, 4)]
     barrier = pltpu.get_barrier_semaphore()
-    for device in [sibling] + others:
-        pl.semaphore_signal(barrier, inc=1, device_id=device, device_id_type=pl.DeviceIdType.MESH)
+    for device in [sibling] + crops + levels:
+        pl.semaphore_signal(barrier, inc=1, device_id=device, device_id_type=mesh_id)
     pl.semaphore_wait(barrier, 7)
 
     def copy(source, target, index, device):
         return pltpu.make_async_remote_copy(
             src_ref=source, dst_ref=target, send_sem=send.at[index], recv_sem=recv.at[index],
-            device_id=device, device_id_type=pl.DeviceIdType.MESH,
+            device_id=device, device_id_type=mesh_id,
         )
 
-    rows = half_s.shape[0]
-    away = pl.multiple_of((1 - side) * rows, 8)
-    here = pl.multiple_of(side * rows, 8)
-    one = copy(part_ref.at[pl.ds(away, rows)], half_s, 0, sibling)
-    one.start()
-    one.wait()
-    crop_s[spot] = part_ref[pl.ds(here, rows)] + half_s[...]
-    sends = [copy(crop_s.at[spot], crop_s.at[spot], 1 + n, others[n]) for n in range(3)]
-    for one in sends:
-        one.start()
-    for one in sends:
-        one.wait()
-    row_s[level] = crop_s[0] + crop_s[1] + crop_s[2] + crop_s[3]
-    sends = [copy(row_s.at[level], row_s.at[level], 4 + n, others[3 + n]) for n in range(3)]
-    for one in sends:
-        one.start()
-    for one in sends:
-        one.wait()
-    full_s[side] = row_s[0] + row_s[1] + row_s[2] + row_s[3]
-    one = copy(full_s.at[side], full_s.at[side], 7, sibling)
-    one.start()
-    one.wait()
-    out_ref[:rows] = full_s[0]
-    out_ref[rows:] = full_s[1]
-
-
-def reduce_all(part):
-    rows, lanes = part.shape[0] // 2, part.shape[1]
+    def run(copies):
+        for one in copies:
+            one.start()
+        for one in copies:
+            one.wait()
+
+    half = full_s.shape[0] // 2
+    quarter, share = half // 4, half // 16
+    row = 0
+    for ref in (pair_ref, left_ref, right_ref):
+        full_s[row : row + ref.shape[0]] = ref[...]
+        row += ref.shape[0]
+    full_s[row:] = jnp.zeros((full_s.shape[0] - row, full_s.shape[1]), F32)
+    base = pl.multiple_of(side * half, 8)
+    run([copy(full_s.at[pl.ds(pl.multiple_of((1 - side) * half, 8), half)], core_s, 0, sibling)])
+    full_s[pl.ds(base, half)] += core_s[...]
+    def part(number):
+        return pl.ds(pl.multiple_of(base + number * quarter, 8), quarter)
+
+    run([copy(full_s.at[part(lax.rem(spot + n, 4))], crop_s.at[spot], n, crops[n - 1]) for n in range(1, 4)])
+    mine = part(spot)
+    crop_s[spot] = full_s[mine]
+    full_s[mine] = crop_s[0] + crop_s[1] + crop_s[2] + crop_s[3]
+    def slot(number):
+        return pl.ds(pl.multiple_of(base + spot * quarter + number * share, 8), share)
+
+    run([copy(full_s.at[slot(lax.rem(level + n, 4))], row_s.at[level], 3 + n, levels[n - 1]) for n in range(1, 4)])
+    own = slot(level)
+    row_s[level] = full_s[own]
+    out_ref[own] = row_s[0] + row_s[1] + row_s[2] + row_s[3]
+    run([copy(out_ref.at[own], out_ref.at[own], 6 + n, levels[n - 1]) for n in range(1, 4)])
+    run([copy(out_ref.at[mine], out_ref.at[mine], 9 + n, crops[n - 1]) for n in range(1, 4)])
+    run([copy(out_ref.at[pl.ds(base, half)], out_ref.at[pl.ds(base, half)], 13, sibling)])
+
+
+ALL_ROWS = 2048
+
+
+def reduce_all(*parts):
+    lanes = parts[0].shape[1]
     return pl.pallas_call(
         reduce_kernel,
-        out_shape=jax.ShapeDtypeStruct(part.shape, F32),
+        out_shape=jax.ShapeDtypeStruct((ALL_ROWS, lanes), F32),
         scratch_shapes=[
-            pltpu.VMEM((rows, lanes), F32),
-            pltpu.VMEM((4, rows, lanes), F32),
-            pltpu.VMEM((4, rows, lanes), F32),
-            pltpu.VMEM((2, rows, lanes), F32),
-            pltpu.SemaphoreType.DMA((8,)),
-            pltpu.SemaphoreType.DMA((8,)),
+            pltpu.VMEM((ALL_ROWS, lanes), F32),
+            pltpu.VMEM((ALL_ROWS // 2, lanes), F32),
+            pltpu.VMEM((4, ALL_ROWS // 8, lanes), F32),
+            pltpu.VMEM((4, ALL_ROWS // 32, lanes), F32),
+            pltpu.SemaphoreType.DMA((14,)),
+            pltpu.SemaphoreType.DMA((14,)),
         ],
-        compiler_params=pltpu.CompilerParams(collective_id=1, has_side_effects=True),
+        compiler_params=pltpu.CompilerParams(
+            collective_id=1, has_side_effects=True, vmem_limit_bytes=VMEM_LIMIT
+        ),
         name="reduce_all",
-    )(part)
+    )(*parts)
 
 
 def flip(a, b):
@@ -778,60 +819,85 @@
     return 2 * lax.rem(a, 2) + a // 2
 
 
-def spread_kernel(acts_ref, wave0_ref, mid1_ref, mid0, plane_send, plane_recv, level_send, level_recv, local):
-    side, spot, level = lax.axis_index("col"), lax.axis_index("crop"), lax.axis_index("row")
+def spread_kernel(
+    acts_ref, wave0_ref, wave1_ref, x_ref, y_ref, mid,
+    plane_send, plane_recv, level_send, level_recv, share_send, share_recv, local,
+):
+    spot, level = lax.axis_index("crop"), lax.axis_index("row")
     chans = acts_ref.shape[0]
     cuts = [(0, chans // 2), (chans // 2, chans - chans // 2)]
+    waves = (wave0_ref, wave1_ref)
+    mesh_id = pl.DeviceIdType.MESH
     barrier = pltpu.get_barrier_semaphore()
     for n in range(1, 4):
         for device in ({"crop": lax.rem(spot + n, 4)}, {"row": lax.rem(level + n, 4)}):
-            pl.semaphore_signal(barrier, inc=1, device_id=device, device_id_type=pl.DeviceIdType.MESH)
+            pl.semaphore_signal(barrier, inc=1, device_id=device, device_id_type=mesh_id)
     pl.semaphore_wait(barrier, 6)
 
     def plane_copy(wave, cut, distance):
-        first, count = cuts[cut] if wave == 0 else (0, chans)
+        first, count = cuts[cut]
         target = flip(spot, distance)
-        rows = pl.ds(pl.multiple_of(32 * target + 16 * wave, 16), 16)
-        source = acts_ref.at[pl.ds(first, count), rows]
-        landing = (mid0 if wave == 0 else mid1_ref).at[distance, pl.ds(first, count)]
-        index = 4 * cut + distance if wave == 0 else 8 + distance
+        source = acts_ref.at[
+            pl.ds(first, count), pl.ds(pl.multiple_of(32 * target + 16 * wave, 16), 16)
+        ]
+        landing = mid.at[wave, distance, pl.ds(first, count)]
+        index = 8 * wave + 4 * cut + distance
         if distance == 0:
             return pltpu.make_async_copy(source, landing, plane_recv.at[index])
         return pltpu.make_async_remote_copy(
             src_ref=source, dst_ref=landing, send_sem=plane_send.at[index], recv_sem=plane_recv.at[index],
-            device_id={"crop": target}, device_id_type=pl.DeviceIdType.MESH,
+            device_id={"crop": target}, device_id_type=mesh_id,
         )
 
-    def level_copy(cut, label, distance):
+    def landed(wave, cut, label):
         first, count = cuts[cut]
-        source = mid0.at[distance, pl.ds(first, count)]
-        landing = wave0_ref.at[pl.ds(first, count), pl.ds(16 * label, 16)]
+        return waves[wave].at[pl.ds(first, count), pl.ds(16 * label, 16)]
+
+    def level_copy(wave, cut, label, distance):
+        first, count = cuts[cut]
+        source = mid.at[wave, distance, pl.ds(first, count)]
         target = swap_bits(flip(spot, distance))
-        index = 4 * cut + label
+        index = 8 * wave + 4 * cut + label
         remote = pltpu.make_async_remote_copy(
-            src_ref=source, dst_ref=landing, send_sem=level_send.at[index], recv_sem=level_recv.at[index],
-            device_id={"row": target}, device_id_type=pl.DeviceIdType.MESH,
+            src_ref=source, dst_ref=landed(wave, cut, label),
+            send_sem=level_send.at[index], recv_sem=level_recv.at[index],
+            device_id={"row": target}, device_id_type=mesh_id,
         )
-        return target, remote, pltpu.make_async_copy(source, landing, local.at[cut])
-
-    def each_level(action):
+        return target, remote, pltpu.make_async_copy(source, landed(wave, cut, label), local.at[2 * wave + cut])
+
+    def each_level(action, wave, cut):
+        for label in range(4):
+            for distance in range(4):
+
+                @pl.when(flip(level, label) == distance)
+                def _(label=label, distance=distance):
+                    action(wave, cut, label, distance)
+
+    def shares(cut, label):
+        first, count = cuts[cut]
+        index = 8 * cut + 2 * label
+        return [
+            pltpu.make_async_remote_copy(
+                src_ref=landed(0, cut, label),
+                dst_ref=ref.at[pl.ds(first, count), pl.ds(16 * label, 16)],
+                send_sem=share_send.at[index + n], recv_sem=share_recv.at[index + n],
+                device_id={"crop": flip(spot, 1 + n)}, device_id_type=mesh_id,
+            )
+            for n, ref in enumerate((x_ref, y_ref))
+        ]
+
+    plane = [
+        [[plane_copy(wave, cut, distance) for distance in range(4)] for cut in range(2)] for wave in range(2)
+    ]
+    for wave in range(2):
         for cut in range(2):
-            for label in range(4):
-                for distance in range(4):
-
-                    @pl.when(flip(level, label) == distance)
-                    def _(cut=cut, label=label, distance=distance):
-                        action(cut, label, distance)
-
-    plane = [plane_copy(0, cut, distance) for cut in range(2) for distance in range(4)]
-    plane += [plane_copy(1, 0, distance) for distance in range(4)]
-    for one in plane:
-        one.start()
-
-    def begin(cut, label, distance):
-        one = plane[4 * cut + distance]
+            for one in plane[wave][cut]:
+                one.start()
+
+    def begin(wave, cut, label, distance):
+        one = plane[wave][cut][distance]
         one.wait() if distance == 0 else one.wait_recv()
-        target, remote, stay = level_copy(cut, label, distance)
+        target, remote, stay = level_copy(wave, cut, label, distance)
 
         @pl.when(target == level)
         def _():
@@ -841,8 +907,8 @@
         def _():
             remote.start()
 
-    def finish(cut, label, distance):
-        target, remote, stay = level_copy(cut, label, distance)
+    def arrive(wave, cut, label, distance):
+        target, remote, stay = level_copy(wave, cut, label, distance)
 
         @pl.when(target == level)
         def _():
@@ -850,18 +916,31 @@
 
         @pl.when(target != level)
         def _():
-            remote.wait()
-
-    each_level(begin)
-    for index, one in enumerate(plane):
-        if index % 4 == 0:
-            if index == 8:
+            remote.wait_recv()
+            remote.wait_send()
+
+    def pass_on(cut):
+        each_level(arrive, 0, cut)
+        for label in range(4):
+            for one in shares(cut, label):
+                one.start()
+
+    each_level(begin, 0, 0)
+    each_level(begin, 0, 1)
+    each_level(begin, 1, 0)
+    pass_on(0)
+    each_level(begin, 1, 1)
+    pass_on(1)
+    for wave in range(2):
+        for cut in range(2):
+            for one in plane[wave][cut][1:]:
+                one.wait_send()
+    each_level(arrive, 1, 0)
+    each_level(arrive, 1, 1)
+    for cut in range(2):
+        for label in range(4):
+            for one in shares(cut, label):
                 one.wait()
-        else:
-            one.wait_send()
-            if index > 8:
-                one.wait_recv()
-    each_level(finish)
 
 
 def spread(acts_major):
@@ -870,19 +949,11 @@
     return pl.pallas_call(
         spread_kernel,
         in_specs=[anywhere],
-        out_specs=[anywhere, anywhere],
-        out_shape=[
-            jax.ShapeDtypeStruct((chans, rows // 2, lanes), BF16),
-            jax.ShapeDtypeStruct((4, chans, rows // 8, lanes), BF16),
-        ],
-        scratch_shapes=[
-            pltpu.VMEM((4, chans, rows // 8, lanes), BF16),
-            pltpu.SemaphoreType.DMA((12,)),
-            pltpu.SemaphoreType.DMA((12,)),
-            pltpu.SemaphoreType.DMA((8,)),
-            pltpu.SemaphoreType.DMA((8,)),
-            pltpu.SemaphoreType.DMA((2,)),
-        ],
+        out_specs=[anywhere] * 4,
+        out_shape=[jax.ShapeDtypeStruct((chans, rows // 2, lanes), BF16)] * 4,
+        scratch_shapes=[pltpu.VMEM((2, 4, chans, rows // 8, lanes), BF16)]
+        + [pltpu.SemaphoreType.DMA((16,)) for _ in range(6)]
+        + [pltpu.SemaphoreType.DMA((4,))],
         compiler_params=pltpu.CompilerParams(
             collective_id=2, has_side_effects=True, vmem_limit_bytes=VMEM_LIMIT
         ),
@@ -890,12 +961,14 @@
     )(acts_major)
 
 
-def update_kernel(early_ref, left_ref, right_ref, *refs):
+def update_kernel(early_ref, *refs):
     ins, outs = refs[:21], refs[21:]
+    left_ref = early_ref.at[pl.ds(SUM_ROWS, SIDE_ROWS)]
+    right_ref = early_ref.at[pl.ds(SUM_ROWS + SIDE_ROWS, SIDE_ROWS)]
     loss_ref, total_ref, norm_ref = outs[21:]
     total = early_ref[LOSS_ROW - 1, 127]
     inverse = 1.0 / total
-    half = left_ref.shape[0] - 16
+    half = SIDE_ROWS - 16
     grads = [
         jnp.concatenate(
             [
@@ -934,7 +1007,7 @@
     total_ref[...] = jnp.full((1, 1), total, F32)
 
 
-def update(early, left, right, params, firsts, seconds):
+def update(early, params, firsts, seconds):
     flat = [v.reshape(1, -1) if v.ndim == 1 else v for v in (*params, *firsts, *seconds)]
     shapes = [v.shape for v in flat] + [(1, 1)] * 3
     outs = pl.pallas_call(
@@ -942,7 +1015,7 @@
         out_shape=[jax.ShapeDtypeStruct(s, F32) for s in shapes],
         compiler_params=pltpu.CompilerParams(vmem_limit_bytes=VMEM_LIMIT),
         name="update",
-    )(early, left, right, *flat)
+    )(early, *flat)
     outs = [v.reshape(-1) if index in (6, 13, 20) else v for index, v in enumerate(outs)]
     return (*outs[:21], *[v[0, 0] for v in outs[21:]])
 
@@ -970,6 +1043,9 @@
     def over_y(v):
         return lax.ppermute(v, "crop", [(g, g ^ 2) for g in range(4)])
 
+    def over_both(v):
+        return lax.ppermute(v, "crop", [(g, g ^ 3) for g in range(4)])
+
     def over_core(v):
         return lax.ppermute(v, "col", [(0, 1), (1, 0)])
 
@@ -980,17 +1056,10 @@
     acts_major = jnp.transpose(pair_acts[0], (2, 0, 1))
 
     acts_major = jnp.concatenate([acts_major, code_own[None]], 0)
-    wave0, mid1 = spread(acts_major)
-
-    def along_z(label):
-        piece = lax.dynamic_index_in_dim(mid1, level ^ label, 0, keepdims=False)
-        pairs = [(g * 4 + z, g * 4 + plane_of[g ^ label ^ z]) for g in range(4) for z in range(4)]
-        stays = sum(((spot * 4 + level) == i).astype(jnp.int32) for i, j in pairs if i == j)
-        moved = lax.ppermute(piece, ("crop", "row"), [(i, j) for i, j in pairs if i != j])
-        return jnp.where(stays > 0, piece, moved)
+    wave0, wave1, wave0_x, wave0_y = spread(acts_major)
 
     count = jnp.sum(own_mask).astype(F32)
-    share = count * count / (lax.axis_size("row") * lax.axis_size("col"))
+    share_count = lax.axis_size("row") * lax.axis_size("col")
     low_in, low_out, low_t1, low_t2, low_dist = [
         weight.astype(BF16) for weight in (w_in, w_out, w_t1, w_t2, w_dist)
     ]
@@ -998,27 +1067,32 @@
     bias_wide = jnp.broadcast_to(dist_bias[:, None], (dist_bias.shape[0], 128))
     in_T = low_in.T
 
-    pieces = [along_z(label) for label in range(4)]
-    acts, a, b_own = [], [], []
-    for h in range(2):
-        acts.append(wave0 if h == 0 else jnp.concatenate([after(v, a[0]) for v in pieces], 1))
-        left, right = project(acts[h], in_T[: 4 * width], ln_wide)
-        a.append(left)
-        b_own.append(right)
-    b_x = [over_x(v) for v in b_own]
-    b_y = [over_y(v) for v in b_own]
-    b_d = [over_y(b_x[0]), over_x(b_y[1])]
-    blocks = [b_own, b_x, b_y, b_d]
+    proj_w = in_T[: 4 * width]
+    acts, left, right = {}, {}, {}
+
+    def share(q, source, shift, half):
+        acts[q, half] = shift(acts[source, half])
+
+    def values(q, half, *earlier):
+        left[q, half], right[q, half] = project(after(acts[q, half], *earlier), proj_w, ln_wide)
+        return right[q, half]
+
+    acts[0, 0], acts[0, 1], acts[1, 0], acts[2, 0] = wave0, wave1, wave0_x, wave0_y
+    share(1, 0, over_x, 1)
+    share(2, 0, over_y, 1)
+    done = values(0, 0)
+    done = values(0, 1, done)
 
     weights = (
         low_out.T, low_out, in_T[4 * width :], low_t1.T, low_t1, low_t2.T, low_t2, low_dist.T, low_dist,
     )
     flags = [(side ^ ((spot ^ q) // 2) ^ (crop // 2)).astype(jnp.int32)[None] for q in range(4)]
-    keeps, recvs, dx_own, dx_other, back = {}, {}, {}, {}, {}
+    keeps, recvs, dx_own, dx_other, seen, seen_other = {}, {}, {}, {}, {}, {}
     sums = []
 
     def forward(q, *earlier):
-        keeps[q], send = triangle(flags[q], [after(v, *earlier) for v in a], blocks[q])
+        mine = [after(left[0, h], *earlier) for h in range(2)]
+        keeps[q], send = triangle(flags[q], mine, [right[q, h] for h in range(2)])
         recvs[q] = over_core(send)
         return send
 
@@ -1029,50 +1103,53 @@
             after(place, *earlier), keeps[q], recvs[q], acts_kj, ln_wide, weights, bias_wide, list(sums), q == 3
         )
         dx_other[q] = over_core(dx_own[q])
+        seen[q] = (lambda v: v, over_x, over_y, over_both)[q](dx_own[q])
+        seen_other[q] = over_core(seen[q]) if q in (1, 2) else dx_other[q]
         return dx_own[q]
 
-    def backward(q, *earlier):
-        back[q] = right_back(after(flags[q], *earlier), dx_own[q], dx_other[q], a)
-        return back[q][0]
-
-    done = forward(0, b_own[1], b_x[0], b_y[0])
-    acts_kj = jnp.swapaxes(jnp.concatenate([after(v, done) for v in acts], 1), 1, 2)
-    done = middle(0, acts_kj)
+    done = forward(0, done)
+    acts_kj = turn(after(acts[0, 0], done), acts[0, 1])
+    done = values(1, 0, acts_kj)
+    done = values(2, 0, done)
+    done = middle(0, done)
+    acts[1, 1], acts[2, 1] = after(acts[1, 1], done), after(acts[2, 1], done)
+    acts[3, 0] = over_y(after(acts[1, 0], done))
+    acts[3, 1] = over_x(acts[2, 1])
+    done = values(1, 1, done)
     done = forward(1, done)
+    done = values(2, 1, done)
     done = forward(2, done)
     done = middle(1, done)
     done = middle(2, done)
-    done = backward(1, done)
-    done = backward(2, done)
+    done = values(3, 0, done)
+    done = values(3, 1, done, seen[1])
     done = forward(3, done)
-    y0, x1 = over_y(back[2][0]), over_x(back[1][1])
-    done = middle(3, done)
-    done = backward(3, done, y0, x1)
-    d0, d1 = over_y(back[3][0]), over_x(back[3][1])
-    done = backward(0, done)
+    done = middle(3, done, seen[2], seen_other[1])
     d_left = left_back(
-        after(flags[0], done),
+        after(flags[0], done, seen_other[2]),
         [dx_own[q] for q in range(4)],
         [dx_other[q] for q in range(4)],
-        [v[0] for v in blocks],
-        [v[1] for v in blocks],
-    )
-    x0 = (back[1][0].astype(F32) + d0.astype(F32)).astype(BF16)
-    y1 = (back[2][1].astype(F32) + d1.astype(F32)).astype(BF16)
-    own = [[back[0][0], y0, over_x(x0)], [back[0][1], x1, over_y(y1)]]
+        [right[q, 0] for q in range(4)],
+        [right[q, 1] for q in range(4)],
+    )
+    pair_sums = sums[0].at[LOSS_ROW - 1, 127].set(count * count / share_count)
+    left_sum, right_sum = [], []
     left_w, right_w = in_T[: 2 * width], in_T[2 * width : 4 * width]
-    left, right = [], []
     for h in range(2):
-        left = input_back(acts[h], left_w, ln_wide, [d_left[h]], left, h == 1)
-    everywhere = ("crop", "row", "col")
-    early = sums[0].at[LOSS_ROW - 1, 127].set(share)
-    early = lax.psum(early, everywhere)
-    own[0][0] = after(own[0][0], left[0])
+        left_sum = input_back(acts[0, h], left_w, ln_wide, [d_left[h]], left_sum, h == 1)
+        if h == 0:
+            seen_other[3] = over_core(after(seen[3], left_sum[0]))
+    d_right = right_back(
+        after(flags[0], left_sum[0]),
+        [seen[q] for q in range(4)],
+        [seen_other[q] for q in range(4)],
+        [left[q, 0] for q in range(4)],
+        [left[q, 1] for q in range(4)],
+    )
     for h in range(2):
-        right = input_back(acts[h], right_w, ln_wide, own[h], right, h == 1)
-    both = reduce_all(jnp.concatenate([left[0], after(right[0], early)], 0))
+        right_sum = input_back(acts[0, h], right_w, ln_wide, [d_right[h]], right_sum, h == 1)
     params = (w_in, w_out, w_t1, w_t2, w_dist, norm_params, dist_bias)
-    return update(early, both[:SIDE_ROWS], both[SIDE_ROWS:], params, firsts, seconds)
+    return update(reduce_all(pair_sums, left_sum[0], right_sum[0]), params, firsts, seconds)
 
 
 def solution(mesh):

time: 885 us -> 749 us (0.85)
  waiting for transfers between devices: 224 us -> 42.1 us
  Pallas kernels: 482 us -> 646 us
  starting transfers between devices: 64.7 us -> 10.2 us
  local copies, waits for them, and re-layouts: 55.9 us -> 31.5 us
  other arithmetic: 34.8 us -> 13.1 us
  between operations: 15.4 us -> 1.82 us
    ppermute x6 -> x3, waiting for transfers between devices: 146 us -> 0.01 us  [over_y(): return lax.ppermute(v, 'crop', [(g, g ^ 2) for g in range(4)])]
    pallas_call x2, Pallas kernels: 144 us -> 245 us  [the longest x1 214 us: spread(): pl.pallas_call(spread_kernel, in_specs=[anywhere], out_specs=[anywhere] *...]
    pallas_call x19 -> x23, Pallas kernels: 334 us -> 396 us  [call(): pl.pallas_call(kernel, grid_spec=pltpu.PrefetchScalarGridSpec(num_scalar_...]
    ppermute x6 -> x3, starting transfers between devices: 38.7 us -> 2.16 us  [over_x(): return lax.ppermute(v, 'crop', [(g, g ^ 1) for g in range(4)])]
    ppermute x4 -> x1, waiting for transfers between devices: 32.4 us -> 10.1 us  [over_both(): return lax.ppermute(v, 'crop', [(g, g ^ 3) for g in range(4)])]
    transpose x1 -> x0, local copies, waits for them, and re-layouts: 12 us -> none  [on_device_planes(): jnp.swapaxes(jnp.concatenate([after(v, done) for v in acts], 1), 1, 2)]
    ppermute x6 -> x3, starting transfers between devices: 14.3 us -> 4.14 us  [over_y(): return lax.ppermute(v, 'crop', [(g, g ^ 2) for g in range(4)])]
    psum x1 -> x0, waiting for transfers between devices: 9.33 us -> none  [on_device_planes(): early = lax.psum(early, everywhere)]
  transfers between devices with their start and end apart: 25 -> 18, of which waited for: 10 -> 4; matrix products, arithmetic and copies ran while one was open for 6% -> 2% of each run, Pallas kernels for 35% -> 47%
where the time goes in v3:
time: 749 us; the launch traced here: 744 us
  Pallas kernels  646 us (86%)
  waiting for transfers between devices  42.1 us (6%)
  local copies, waits for them, and re-layouts  31.5 us (4%)
  other arithmetic  13.1 us (2%)
  starting transfers between devices  10.2 us (1%)
    pallas_call x23, Pallas kernels, call(): pl.pallas_call(kernel, grid_spec=pltpu.PrefetchScalarGridSpec(num_scalar_...  396 us
    pallas_call x1, Pallas kernels, spread(): pl.pallas_call(spread_kernel, in_specs=[anywhere], out_specs=[anywhere] *...  214 us
    pallas_call x1, Pallas kernels, reduce_all(): pl.pallas_call(reduce_kernel, out_shape=jax.ShapeDtypeStruct((ALL_ROWS, l...  30.2 us
    ppermute x3, waiting for transfers between devices, over_x(): return lax.ppermute(v, 'crop', [(g, g ^ 1) for g in range(4)])  27.4 us
    unnamed x44, local copies, waits for them, and re-layouts  22.2 us
  transfers between devices with their start and end apart: 18, of which 4 were waited for; matrix products, arithmetic and copies ran while one was open for 2% of the time, Pallas kernels for 47%

profile of v3, /device:TPU:0, one launch (start us, length us, event | category | flops | bytes accessed | tf_op | source)
XLA Modules:
  0.0 744.3 jit_solution(9684773443226479428)
XLA Ops:
  2.0 12.7 %copy.48 = bf16[1,128,256,128]{2,1,3,0:T(8,128)(2,1)} copy(bf16[1,128,256,128]{3,2,1,0:T(8,128)(2,1)} %param.26) | data formatting | bytes 16777216 | tf_op args[0]
  22.2 214.3 %spread.1 = (bf16[129,64,256]{2,1,0:T(8,128)(2,1)}, bf16[129,64,256]{2,1,0:T(8,128)(2,1)}, bf16[129,64,256]{2,1,0:T(8,128)(2,1)}, bf16[129,64,256]{2,1,0:T(8,128)(2,1)}) custom-call(bf16[129,128,256]{2,1,0:T(8,128)(2,1)} %pad_maximum_fusion.acts_ref), custom_call_target="tpu_custom_call" | custom-call | tf_op jit(solution)/shard_map/spread/pallas_call | solution.py:949
  240.4 13.5 %project.8 = (bf16[128,64,256]{2,1,0:T(8,128)(2,1)}, bf16[128,64,256]{2,1,0:T(8,128)(2,1)}) custom-call(bf16[129,64,256]{2,1,0:T(8,128)(2,1)} %get-tuple-element.148.acts_ref.code_ref.first, bf16[129,64,256]{2,1,0:T(8,128)(2,1)} %get-tuple-element.148.acts_ref.code_ref.first, bf16[512,128]{1,0:T(8,128)(2,1)} %slice.35.w_ref, ...), custom_call_target="tpu_custom_call" | custom-call | flops 15000 | bytes 1 | tf_op jit(solution)/shard_map/project/pallas_call | solution.py:293
  253.9 13.4 %project.9 = (bf16[128,64,256]{2,1,0:T(8,128)(2,1)}, bf16[128,64,256]{2,1,0:T(8,128)(2,1)}) custom-call(bf16[129,64,256]{2,1,0:T(8,128)(2,1)} %get-tuple-element.143.acts_ref.code_ref.second, bf16[129,64,256]{2,1,0:T(8,128)(2,1)} %get-tuple-element.143.acts_ref.code_ref.second, bf16[512,128]{1,0:T(8,128)(2,1)} %slice.35.w_ref, ...), custom_call_target="tpu_custom_call" | custom-call | flops 15000 | bytes 1 | tf_op jit(solution)/shard_map/project/pallas_call | solution.py:293
  267.3 12.6 %triangle.4 = (f32[128,64,128]{2,1,0:T(8,128)}, bf16[128,64,128]{2,1,0:T(8,128)(2,1)}) custom-call(s32[1]{0:T(128)} %bitcast.10.flag, bf16[128,64,256]{2,1,0:T(8,128)(2,1)} %get-tuple-element.183.a0.refs_8_, bf16[128,64,256]{2,1,0:T(8,128)(2,1)} %get-tuple-element.184.a1.refs_12_, bf16[128,64,256]{2,1,0:T(8,128)(2,1)} %get-tuple-element.142.b0.refs_8_, ...), custom_call_target="tpu_custom_call" | custom-call | flops 14000 | bytes 1 | tf_op jit(solution)/shard_map/triangle/pallas_call | solution.py:293
  288.7 13.5 %project.10 = (bf16[128,64,256]{2,1,0:T(8,128)(2,1)}, bf16[128,64,256]{2,1,0:T(8,128)(2,1)}) custom-call(bf16[129,64,256]{2,1,0:T(8,128)(2,1)} %get-tuple-element.157.acts_ref.code_ref, bf16[129,64,256]{2,1,0:T(8,128)(2,1)} %get-tuple-element.157.acts_ref.code_ref, bf16[512,128]{1,0:T(8,128)(2,1)} %slice.35.w_ref, f32[6,128,128]{2,1,0:T(8,128)} %broadcast_in_dim.33.ln_ref), custom_call_target="tpu_custom_call" | custom-call | flops 15000 | bytes 1 | tf_op jit(solution)/shard_map/project/pallas_call | solution.py:293
  302.2 13.6 %project.11 = (bf16[128,64,256]{2,1,0:T(8,128)(2,1)}, bf16[128,64,256]{2,1,0:T(8,128)(2,1)}) custom-call(bf16[129,64,256]{2,1,0:T(8,128)(2,1)} %get-tuple-element.151.acts_ref.code_ref, bf16[129,64,256]{2,1,0:T(8,128)(2,1)} %get-tuple-element.151.acts_ref.code_ref, bf16[512,128]{1,0:T(8,128)(2,1)} %slice.35.w_ref, f32[6,128,128]{2,1,0:T(8,128)} %broadcast_in_dim.33.ln_ref), custom_call_target="tpu_custom_call" | custom-call | flops 15000 | bytes 1 | tf_op jit(solution)/shard_map/project/pallas_call | solution.py:293
  324.1 32.0 %pair.4 = (bf16[128,64,128]{2,1,0:T(8,128)(2,1)}, f32[1352,128]{1,0:T(8,128)}, f32[7,128,128]{2,1,0:T(8,128)}) custom-call(s32[2]{0:T(128)} %pad_add_fusion.1.place, f32[128,64,128]{2,1,0:T(8,128)} %get-tuple-element.154.x_keep, bf16[128,64,128]{2,1,0:T(8,128)(2,1)} %copy-done.4, bf16[129,256,128]{2,1,0:T(8,128)(2,1)} %turn.1.acts_ref.code_ref, ...), custom_call_target="tpu_custom_call" | custom-call | flops 35000 | bytes 1 | tf_op jit(solution)/shard_map/pair/pallas_call | solution.py:293
  356.1 13.5 %project.12 = (bf16[128,64,256]{2,1,0:T(8,128)(2,1)}, bf16[128,64,256]{2,1,0:T(8,128)(2,1)}) custom-call(bf16[129,64,256]{2,1,0:T(8,128)(2,1)} %collective-permute-done.4.acts_ref.code_ref, bf16[129,64,256]{2,1,0:T(8,128)(2,1)} %collective-permute-done.4.acts_ref.code_ref, bf16[512,128]{1,0:T(8,128)(2,1)} %slice.35.w_ref, f32[6,128,128]{2,1,0:T(8,128)} %broadcast_in_dim.33.ln_ref), custom_call_target="tpu_custom_call" | custom-call | flops 15000 | bytes 1 | tf_op jit(solution)/shard_map/project/pallas_call | solution.py:293
  384.7 13.4 %project.13 = (bf16[128,64,256]{2,1,0:T(8,128)(2,1)}, bf16[128,64,256]{2,1,0:T(8,128)(2,1)}) custom-call(bf16[129,64,256]{2,1,0:T(8,128)(2,1)} %collective-permute-done.acts_ref.code_ref, bf16[129,64,256]{2,1,0:T(8,128)(2,1)} %collective-permute-done.acts_ref.code_ref, bf16[512,128]{1,0:T(8,128)(2,1)} %slice.35.w_ref, f32[6,128,128]{2,1,0:T(8,128)} %broadcast_in_dim.33.ln_ref), custom_call_target="tpu_custom_call" | custom-call | flops 15000 | bytes 1 | tf_op jit(solution)/shard_map/project/pallas_call | solution.py:293
  412.6 32.6 %pair.5 = (bf16[128,64,128]{2,1,0:T(8,128)(2,1)}, f32[1352,128]{1,0:T(8,128)}, f32[7,128,128]{2,1,0:T(8,128)}) custom-call(s32[2]{0:T(128)} %pad_add_fusion.3.place, f32[128,64,128]{2,1,0:T(8,128)} %get-tuple-element.170.x_keep, bf16[128,64,128]{2,1,0:T(8,128)(2,1)} %copy-done.7, bf16[129,256,128]{2,1,0:T(8,128)(2,1)} %turn.1.acts_ref.code_ref, ...), custom_call_target="tpu_custom_call" | custom-call | flops 35000 | bytes 1 | tf_op jit(solution)/shard_map/pair/pallas_call | solution.py:293
  445.9 32.3 %pair.6 = (bf16[128,64,128]{2,1,0:T(8,128)(2,1)}, f32[1352,128]{1,0:T(8,128)}, f32[7,128,128]{2,1,0:T(8,128)}) custom-call(s32[2]{0:T(128)} %pad_add_fusion.2.place, f32[128,64,128]{2,1,0:T(8,128)} %get-tuple-element.175.x_keep, bf16[128,64,128]{2,1,0:T(8,128)(2,1)} %collective-permute-done.6.x_recv, bf16[129,256,128]{2,1,0:T(8,128)(2,1)} %turn.1.acts_ref.code_ref, ...), custom_call_target="tpu_custom_call" | custom-call | flops 35000 | bytes 1 | tf_op jit(solution)/shard_map/pair/pallas_call | solution.py:293
  480.3 13.5 %project.14 = (bf16[128,64,256]{2,1,0:T(8,128)(2,1)}, bf16[128,64,256]{2,1,0:T(8,128)(2,1)}) custom-call(bf16[129,64,256]{2,1,0:T(8,128)(2,1)} %collective-permute-done.3.acts_ref.code_ref, bf16[129,64,256]{2,1,0:T(8,128)(2,1)} %collective-permute-done.3.acts_ref.code_ref, bf16[512,128]{1,0:T(8,128)(2,1)} %slice.35.w_ref, f32[6,128,128]{2,1,0:T(8,128)} %broadcast_in_dim.33.ln_ref), custom_call_target="tpu_custom_call" | custom-call | flops 15000 | bytes 1 | tf_op jit(solution)/shard_map/project/pallas_call | solution.py:293
  493.8 27.4 %collective-permute-done.7.refs_1_ = bf16[128,64,128]{2,1,0:T(8,128)(2,1)} collective-permute-done((bf16[128,64,128]{2,1,0:T(8,128)(2,1)}, bf16[128,64,128]{2,1,0:T(8,128)(2,1)}, u32[]{:S(2)}, u32[]{:S(2)}) %collective-permute-start.7) | collective-permute-done | bytes 2097184 | tf_op jit(solution)/shard_map/ppermute | solution.py:1041
  521.3 13.5 %project.15 = (bf16[128,64,256]{2,1,0:T(8,128)(2,1)}, bf16[128,64,256]{2,1,0:T(8,128)(2,1)}) custom-call(bf16[129,64,256]{2,1,0:T(8,128)(2,1)} %collective-permute-done.2.acts_ref.code_ref, bf16[129,64,256]{2,1,0:T(8,128)(2,1)} %collective-permute-done.2.acts_ref.code_ref, bf16[512,128]{1,0:T(8,128)(2,1)} %slice.35.w_ref, f32[6,128,128]{2,1,0:T(8,128)} %broadcast_in_dim.33.ln_ref), custom_call_target="tpu_custom_call" | custom-call | flops 15000 | bytes 1 | tf_op jit(solution)/shard_map/project/pallas_call | solution.py:293
  534.8 12.7 %triangle.7 = (f32[128,64,128]{2,1,0:T(8,128)}, bf16[128,64,128]{2,1,0:T(8,128)(2,1)}) custom-call(s32[1]{0:T(128)} %bitcast.2.flag, bf16[128,64,256]{2,1,0:T(8,128)(2,1)} %get-tuple-element.183.a0.refs_8_, bf16[128,64,256]{2,1,0:T(8,128)(2,1)} %get-tuple-element.184.a1.refs_12_, bf16[128,64,256]{2,1,0:T(8,128)(2,1)} %get-tuple-element.180.b0.refs_11_, ...), custom_call_target="tpu_custom_call" | custom-call | flops 14000 | bytes 1 | tf_op jit(solution)/shard_map/triangle/pallas_call | solution.py:293
  552.1 32.6 %pair.7 = (bf16[128,64,128]{2,1,0:T(8,128)(2,1)}, f32[1352,128]{1,0:T(8,128)}, f32[7,128,128]{2,1,0:T(8,128)}) custom-call(s32[2]{0:T(128)} %pad_add_fusion.place, f32[128,64,128]{2,1,0:T(8,128)} %get-tuple-element.187.x_keep, bf16[128,64,128]{2,1,0:T(8,128)(2,1)} %collective-permute-done.10.x_recv, bf16[129,256,128]{2,1,0:T(8,128)(2,1)} %turn.1.acts_ref.code_ref, ...), custom_call_target="tpu_custom_call" | custom-call | flops 35000 | bytes 1 | tf_op jit(solution)/shard_map/pair/pallas_call | solution.py:293
  589.3 19.8 %left_back.1 = (bf16[128,64,256]{2,1,0:T(8,128)(2,1)}, bf16[128,64,256]{2,1,0:T(8,128)(2,1)}) custom-call(s32[1]{0:T(128)} %bitcast.10.flag, bf16[128,64,128]{2,1,0:T(8,128)(2,1)} %get-tuple-element.155.refs_0_, bf16[128,64,128]{2,1,0:T(8,128)(2,1)} %get-tuple-element.173.refs_1_, bf16[128,64,128]{2,1,0:T(8,128)(2,1)} %get-tuple-element.178.refs_2_, ...), custom_call_target="tpu_custom_call" | custom-call | flops 25000 | bytes 1 | tf_op jit(solution)/shard_map/left_back/pallas_call | solution.py:293
  609.1 14.8 %input_back.4 = (f32[272,128]{1,0:T(8,128)}, f32[256,128]{1,0:T(8,128)}, f32[256,128]{1,0:T(8,128)}) custom-call(bf16[129,64,256]{2,1,0:T(8,128)(2,1)} %get-tuple-element.148.acts_ref.code_ref.first, bf16[129,64,256]{2,1,0:T(8,128)(2,1)} %get-tuple-element.148.acts_ref.code_ref.first, bf16[256,128]{1,0:T(8,128)(2,1)} %get-tuple-element.262.w_ref, ...), custom_call_target="tpu_custom_call" | custom-call | flops 16000 | bytes 1 | tf_op jit(solution)/shard_map/input_back/pallas_call | solution.py:293
  638.2 15.3 %input_back.5 = (f32[272,128]{1,0:T(8,128)}, f32[256,128]{1,0:T(8,128)}, f32[256,128]{1,0:T(8,128)}) custom-call(bf16[129,64,256]{2,1,0:T(8,128)(2,1)} %get-tuple-element.143.acts_ref.code_ref.second, bf16[129,64,256]{2,1,0:T(8,128)(2,1)} %get-tuple-element.143.acts_ref.code_ref.second, bf16[256,128]{1,0:T(8,128)(2,1)} %get-tuple-element.262.w_ref, ...), custom_call_target="tpu_custom_call" | custom-call | flops 16000 | bytes 1 | tf_op jit(solution)/shard_map/input_back/pallas_call | solution.py:293
  654.8 19.6 %right_back.1 = (bf16[128,64,256]{2,1,0:T(8,128)(2,1)}, bf16[128,64,256]{2,1,0:T(8,128)(2,1)}) custom-call(s32[1]{0:T(128)} %bitcast.10.flag, bf16[128,64,128]{2,1,0:T(8,128)(2,1)} %get-tuple-element.155.refs_0_, bf16[128,64,128]{2,1,0:T(8,128)(2,1)} %collective-permute-done.7.refs_1_, bf16[128,64,128]{2,1,0:T(8,128)(2,1)} %collective-permute-done.8.refs_2_, ...), custom_call_target="tpu_custom_call" | custom-call | flops 25000 | bytes 1 | tf_op jit(solution)/shard_map/right_back/pallas_call | solution.py:293
  674.4 14.8 %input_back.6 = (f32[272,128]{1,0:T(8,128)}, f32[256,128]{1,0:T(8,128)}, f32[256,128]{1,0:T(8,128)}) custom-call(bf16[129,64,256]{2,1,0:T(8,128)(2,1)} %get-tuple-element.148.acts_ref.code_ref.first, bf16[129,64,256]{2,1,0:T(8,128)(2,1)} %get-tuple-element.148.acts_ref.code_ref.first, bf16[256,128]{1,0:T(8,128)(2,1)} %get-tuple-element.261.w_ref, ...), custom_call_target="tpu_custom_call" | custom-call | flops 16000 | bytes 1 | tf_op jit(solution)/shard_map/input_back/pallas_call | solution.py:293
  689.2 15.1 %input_back.7 = (f32[272,128]{1,0:T(8,128)}, f32[256,128]{1,0:T(8,128)}, f32[256,128]{1,0:T(8,128)}) custom-call(bf16[129,64,256]{2,1,0:T(8,128)(2,1)} %get-tuple-element.143.acts_ref.code_ref.second, bf16[129,64,256]{2,1,0:T(8,128)(2,1)} %get-tuple-element.143.acts_ref.code_ref.second, bf16[256,128]{1,0:T(8,128)(2,1)} %get-tuple-element.261.w_ref, ...), custom_call_target="tpu_custom_call" | custom-call | flops 16000 | bytes 1 | tf_op jit(solution)/shard_map/input_back/pallas_call | solution.py:293
  704.3 30.2 %reduce_all.1.early_ref = f32[2048,128]{1,0:T(8,128)} custom-call(f32[1352,128]{1,0:T(8,128)} %scatter.4.pair_ref, f32[272,128]{1,0:T(8,128)} %get-tuple-element.198.left_ref, f32[272,128]{1,0:T(8,128)} %get-tuple-element.212.right_ref), custom_call_target="tpu_custom_call" | custom-call | tf_op jit(solution)/shard_map/reduce_all/pallas_call | solution.py:796
  (109 shorter events, 95.7 us)
Async XLA Ops:
  22.2 216.4 %copy-start.8 = (f32[128,640]{1,0:T(8,128)S(1)}, f32[128,640]{1,0:T(8,128)}, u32[]{:S(2)}) copy-start(f32[128,640]{1,0:T(8,128)} %refs_0_.1) | copy-start | bytes 983044
  22.2 217.3 %copy-start.15 = (f32[6,128]{1,0:T(8,128)S(1)}, f32[6,128]{1,0:T(8,128)}, u32[]{:S(2)}) copy-start(f32[6,128]{1,0:T(8,128)} %refs_5_.1) | copy-start | bytes 9220
  236.5 119.6 %collective-permute-start.4 = (bf16[129,64,256]{2,1,0:T(8,128)(2,1)}, bf16[129,64,256]{2,1,0:T(8,128)(2,1)}, u32[]{:S(2)}, u32[]{:S(2)}) collective-permute-start(bf16[129,64,256]{2,1,0:T(8,128)(2,1)} %get-tuple-element.143.acts_ref.code_ref.second), channel_id=1, source_target_pairs={{0,8},{8,0},{16,24},{24,16},{1,9},{9,1},{17,25},{25,17},{2,10},{10... | collective-permute-start | bytes 12681224 | tf_op jit(solution)/shard_map/ppermute | solution.py:1041
  236.6 146.1 %collective-permute-start = (bf16[129,64,256]{2,1,0:T(8,128)(2,1)}, bf16[129,64,256]{2,1,0:T(8,128)(2,1)}, u32[]{:S(2)}, u32[]{:S(2)}) collective-permute-start(bf16[129,64,256]{2,1,0:T(8,128)(2,1)} %get-tuple-element.143.acts_ref.code_ref.second), channel_id=1, source_target_pairs={{0,16},{8,24},{16,0},{24,8},{1,17},{9,25},{17,1},{25,9},{2,18},{10... | collective-permute-start | bytes 12681224 | tf_op jit(solution)/shard_map/ppermute | solution.py:1044
  279.9 42.9 %collective-permute-start.1 = (bf16[128,64,128]{2,1,0:T(8,128)(2,1)}, bf16[128,64,128]{2,1,0:T(8,128)(2,1)S(1)}, u32[]{:S(2)}, u32[]{:S(2)}) collective-permute-start(bf16[128,64,128]{2,1,0:T(8,128)(2,1)} %get-tuple-element.147), channel_id=1, source_target_pairs={{0,1},{1,0},{2,3},{3,2},{4,5},{5,4},{6,7},{7,6},{8,9},{9,8},{10,11... | collective-permute-start | bytes 6291464 | tf_op jit(solution)/shard_map/ppermute | solution.py:1050
  321.4 34.7 %copy-start.9 = (f32[128,64]{1,0:T(8,128)}, f32[128,64]{1,0:T(8,128)S(1)}, u32[]{:S(2)}) copy-start(f32[128,64]{1,0:T(8,128)S(1)} %copy.50.refs_4_) | copy-start | bytes 98308
  382.2 29.1 %collective-permute-start.5 = (bf16[128,64,128]{2,1,0:T(8,128)(2,1)}, bf16[128,64,128]{2,1,0:T(8,128)(2,1)S(1)}, u32[]{:S(2)}, u32[]{:S(2)}) collective-permute-start(bf16[128,64,128]{2,1,0:T(8,128)(2,1)} %get-tuple-element.163), channel_id=1, source_target_pairs={{0,1},{1,0},{2,3},{3,2},{4,5},{5,4},{6,7},{7,6},{8,9},{9,8},{10,11... | collective-permute-start | bytes 6291464 | tf_op jit(solution)/shard_map/ppermute | solution.py:1050
  382.7 97.6 %collective-permute-start.3 = (bf16[129,64,256]{2,1,0:T(8,128)(2,1)}, bf16[129,64,256]{2,1,0:T(8,128)(2,1)}, u32[]{:S(2)}, u32[]{:S(2)}) collective-permute-start(bf16[129,64,256]{2,1,0:T(8,128)(2,1)} %get-tuple-element.157.acts_ref.code_ref), channel_id=1, source_target_pairs={{0,16},{8,24},{16,0},{24,8},{1,17},{9,25},{17,1},{25,9},{2,18},{10... | collective-permute-start | bytes 12681224 | tf_op jit(solution)/shard_map/ppermute | solution.py:1044
  382.7 138.5 %collective-permute-start.2 = (bf16[129,64,256]{2,1,0:T(8,128)(2,1)}, bf16[129,64,256]{2,1,0:T(8,128)(2,1)}, u32[]{:S(2)}, u32[]{:S(2)}) collective-permute-start(bf16[129,64,256]{2,1,0:T(8,128)(2,1)} %collective-permute-done.acts_ref.code_ref), channel_id=1, source_target_pairs={{0,8},{8,0},{16,24},{24,16},{1,9},{9,1},{17,25},{25,17},{2,10},{10... | collective-permute-start | bytes 12681224 | tf_op jit(solution)/shard_map/ppermute | solution.py:1041
  410.7 35.2 %collective-permute-start.6 = (bf16[128,64,128]{2,1,0:T(8,128)(2,1)}, bf16[128,64,128]{2,1,0:T(8,128)(2,1)}, u32[]{:S(2)}, u32[]{:S(2)}) collective-permute-start(bf16[128,64,128]{2,1,0:T(8,128)(2,1)} %get-tuple-element.168), channel_id=1, source_target_pairs={{0,1},{1,0},{2,3},{3,2},{4,5},{5,4},{6,7},{7,6},{8,9},{9,8},{10,11... | collective-permute-start | bytes 6291464 | tf_op jit(solution)/shard_map/ppermute | solution.py:1050
  445.2 76.0 %collective-permute-start.7 = (bf16[128,64,128]{2,1,0:T(8,128)(2,1)}, bf16[128,64,128]{2,1,0:T(8,128)(2,1)}, u32[]{:S(2)}, u32[]{:S(2)}) collective-permute-start(bf16[128,64,128]{2,1,0:T(8,128)(2,1)} %get-tuple-element.173.refs_1_), channel_id=1, source_target_pairs={{0,8},{8,0},{16,24},{24,16},{1,9},{9,1},{17,25},{25,17},{2,10},{10... | collective-permute-start | bytes 6291464 | tf_op jit(solution)/shard_map/ppermute | solution.py:1041
  478.3 69.7 %collective-permute-start.8 = (bf16[128,64,128]{2,1,0:T(8,128)(2,1)}, bf16[128,64,128]{2,1,0:T(8,128)(2,1)}, u32[]{:S(2)}, u32[]{:S(2)}) collective-permute-start(bf16[128,64,128]{2,1,0:T(8,128)(2,1)} %get-tuple-element.178.refs_2_), channel_id=1, source_target_pairs={{0,16},{8,24},{16,0},{24,8},{1,17},{9,25},{17,1},{25,9},{2,18},{10... | collective-permute-start | bytes 6291464 | tf_op jit(solution)/shard_map/ppermute | solution.py:1044
  521.3 27.9 %collective-permute-start.9 = (bf16[128,64,128]{2,1,0:T(8,128)(2,1)}, bf16[128,64,128]{2,1,0:T(8,128)(2,1)}, u32[]{:S(2)}, u32[]{:S(2)}) collective-permute-start(bf16[128,64,128]{2,1,0:T(8,128)(2,1)} %collective-permute-done.7.refs_1_), channel_id=1, source_target_pairs={{0,1},{1,0},{2,3},{3,2},{4,5},{5,4},{6,7},{7,6},{8,9},{9,8},{10,11... | collective-permute-start | bytes 6291464 | tf_op jit(solution)/shard_map/ppermute | solution.py:1050
  547.5 4.6 collective-permute-start.10
  548.0 37.2 %collective-permute-start.11 = (bf16[128,64,128]{2,1,0:T(8,128)(2,1)}, bf16[128,64,128]{2,1,0:T(8,128)(2,1)}, u32[]{:S(2)}, u32[]{:S(2)}) collective-permute-start(bf16[128,64,128]{2,1,0:T(8,128)(2,1)} %collective-permute-done.8.refs_2_), channel_id=1, source_target_pairs={{0,1},{1,0},{2,3},{3,2},{4,5},{5,4},{6,7},{7,6},{8,9},{9,8},{10,11... | collective-permute-start | bytes 6291464 | tf_op jit(solution)/shard_map/ppermute | solution.py:1050
  548.7 38.6 %collective-permute-start.12 = (bf16[128,64,128]{2,1,0:T(8,128)(2,1)S(1)}, bf16[128,64,128]{2,1,0:T(8,128)(2,1)S(1)}, u32[]{:S(2)}, u32[]{:S(2)}) collective-permute-start(bf16[128,64,128]{2,1,0:T(8,128)(2,1)S(1)} %copy-done), channel_id=1, source_target_pairs={{0,1},{1,0},{2,3},{3,2},{4,5},{5,4},{6,7},{7,6},{8,9},{9,8},{10,11... | collective-permute-start | bytes 6291464 | tf_op jit(solution)/shard_map/ppermute | solution.py:1050
  549.1 38.2 %collective-permute-start.13 = (bf16[128,64,128]{2,1,0:T(8,128)(2,1)}, bf16[128,64,128]{2,1,0:T(8,128)(2,1)S(1)}, u32[]{:S(2)}, u32[]{:S(2)}) collective-permute-start(bf16[128,64,128]{2,1,0:T(8,128)(2,1)} %get-tuple-element.173.refs_1_), channel_id=1, source_target_pairs={{0,1},{1,0},{2,3},{3,2},{4,5},{5,4},{6,7},{7,6},{8,9},{9,8},{10,11... | collective-permute-start | bytes 6291464 | tf_op jit(solution)/shard_map/ppermute | solution.py:1050
  549.2 38.1 %collective-permute-start.14 = (bf16[128,64,128]{2,1,0:T(8,128)(2,1)}, bf16[128,64,128]{2,1,0:T(8,128)(2,1)}, u32[]{:S(2)}, u32[]{:S(2)}) collective-permute-start(bf16[128,64,128]{2,1,0:T(8,128)(2,1)} %get-tuple-element.178.refs_2_), channel_id=1, source_target_pairs={{0,1},{1,0},{2,3},{3,2},{4,5},{5,4},{6,7},{7,6},{8,9},{9,8},{10,11... | collective-permute-start | bytes 6291464 | tf_op jit(solution)/shard_map/ppermute | solution.py:1050
  584.7 4.6 collective-permute-start.15
  585.2 48.9 %collective-permute-start.16 = (bf16[128,64,128]{2,1,0:T(8,128)(2,1)}, bf16[128,64,128]{2,1,0:T(8,128)(2,1)}, u32[]{:S(2)}, u32[]{:S(2)}) collective-permute-start(bf16[128,64,128]{2,1,0:T(8,128)(2,1)} %get-tuple-element.191.refs_3_), channel_id=1, source_target_pairs={{0,24},{8,16},{16,8},{24,0},{1,25},{9,17},{17,9},{25,1},{2,26},{10... | collective-permute-start | bytes 6291464 | tf_op jit(solution)/shard_map/ppermute | solution.py:1047
  609.1 25.0 %copy-start.16 = (s32[1,512]{1,0:T(1,128)S(1)}, s32[1,512]{1,0:T(1,128)}, u32[]{:S(2)}) copy-start(s32[1,512]{1,0:T(1,128)} %param.27) | copy-start | bytes 6148
  609.1 26.3 %copy-start.13 = (f32[128,64]{0,1:T(8,128)S(1)}, f32[128,64]{0,1:T(8,128)}, u32[]{:S(2)}) copy-start(f32[128,64]{0,1:T(8,128)} %param.40) | copy-start | bytes 98308
  609.1 27.0 %copy-start.14 = (f32[128,64]{0,1:T(8,128)S(1)}, f32[128,64]{0,1:T(8,128)}, u32[]{:S(2)}) copy-start(f32[128,64]{0,1:T(8,128)} %param.47) | copy-start | bytes 98308
  634.1 19.4 %collective-permute-start.17 = (bf16[128,64,128]{2,1,0:T(8,128)(2,1)}, bf16[128,64,128]{2,1,0:T(8,128)(2,1)S(1)}, u32[]{:S(2)}, u32[]{:S(2)}) collective-permute-start(bf16[128,64,128]{2,1,0:T(8,128)(2,1)} %collective-permute-done.16.refs_3_), channel_id=1, source_target_pairs={{0,1},{1,0},{2,3},{3,2},{4,5},{5,4},{6,7},{7,6},{8,9},{9,8},{10,11... | collective-permute-start | bytes 6291464 | tf_op jit(solution)/shard_map/ppermute | solution.py:1050
  (12 other events, 123.1 us)

commit v4 on v3

--- a/solution.py
+++ b/solution.py
@@ -320,6 +320,58 @@
 INPUT_GROUP = 8
 
 
+def prepare_kernel(
+    acts_ref, code_ref, w_in, w_out, w_t1, w_t2, w_dist, norms, bias,
+    out_ref, projT, ogT, outT, out_w, t1T, t1, t2T, t2, distT, dist, ln_ref, bias_ref, rows_s,
+):
+    chans = acts_ref.shape[2]
+    for row in range(ROWS):
+        rows_s[row] = jnp.transpose(acts_ref[row])
+    out_ref[:chans] = jnp.swapaxes(rows_s[...], 0, 1)
+    out_ref[chans] = code_ref[...]
+
+    @pl.when(pl.program_id(0) == 0)
+    def _():
+        count = projT.shape[0]
+        projT[...] = jnp.transpose(w_in[:, :count]).astype(BF16)
+        ogT[...] = jnp.transpose(w_in[:, count:]).astype(BF16)
+        for weight, plain, turned in (
+            (w_out, out_w, outT), (w_t1, t1, t1T), (w_t2, t2, t2T), (w_dist, distT, dist)
+        ):
+            plain[...] = weight[...].astype(BF16)
+            turned[...] = jnp.transpose(weight[...]).astype(BF16)
+        for index in range(6):
+            ln_ref[index] = jnp.transpose(jnp.broadcast_to(norms[index : index + 1, :], (128, chans)))
+        bias_ref[...] = jnp.transpose(jnp.broadcast_to(bias[...], (128, bias.shape[1])))
+
+
+def prepare(acts, code, w_in, w_out, w_t1, w_t2, w_dist, norms, bias):
+    rows, lanes, chans = acts.shape
+    width = w_out.shape[0]
+    params = (w_in, w_out, w_t1, w_t2, w_dist.T, norms, bias.reshape(1, -1))
+    shapes = [(4 * width, chans), (chans, chans)]
+    for weight in (w_out, w_t1, w_t2, w_dist):
+        turned = (weight.shape[1], weight.shape[0])
+        shapes += [turned, weight.shape]
+    shapes = [(shape, BF16) for shape in shapes]
+    shapes += [((6, chans, 128), F32), ((bias.shape[0], 128), F32)]
+    return call(
+        prepare_kernel,
+        (rows // ROWS,),
+        [],
+        [
+            (acts, (ROWS, lanes, chans), lambda i, *_: (i, 0, 0)),
+            (code, (ROWS, lanes), lambda i, *_: (i, 0)),
+        ]
+        + [(v, v.shape, fixed(*([0] * v.ndim))) for v in params],
+        [((chans + 1, rows, lanes), BF16, (chans + 1, ROWS, lanes), lambda i, *_: (0, i, 0))]
+        + [(shape, dtype, shape, fixed(*([0] * len(shape)))) for shape, dtype in shapes],
+        [pltpu.VMEM((ROWS, chans, lanes), BF16)],
+        1,
+        "prepare",
+    )
+
+
 def project_kernel(acts_ref, code_ref, w_ref, ln_ref, a_ref, b_ref, acts_s, a_s, b_s, code_s):
     width = a_ref.shape[0]
     code_s[...] = code_ref[0].astype(F32)
@@ -372,6 +424,7 @@
 
 
 CHANS = 16
+TRIANGLE_CHANS = 32
 
 
 def ordered(flag, own, other):
@@ -383,30 +436,33 @@
     return jnp.concatenate(waves, 0)
 
 
-def triangle_kernel(flag, a0, a1, b0, b1, keep_ref, send_ref):
-    kept_first = flag[0] == 0
+def kept_first(ids, q):
+    return ids[2] ^ ((ids[0] ^ q) // 2) ^ (ids[1] // 2) == 0
+
+
+def triangle_kernel(q, ids, a0, a1, b0, b1, keep_ref, send_ref):
+    first = kept_first(ids, q)
     part = b0.shape[1] // 2
-    for chan in range(CHANS):
+    for chan in range(TRIANGLE_CHANS):
         rows = jnp.concatenate([a0[chan], a1[chan]], 0)
-        one, two = [
-            dot(jnp.concatenate([b[chan, part * u : part * u + part] for b in (b0, b1)], 0), rows, NT)
-            for u in range(2)
-        ]
-        keep_ref[chan] = jnp.where(kept_first, one, two)
-        send_ref[chan] = jnp.where(kept_first, two, one).astype(BF16)
-
-
-def triangle(which, a, b):
+        x = dot(jnp.concatenate([b0[chan], b1[chan]], 0), rows, NT)
+        one = jnp.concatenate([x[:part], x[2 * part : 3 * part]], 0)
+        two = jnp.concatenate([x[part : 2 * part], x[3 * part :]], 0)
+        keep_ref[chan] = jnp.where(first, one, two)
+        send_ref[chan] = jnp.where(first, two, one).astype(BF16)
+
+
+def triangle(q, ids, a, b):
     chans, half, lanes = a[0].shape
     lead = lambda i, *_: (i, 0, 0)
-    block = (CHANS, half, lanes)
+    block = (TRIANGLE_CHANS, half, lanes)
     out = (chans, half, 2 * half)
     return call(
-        triangle_kernel,
-        (chans // CHANS,),
-        [which],
+        functools.partial(triangle_kernel, q),
+        (chans // TRIANGLE_CHANS,),
+        [ids],
         [(v, block, lead) for v in (*a, *b)],
-        [(out, F32, (CHANS, half, 2 * half), lead), (out, BF16, (CHANS, half, 2 * half), lead)],
+        [(out, F32, (TRIANGLE_CHANS, half, 2 * half), lead), (out, BF16, (TRIANGLE_CHANS, half, 2 * half), lead)],
         [],
         14 * MICRO,
         "triangle",
@@ -427,7 +483,7 @@
 
 def pair_kernel(
     first_call, last_call,
-    place, x_keep, x_recv, acts_ref, code_ref, ln_ref, w_outT, w_out, w_ogT, w_t1T, w_t1,
+    ids, x_keep, x_recv, acts_ref, code_ref, ln_ref, w_outT, w_out, w_ogT, w_t1T, w_t1,
     w_t2T, w_t2, w_distT, w_dist, bias_ref, *rest,
 ):
     prior = () if first_call else rest[:2]
@@ -502,9 +558,7 @@
         d_out = d_gated.astype(BF16)
         d_og = (d_gated * out * (1.0 - gate)).astype(BF16)
         add(OUT_ROW, dot(d_out, tri, NT))
-        g_og = dot(d_og, jnp.concatenate([low, normed_one.astype(BF16)], 0), NT)
-        add(OG_ROW, g_og[:, :chans])
-        wide[6] += g_og[:, chans:]
+        wide[6] += dot(d_og, normed_one.astype(BF16), NT)
         wide[4] += fold(d_og.astype(F32))
         d_xn = dot(w_out[...], d_out)
         wide[0] += fold(d_xn * normed_two)
@@ -523,30 +577,33 @@
             gate_w = w_ogT[...].astype(F32)
             for index in range(4):
                 add(NORM_ROW + index, row_sums(wide[index]))
+            total = jnp.sum(wide[4], 1, keepdims=True)
+            add(OG_ROW, affine_grad(wide[6], total, ln_ref))
             add(NORM_ROW + 4, jnp.sum(gate_w * wide[6], 0, keepdims=True))
-            add(NORM_ROW + 5, jnp.sum(gate_w * jnp.sum(wide[4], 1, keepdims=True), 0, keepdims=True))
+            add(NORM_ROW + 5, jnp.sum(gate_w * total, 0, keepdims=True))
             add(BIAS_ROW, row_sums(wide[5]))
 
 
-def pair_block(place, x_keep, x_recv, acts_kj, ln_wide, weights, bias, prior, last_call):
+def pair_block(q, ids, x_keep, x_recv, acts_kj, ln_wide, weights, bias, prior, last_call):
     chans, rows, lanes = x_keep.shape
     block = (chans, ROWS, lanes)
     mid = lambda i, *_: (0, i, 0)
 
-    def where(i, spot):
-        return 8 * ((i % 2) ^ spot[0]) + 2 * spot[1] + i // 2
+    def where(i, ids):
+        owner = ids[0] ^ q
+        return 8 * ((i % 2) ^ (owner % 2) ^ (ids[1] % 2)) + 2 * owner + i // 2
 
     full = [(w, w.shape, fixed(*([0] * w.ndim))) for w in (ln_wide, *weights, bias, *prior)]
     shapes = [(SUM_ROWS, 128), (7, 128, 128)]
     return call(
         functools.partial(pair_kernel, not prior, last_call),
         (rows // ROWS,),
-        [place],
+        [ids],
         [
             (x_keep, block, mid),
             (x_recv, block, mid),
-            (acts_kj, block, lambda i, spot: (0, where(i, spot), 0)),
-            (acts_kj, (1, ROWS, lanes), lambda i, spot: (chans, where(i, spot), 0)),
+            (acts_kj, block, lambda i, ids: (0, where(i, ids), 0)),
+            (acts_kj, (1, ROWS, lanes), lambda i, ids: (chans, where(i, ids), 0)),
         ]
         + full,
         [((chans, rows, lanes), BF16, block, mid)]
@@ -557,11 +614,11 @@
     )
 
 
-def right_back_kernel(flag, *refs):
+def right_back_kernel(ids, *refs):
     owns, others, firsts, seconds = refs[:4], refs[4:8], refs[8:12], refs[12:16]
     out0, out1 = refs[16:]
     half = out0.shape[1]
-    own_first = flag[0] == 0
+    own_first = kept_first(ids, 0)
     for chan in range(CHANS):
         grads = jnp.concatenate(
             [ordered(own_first, owns[q][chan], others[q][chan]) for q in range(4)], 1
@@ -572,14 +629,14 @@
         out1[chan] = total[half:]
 
 
-def right_back(which, owns, others, firsts, seconds):
+def right_back(ids, owns, others, firsts, seconds):
     chans, half, lanes = firsts[0].shape
     lead = lambda i, *_: (i, 0, 0)
     out = ((chans, half, lanes), BF16, (CHANS, half, lanes), lead)
     return call(
         right_back_kernel,
         (chans // CHANS,),
-        [which],
+        [ids],
         [(v, (CHANS, half, 2 * half), lead) for v in (*owns, *others)]
         + [(v, (CHANS, half, lanes), lead) for v in (*firsts, *seconds)],
         [out, out],
@@ -611,14 +668,14 @@
     )[0]
 
 
-def left_back_kernel(flag, *refs):
+def left_back_kernel(ids, *refs):
     owns, others, firsts, seconds = refs[:4], refs[4:8], refs[8:12], refs[12:16]
     out0, out1 = refs[16:]
     half = out0.shape[1]
     for chan in range(CHANS):
         total = None
         for pair in range(2):
-            own_first = flag[0] == pair
+            own_first = kept_first(ids, 2 * pair)
             grads, values = [], []
             for q in (2 * pair, 2 * pair + 1):
                 grads.append(ordered(own_first, owns[q][chan], others[q][chan]))
@@ -630,14 +687,14 @@
         out1[chan] = total[half:]
 
 
-def left_back(which, owns, others, firsts, seconds):
+def left_back(ids, owns, others, firsts, seconds):
     chans, half, lanes = firsts[0].shape
     lead = lambda i, *_: (i, 0, 0)
     out = ((chans, half, lanes), BF16, (CHANS, half, lanes), lead)
     return call(
         left_back_kernel,
         (chans // CHANS,),
-        [which],
+        [ids],
         [(v, (CHANS, half, 2 * half), lead) for v in (*owns, *others)]
         + [(v, (CHANS, half, lanes), lead) for v in (*firsts, *seconds)],
         [out, out],
@@ -648,6 +705,11 @@
 
 
 SIDE_ROWS = 272
+
+
+def affine_grad(normed_grad, total, ln_ref):
+    gain, shift = jnp.transpose(ln_ref[0])[:1], jnp.transpose(ln_ref[1])[:1]
+    return normed_grad * gain + total * shift
 
 
 def input_back_kernel(count, first_call, last_call, acts_ref, code_ref, w_ref, ln_ref, *rest):
@@ -687,9 +749,7 @@
         d_value = take_rows(grad_s, start, INPUT_GROUP) * mask * gate
         d_gate = d_value * proj[:width] * (1.0 - gate)
         d_proj = jnp.concatenate([d_value.astype(BF16), d_gate.astype(BF16)], 0)
-        g_all = dot(d_proj, jnp.concatenate([low, normed.astype(BF16)], 0), NT)
-        out_ref[: 2 * width] += g_all[:, :chans]
-        g_ref[...] += g_all[:, chans:]
+        g_ref[...] += dot(d_proj, normed.astype(BF16), NT)
         wide = d_proj.astype(F32)
         sum_ref[...] += sum(wide[:, 128 * u : 128 * u + 128] for u in range(lanes // 128))
         return carry
@@ -701,17 +761,19 @@
         @pl.when(pl.program_id(0) == pl.num_programs(0) - 1)
         def _():
             part = w_ref[...].astype(F32)
+            total = jnp.sum(sum_ref[...], 1, keepdims=True)
             gain = jnp.sum(part * g_ref[...], 0, keepdims=True)
-            shift = jnp.sum(part * jnp.sum(sum_ref[...], 1, keepdims=True), 0, keepdims=True)
+            shift = jnp.sum(part * total, 0, keepdims=True)
+            out_ref[: 2 * width] = affine_grad(g_ref[...], total, ln_ref)
             out_ref[2 * width : 2 * width + 1] = gain
             out_ref[2 * width + 1 : 2 * width + 2] = shift
 
 
-def input_back(acts, w_part, ln_wide, grads, prior, last_call):
+def input_back(acts, part, w_proj, ln_wide, grads, prior, last_call):
     chans, rows, lanes = acts.shape[0] - 1, acts.shape[1], acts.shape[2]
     block = (chans, ROWS, lanes)
     mid = lambda i, *_: (0, i, 0)
-    depth = w_part.shape[0]
+    depth = w_proj.shape[0] // 2
     shapes = [(SIDE_ROWS, chans), (depth, chans), (depth, 128)]
     return call(
         functools.partial(input_back_kernel, len(grads), not prior, last_call),
@@ -720,7 +782,7 @@
         [
             (acts, block, mid),
             (acts, (1, ROWS, lanes), lambda i, *_: (chans, i, 0)),
-            (w_part, w_part.shape, fixed(0, 0)),
+            (w_proj, (depth, chans), fixed(part, 0)),
             (ln_wide, ln_wide.shape, fixed(0, 0, 0)),
         ]
         + [(v, block, mid) for v in grads]
@@ -820,12 +882,14 @@
 
 
 def spread_kernel(
-    acts_ref, wave0_ref, wave1_ref, x_ref, y_ref, mid,
-    plane_send, plane_recv, level_send, level_recv, share_send, share_recv, local,
+    acts_ref, w_ref, ln_ref, wave0_ref, wave1_ref, x_ref, y_ref, a_ref, b_ref, mid,
+    plane_send, plane_recv, share_send, share_recv, level_send, level_recv, local,
+    wave_v, a_v, b_v, acts_s, a_s, b_s, code_s,
 ):
     spot, level = lax.axis_index("crop"), lax.axis_index("row")
     chans = acts_ref.shape[0]
-    cuts = [(0, chans // 2), (chans // 2, chans - chans // 2)]
+    early, middle = chans // 4, 5 * chans // 8
+    cuts = [[(0, early), (early, middle - early), (middle, chans - middle)], [(0, chans)]]
     waves = (wave0_ref, wave1_ref)
     mesh_id = pl.DeviceIdType.MESH
     barrier = pltpu.get_barrier_semaphore()
@@ -835,13 +899,13 @@
     pl.semaphore_wait(barrier, 6)
 
     def plane_copy(wave, cut, distance):
-        first, count = cuts[cut]
+        first, count = cuts[wave][cut]
         target = flip(spot, distance)
         source = acts_ref.at[
             pl.ds(first, count), pl.ds(pl.multiple_of(32 * target + 16 * wave, 16), 16)
         ]
         landing = mid.at[wave, distance, pl.ds(first, count)]
-        index = 8 * wave + 4 * cut + distance
+        index = 12 * wave + 4 * cut + distance
         if distance == 0:
             return pltpu.make_async_copy(source, landing, plane_recv.at[index])
         return pltpu.make_async_remote_copy(
@@ -850,20 +914,20 @@
         )
 
     def landed(wave, cut, label):
-        first, count = cuts[cut]
+        first, count = cuts[wave][cut]
         return waves[wave].at[pl.ds(first, count), pl.ds(16 * label, 16)]
 
     def level_copy(wave, cut, label, distance):
-        first, count = cuts[cut]
+        first, count = cuts[wave][cut]
         source = mid.at[wave, distance, pl.ds(first, count)]
         target = swap_bits(flip(spot, distance))
-        index = 8 * wave + 4 * cut + label
+        index = 12 * wave + 4 * cut + label
         remote = pltpu.make_async_remote_copy(
             src_ref=source, dst_ref=landed(wave, cut, label),
             send_sem=level_send.at[index], recv_sem=level_recv.at[index],
             device_id={"row": target}, device_id_type=mesh_id,
         )
-        return target, remote, pltpu.make_async_copy(source, landed(wave, cut, label), local.at[2 * wave + cut])
+        return target, remote, pltpu.make_async_copy(source, landed(wave, cut, label), local.at[3 * wave + cut])
 
     def each_level(action, wave, cut):
         for label in range(4):
@@ -874,7 +938,7 @@
                     action(wave, cut, label, distance)
 
     def shares(cut, label):
-        first, count = cuts[cut]
+        first, count = cuts[0][cut]
         index = 8 * cut + 2 * label
         return [
             pltpu.make_async_remote_copy(
@@ -887,12 +951,12 @@
         ]
 
     plane = [
-        [[plane_copy(wave, cut, distance) for distance in range(4)] for cut in range(2)] for wave in range(2)
+        [[plane_copy(wave, cut, distance) for distance in range(4)] for cut in range(len(cuts[wave]))]
+        for wave in range(2)
     ]
-    for wave in range(2):
-        for cut in range(2):
-            for one in plane[wave][cut]:
-                one.start()
+    for copies in plane[0] + plane[1]:
+        for one in copies:
+            one.start()
 
     def begin(wave, cut, label, distance):
         one = plane[wave][cut][distance]
@@ -925,40 +989,68 @@
             for one in shares(cut, label):
                 one.start()
 
-    each_level(begin, 0, 0)
-    each_level(begin, 0, 1)
+    for cut in range(3):
+        each_level(begin, 0, cut)
     each_level(begin, 1, 0)
-    pass_on(0)
-    each_level(begin, 1, 1)
-    pass_on(1)
-    for wave in range(2):
-        for cut in range(2):
-            for one in plane[wave][cut][1:]:
-                one.wait_send()
-    each_level(arrive, 1, 0)
-    each_level(arrive, 1, 1)
-    for cut in range(2):
+    for cut in range(3):
+        pass_on(cut)
+    fetch = pltpu.make_async_copy(wave0_ref, wave_v, local.at[4])
+    fetch.start()
+    fetch.wait()
+    width = a_v.shape[0]
+
+    def project_rows(step, carry):
+        rows = pl.ds(pl.multiple_of(step * ROWS, ROWS), ROWS)
+        project_kernel(
+            wave_v.at[pl.ds(0, width), rows], wave_v.at[pl.ds(width, 1), rows], w_ref, ln_ref,
+            a_v.at[:, rows], b_v.at[:, rows], acts_s, a_s, b_s, code_s,
+        )
+        return carry
+
+    lax.fori_loop(0, wave_v.shape[1] // ROWS, project_rows, 0)
+    results = [
+        pltpu.make_async_copy(a_v, a_ref, local.at[5]), pltpu.make_async_copy(b_v, b_ref, local.at[6])
+    ]
+    for one in results:
+        one.start()
+    for copies in plane[0] + plane[1]:
+        for one in copies[1:]:
+            one.wait_send()
+    for cut in range(3):
         for label in range(4):
             for one in shares(cut, label):
                 one.wait()
-
-
-def spread(acts_major):
+    for one in results:
+        one.wait()
+    each_level(arrive, 1, 0)
+
+
+def spread(acts_major, w_proj, ln_wide):
     chans, rows, lanes = acts_major.shape
+    half, width = rows // 2, chans - 1
     anywhere = pl.BlockSpec(memory_space=pl.ANY)
+    whole = pl.BlockSpec(memory_space=pltpu.VMEM)
+    staged = pltpu.VMEM((ROWS, width, lanes), BF16)
     return pl.pallas_call(
         spread_kernel,
-        in_specs=[anywhere],
-        out_specs=[anywhere] * 4,
-        out_shape=[jax.ShapeDtypeStruct((chans, rows // 2, lanes), BF16)] * 4,
+        in_specs=[anywhere, whole, whole],
+        out_specs=[anywhere] * 6,
+        out_shape=[jax.ShapeDtypeStruct((chans, half, lanes), BF16)] * 4
+        + [jax.ShapeDtypeStruct((width, half, lanes), BF16)] * 2,
         scratch_shapes=[pltpu.VMEM((2, 4, chans, rows // 8, lanes), BF16)]
-        + [pltpu.SemaphoreType.DMA((16,)) for _ in range(6)]
-        + [pltpu.SemaphoreType.DMA((4,))],
+        + [pltpu.SemaphoreType.DMA((16,)) for _ in range(2)]
+        + [pltpu.SemaphoreType.DMA((24,)) for _ in range(2)]
+        + [pltpu.SemaphoreType.DMA((16,)) for _ in range(2)]
+        + [pltpu.SemaphoreType.DMA((7,))]
+        + [pltpu.VMEM((chans, half, lanes), BF16)]
+        + [pltpu.VMEM((width, half, lanes), BF16)] * 2
+        + [staged] * 3
+        + [pltpu.VMEM((ROWS, lanes), F32)],
         compiler_params=pltpu.CompilerParams(
             collective_id=2, has_side_effects=True, vmem_limit_bytes=VMEM_LIMIT
         ),
         name="spread",
-    )(acts_major)
+    )(acts_major, w_proj, ln_wide)
 
 
 def update_kernel(early_ref, *refs):
@@ -981,7 +1073,7 @@
         jnp.transpose(early_ref[OUT_ROW : OUT_ROW + 128]),
         jnp.transpose(early_ref[T1_ROW : T1_ROW + 512]),
         early_ref[T2_ROW : T2_ROW + 512],
-        jnp.transpose(early_ref[DIST_ROW : DIST_ROW + 64]),
+        early_ref[DIST_ROW : DIST_ROW + 64],
         jnp.concatenate(
             [
                 left_ref[half : half + 2] + right_ref[half : half + 2] + early_ref[NORM_ROW + 4 : NORM_ROW + 6],
@@ -998,17 +1090,18 @@
     rates = (LEARN_RATE,) * 5 + (GAIN_RATE,) * 2
     for index in range(7):
         new = adamw_update(
-            ins[index][...], ins[7 + index][...], ins[14 + index][...], grads[index], scale, rates[index]
+            *[ins[7 * part + index][...].reshape(grads[index].shape) for part in range(3)],
+            grads[index], scale, rates[index],
         )
         for part in range(3):
-            outs[7 * part + index][...] = new[part]
+            outs[7 * part + index][...] = new[part].reshape(outs[7 * part + index].shape)
     norm_ref[...] = grad_norm
     loss_ref[...] = jnp.sum(early_ref[LOSS_ROW : LOSS_ROW + 1], keepdims=True).reshape(1, 1)
     total_ref[...] = jnp.full((1, 1), total, F32)
 
 
 def update(early, params, firsts, seconds):
-    flat = [v.reshape(1, -1) if v.ndim == 1 else v for v in (*params, *firsts, *seconds)]
+    flat = [v.T if index % 7 == 4 else v for index, v in enumerate((*params, *firsts, *seconds))]
     shapes = [v.shape for v in flat] + [(1, 1)] * 3
     outs = pl.pallas_call(
         update_kernel,
@@ -1016,7 +1109,7 @@
         compiler_params=pltpu.CompilerParams(vmem_limit_bytes=VMEM_LIMIT),
         name="update",
     )(early, *flat)
-    outs = [v.reshape(-1) if index in (6, 13, 20) else v for index, v in enumerate(outs)]
+    outs = [v.T if index in (4, 11, 18) else v for index, v in enumerate(outs)]
     return (*outs[:21], *[v[0, 0] for v in outs[21:]])
 
 
@@ -1053,21 +1146,16 @@
     row_own = lax.dynamic_slice_in_dim(own_mask, rows * level, rows)
     col_own = lax.dynamic_slice_in_dim(own_mask, cols * side, cols)
     code_own = jnp.where((row_own[:, None] * col_own[None, :]) > 0, dist_bins[0], -1).astype(BF16)
-    acts_major = jnp.transpose(pair_acts[0], (2, 0, 1))
-
-    acts_major = jnp.concatenate([acts_major, code_own[None]], 0)
-    wave0, wave1, wave0_x, wave0_y = spread(acts_major)
+    acts_major, proj_w, *weights, ln_wide, bias_wide = prepare(
+        pair_acts[0], code_own, w_in, w_out, w_t1, w_t2, w_dist, norm_params, dist_bias
+    )
+    og_T, out_T, out_w, t1_T, t1_w, t2_T, t2_w, dist_T, dist_w = weights
+    weights = (out_T, out_w, og_T, t1_T, t1_w, t2_T, t2_w, dist_T, dist_w)
+
+    wave0, wave1, wave0_x, wave0_y, left_own, right_own = spread(acts_major, proj_w, ln_wide)
 
     count = jnp.sum(own_mask).astype(F32)
     share_count = lax.axis_size("row") * lax.axis_size("col")
-    low_in, low_out, low_t1, low_t2, low_dist = [
-        weight.astype(BF16) for weight in (w_in, w_out, w_t1, w_t2, w_dist)
-    ]
-    ln_wide = jnp.broadcast_to(norm_params[:, :, None], (*norm_params.shape, 128))
-    bias_wide = jnp.broadcast_to(dist_bias[:, None], (dist_bias.shape[0], 128))
-    in_T = low_in.T
-
-    proj_w = in_T[: 4 * width]
     acts, left, right = {}, {}, {}
 
     def share(q, source, shift, half):
@@ -1080,27 +1168,23 @@
     acts[0, 0], acts[0, 1], acts[1, 0], acts[2, 0] = wave0, wave1, wave0_x, wave0_y
     share(1, 0, over_x, 1)
     share(2, 0, over_y, 1)
-    done = values(0, 0)
-    done = values(0, 1, done)
-
-    weights = (
-        low_out.T, low_out, in_T[4 * width :], low_t1.T, low_t1, low_t2.T, low_t2, low_dist.T, low_dist,
-    )
-    flags = [(side ^ ((spot ^ q) // 2) ^ (crop // 2)).astype(jnp.int32)[None] for q in range(4)]
+    left[0, 0], right[0, 0] = left_own, right_own
+    done = values(0, 1)
+
+    ids = jnp.stack([spot, crop, side]).astype(jnp.int32)
     keeps, recvs, dx_own, dx_other, seen, seen_other = {}, {}, {}, {}, {}, {}
     sums = []
 
     def forward(q, *earlier):
-        mine = [after(left[0, h], *earlier) for h in range(2)]
-        keeps[q], send = triangle(flags[q], mine, [right[q, h] for h in range(2)])
+        keeps[q], send = triangle(
+            q, after(ids, *earlier), [left[0, h] for h in range(2)], [right[q, h] for h in range(2)]
+        )
         recvs[q] = over_core(send)
         return send
 
     def middle(q, *earlier):
-        owner = spot ^ q
-        place = jnp.stack([(owner ^ crop) & 1, owner]).astype(jnp.int32)
         dx_own[q], *sums[:] = pair_block(
-            after(place, *earlier), keeps[q], recvs[q], acts_kj, ln_wide, weights, bias_wide, list(sums), q == 3
+            q, after(ids, *earlier), keeps[q], recvs[q], acts_kj, ln_wide, weights, bias_wide, list(sums), q == 3
         )
         dx_other[q] = over_core(dx_own[q])
         seen[q] = (lambda v: v, over_x, over_y, over_both)[q](dx_own[q])
@@ -1122,11 +1206,11 @@
     done = middle(1, done)
     done = middle(2, done)
     done = values(3, 0, done)
-    done = values(3, 1, done, seen[1])
+    done = values(3, 1, done)
     done = forward(3, done)
-    done = middle(3, done, seen[2], seen_other[1])
+    done = middle(3, done, seen[1], seen[2])
     d_left = left_back(
-        after(flags[0], done, seen_other[2]),
+        after(ids, done, seen_other[1]),
         [dx_own[q] for q in range(4)],
         [dx_other[q] for q in range(4)],
         [right[q, 0] for q in range(4)],
@@ -1134,20 +1218,19 @@
     )
     pair_sums = sums[0].at[LOSS_ROW - 1, 127].set(count * count / share_count)
     left_sum, right_sum = [], []
-    left_w, right_w = in_T[: 2 * width], in_T[2 * width : 4 * width]
     for h in range(2):
-        left_sum = input_back(acts[0, h], left_w, ln_wide, [d_left[h]], left_sum, h == 1)
+        left_sum = input_back(acts[0, h], 0, proj_w, ln_wide, [d_left[h]], left_sum, h == 1)
         if h == 0:
             seen_other[3] = over_core(after(seen[3], left_sum[0]))
     d_right = right_back(
-        after(flags[0], left_sum[0]),
+        after(ids, left_sum[0], seen_other[2]),
         [seen[q] for q in range(4)],
         [seen_other[q] for q in range(4)],
         [left[q, 0] for q in range(4)],
         [left[q, 1] for q in range(4)],
     )
     for h in range(2):
-        right_sum = input_back(acts[0, h], right_w, ln_wide, [d_right[h]], right_sum, h == 1)
+        right_sum = input_back(acts[0, h], 1, proj_w, ln_wide, [d_right[h]], right_sum, h == 1)
     params = (w_in, w_out, w_t1, w_t2, w_dist, norm_params, dist_bias)
     return update(reduce_all(pair_sums, left_sum[0], right_sum[0]), params, firsts, seconds)
 

time: 749 us -> 673 us (0.90)
  local copies, waits for them, and re-layouts: 31.5 us -> 6.7 us
  Pallas kernels: 646 us -> 626 us
  waiting for transfers between devices: 42.1 us -> 22.7 us
  other arithmetic: 13.1 us -> 2.85 us
    ppermute x3, waiting for transfers between devices: 27.4 us -> 0.01 us  [over_x(): return lax.ppermute(v, 'crop', [(g, g ^ 1) for g in range(4)])]
    unnamed x44 -> x18, local copies, waits for them, and re-layouts: 22.2 us -> 3.99 us
    pallas_call x1, Pallas kernels: 214 us -> 200 us  [spread(): pl.pallas_call(spread_kernel, in_specs=[anywhere, whole, whole], out_spec...]
    ppermute x3, waiting for transfers between devices: 0.01 us -> 9.04 us  [over_y(): return lax.ppermute(v, 'crop', [(g, g ^ 2) for g in range(4)])]
  transfers between devices with their start and end apart: 18 -> 18, of which waited for: 4 -> 3; matrix products, arithmetic and copies ran while one was open for 2% -> 0% of each run, Pallas kernels for 47% -> 49%
where the time goes in v4:
time: 673 us; the launch traced here: 670 us
  Pallas kernels  626 us (93%)
  waiting for transfers between devices  22.7 us (3%)
  starting transfers between devices  10.2 us (2%)
    pallas_call x23, Pallas kernels, call(): pl.pallas_call(kernel, grid_spec=pltpu.PrefetchScalarGridSpec(num_scalar_...  391 us
    pallas_call x1, Pallas kernels, spread(): pl.pallas_call(spread_kernel, in_specs=[anywhere, whole, whole], out_spec...  200 us
    pallas_call x1, Pallas kernels, reduce_all(): pl.pallas_call(reduce_kernel, out_shape=jax.ShapeDtypeStruct((ALL_ROWS, l...  29.3 us
  transfers between devices with their start and end apart: 18, of which 3 were waited for; matrix products, arithmetic and copies ran while one was open for 0% of the time, Pallas kernels for 49%

profile of v4, /device:TPU:0, one launch (start us, length us, event | category | flops | bytes accessed | tf_op | source)
XLA Modules:
  0.0 669.8 jit_solution(10417493873057650619)
XLA Ops:
  3.6 11.4 %prepare.1 = (bf16[129,128,256]{2,1,0:T(8,128)(2,1)}, bf16[512,128]{1,0:T(8,128)(2,1)}, bf16[128,128]{1,0:T(8,128)(2,1)}, bf16[128,128]{1,0:T(8,128)(2,1)}, bf16...) custom-call(bf16[128,256,128]{2,1,0:T(8,128)(2,1)} %bitcast.24, ...), custom_call_target="tpu_custom_call" | custom-call | flops 1 | bytes 1 | tf_op jit(solution)/shard_map/prepare/pallas_call | solution.py:293
  15.0 200.4 %spread.1 = (bf16[129,64,256]{2,1,0:T(8,128)(2,1)}, bf16[129,64,256]{2,1,0:T(8,128)(2,1)}, bf16[129,64,256]{2,1,0:T(8,128)(2,1)}, bf16[129,64,256]{2,1,0:T(8,128...) custom-call(bf16[129,128,256]{2,1,0:T(8,128)(2,1)} %get-tuple-element.145.acts_ref, ...), custom_call_target="tpu_custom_call" | custom-call | tf_op jit(solution)/shard_map/spread/pallas_call | solution.py:1034
  219.0 13.5 %project.7 = (bf16[128,64,256]{2,1,0:T(8,128)(2,1)}, bf16[128,64,256]{2,1,0:T(8,128)(2,1)}) custom-call(bf16[129,64,256]{2,1,0:T(8,128)(2,1)} %get-tuple-element.148.acts_ref.code_ref.second, bf16[129,64,256]{2,1,0:T(8,128)(2,1)} %get-tuple-element.148.acts_ref.code_ref.second, bf16[512,128]{1,0:T(8,128)(2,1)} %get-tuple-element.146.w_ref, ...), custom_call_target="tpu_custom_call" | custom-call | flops 15000 | bytes 1 | tf_op jit(solution)/shard_map/project/pallas_call | solution.py:293
  233.1 10.1 %triangle.4 = (f32[128,64,128]{2,1,0:T(8,128)}, bf16[128,64,128]{2,1,0:T(8,128)(2,1)}) custom-call(s32[3]{0:T(128)} %pad_add_fusion.ids, bf16[128,64,256]{2,1,0:T(8,128)(2,1)} %get-tuple-element.154.a0.refs_8_, bf16[128,64,256]{2,1,0:T(8,128)(2,1)} %get-tuple-element.155.a1.refs_12_, bf16[128,64,256]{2,1,0:T(8,128)(2,1)} %get-tuple-element.156.b0.refs_8_, ...), custom_call_target="tpu_custom_call" | custom-call | flops 14000 | bytes 1 | tf_op jit(solution)/shard_map/triangle/pallas_call | solution.py:293
  251.9 13.5 %project.8 = (bf16[128,64,256]{2,1,0:T(8,128)(2,1)}, bf16[128,64,256]{2,1,0:T(8,128)(2,1)}) custom-call(bf16[129,64,256]{2,1,0:T(8,128)(2,1)} %get-tuple-element.177.acts_ref.code_ref, bf16[129,64,256]{2,1,0:T(8,128)(2,1)} %get-tuple-element.177.acts_ref.code_ref, bf16[512,128]{1,0:T(8,128)(2,1)} %get-tuple-element.146.w_ref, ...), custom_call_target="tpu_custom_call" | custom-call | flops 15000 | bytes 1 | tf_op jit(solution)/shard_map/project/pallas_call | solution.py:293
  265.4 13.7 %project.9 = (bf16[128,64,256]{2,1,0:T(8,128)(2,1)}, bf16[128,64,256]{2,1,0:T(8,128)(2,1)}) custom-call(bf16[129,64,256]{2,1,0:T(8,128)(2,1)} %get-tuple-element.161.acts_ref.code_ref, bf16[129,64,256]{2,1,0:T(8,128)(2,1)} %get-tuple-element.161.acts_ref.code_ref, bf16[512,128]{1,0:T(8,128)(2,1)} %get-tuple-element.146.w_ref, ...), custom_call_target="tpu_custom_call" | custom-call | flops 15000 | bytes 1 | tf_op jit(solution)/shard_map/project/pallas_call | solution.py:293
  280.5 33.8 %pair.4 = (bf16[128,64,128]{2,1,0:T(8,128)(2,1)}, f32[1352,128]{1,0:T(8,128)}, f32[7,128,128]{2,1,0:T(8,128)}) custom-call(s32[3]{0:T(128)} %pad_add_fusion.ids, f32[128,64,128]{2,1,0:T(8,128)} %get-tuple-element.164.x_keep, bf16[128,64,128]{2,1,0:T(8,128)(2,1)} %copy-done.4, bf16[129,256,128]{2,1,0:T(8,128)(2,1)} %turn.1.acts_ref.code_ref, ...), custom_call_target="tpu_custom_call" | custom-call | flops 35000 | bytes 1 | tf_op jit(solution)/shard_map/pair/pallas_call | solution.py:293
  316.3 13.5 %project.10 = (bf16[128,64,256]{2,1,0:T(8,128)(2,1)}, bf16[128,64,256]{2,1,0:T(8,128)(2,1)}) custom-call(bf16[129,64,256]{2,1,0:T(8,128)(2,1)} %collective-permute-done.4.acts_ref.code_ref, bf16[129,64,256]{2,1,0:T(8,128)(2,1)} %collective-permute-done.4.acts_ref.code_ref, bf16[512,128]{1,0:T(8,128)(2,1)} %get-tuple-element.146.w_ref, ...), custom_call_target="tpu_custom_call" | custom-call | flops 15000 | bytes 1 | tf_op jit(solution)/shard_map/project/pallas_call | solution.py:293
  329.8 10.1 %triangle.5 = (f32[128,64,128]{2,1,0:T(8,128)}, bf16[128,64,128]{2,1,0:T(8,128)(2,1)}) custom-call(s32[3]{0:T(128)} %pad_add_fusion.ids, bf16[128,64,256]{2,1,0:T(8,128)(2,1)} %get-tuple-element.154.a0.refs_8_, bf16[128,64,256]{2,1,0:T(8,128)(2,1)} %get-tuple-element.155.a1.refs_12_, bf16[128,64,256]{2,1,0:T(8,128)(2,1)} %get-tuple-element.160.b0.refs_9_, ...), custom_call_target="tpu_custom_call" | custom-call | flops 14000 | bytes 1 | tf_op jit(solution)/shard_map/triangle/pallas_call | solution.py:293
  340.1 13.5 %project.11 = (bf16[128,64,256]{2,1,0:T(8,128)(2,1)}, bf16[128,64,256]{2,1,0:T(8,128)(2,1)}) custom-call(bf16[129,64,256]{2,1,0:T(8,128)(2,1)} %collective-permute-done.acts_ref.code_ref, bf16[129,64,256]{2,1,0:T(8,128)(2,1)} %collective-permute-done.acts_ref.code_ref, bf16[512,128]{1,0:T(8,128)(2,1)} %get-tuple-element.146.w_ref, ...), custom_call_target="tpu_custom_call" | custom-call | flops 15000 | bytes 1 | tf_op jit(solution)/shard_map/project/pallas_call | solution.py:293
  353.6 10.5 %triangle.6 = (f32[128,64,128]{2,1,0:T(8,128)}, bf16[128,64,128]{2,1,0:T(8,128)(2,1)}) custom-call(s32[3]{0:T(128)} %pad_add_fusion.ids, bf16[128,64,256]{2,1,0:T(8,128)(2,1)} %get-tuple-element.154.a0.refs_8_, bf16[128,64,256]{2,1,0:T(8,128)(2,1)} %get-tuple-element.155.a1.refs_12_, bf16[128,64,256]{2,1,0:T(8,128)(2,1)} %get-tuple-element.162.b0.refs_10_, ...), custom_call_target="tpu_custom_call" | custom-call | flops 14000 | bytes 1 | tf_op jit(solution)/shard_map/triangle/pallas_call | solution.py:293
  364.4 33.8 %pair.5 = (bf16[128,64,128]{2,1,0:T(8,128)(2,1)}, f32[1352,128]{1,0:T(8,128)}, f32[7,128,128]{2,1,0:T(8,128)}) custom-call(s32[3]{0:T(128)} %pad_add_fusion.ids, f32[128,64,128]{2,1,0:T(8,128)} %get-tuple-element.188.x_keep, bf16[128,64,128]{2,1,0:T(8,128)(2,1)} %collective-permute-done.5.x_recv, bf16[129,256,128]{2,1,0:T(8,128)(2,1)} %turn.1.acts_ref.code_ref, ...), custom_call_target="tpu_custom_call" | custom-call | flops 35000 | bytes 1 | tf_op jit(solution)/shard_map/pair/pallas_call | solution.py:293
  401.6 34.0 %pair.6 = (bf16[128,64,128]{2,1,0:T(8,128)(2,1)}, f32[1352,128]{1,0:T(8,128)}, f32[7,128,128]{2,1,0:T(8,128)}) custom-call(s32[3]{0:T(128)} %pad_add_fusion.ids, f32[128,64,128]{2,1,0:T(8,128)} %get-tuple-element.193.x_keep, bf16[128,64,128]{2,1,0:T(8,128)(2,1)} %copy-done.5, bf16[129,256,128]{2,1,0:T(8,128)(2,1)} %turn.1.acts_ref.code_ref, ...), custom_call_target="tpu_custom_call" | custom-call | flops 35000 | bytes 1 | tf_op jit(solution)/shard_map/pair/pallas_call | solution.py:293
  435.7 13.5 %project.12 = (bf16[128,64,256]{2,1,0:T(8,128)(2,1)}, bf16[128,64,256]{2,1,0:T(8,128)(2,1)}) custom-call(bf16[129,64,256]{2,1,0:T(8,128)(2,1)} %collective-permute-done.3.acts_ref.code_ref, bf16[129,64,256]{2,1,0:T(8,128)(2,1)} %collective-permute-done.3.acts_ref.code_ref, bf16[512,128]{1,0:T(8,128)(2,1)} %get-tuple-element.146.w_ref, ...), custom_call_target="tpu_custom_call" | custom-call | flops 15000 | bytes 1 | tf_op jit(solution)/shard_map/project/pallas_call | solution.py:293
  449.2 13.5 %project.13 = (bf16[128,64,256]{2,1,0:T(8,128)(2,1)}, bf16[128,64,256]{2,1,0:T(8,128)(2,1)}) custom-call(bf16[129,64,256]{2,1,0:T(8,128)(2,1)} %collective-permute-done.2.acts_ref.code_ref, bf16[129,64,256]{2,1,0:T(8,128)(2,1)} %collective-permute-done.2.acts_ref.code_ref, bf16[512,128]{1,0:T(8,128)(2,1)} %get-tuple-element.146.w_ref, ...), custom_call_target="tpu_custom_call" | custom-call | flops 15000 | bytes 1 | tf_op jit(solution)/shard_map/project/pallas_call | solution.py:293
  462.7 10.4 %triangle.7 = (f32[128,64,128]{2,1,0:T(8,128)}, bf16[128,64,128]{2,1,0:T(8,128)(2,1)}) custom-call(s32[3]{0:T(128)} %pad_add_fusion.ids, bf16[128,64,256]{2,1,0:T(8,128)(2,1)} %get-tuple-element.154.a0.refs_8_, bf16[128,64,256]{2,1,0:T(8,128)(2,1)} %get-tuple-element.155.a1.refs_12_, bf16[128,64,256]{2,1,0:T(8,128)(2,1)} %get-tuple-element.198.b0.refs_11_, ...), custom_call_target="tpu_custom_call" | custom-call | flops 14000 | bytes 1 | tf_op jit(solution)/shard_map/triangle/pallas_call | solution.py:293
  483.2 34.1 %pair.7 = (bf16[128,64,128]{2,1,0:T(8,128)(2,1)}, f32[1352,128]{1,0:T(8,128)}, f32[7,128,128]{2,1,0:T(8,128)}) custom-call(s32[3]{0:T(128)} %pad_add_fusion.ids, f32[128,64,128]{2,1,0:T(8,128)} %get-tuple-element.204.x_keep, bf16[128,64,128]{2,1,0:T(8,128)(2,1)} %collective-permute-done.9.x_recv, bf16[129,256,128]{2,1,0:T(8,128)(2,1)} %turn.1.acts_ref.code_ref, ...), custom_call_target="tpu_custom_call" | custom-call | flops 35000 | bytes 1 | tf_op jit(solution)/shard_map/pair/pallas_call | solution.py:293
  522.0 20.5 %left_back.1 = (bf16[128,64,256]{2,1,0:T(8,128)(2,1)}, bf16[128,64,256]{2,1,0:T(8,128)(2,1)}) custom-call(s32[3]{0:T(128)} %pad_add_fusion.ids, bf16[128,64,128]{2,1,0:T(8,128)(2,1)} %get-tuple-element.175.refs_0_, bf16[128,64,128]{2,1,0:T(8,128)(2,1)} %get-tuple-element.191.refs_1_, bf16[128,64,128]{2,1,0:T(8,128)(2,1)} %get-tuple-element.196.refs_2_, ...), custom_call_target="tpu_custom_call" | custom-call | flops 25000 | bytes 1 | tf_op jit(solution)/shard_map/left_back/pallas_call | solution.py:293
  542.5 14.5 %input_back.4 = (f32[272,128]{1,0:T(8,128)}, f32[256,128]{1,0:T(8,128)}, f32[256,128]{1,0:T(8,128)}) custom-call(bf16[129,64,256]{2,1,0:T(8,128)(2,1)} %get-tuple-element.158.first.acts_ref.code_ref, bf16[129,64,256]{2,1,0:T(8,128)(2,1)} %get-tuple-element.158.first.acts_ref.code_ref, bf16[512,128]{1,0:T(8,128)(2,1)} %get-tuple-element.146.w_ref, ...), custom_call_target="tpu_custom_call" | custom-call | flops 16000 | bytes 1 | tf_op jit(solution)/shard_map/input_back/pallas_call | solution.py:293
  569.4 15.1 %input_back.5 = (f32[272,128]{1,0:T(8,128)}, f32[256,128]{1,0:T(8,128)}, f32[256,128]{1,0:T(8,128)}) custom-call(bf16[129,64,256]{2,1,0:T(8,128)(2,1)} %get-tuple-element.148.acts_ref.code_ref.second, bf16[129,64,256]{2,1,0:T(8,128)(2,1)} %get-tuple-element.148.acts_ref.code_ref.second, bf16[512,128]{1,0:T(8,128)(2,1)} %get-tuple-element.146.w_ref, ...), custom_call_target="tpu_custom_call" | custom-call | flops 16000 | bytes 1 | tf_op jit(solution)/shard_map/input_back/pallas_call | solution.py:293
  585.8 20.3 %right_back.1 = (bf16[128,64,256]{2,1,0:T(8,128)(2,1)}, bf16[128,64,256]{2,1,0:T(8,128)(2,1)}) custom-call(s32[3]{0:T(128)} %pad_add_fusion.ids, bf16[128,64,128]{2,1,0:T(8,128)(2,1)} %get-tuple-element.175.refs_0_, bf16[128,64,128]{2,1,0:T(8,128)(2,1)} %collective-permute-done.7.refs_1_, bf16[128,64,128]{2,1,0:T(8,128)(2,1)} %collective-permute-done.8.refs_2_, ...), custom_call_target="tpu_custom_call" | custom-call | flops 25000 | bytes 1 | tf_op jit(solution)/shard_map/right_back/pallas_call | solution.py:293
  606.1 14.5 %input_back.6 = (f32[272,128]{1,0:T(8,128)}, f32[256,128]{1,0:T(8,128)}, f32[256,128]{1,0:T(8,128)}) custom-call(bf16[129,64,256]{2,1,0:T(8,128)(2,1)} %get-tuple-element.158.first.acts_ref.code_ref, bf16[129,64,256]{2,1,0:T(8,128)(2,1)} %get-tuple-element.158.first.acts_ref.code_ref, bf16[512,128]{1,0:T(8,128)(2,1)} %get-tuple-element.146.w_ref, ...), custom_call_target="tpu_custom_call" | custom-call | flops 16000 | bytes 1 | tf_op jit(solution)/shard_map/input_back/pallas_call | solution.py:293
  620.6 14.8 %input_back.7 = (f32[272,128]{1,0:T(8,128)}, f32[256,128]{1,0:T(8,128)}, f32[256,128]{1,0:T(8,128)}) custom-call(bf16[129,64,256]{2,1,0:T(8,128)(2,1)} %get-tuple-element.148.acts_ref.code_ref.second, bf16[129,64,256]{2,1,0:T(8,128)(2,1)} %get-tuple-element.148.acts_ref.code_ref.second, bf16[512,128]{1,0:T(8,128)(2,1)} %get-tuple-element.146.w_ref, ...), custom_call_target="tpu_custom_call" | custom-call | flops 16000 | bytes 1 | tf_op jit(solution)/shard_map/input_back/pallas_call | solution.py:293
  635.4 29.3 %reduce_all.1.early_ref = f32[2048,128]{1,0:T(8,128)} custom-call(f32[1352,128]{1,0:T(8,128)} %scatter.4.pair_ref, f32[272,128]{1,0:T(8,128)} %get-tuple-element.215.left_ref, f32[272,128]{1,0:T(8,128)} %get-tuple-element.229.right_ref), custom_call_target="tpu_custom_call" | custom-call | tf_op jit(solution)/shard_map/reduce_all/pallas_call | solution.py:858
  (63 shorter events, 55.9 us)
Async XLA Ops:
  215.4 100.9 %collective-permute-start = (bf16[129,64,256]{2,1,0:T(8,128)(2,1)}, bf16[129,64,256]{2,1,0:T(8,128)(2,1)}, u32[]{:S(2)}, u32[]{:S(2)}) collective-permute-start(bf16[129,64,256]{2,1,0:T(8,128)(2,1)} %get-tuple-element.148.acts_ref.code_ref.second), channel_id=1, source_target_pairs={{0,16},{8,24},{16,0},{24,8},{1,17},{9,25},{17,1},{25,9},{2,18},{10... | collective-permute-start | bytes 12681224 | tf_op jit(solution)/shard_map/ppermute | solution.py:1137
  215.5 100.8 %collective-permute-start.4 = (bf16[129,64,256]{2,1,0:T(8,128)(2,1)}, bf16[129,64,256]{2,1,0:T(8,128)(2,1)}, u32[]{:S(2)}, u32[]{:S(2)}) collective-permute-start(bf16[129,64,256]{2,1,0:T(8,128)(2,1)} %get-tuple-element.148.acts_ref.code_ref.second), channel_id=1, source_target_pairs={{0,8},{8,0},{16,24},{24,16},{1,9},{9,1},{17,25},{25,17},{2,10},{10... | collective-permute-start | bytes 12681224 | tf_op jit(solution)/shard_map/ppermute | solution.py:1134
  243.2 36.0 %collective-permute-start.1 = (bf16[128,64,128]{2,1,0:T(8,128)(2,1)}, bf16[128,64,128]{2,1,0:T(8,128)(2,1)S(1)}, u32[]{:S(2)}, u32[]{:S(2)}) collective-permute-start(bf16[128,64,128]{2,1,0:T(8,128)(2,1)} %get-tuple-element.157), channel_id=1, source_target_pairs={{0,1},{1,0},{2,3},{3,2},{4,5},{5,4},{6,7},{7,6},{8,9},{9,8},{10,11... | collective-permute-start | bytes 6291464 | tf_op jit(solution)/shard_map/ppermute | solution.py:1143
  265.4 48.8 %slice-start = ((s8[4227072]{0:T(1024)(128)(4,1)}), s8[4194304]{0:T(1024)(128)(4,1)S(1)}, s32[]{:S(2)}) async-start(s8[4227072]{0:T(1024)(128)(4,1)} %bitcast.22), calls=%async_computation | async-start | bytes 8388608
  280.5 33.8 %slice-start.1 = ((s8[4227072]{0:T(1024)(128)(4,1)}), s8[32768]{0:T(1024)(128)(4,1)S(1)}, s32[]{:S(2)}) async-start(s8[4227072]{0:T(1024)(128)(4,1)} %bitcast.22), calls=%async_computation.1 | async-start | bytes 65536
  314.3 121.5 %collective-permute-start.3 = (bf16[129,64,256]{2,1,0:T(8,128)(2,1)S(1)}, bf16[129,64,256]{2,1,0:T(8,128)(2,1)}, u32[]{:S(2)}, u32[]{:S(2)}) collective-permute-start(bf16[129,64,256]{2,1,0:T(8,128)(2,1)S(1)} %bitcast.23), channel_id=1, source_target_pairs={{0,16},{8,24},{16,0},{24,8},{1,17},{9,25},{17,1},{25,9},{2,18},{10... | collective-permute-start | bytes 12681224 | tf_op jit(solution)/shard_map/ppermute | solution.py:1137
  316.3 132.9 %collective-permute-start.2 = (bf16[129,64,256]{2,1,0:T(8,128)(2,1)}, bf16[129,64,256]{2,1,0:T(8,128)(2,1)}, u32[]{:S(2)}, u32[]{:S(2)}) collective-permute-start(bf16[129,64,256]{2,1,0:T(8,128)(2,1)} %collective-permute-done.acts_ref.code_ref), channel_id=1, source_target_pairs={{0,8},{8,0},{16,24},{24,16},{1,9},{9,1},{17,25},{25,17},{2,10},{10... | collective-permute-start | bytes 12681224 | tf_op jit(solution)/shard_map/ppermute | solution.py:1134
  339.9 24.5 %collective-permute-start.5 = (bf16[128,64,128]{2,1,0:T(8,128)(2,1)}, bf16[128,64,128]{2,1,0:T(8,128)(2,1)}, u32[]{:S(2)}, u32[]{:S(2)}) collective-permute-start(bf16[128,64,128]{2,1,0:T(8,128)(2,1)} %get-tuple-element.182), channel_id=1, source_target_pairs={{0,1},{1,0},{2,3},{3,2},{4,5},{5,4},{6,7},{7,6},{8,9},{9,8},{10,11... | collective-permute-start | bytes 6291464 | tf_op jit(solution)/shard_map/ppermute | solution.py:1143
  364.0 36.2 %collective-permute-start.6 = (bf16[128,64,128]{2,1,0:T(8,128)(2,1)}, bf16[128,64,128]{2,1,0:T(8,128)(2,1)S(1)}, u32[]{:S(2)}, u32[]{:S(2)}) collective-permute-start(bf16[128,64,128]{2,1,0:T(8,128)(2,1)} %get-tuple-element.186), channel_id=1, source_target_pairs={{0,1},{1,0},{2,3},{3,2},{4,5},{5,4},{6,7},{7,6},{8,9},{9,8},{10,11... | collective-permute-start | bytes 6291464 | tf_op jit(solution)/shard_map/ppermute | solution.py:1143
  398.2 75.0 %collective-permute-start.7 = (bf16[128,64,128]{2,1,0:T(8,128)(2,1)}, bf16[128,64,128]{2,1,0:T(8,128)(2,1)}, u32[]{:S(2)}, u32[]{:S(2)}) collective-permute-start(bf16[128,64,128]{2,1,0:T(8,128)(2,1)} %get-tuple-element.191.refs_1_), channel_id=1, source_target_pairs={{0,8},{8,0},{16,24},{24,16},{1,9},{9,1},{17,25},{25,17},{2,10},{10... | collective-permute-start | bytes 6291464 | tf_op jit(solution)/shard_map/ppermute | solution.py:1134
  435.5 47.7 %collective-permute-start.8 = (bf16[128,64,128]{2,1,0:T(8,128)(2,1)}, bf16[128,64,128]{2,1,0:T(8,128)(2,1)}, u32[]{:S(2)}, u32[]{:S(2)}) collective-permute-start(bf16[128,64,128]{2,1,0:T(8,128)(2,1)} %get-tuple-element.196.refs_2_), channel_id=1, source_target_pairs={{0,16},{8,24},{16,0},{24,8},{1,17},{9,25},{17,1},{25,9},{2,18},{10... | collective-permute-start | bytes 6291464 | tf_op jit(solution)/shard_map/ppermute | solution.py:1137
  462.7 11.0 %copy-start = (bf16[128,64,128]{2,1,0:T(8,128)(2,1)S(1)}, bf16[128,64,128]{2,1,0:T(8,128)(2,1)}, u32[]{:S(2)}) copy-start(bf16[128,64,128]{2,1,0:T(8,128)(2,1)} %get-tuple-element.175.refs_0_) | copy-start | bytes 6291460
  473.1 10.1 %collective-permute-start.9 = (bf16[128,64,128]{2,1,0:T(8,128)(2,1)}, bf16[128,64,128]{2,1,0:T(8,128)(2,1)}, u32[]{:S(2)}, u32[]{:S(2)}) collective-permute-start(bf16[128,64,128]{2,1,0:T(8,128)(2,1)} %get-tuple-element.202), channel_id=1, source_target_pairs={{0,1},{1,0},{2,3},{3,2},{4,5},{5,4},{6,7},{7,6},{8,9},{9,8},{10,11... | collective-permute-start | bytes 6291464 | tf_op jit(solution)/shard_map/ppermute | solution.py:1143
  473.2 44.7 %collective-permute-start.10 = (bf16[128,64,128]{2,1,0:T(8,128)(2,1)}, bf16[128,64,128]{2,1,0:T(8,128)(2,1)S(1)}, u32[]{:S(2)}, u32[]{:S(2)}) collective-permute-start(bf16[128,64,128]{2,1,0:T(8,128)(2,1)} %collective-permute-done.7.refs_1_), channel_id=1, source_target_pairs={{0,1},{1,0},{2,3},{3,2},{4,5},{5,4},{6,7},{7,6},{8,9},{9,8},{10,11... | collective-permute-start | bytes 6291464 | tf_op jit(solution)/shard_map/ppermute | solution.py:1143
  473.7 44.2 %collective-permute-start.11 = (bf16[128,64,128]{2,1,0:T(8,128)(2,1)S(1)}, bf16[128,64,128]{2,1,0:T(8,128)(2,1)S(1)}, u32[]{:S(2)}, u32[]{:S(2)}) collective-permute-start(bf16[128,64,128]{2,1,0:T(8,128)(2,1)S(1)} %copy-done), channel_id=1, source_target_pairs={{0,1},{1,0},{2,3},{3,2},{4,5},{5,4},{6,7},{7,6},{8,9},{9,8},{10,11... | collective-permute-start | bytes 6291464 | tf_op jit(solution)/shard_map/ppermute | solution.py:1143
  473.8 44.3 %collective-permute-start.12 = (bf16[128,64,128]{2,1,0:T(8,128)(2,1)}, bf16[128,64,128]{2,1,0:T(8,128)(2,1)}, u32[]{:S(2)}, u32[]{:S(2)}) collective-permute-start(bf16[128,64,128]{2,1,0:T(8,128)(2,1)} %get-tuple-element.191.refs_1_), channel_id=1, source_target_pairs={{0,1},{1,0},{2,3},{3,2},{4,5},{5,4},{6,7},{7,6},{8,9},{9,8},{10,11... | collective-permute-start | bytes 6291464 | tf_op jit(solution)/shard_map/ppermute | solution.py:1143
  483.2 34.9 %collective-permute-start.13 = (bf16[128,64,128]{2,1,0:T(8,128)(2,1)}, bf16[128,64,128]{2,1,0:T(8,128)(2,1)}, u32[]{:S(2)}, u32[]{:S(2)}) collective-permute-start(bf16[128,64,128]{2,1,0:T(8,128)(2,1)} %get-tuple-element.196.refs_2_), channel_id=1, source_target_pairs={{0,1},{1,0},{2,3},{3,2},{4,5},{5,4},{6,7},{7,6},{8,9},{9,8},{10,11... | collective-permute-start | bytes 6291464 | tf_op jit(solution)/shard_map/ppermute | solution.py:1143
  517.3 4.7 collective-permute-start.14
  517.9 24.6 %copy-start.2 = (bf16[128,64,128]{2,1,0:T(8,128)(2,1)}, bf16[128,64,128]{2,1,0:T(8,128)(2,1)S(1)}, u32[]{:S(2)}) copy-start(bf16[128,64,128]{2,1,0:T(8,128)(2,1)S(1)} %collective-permute-done.10.refs_5_) | copy-start | bytes 6291460
  517.9 48.8 %collective-permute-start.16 = (bf16[128,64,128]{2,1,0:T(8,128)(2,1)}, bf16[128,64,128]{2,1,0:T(8,128)(2,1)}, u32[]{:S(2)}, u32[]{:S(2)}) collective-permute-start(bf16[128,64,128]{2,1,0:T(8,128)(2,1)} %get-tuple-element.208.refs_3_), channel_id=1, source_target_pairs={{0,24},{8,16},{16,8},{24,0},{1,25},{9,17},{17,9},{25,1},{2,26},{10... | collective-permute-start | bytes 6291464 | tf_op jit(solution)/shard_map/ppermute | solution.py:1140
  517.9 4.1 copy-start.1
  517.9 66.5 %collective-permute-start.15 = (bf16[128,64,128]{2,1,0:T(8,128)(2,1)}, bf16[128,64,128]{2,1,0:T(8,128)(2,1)}, u32[]{:S(2)}, u32[]{:S(2)}) collective-permute-start(bf16[128,64,128]{2,1,0:T(8,128)(2,1)} %collective-permute-done.8.refs_2_), channel_id=1, source_target_pairs={{0,1},{1,0},{2,3},{3,2},{4,5},{5,4},{6,7},{7,6},{8,9},{9,8},{10,11... | collective-permute-start | bytes 6291464 | tf_op jit(solution)/shard_map/ppermute | solution.py:1143
  542.5 24.2 %copy-start.6 = (s32[1,512]{1,0:T(1,128)S(1)}, s32[1,512]{1,0:T(1,128)}, u32[]{:S(2)}) copy-start(s32[1,512]{1,0:T(1,128)} %param.27) | copy-start | bytes 6148
  566.7 17.7 %collective-permute-start.17 = (bf16[128,64,128]{2,1,0:T(8,128)(2,1)}, bf16[128,64,128]{2,1,0:T(8,128)(2,1)S(1)}, u32[]{:S(2)}, u32[]{:S(2)}) collective-permute-start(bf16[128,64,128]{2,1,0:T(8,128)(2,1)} %collective-permute-done.16.refs_3_), channel_id=1, source_target_pairs={{0,1},{1,0},{2,3},{3,2},{4,5},{5,4},{6,7},{7,6},{8,9},{9,8},{10,11... | collective-permute-start | bytes 6291464 | tf_op jit(solution)/shard_map/ppermute | solution.py:1143
  (3 other events, 4.0 us)

commit v5 on v4

--- a/solution.py
+++ b/solution.py
@@ -249,10 +249,6 @@
     return lax.dot_general(left, right, dims, preferred_element_type=F32)
 
 
-def sigmoid(values):
-    return 0.5 * jnp.tanh(0.5 * values) + 0.5
-
-
 def column_stats(values):
     center = values - jnp.mean(values, 0, keepdims=True)
     rstd = lax.rsqrt(jnp.mean(center * center, 0, keepdims=True) + NORM_EPS)
@@ -317,59 +313,25 @@
 
 ROWS = 16
 PROJECT_GROUP = 8
-INPUT_GROUP = 8
-
-
-def prepare_kernel(
-    acts_ref, code_ref, w_in, w_out, w_t1, w_t2, w_dist, norms, bias,
-    out_ref, projT, ogT, outT, out_w, t1T, t1, t2T, t2, distT, dist, ln_ref, bias_ref, rows_s,
-):
-    chans = acts_ref.shape[2]
-    for row in range(ROWS):
-        rows_s[row] = jnp.transpose(acts_ref[row])
-    out_ref[:chans] = jnp.swapaxes(rows_s[...], 0, 1)
-    out_ref[chans] = code_ref[...]
-
-    @pl.when(pl.program_id(0) == 0)
-    def _():
-        count = projT.shape[0]
-        projT[...] = jnp.transpose(w_in[:, :count]).astype(BF16)
-        ogT[...] = jnp.transpose(w_in[:, count:]).astype(BF16)
-        for weight, plain, turned in (
-            (w_out, out_w, outT), (w_t1, t1, t1T), (w_t2, t2, t2T), (w_dist, distT, dist)
-        ):
-            plain[...] = weight[...].astype(BF16)
-            turned[...] = jnp.transpose(weight[...]).astype(BF16)
-        for index in range(6):
-            ln_ref[index] = jnp.transpose(jnp.broadcast_to(norms[index : index + 1, :], (128, chans)))
-        bias_ref[...] = jnp.transpose(jnp.broadcast_to(bias[...], (128, bias.shape[1])))
-
-
-def prepare(acts, code, w_in, w_out, w_t1, w_t2, w_dist, norms, bias):
-    rows, lanes, chans = acts.shape
-    width = w_out.shape[0]
-    params = (w_in, w_out, w_t1, w_t2, w_dist.T, norms, bias.reshape(1, -1))
-    shapes = [(4 * width, chans), (chans, chans)]
-    for weight in (w_out, w_t1, w_t2, w_dist):
-        turned = (weight.shape[1], weight.shape[0])
-        shapes += [turned, weight.shape]
-    shapes = [(shape, BF16) for shape in shapes]
-    shapes += [((6, chans, 128), F32), ((bias.shape[0], 128), F32)]
-    return call(
-        prepare_kernel,
-        (rows // ROWS,),
-        [],
-        [
-            (acts, (ROWS, lanes, chans), lambda i, *_: (i, 0, 0)),
-            (code, (ROWS, lanes), lambda i, *_: (i, 0)),
-        ]
-        + [(v, v.shape, fixed(*([0] * v.ndim))) for v in params],
-        [((chans + 1, rows, lanes), BF16, (chans + 1, ROWS, lanes), lambda i, *_: (0, i, 0))]
-        + [(shape, dtype, shape, fixed(*([0] * len(shape)))) for shape, dtype in shapes],
-        [pltpu.VMEM((ROWS, chans, lanes), BF16)],
-        1,
-        "prepare",
-    )
+INPUT_GROUP = 16
+
+
+def prepare_weights(w_in, w_out, w_t1, w_t2, w_dist, norms, bias, outs):
+    projT, ogT, outT, out_w, t1T, t1, t2T, t2, distT, dist, ln_ref, bias_ref = outs
+    count, chans = projT.shape
+    projT[...] = (0.5 * jnp.transpose(w_in[:, :count])).astype(BF16)
+    ogT[...] = (0.5 * jnp.transpose(w_in[:, count:])).astype(BF16)
+    for weight, plain, turned, plain_scale, turned_scale in (
+        (w_out, out_w, outT, 1.0, 1.0),
+        (w_t1, t1, t1T, 1.0, 0.5),
+        (w_t2, t2, t2T, 0.5, 1.0),
+        (w_dist, distT, dist, 1.0, 1.0),
+    ):
+        plain[...] = (plain_scale * weight[...]).astype(BF16)
+        turned[...] = (turned_scale * jnp.transpose(weight[...])).astype(BF16)
+    for index in range(6):
+        ln_ref[index] = jnp.transpose(jnp.broadcast_to(norms[index : index + 1, :], (128, chans)))
+    bias_ref[...] = jnp.transpose(jnp.broadcast_to(bias[...], (128, bias.shape[1])))
 
 
 def project_kernel(acts_ref, code_ref, w_ref, ln_ref, a_ref, b_ref, acts_s, a_s, b_s, code_s):
@@ -382,11 +344,11 @@
         values = take_rows(acts_s, start, PROJECT_GROUP)
         lanes = values.shape[1]
         normed, _ = column_stats(values)
-        low = (normed * widen(ln_ref[0], lanes) + widen(ln_ref[1], lanes)).astype(BF16)
+        low = normed * widen(ln_ref[0], lanes) + widen(ln_ref[1], lanes)
+        low = (low * present_rows(code_s, start, PROJECT_GROUP)).astype(BF16)
         proj = dot(w_ref[...], low)
-        mask = present_rows(code_s, start, PROJECT_GROUP)
-        left = proj[:width] * sigmoid(proj[width : 2 * width]) * mask
-        right = proj[2 * width : 3 * width] * sigmoid(proj[3 * width :]) * mask
+        left = proj[:width] * (jnp.tanh(proj[width : 2 * width]) + 1.0)
+        right = proj[2 * width : 3 * width] * (jnp.tanh(proj[3 * width :]) + 1.0)
         put_rows(a_s, start, PROJECT_GROUP, left)
         put_rows(b_s, start, PROJECT_GROUP, right)
         return carry
@@ -524,15 +486,15 @@
         out = dot(w_outT[...], tri)
         normed_one, _ = column_stats(acts)
         low = (normed_one * param[0] + param[1]).astype(BF16)
-        gate = sigmoid(dot(w_ogT[...], low))
+        gate = 0.5 * jnp.tanh(dot(w_ogT[...], low)) + 0.5
         z1 = acts + gate * out
         normed_three, rstd_three = column_stats(z1)
         trans = (normed_three * param[4] + param[5]).astype(BF16)
         pre = dot(w_t1T[...], trans)
-        sig = sigmoid(pre)
-        act = pre * sig
-        hidden = act.astype(BF16)
-        slope = sig * (1.0 + (pre - act))
+        tanh = jnp.tanh(pre)
+        bent = pre * tanh
+        hidden = (pre + bent).astype(BF16)
+        slope = (1.0 + tanh) * (1.0 + (pre - bent))
         final = (z1 + dot(w_t2T[...], hidden)).astype(BF16)
         logits = dot(w_distT[...], final) + widen(bias_ref[...], lanes)
         top = jnp.max(logits, 0, keepdims=True)
@@ -558,7 +520,9 @@
         d_out = d_gated.astype(BF16)
         d_og = (d_gated * out * (1.0 - gate)).astype(BF16)
         add(OUT_ROW, dot(d_out, tri, NT))
-        wide[6] += dot(d_og, normed_one.astype(BF16), NT)
+        g_og = dot(d_og, jnp.concatenate([low, normed_one.astype(BF16)], 0), NT)
+        add(OG_ROW, g_og[:, :chans])
+        wide[6] += g_og[:, chans:]
         wide[4] += fold(d_og.astype(F32))
         d_xn = dot(w_out[...], d_out)
         wide[0] += fold(d_xn * normed_two)
@@ -574,11 +538,10 @@
 
         @pl.when(pl.program_id(0) == pl.num_programs(0) - 1)
         def _():
-            gate_w = w_ogT[...].astype(F32)
+            gate_w = 2.0 * w_ogT[...].astype(F32)
             for index in range(4):
                 add(NORM_ROW + index, row_sums(wide[index]))
             total = jnp.sum(wide[4], 1, keepdims=True)
-            add(OG_ROW, affine_grad(wide[6], total, ln_ref))
             add(NORM_ROW + 4, jnp.sum(gate_w * wide[6], 0, keepdims=True))
             add(NORM_ROW + 5, jnp.sum(gate_w * total, 0, keepdims=True))
             add(BIAS_ROW, row_sums(wide[5]))
@@ -732,10 +695,7 @@
 
     code_s[...] = code_ref[0].astype(F32)
     spread_rows(acts_s, acts_ref[...])
-    total = grads[0][...].astype(F32)
-    for ref in grads[1:]:
-        total = total + ref[...].astype(F32)
-    spread_rows(grad_s, total)
+    spread_rows(grad_s, grads[0][...])
 
     def some(step, carry):
         start = step * INPUT_GROUP
@@ -744,14 +704,17 @@
         normed, _ = column_stats(values)
         low = (normed * widen(ln_ref[0], lanes) + widen(ln_ref[1], lanes)).astype(BF16)
         proj = dot(w_ref[...], low)
-        gate = sigmoid(proj[width:])
-        mask = present_rows(code_s, start, INPUT_GROUP)
-        d_value = take_rows(grad_s, start, INPUT_GROUP) * mask * gate
-        d_gate = d_value * proj[:width] * (1.0 - gate)
+        tanh = jnp.tanh(proj[width:])
+        d_half = take_rows(grad_s, start, INPUT_GROUP) * (0.5 * present_rows(code_s, start, INPUT_GROUP))
+        d_tanh = d_half * tanh
+        d_value = d_half + d_tanh
+        d_gate = proj[:width] * (d_half - d_tanh * tanh)
         d_proj = jnp.concatenate([d_value.astype(BF16), d_gate.astype(BF16)], 0)
         g_ref[...] += dot(d_proj, normed.astype(BF16), NT)
-        wide = d_proj.astype(F32)
-        sum_ref[...] += sum(wide[:, 128 * u : 128 * u + 128] for u in range(lanes // 128))
+        for first, part in ((0, d_value), (width, d_gate)):
+            sum_ref[first : first + width] += sum(
+                part[:, 128 * u : 128 * u + 128] for u in range(lanes // 128)
+            )
         return carry
 
     lax.fori_loop(0, ROWS // INPUT_GROUP, some, 0)
@@ -760,7 +723,7 @@
 
         @pl.when(pl.program_id(0) == pl.num_programs(0) - 1)
         def _():
-            part = w_ref[...].astype(F32)
+            part = 2.0 * w_ref[...].astype(F32)
             total = jnp.sum(sum_ref[...], 1, keepdims=True)
             gain = jnp.sum(part * g_ref[...], 0, keepdims=True)
             shift = jnp.sum(part * total, 0, keepdims=True)
@@ -790,7 +753,7 @@
         [(s, F32, s, fixed(0, 0)) for s in shapes],
         [
             pltpu.VMEM((ROWS, chans, lanes), BF16),
-            pltpu.VMEM((ROWS, chans, lanes), F32),
+            pltpu.VMEM((ROWS, chans, lanes), BF16),
             pltpu.VMEM((ROWS, lanes), F32),
         ],
         16 * MICRO,
@@ -882,16 +845,41 @@
 
 
 def spread_kernel(
-    acts_ref, w_ref, ln_ref, wave0_ref, wave1_ref, x_ref, y_ref, a_ref, b_ref, mid,
-    plane_send, plane_recv, share_send, share_recv, level_send, level_recv, local,
+    acts_ref, code_ref, w_in, w_out, w_t1, w_t2, w_dist, norms, bias,
+    wave0_ref, wave1_ref, x_ref, y_ref, a_ref, b_ref,
+    projT, ogT, outT, out_w, t1T, t1, t2T, t2, distT, dist, ln_ref, bias_ref,
+    mid, taken, made, fetched, plane_send, plane_recv, share_send, share_recv, level_send, level_recv, local,
     wave_v, a_v, b_v, acts_s, a_s, b_s, code_s,
 ):
     spot, level = lax.axis_index("crop"), lax.axis_index("row")
-    chans = acts_ref.shape[0]
+    chans = mid.shape[2]
     early, middle = chans // 4, 5 * chans // 8
     cuts = [[(0, early), (early, middle - early), (middle, chans - middle)], [(0, chans)]]
     waves = (wave0_ref, wave1_ref)
     mesh_id = pl.DeviceIdType.MESH
+
+    def block_rows(wave, distance):
+        return pl.ds(pl.multiple_of(32 * flip(spot, distance) + 16 * wave, 16), 16)
+
+    def fetch_block(wave, distance):
+        return pltpu.make_async_copy(
+            acts_ref.at[block_rows(wave, distance)], taken.at[wave, distance], fetched.at[4 * wave + distance]
+        )
+
+    def make_block(wave, distance):
+        fetch_block(wave, distance).wait()
+
+        def turn_row(row, carry):
+            acts_s[row] = jnp.transpose(taken[wave, distance, row])
+            return carry
+
+        lax.fori_loop(0, ROWS, turn_row, 0, unroll=8)
+        made[wave, distance, : chans - 1] = jnp.swapaxes(acts_s[...], 0, 1)
+        made[wave, distance, chans - 1] = code_ref[block_rows(wave, distance), :]
+
+    for wave in range(2):
+        for distance in range(4):
+            fetch_block(wave, distance).start()
     barrier = pltpu.get_barrier_semaphore()
     for n in range(1, 4):
         for device in ({"crop": lax.rem(spot + n, 4)}, {"row": lax.rem(level + n, 4)}):
@@ -901,9 +889,7 @@
     def plane_copy(wave, cut, distance):
         first, count = cuts[wave][cut]
         target = flip(spot, distance)
-        source = acts_ref.at[
-            pl.ds(first, count), pl.ds(pl.multiple_of(32 * target + 16 * wave, 16), 16)
-        ]
+        source = made.at[wave, distance, pl.ds(first, count)]
         landing = mid.at[wave, distance, pl.ds(first, count)]
         index = 12 * wave + 4 * cut + distance
         if distance == 0:
@@ -954,9 +940,15 @@
         [[plane_copy(wave, cut, distance) for distance in range(4)] for cut in range(len(cuts[wave]))]
         for wave in range(2)
     ]
-    for copies in plane[0] + plane[1]:
+    for distance in (1, 3, 2, 0):
+        make_block(0, distance)
+        plane[0][0][distance].start()
+    for copies in plane[0][1:]:
         for one in copies:
             one.start()
+    for distance in (1, 3, 2, 0):
+        make_block(1, distance)
+        plane[1][0][distance].start()
 
     def begin(wave, cut, label, distance):
         one = plane[wave][cut][distance]
@@ -989,8 +981,13 @@
             for one in shares(cut, label):
                 one.start()
 
-    for cut in range(3):
-        each_level(begin, 0, cut)
+    each_level(begin, 0, 0)
+    prepare_weights(
+        w_in, w_out, w_t1, w_t2, w_dist, norms, bias,
+        (projT, ogT, outT, out_w, t1T, t1, t2T, t2, distT, dist, ln_ref, bias_ref),
+    )
+    each_level(begin, 0, 1)
+    each_level(begin, 0, 2)
     each_level(begin, 1, 0)
     for cut in range(3):
         pass_on(cut)
@@ -1002,7 +999,7 @@
     def project_rows(step, carry):
         rows = pl.ds(pl.multiple_of(step * ROWS, ROWS), ROWS)
         project_kernel(
-            wave_v.at[pl.ds(0, width), rows], wave_v.at[pl.ds(width, 1), rows], w_ref, ln_ref,
+            wave_v.at[pl.ds(0, width), rows], wave_v.at[pl.ds(width, 1), rows], projT, ln_ref,
             a_v.at[:, rows], b_v.at[:, rows], acts_s, a_s, b_s, code_s,
         )
         return carry
@@ -1025,19 +1022,28 @@
     each_level(arrive, 1, 0)
 
 
-def spread(acts_major, w_proj, ln_wide):
-    chans, rows, lanes = acts_major.shape
-    half, width = rows // 2, chans - 1
+def spread(acts, code, w_in, w_out, w_t1, w_t2, w_dist, norms, bias):
+    rows, lanes, width = acts.shape
+    chans, half = width + 1, rows // 2
     anywhere = pl.BlockSpec(memory_space=pl.ANY)
     whole = pl.BlockSpec(memory_space=pltpu.VMEM)
     staged = pltpu.VMEM((ROWS, width, lanes), BF16)
+    shapes = [(4 * width, width), (width, width)]
+    for weight in (w_out, w_t1, w_t2, w_dist):
+        shapes += [(weight.shape[1], weight.shape[0]), weight.shape]
+    shapes = [jax.ShapeDtypeStruct(shape, BF16) for shape in shapes]
+    shapes += [jax.ShapeDtypeStruct((6, width, 128), F32), jax.ShapeDtypeStruct((bias.shape[0], 128), F32)]
     return pl.pallas_call(
         spread_kernel,
-        in_specs=[anywhere, whole, whole],
-        out_specs=[anywhere] * 6,
+        in_specs=[anywhere] + [whole] * 8,
+        out_specs=[anywhere] * 6 + [whole] * len(shapes),
         out_shape=[jax.ShapeDtypeStruct((chans, half, lanes), BF16)] * 4
-        + [jax.ShapeDtypeStruct((width, half, lanes), BF16)] * 2,
-        scratch_shapes=[pltpu.VMEM((2, 4, chans, rows // 8, lanes), BF16)]
+        + [jax.ShapeDtypeStruct((width, half, lanes), BF16)] * 2
+        + shapes,
+        scratch_shapes=[pltpu.VMEM((2, 4, chans, ROWS, lanes), BF16)]
+        + [pltpu.VMEM((2, 4, ROWS, lanes, width), BF16)]
+        + [pltpu.VMEM((2, 4, chans, ROWS, lanes), BF16)]
+        + [pltpu.SemaphoreType.DMA((8,))]
         + [pltpu.SemaphoreType.DMA((16,)) for _ in range(2)]
         + [pltpu.SemaphoreType.DMA((24,)) for _ in range(2)]
         + [pltpu.SemaphoreType.DMA((16,)) for _ in range(2)]
@@ -1050,7 +1056,7 @@
             collective_id=2, has_side_effects=True, vmem_limit_bytes=VMEM_LIMIT
         ),
         name="spread",
-    )(acts_major, w_proj, ln_wide)
+    )(acts, code, w_in, w_out, w_t1, w_t2, w_dist.T, norms, bias.reshape(1, -1))
 
 
 def update_kernel(early_ref, *refs):
@@ -1146,13 +1152,12 @@
     row_own = lax.dynamic_slice_in_dim(own_mask, rows * level, rows)
     col_own = lax.dynamic_slice_in_dim(own_mask, cols * side, cols)
     code_own = jnp.where((row_own[:, None] * col_own[None, :]) > 0, dist_bins[0], -1).astype(BF16)
-    acts_major, proj_w, *weights, ln_wide, bias_wide = prepare(
+
+    wave0, wave1, wave0_x, wave0_y, left_own, right_own, proj_w, *weights, ln_wide, bias_wide = spread(
         pair_acts[0], code_own, w_in, w_out, w_t1, w_t2, w_dist, norm_params, dist_bias
     )
     og_T, out_T, out_w, t1_T, t1_w, t2_T, t2_w, dist_T, dist_w = weights
     weights = (out_T, out_w, og_T, t1_T, t1_w, t2_T, t2_w, dist_T, dist_w)
-
-    wave0, wave1, wave0_x, wave0_y, left_own, right_own = spread(acts_major, proj_w, ln_wide)
 
     count = jnp.sum(own_mask).astype(F32)
     share_count = lax.axis_size("row") * lax.axis_size("col")

time: 673 us -> 650 us (0.966)
  Pallas kernels: 626 us -> 596 us
    pallas_call x23 -> x22, Pallas kernels: 391 us -> 360 us  [call(): pl.pallas_call(kernel, grid_spec=pltpu.PrefetchScalarGridSpec(num_scalar_...]
where the time goes in v5:
time: 650 us; the launch traced here: 645 us
  Pallas kernels  596 us (92%)
  waiting for transfers between devices  25.6 us (4%)
  starting transfers between devices  11.5 us (2%)
  local copies, waits for them, and re-layouts  6.66 us (1%)
    pallas_call x22, Pallas kernels, call(): pl.pallas_call(kernel, grid_spec=pltpu.PrefetchScalarGridSpec(num_scalar_...  360 us
    pallas_call x1, Pallas kernels, spread(): pl.pallas_call(spread_kernel, in_specs=[anywhere] + [whole] * 8, out_spec...  203 us
    pallas_call x1, Pallas kernels, reduce_all(): pl.pallas_call(reduce_kernel, out_shape=jax.ShapeDtypeStruct((ALL_ROWS, l...  29.3 us
  transfers between devices with their start and end apart: 18, of which 3 were waited for; matrix products, arithmetic and copies ran while one was open for 0% of the time, Pallas kernels for 49%

profile of v5, /device:TPU:0, one launch (start us, length us, event | category | flops | bytes accessed | tf_op | source)
XLA Modules:
  0.0 645.0 jit_solution(16041846140619354837)
XLA Ops:
  3.6 202.6 %spread.1 = (bf16[129,64,256]{2,1,0:T(8,128)(2,1)}, bf16[129,64,256]{2,1,0:T(8,128)(2,1)}, bf16[129,64,256]{2,1,0:T(8,128)(2,1)}, bf16[129,64,256]{2,1,0:T(8,128...) custom-call(bf16[128,256,128]{2,1,0:T(8,128)(2,1)} %bitcast.24, ...), custom_call_target="tpu_custom_call" | custom-call | tf_op jit(solution)/shard_map/spread/pallas_call | solution.py:1036
  210.6 12.4 %project.7 = (bf16[128,64,256]{2,1,0:T(8,128)(2,1)}, bf16[128,64,256]{2,1,0:T(8,128)(2,1)}) custom-call(bf16[129,64,256]{2,1,0:T(8,128)(2,1)} %get-tuple-element.144.acts_ref.code_ref.second, bf16[129,64,256]{2,1,0:T(8,128)(2,1)} %get-tuple-element.144.acts_ref.code_ref.second, bf16[512,128]{1,0:T(8,128)(2,1)} %get-tuple-element.148.w_ref, ...), custom_call_target="tpu_custom_call" | custom-call | flops 15000 | bytes 1 | tf_op jit(solution)/shard_map/project/pallas_call | solution.py:289
  242.4 12.5 %project.8 = (bf16[128,64,256]{2,1,0:T(8,128)(2,1)}, bf16[128,64,256]{2,1,0:T(8,128)(2,1)}) custom-call(bf16[129,64,256]{2,1,0:T(8,128)(2,1)} %get-tuple-element.175.acts_ref.code_ref, bf16[129,64,256]{2,1,0:T(8,128)(2,1)} %get-tuple-element.175.acts_ref.code_ref, bf16[512,128]{1,0:T(8,128)(2,1)} %get-tuple-element.148.w_ref, ...), custom_call_target="tpu_custom_call" | custom-call | flops 15000 | bytes 1 | tf_op jit(solution)/shard_map/project/pallas_call | solution.py:289
  254.9 12.7 %project.9 = (bf16[128,64,256]{2,1,0:T(8,128)(2,1)}, bf16[128,64,256]{2,1,0:T(8,128)(2,1)}) custom-call(bf16[129,64,256]{2,1,0:T(8,128)(2,1)} %get-tuple-element.159.acts_ref.code_ref, bf16[129,64,256]{2,1,0:T(8,128)(2,1)} %get-tuple-element.159.acts_ref.code_ref, bf16[512,128]{1,0:T(8,128)(2,1)} %get-tuple-element.148.w_ref, ...), custom_call_target="tpu_custom_call" | custom-call | flops 15000 | bytes 1 | tf_op jit(solution)/shard_map/project/pallas_call | solution.py:289
  269.0 31.9 %pair.4 = (bf16[128,64,128]{2,1,0:T(8,128)(2,1)}, f32[1352,128]{1,0:T(8,128)}, f32[7,128,128]{2,1,0:T(8,128)}) custom-call(s32[3]{0:T(128)} %pad_add_fusion.ids, f32[128,64,128]{2,1,0:T(8,128)} %get-tuple-element.162.x_keep, bf16[128,64,128]{2,1,0:T(8,128)(2,1)} %copy-done.4, bf16[129,256,128]{2,1,0:T(8,128)(2,1)} %turn.1.acts_ref.code_ref, ...), custom_call_target="tpu_custom_call" | custom-call | flops 35000 | bytes 1 | tf_op jit(solution)/shard_map/pair/pallas_call | solution.py:289
  303.8 12.5 %project.10 = (bf16[128,64,256]{2,1,0:T(8,128)(2,1)}, bf16[128,64,256]{2,1,0:T(8,128)(2,1)}) custom-call(bf16[129,64,256]{2,1,0:T(8,128)(2,1)} %collective-permute-done.4.acts_ref.code_ref, bf16[129,64,256]{2,1,0:T(8,128)(2,1)} %collective-permute-done.4.acts_ref.code_ref, bf16[512,128]{1,0:T(8,128)(2,1)} %get-tuple-element.148.w_ref, ...), custom_call_target="tpu_custom_call" | custom-call | flops 15000 | bytes 1 | tf_op jit(solution)/shard_map/project/pallas_call | solution.py:289
  316.2 10.1 %triangle.5 = (f32[128,64,128]{2,1,0:T(8,128)}, bf16[128,64,128]{2,1,0:T(8,128)(2,1)}) custom-call(s32[3]{0:T(128)} %pad_add_fusion.ids, bf16[128,64,256]{2,1,0:T(8,128)(2,1)} %get-tuple-element.152.a0.refs_8_, bf16[128,64,256]{2,1,0:T(8,128)(2,1)} %get-tuple-element.153.a1.refs_12_, bf16[128,64,256]{2,1,0:T(8,128)(2,1)} %get-tuple-element.158.b0.refs_9_, ...), custom_call_target="tpu_custom_call" | custom-call | flops 14000 | bytes 1 | tf_op jit(solution)/shard_map/triangle/pallas_call | solution.py:289
  326.3 12.6 %project.11 = (bf16[128,64,256]{2,1,0:T(8,128)(2,1)}, bf16[128,64,256]{2,1,0:T(8,128)(2,1)}) custom-call(bf16[129,64,256]{2,1,0:T(8,128)(2,1)} %collective-permute-done.acts_ref.code_ref, bf16[129,64,256]{2,1,0:T(8,128)(2,1)} %collective-permute-done.acts_ref.code_ref, bf16[512,128]{1,0:T(8,128)(2,1)} %get-tuple-element.148.w_ref, ...), custom_call_target="tpu_custom_call" | custom-call | flops 15000 | bytes 1 | tf_op jit(solution)/shard_map/project/pallas_call | solution.py:289
  338.9 10.6 %triangle.6 = (f32[128,64,128]{2,1,0:T(8,128)}, bf16[128,64,128]{2,1,0:T(8,128)(2,1)}) custom-call(s32[3]{0:T(128)} %pad_add_fusion.ids, bf16[128,64,256]{2,1,0:T(8,128)(2,1)} %get-tuple-element.152.a0.refs_8_, bf16[128,64,256]{2,1,0:T(8,128)(2,1)} %get-tuple-element.153.a1.refs_12_, bf16[128,64,256]{2,1,0:T(8,128)(2,1)} %get-tuple-element.160.b0.refs_10_, ...), custom_call_target="tpu_custom_call" | custom-call | flops 14000 | bytes 1 | tf_op jit(solution)/shard_map/triangle/pallas_call | solution.py:289
  350.0 31.9 %pair.5 = (bf16[128,64,128]{2,1,0:T(8,128)(2,1)}, f32[1352,128]{1,0:T(8,128)}, f32[7,128,128]{2,1,0:T(8,128)}) custom-call(s32[3]{0:T(128)} %pad_add_fusion.ids, f32[128,64,128]{2,1,0:T(8,128)} %get-tuple-element.186.x_keep, bf16[128,64,128]{2,1,0:T(8,128)(2,1)} %collective-permute-done.5.x_recv, bf16[129,256,128]{2,1,0:T(8,128)(2,1)} %turn.1.acts_ref.code_ref, ...), custom_call_target="tpu_custom_call" | custom-call | flops 35000 | bytes 1 | tf_op jit(solution)/shard_map/pair/pallas_call | solution.py:289
  384.5 32.1 %pair.6 = (bf16[128,64,128]{2,1,0:T(8,128)(2,1)}, f32[1352,128]{1,0:T(8,128)}, f32[7,128,128]{2,1,0:T(8,128)}) custom-call(s32[3]{0:T(128)} %pad_add_fusion.ids, f32[128,64,128]{2,1,0:T(8,128)} %get-tuple-element.191.x_keep, bf16[128,64,128]{2,1,0:T(8,128)(2,1)} %copy-done.5, bf16[129,256,128]{2,1,0:T(8,128)(2,1)} %turn.1.acts_ref.code_ref, ...), custom_call_target="tpu_custom_call" | custom-call | flops 35000 | bytes 1 | tf_op jit(solution)/shard_map/pair/pallas_call | solution.py:289
  417.2 12.5 %project.12 = (bf16[128,64,256]{2,1,0:T(8,128)(2,1)}, bf16[128,64,256]{2,1,0:T(8,128)(2,1)}) custom-call(bf16[129,64,256]{2,1,0:T(8,128)(2,1)} %collective-permute-done.3.acts_ref.code_ref, bf16[129,64,256]{2,1,0:T(8,128)(2,1)} %collective-permute-done.3.acts_ref.code_ref, bf16[512,128]{1,0:T(8,128)(2,1)} %get-tuple-element.148.w_ref, ...), custom_call_target="tpu_custom_call" | custom-call | flops 15000 | bytes 1 | tf_op jit(solution)/shard_map/project/pallas_call | solution.py:289
  429.7 12.5 %project.13 = (bf16[128,64,256]{2,1,0:T(8,128)(2,1)}, bf16[128,64,256]{2,1,0:T(8,128)(2,1)}) custom-call(bf16[129,64,256]{2,1,0:T(8,128)(2,1)} %collective-permute-done.2.acts_ref.code_ref, bf16[129,64,256]{2,1,0:T(8,128)(2,1)} %collective-permute-done.2.acts_ref.code_ref, bf16[512,128]{1,0:T(8,128)(2,1)} %get-tuple-element.148.w_ref, ...), custom_call_target="tpu_custom_call" | custom-call | flops 15000 | bytes 1 | tf_op jit(solution)/shard_map/project/pallas_call | solution.py:289
  442.2 10.3 %triangle.7 = (f32[128,64,128]{2,1,0:T(8,128)}, bf16[128,64,128]{2,1,0:T(8,128)(2,1)}) custom-call(s32[3]{0:T(128)} %pad_add_fusion.ids, bf16[128,64,256]{2,1,0:T(8,128)(2,1)} %get-tuple-element.152.a0.refs_8_, bf16[128,64,256]{2,1,0:T(8,128)(2,1)} %get-tuple-element.153.a1.refs_12_, bf16[128,64,256]{2,1,0:T(8,128)(2,1)} %get-tuple-element.196.b0.refs_11_, ...), custom_call_target="tpu_custom_call" | custom-call | flops 14000 | bytes 1 | tf_op jit(solution)/shard_map/triangle/pallas_call | solution.py:289
  453.6 10.8 %collective-permute-done.8.refs_2_ = bf16[128,64,128]{2,1,0:T(8,128)(2,1)} collective-permute-done((bf16[128,64,128]{2,1,0:T(8,128)(2,1)}, bf16[128,64,128]{2,1,0:T(8,128)(2,1)}, u32[]{:S(2)}, u32[]{:S(2)}) %collective-permute-start.8) | collective-permute-done | bytes 2097184 | tf_op jit(solution)/shard_map/ppermute | solution.py:1143
  464.3 32.4 %pair.7 = (bf16[128,64,128]{2,1,0:T(8,128)(2,1)}, f32[1352,128]{1,0:T(8,128)}, f32[7,128,128]{2,1,0:T(8,128)}) custom-call(s32[3]{0:T(128)} %pad_add_fusion.ids, f32[128,64,128]{2,1,0:T(8,128)} %get-tuple-element.202.x_keep, bf16[128,64,128]{2,1,0:T(8,128)(2,1)} %collective-permute-done.9.x_recv, bf16[129,256,128]{2,1,0:T(8,128)(2,1)} %turn.1.acts_ref.code_ref, ...), custom_call_target="tpu_custom_call" | custom-call | flops 35000 | bytes 1 | tf_op jit(solution)/shard_map/pair/pallas_call | solution.py:289
  501.5 20.5 %left_back.1 = (bf16[128,64,256]{2,1,0:T(8,128)(2,1)}, bf16[128,64,256]{2,1,0:T(8,128)(2,1)}) custom-call(s32[3]{0:T(128)} %pad_add_fusion.ids, bf16[128,64,128]{2,1,0:T(8,128)(2,1)} %get-tuple-element.173.refs_0_, bf16[128,64,128]{2,1,0:T(8,128)(2,1)} %get-tuple-element.189.refs_1_, bf16[128,64,128]{2,1,0:T(8,128)(2,1)} %get-tuple-element.194.refs_2_, ...), custom_call_target="tpu_custom_call" | custom-call | flops 25000 | bytes 1 | tf_op jit(solution)/shard_map/left_back/pallas_call | solution.py:289
  522.1 13.0 %input_back.4 = (f32[272,128]{1,0:T(8,128)}, f32[256,128]{1,0:T(8,128)}, f32[256,128]{1,0:T(8,128)}) custom-call(bf16[129,64,256]{2,1,0:T(8,128)(2,1)} %get-tuple-element.156.first.acts_ref.code_ref, bf16[129,64,256]{2,1,0:T(8,128)(2,1)} %get-tuple-element.156.first.acts_ref.code_ref, bf16[512,128]{1,0:T(8,128)(2,1)} %get-tuple-element.148.w_ref, ...), custom_call_target="tpu_custom_call" | custom-call | flops 16000 | bytes 1 | tf_op jit(solution)/shard_map/input_back/pallas_call | solution.py:289
  535.0 11.2 %collective-permute-done.16.refs_3_ = bf16[128,64,128]{2,1,0:T(8,128)(2,1)} collective-permute-done((bf16[128,64,128]{2,1,0:T(8,128)(2,1)}, bf16[128,64,128]{2,1,0:T(8,128)(2,1)}, u32[]{:S(2)}, u32[]{:S(2)}) %collective-permute-start.16) | collective-permute-done | bytes 2097184 | tf_op jit(solution)/shard_map/ppermute | solution.py:1146
  548.9 13.6 %input_back.5 = (f32[272,128]{1,0:T(8,128)}, f32[256,128]{1,0:T(8,128)}, f32[256,128]{1,0:T(8,128)}) custom-call(bf16[129,64,256]{2,1,0:T(8,128)(2,1)} %get-tuple-element.144.acts_ref.code_ref.second, bf16[129,64,256]{2,1,0:T(8,128)(2,1)} %get-tuple-element.144.acts_ref.code_ref.second, bf16[512,128]{1,0:T(8,128)(2,1)} %get-tuple-element.148.w_ref, ...), custom_call_target="tpu_custom_call" | custom-call | flops 16000 | bytes 1 | tf_op jit(solution)/shard_map/input_back/pallas_call | solution.py:289
  563.8 20.3 %right_back.1 = (bf16[128,64,256]{2,1,0:T(8,128)(2,1)}, bf16[128,64,256]{2,1,0:T(8,128)(2,1)}) custom-call(s32[3]{0:T(128)} %pad_add_fusion.ids, bf16[128,64,128]{2,1,0:T(8,128)(2,1)} %get-tuple-element.173.refs_0_, bf16[128,64,128]{2,1,0:T(8,128)(2,1)} %collective-permute-done.7.refs_1_, bf16[128,64,128]{2,1,0:T(8,128)(2,1)} %collective-permute-done.8.refs_2_, ...), custom_call_target="tpu_custom_call" | custom-call | flops 25000 | bytes 1 | tf_op jit(solution)/shard_map/right_back/pallas_call | solution.py:289
  584.1 13.0 %input_back.6 = (f32[272,128]{1,0:T(8,128)}, f32[256,128]{1,0:T(8,128)}, f32[256,128]{1,0:T(8,128)}) custom-call(bf16[129,64,256]{2,1,0:T(8,128)(2,1)} %get-tuple-element.156.first.acts_ref.code_ref, bf16[129,64,256]{2,1,0:T(8,128)(2,1)} %get-tuple-element.156.first.acts_ref.code_ref, bf16[512,128]{1,0:T(8,128)(2,1)} %get-tuple-element.148.w_ref, ...), custom_call_target="tpu_custom_call" | custom-call | flops 16000 | bytes 1 | tf_op jit(solution)/shard_map/input_back/pallas_call | solution.py:289
  597.0 13.3 %input_back.7 = (f32[272,128]{1,0:T(8,128)}, f32[256,128]{1,0:T(8,128)}, f32[256,128]{1,0:T(8,128)}) custom-call(bf16[129,64,256]{2,1,0:T(8,128)(2,1)} %get-tuple-element.144.acts_ref.code_ref.second, bf16[129,64,256]{2,1,0:T(8,128)(2,1)} %get-tuple-element.144.acts_ref.code_ref.second, bf16[512,128]{1,0:T(8,128)(2,1)} %get-tuple-element.148.w_ref, ...), custom_call_target="tpu_custom_call" | custom-call | flops 16000 | bytes 1 | tf_op jit(solution)/shard_map/input_back/pallas_call | solution.py:289
  610.4 29.3 %reduce_all.1.early_ref = f32[2048,128]{1,0:T(8,128)} custom-call(f32[1352,128]{1,0:T(8,128)} %scatter.4.pair_ref, f32[272,128]{1,0:T(8,128)} %get-tuple-element.213.left_ref, f32[272,128]{1,0:T(8,128)} %get-tuple-element.227.right_ref), custom_call_target="tpu_custom_call" | custom-call | tf_op jit(solution)/shard_map/reduce_all/pallas_call | solution.py:821
  (62 shorter events, 48.3 us)
Async XLA Ops:
  206.3 96.7 %collective-permute-start = (bf16[129,64,256]{2,1,0:T(8,128)(2,1)}, bf16[129,64,256]{2,1,0:T(8,128)(2,1)}, u32[]{:S(2)}, u32[]{:S(2)}) collective-permute-start(bf16[129,64,256]{2,1,0:T(8,128)(2,1)} %get-tuple-element.144.acts_ref.code_ref.second), channel_id=1, source_target_pairs={{0,16},{8,24},{16,0},{24,8},{1,17},{9,25},{17,1},{25,9},{2,18},{10... | collective-permute-start | bytes 12681224 | tf_op jit(solution)/shard_map/ppermute | solution.py:1143
  206.3 97.4 %collective-permute-start.4 = (bf16[129,64,256]{2,1,0:T(8,128)(2,1)}, bf16[129,64,256]{2,1,0:T(8,128)(2,1)}, u32[]{:S(2)}, u32[]{:S(2)}) collective-permute-start(bf16[129,64,256]{2,1,0:T(8,128)(2,1)} %get-tuple-element.144.acts_ref.code_ref.second), channel_id=1, source_target_pairs={{0,8},{8,0},{16,24},{24,16},{1,9},{9,1},{17,25},{25,17},{2,10},{10... | collective-permute-start | bytes 12681224 | tf_op jit(solution)/shard_map/ppermute | solution.py:1140
  233.7 34.0 %collective-permute-start.1 = (bf16[128,64,128]{2,1,0:T(8,128)(2,1)}, bf16[128,64,128]{2,1,0:T(8,128)(2,1)S(1)}, u32[]{:S(2)}, u32[]{:S(2)}) collective-permute-start(bf16[128,64,128]{2,1,0:T(8,128)(2,1)} %get-tuple-element.155), channel_id=1, source_target_pairs={{0,1},{1,0},{2,3},{3,2},{4,5},{5,4},{6,7},{7,6},{8,9},{9,8},{10,11... | collective-permute-start | bytes 6291464 | tf_op jit(solution)/shard_map/ppermute | solution.py:1149
  254.9 46.0 %slice-start = ((s8[4227072]{0:T(1024)(128)(4,1)}), s8[4194304]{0:T(1024)(128)(4,1)S(1)}, s32[]{:S(2)}) async-start(s8[4227072]{0:T(1024)(128)(4,1)} %bitcast.22), calls=%async_computation | async-start | bytes 8388608
  269.0 31.9 %slice-start.1 = ((s8[4227072]{0:T(1024)(128)(4,1)}), s8[32768]{0:T(1024)(128)(4,1)S(1)}, s32[]{:S(2)}) async-start(s8[4227072]{0:T(1024)(128)(4,1)} %bitcast.22), calls=%async_computation.1 | async-start | bytes 65536
  301.0 116.3 %collective-permute-start.3 = (bf16[129,64,256]{2,1,0:T(8,128)(2,1)S(1)}, bf16[129,64,256]{2,1,0:T(8,128)(2,1)}, u32[]{:S(2)}, u32[]{:S(2)}) collective-permute-start(bf16[129,64,256]{2,1,0:T(8,128)(2,1)S(1)} %bitcast.23), channel_id=1, source_target_pairs={{0,16},{8,24},{16,0},{24,8},{1,17},{9,25},{17,1},{25,9},{2,18},{10... | collective-permute-start | bytes 12681224 | tf_op jit(solution)/shard_map/ppermute | solution.py:1143
  303.0 126.8 %collective-permute-start.2 = (bf16[129,64,256]{2,1,0:T(8,128)(2,1)}, bf16[129,64,256]{2,1,0:T(8,128)(2,1)}, u32[]{:S(2)}, u32[]{:S(2)}) collective-permute-start(bf16[129,64,256]{2,1,0:T(8,128)(2,1)} %collective-permute-done.acts_ref.code_ref), channel_id=1, source_target_pairs={{0,8},{8,0},{16,24},{24,16},{1,9},{9,1},{17,25},{25,17},{2,10},{10... | collective-permute-start | bytes 12681224 | tf_op jit(solution)/shard_map/ppermute | solution.py:1140
  326.3 23.6 %collective-permute-start.5 = (bf16[128,64,128]{2,1,0:T(8,128)(2,1)}, bf16[128,64,128]{2,1,0:T(8,128)(2,1)}, u32[]{:S(2)}, u32[]{:S(2)}) collective-permute-start(bf16[128,64,128]{2,1,0:T(8,128)(2,1)} %get-tuple-element.180), channel_id=1, source_target_pairs={{0,1},{1,0},{2,3},{3,2},{4,5},{5,4},{6,7},{7,6},{8,9},{9,8},{10,11... | collective-permute-start | bytes 6291464 | tf_op jit(solution)/shard_map/ppermute | solution.py:1149
  349.5 33.7 %collective-permute-start.6 = (bf16[128,64,128]{2,1,0:T(8,128)(2,1)}, bf16[128,64,128]{2,1,0:T(8,128)(2,1)S(1)}, u32[]{:S(2)}, u32[]{:S(2)}) collective-permute-start(bf16[128,64,128]{2,1,0:T(8,128)(2,1)} %get-tuple-element.184), channel_id=1, source_target_pairs={{0,1},{1,0},{2,3},{3,2},{4,5},{5,4},{6,7},{7,6},{8,9},{9,8},{10,11... | collective-permute-start | bytes 6291464 | tf_op jit(solution)/shard_map/ppermute | solution.py:1149
  381.9 70.6 %collective-permute-start.7 = (bf16[128,64,128]{2,1,0:T(8,128)(2,1)}, bf16[128,64,128]{2,1,0:T(8,128)(2,1)}, u32[]{:S(2)}, u32[]{:S(2)}) collective-permute-start(bf16[128,64,128]{2,1,0:T(8,128)(2,1)} %get-tuple-element.189.refs_1_), channel_id=1, source_target_pairs={{0,8},{8,0},{16,24},{24,16},{1,9},{9,1},{17,25},{25,17},{2,10},{10... | collective-permute-start | bytes 6291464 | tf_op jit(solution)/shard_map/ppermute | solution.py:1140
  416.7 47.7 %collective-permute-start.8 = (bf16[128,64,128]{2,1,0:T(8,128)(2,1)}, bf16[128,64,128]{2,1,0:T(8,128)(2,1)}, u32[]{:S(2)}, u32[]{:S(2)}) collective-permute-start(bf16[128,64,128]{2,1,0:T(8,128)(2,1)} %get-tuple-element.194.refs_2_), channel_id=1, source_target_pairs={{0,16},{8,24},{16,0},{24,8},{1,17},{9,25},{17,1},{25,9},{2,18},{10... | collective-permute-start | bytes 6291464 | tf_op jit(solution)/shard_map/ppermute | solution.py:1143
  442.2 10.8 %copy-start = (bf16[128,64,128]{2,1,0:T(8,128)(2,1)S(1)}, bf16[128,64,128]{2,1,0:T(8,128)(2,1)}, u32[]{:S(2)}) copy-start(bf16[128,64,128]{2,1,0:T(8,128)(2,1)} %get-tuple-element.173.refs_0_) | copy-start | bytes 6291460
  452.5 11.8 %collective-permute-start.9 = (bf16[128,64,128]{2,1,0:T(8,128)(2,1)}, bf16[128,64,128]{2,1,0:T(8,128)(2,1)}, u32[]{:S(2)}, u32[]{:S(2)}) collective-permute-start(bf16[128,64,128]{2,1,0:T(8,128)(2,1)} %get-tuple-element.200), channel_id=1, source_target_pairs={{0,1},{1,0},{2,3},{3,2},{4,5},{5,4},{6,7},{7,6},{8,9},{9,8},{10,11... | collective-permute-start | bytes 6291464 | tf_op jit(solution)/shard_map/ppermute | solution.py:1149
  452.6 44.8 %collective-permute-start.10 = (bf16[128,64,128]{2,1,0:T(8,128)(2,1)}, bf16[128,64,128]{2,1,0:T(8,128)(2,1)S(1)}, u32[]{:S(2)}, u32[]{:S(2)}) collective-permute-start(bf16[128,64,128]{2,1,0:T(8,128)(2,1)} %collective-permute-done.7.refs_1_), channel_id=1, source_target_pairs={{0,1},{1,0},{2,3},{3,2},{4,5},{5,4},{6,7},{7,6},{8,9},{9,8},{10,11... | collective-permute-start | bytes 6291464 | tf_op jit(solution)/shard_map/ppermute | solution.py:1149
  453.1 44.8 %collective-permute-start.11 = (bf16[128,64,128]{2,1,0:T(8,128)(2,1)S(1)}, bf16[128,64,128]{2,1,0:T(8,128)(2,1)S(1)}, u32[]{:S(2)}, u32[]{:S(2)}) collective-permute-start(bf16[128,64,128]{2,1,0:T(8,128)(2,1)S(1)} %copy-done), channel_id=1, source_target_pairs={{0,1},{1,0},{2,3},{3,2},{4,5},{5,4},{6,7},{7,6},{8,9},{9,8},{10,11... | collective-permute-start | bytes 6291464 | tf_op jit(solution)/shard_map/ppermute | solution.py:1149
  453.1 44.7 %collective-permute-start.12 = (bf16[128,64,128]{2,1,0:T(8,128)(2,1)}, bf16[128,64,128]{2,1,0:T(8,128)(2,1)}, u32[]{:S(2)}, u32[]{:S(2)}) collective-permute-start(bf16[128,64,128]{2,1,0:T(8,128)(2,1)} %get-tuple-element.189.refs_1_), channel_id=1, source_target_pairs={{0,1},{1,0},{2,3},{3,2},{4,5},{5,4},{6,7},{7,6},{8,9},{9,8},{10,11... | collective-permute-start | bytes 6291464 | tf_op jit(solution)/shard_map/ppermute | solution.py:1149
  464.3 33.6 %collective-permute-start.13 = (bf16[128,64,128]{2,1,0:T(8,128)(2,1)}, bf16[128,64,128]{2,1,0:T(8,128)(2,1)}, u32[]{:S(2)}, u32[]{:S(2)}) collective-permute-start(bf16[128,64,128]{2,1,0:T(8,128)(2,1)} %get-tuple-element.194.refs_2_), channel_id=1, source_target_pairs={{0,1},{1,0},{2,3},{3,2},{4,5},{5,4},{6,7},{7,6},{8,9},{9,8},{10,11... | collective-permute-start | bytes 6291464 | tf_op jit(solution)/shard_map/ppermute | solution.py:1149
  496.8 4.7 collective-permute-start.14
  497.4 24.7 %copy-start.2 = (bf16[128,64,128]{2,1,0:T(8,128)(2,1)}, bf16[128,64,128]{2,1,0:T(8,128)(2,1)S(1)}, u32[]{:S(2)}) copy-start(bf16[128,64,128]{2,1,0:T(8,128)(2,1)S(1)} %collective-permute-done.10.refs_5_) | copy-start | bytes 6291460
  497.4 48.8 %collective-permute-start.16 = (bf16[128,64,128]{2,1,0:T(8,128)(2,1)}, bf16[128,64,128]{2,1,0:T(8,128)(2,1)}, u32[]{:S(2)}, u32[]{:S(2)}) collective-permute-start(bf16[128,64,128]{2,1,0:T(8,128)(2,1)} %get-tuple-element.206.refs_3_), channel_id=1, source_target_pairs={{0,24},{8,16},{16,8},{24,0},{1,25},{9,17},{17,9},{25,1},{2,26},{10... | collective-permute-start | bytes 6291464 | tf_op jit(solution)/shard_map/ppermute | solution.py:1146
  497.9 3.6 copy-start.1
  497.9 64.6 %collective-permute-start.15 = (bf16[128,64,128]{2,1,0:T(8,128)(2,1)}, bf16[128,64,128]{2,1,0:T(8,128)(2,1)}, u32[]{:S(2)}, u32[]{:S(2)}) collective-permute-start(bf16[128,64,128]{2,1,0:T(8,128)(2,1)} %collective-permute-done.8.refs_2_), channel_id=1, source_target_pairs={{0,1},{1,0},{2,3},{3,2},{4,5},{5,4},{6,7},{7,6},{8,9},{9,8},{10,11... | collective-permute-start | bytes 6291464 | tf_op jit(solution)/shard_map/ppermute | solution.py:1149
  522.0 24.2 %copy-start.6 = (s32[1,512]{1,0:T(1,128)S(1)}, s32[1,512]{1,0:T(1,128)}, u32[]{:S(2)}) copy-start(s32[1,512]{1,0:T(1,128)} %param.27) | copy-start | bytes 6148
  546.2 16.2 %collective-permute-start.17 = (bf16[128,64,128]{2,1,0:T(8,128)(2,1)}, bf16[128,64,128]{2,1,0:T(8,128)(2,1)S(1)}, u32[]{:S(2)}, u32[]{:S(2)}) collective-permute-start(bf16[128,64,128]{2,1,0:T(8,128)(2,1)} %collective-permute-done.16.refs_3_), channel_id=1, source_target_pairs={{0,1},{1,0},{2,3},{3,2},{4,5},{5,4},{6,7},{7,6},{8,9},{9,8},{10,11... | collective-permute-start | bytes 6291464 | tf_op jit(solution)/shard_map/ppermute | solution.py:1149
  (3 other events, 3.9 us)

commit v6 on v5

--- a/solution.py
+++ b/solution.py
@@ -358,6 +358,41 @@
     gather_rows(b_s, b_ref)
 
 
+def project_two_kernel(acts0, code0, acts1, code1, w_ref, ln_ref, a0, b0, a1, b1, *scratch):
+    steps = pl.num_programs(0) // 2
+
+    @pl.when(pl.program_id(0) < steps)
+    def _():
+        project_kernel(acts0, code0, w_ref, ln_ref, a0, b0, *scratch)
+
+    @pl.when(pl.program_id(0) >= steps)
+    def _():
+        project_kernel(acts1, code1, w_ref, ln_ref, a1, b1, *scratch)
+
+
+def project_two(first, second, w_proj, ln_wide):
+    chans, rows, lanes = first.shape[0] - 1, first.shape[1], first.shape[2]
+    block = (chans, ROWS, lanes)
+    steps = rows // ROWS
+    spots = [lambda i: jnp.minimum(i, steps - 1), lambda i: jnp.maximum(i - steps, 0)]
+    staged = pltpu.VMEM((ROWS, chans, lanes), BF16)
+    ins, outs = [], []
+    for acts, spot in zip((first, second), spots):
+        ins.append((acts, block, lambda i, *_, spot=spot: (0, spot(i), 0)))
+        ins.append((acts, (1, ROWS, lanes), lambda i, *_, spot=spot: (chans, spot(i), 0)))
+        outs += [((chans, rows, lanes), BF16, block, lambda i, *_, spot=spot: (0, spot(i), 0))] * 2
+    return call(
+        project_two_kernel,
+        (2 * steps,),
+        [],
+        ins + [(w_proj, w_proj.shape, fixed(0, 0)), (ln_wide, ln_wide.shape, fixed(0, 0, 0))],
+        outs,
+        [staged, staged, staged, pltpu.VMEM((ROWS, lanes), F32)],
+        30 * MICRO,
+        "project_two",
+    )
+
+
 def fixed(*zeros):
     return lambda i, *_: zeros
 
@@ -617,11 +652,11 @@
 def turn(first, second):
     chans, half, lanes = first.shape
     lead = lambda i, *_: (i, 0, 0)
-    count = next(n for n in (43, 16, 8, 4, 2, 1) if chans % n == 0)
+    count = (chans + 1) // 2
     block = (count, half, lanes)
     return call(
         turn_kernel,
-        (chans // count,),
+        (2,),
         [],
         [(first, block, lead), (second, block, lead)],
         [((chans, lanes, 2 * half), BF16, (count, lanes, 2 * half), lead)],
@@ -675,12 +710,11 @@
     return normed_grad * gain + total * shift
 
 
-def input_back_kernel(count, first_call, last_call, acts_ref, code_ref, w_ref, ln_ref, *rest):
-    grads, rest = rest[:count], rest[count:]
+def input_back_kernel(count, first_call, last_call, w_ref, ln_ref, *rest):
+    halves, rest = [rest[3 * n : 3 * n + 3] for n in range(count)], rest[3 * count :]
     prior = () if first_call else rest[:3]
     out_ref, g_ref, sum_ref, acts_s, grad_s, code_s = rest[len(prior) :]
-    width = grads[0].shape[0]
-    chans = acts_ref.shape[0]
+    width = halves[0][2].shape[0]
 
     @pl.when(pl.program_id(0) == 0)
     def _():
@@ -693,9 +727,14 @@
             g_ref[...] = prior[1][...]
             sum_ref[...] = prior[2][...]
 
-    code_s[...] = code_ref[0].astype(F32)
-    spread_rows(acts_s, acts_ref[...])
-    spread_rows(grad_s, grads[0][...])
+    steps = pl.num_programs(0) // count
+    for number, (acts_ref, code_ref, grad_ref) in enumerate(halves):
+
+        @pl.when(pl.program_id(0) // steps == number)
+        def _(acts_ref=acts_ref, code_ref=code_ref, grad_ref=grad_ref):
+            code_s[...] = code_ref[0].astype(F32)
+            spread_rows(acts_s, acts_ref[...])
+            spread_rows(grad_s, grad_ref[...])
 
     def some(step, carry):
         start = step * INPUT_GROUP
@@ -732,23 +771,27 @@
             out_ref[2 * width + 1 : 2 * width + 2] = shift
 
 
-def input_back(acts, part, w_proj, ln_wide, grads, prior, last_call):
-    chans, rows, lanes = acts.shape[0] - 1, acts.shape[1], acts.shape[2]
+def input_back(halves, part, w_proj, ln_wide, prior, last_call):
+    chans, rows, lanes = halves[0][1].shape
     block = (chans, ROWS, lanes)
-    mid = lambda i, *_: (0, i, 0)
+    steps = rows // ROWS
     depth = w_proj.shape[0] // 2
     shapes = [(SIDE_ROWS, chans), (depth, chans), (depth, 128)]
+    ins = []
+    for number, (acts, grad) in enumerate(halves):
+        spot = lambda i, number=number: jnp.clip(i - number * steps, 0, steps - 1)
+        mid = lambda i, *_, spot=spot: (0, spot(i), 0)
+        ins += [
+            (acts, block, mid),
+            (acts, (1, ROWS, lanes), lambda i, *_, spot=spot: (chans, spot(i), 0)),
+            (grad, block, mid),
+        ]
     return call(
-        functools.partial(input_back_kernel, len(grads), not prior, last_call),
-        (rows // ROWS,),
+        functools.partial(input_back_kernel, len(halves), not prior, last_call),
+        (len(halves) * steps,),
         [],
-        [
-            (acts, block, mid),
-            (acts, (1, ROWS, lanes), lambda i, *_: (chans, i, 0)),
-            (w_proj, (depth, chans), fixed(part, 0)),
-            (ln_wide, ln_wide.shape, fixed(0, 0, 0)),
-        ]
-        + [(v, block, mid) for v in grads]
+        [(w_proj, (depth, chans), fixed(part, 0)), (ln_wide, ln_wide.shape, fixed(0, 0, 0))]
+        + ins
         + [(v, v.shape, fixed(0, 0)) for v in prior],
         [(s, F32, s, fixed(0, 0)) for s in shapes],
         [
@@ -1177,6 +1220,11 @@
     done = values(0, 1)
 
     ids = jnp.stack([spot, crop, side]).astype(jnp.int32)
+    def values_two(one, two, *earlier):
+        results = project_two(after(acts[one], *earlier), acts[two], proj_w, ln_wide)
+        left[one], right[one], left[two], right[two] = results
+        return results[0]
+
     keeps, recvs, dx_own, dx_other, seen, seen_other = {}, {}, {}, {}, {}, {}
     sums = []
 
@@ -1198,8 +1246,7 @@
 
     done = forward(0, done)
     acts_kj = turn(after(acts[0, 0], done), acts[0, 1])
-    done = values(1, 0, acts_kj)
-    done = values(2, 0, done)
+    done = values_two((1, 0), (2, 0), acts_kj)
     done = middle(0, done)
     acts[1, 1], acts[2, 1] = after(acts[1, 1], done), after(acts[2, 1], done)
     acts[3, 0] = over_y(after(acts[1, 0], done))
@@ -1210,8 +1257,7 @@
     done = forward(2, done)
     done = middle(1, done)
     done = middle(2, done)
-    done = values(3, 0, done)
-    done = values(3, 1, done)
+    done = values_two((3, 0), (3, 1), done)
     done = forward(3, done)
     done = middle(3, done, seen[1], seen[2])
     d_left = left_back(
@@ -1222,9 +1268,9 @@
         [right[q, 1] for q in range(4)],
     )
     pair_sums = sums[0].at[LOSS_ROW - 1, 127].set(count * count / share_count)
-    left_sum, right_sum = [], []
+    left_sum = []
     for h in range(2):
-        left_sum = input_back(acts[0, h], 0, proj_w, ln_wide, [d_left[h]], left_sum, h == 1)
+        left_sum = input_back([(acts[0, h], d_left[h])], 0, proj_w, ln_wide, left_sum, h == 1)
         if h == 0:
             seen_other[3] = over_core(after(seen[3], left_sum[0]))
     d_right = right_back(
@@ -1234,8 +1280,7 @@
         [left[q, 0] for q in range(4)],
         [left[q, 1] for q in range(4)],
     )
-    for h in range(2):
-        right_sum = input_back(acts[0, h], 1, proj_w, ln_wide, [d_right[h]], right_sum, h == 1)
+    right_sum = input_back([(acts[0, h], d_right[h]) for h in range(2)], 1, proj_w, ln_wide, [], True)
     params = (w_in, w_out, w_t1, w_t2, w_dist, norm_params, dist_bias)
     return update(reduce_all(pair_sums, left_sum[0], right_sum[0]), params, firsts, seconds)
 

time: 650 us -> 649 us (level)
    pallas_call x22 -> x19, Pallas kernels: 360 us -> 353 us  [call(): pl.pallas_call(kernel, grid_spec=pltpu.PrefetchScalarGridSpec(num_scalar_...]
  transfers between devices with their start and end apart: 18 -> 18, of which waited for: 3 -> 3; matrix products, arithmetic and copies ran while one was open for 0% -> 0% of each run, Pallas kernels for 49% -> 48%
where the time goes in v6:
time: 649 us; the launch traced here: 644 us
  Pallas kernels  590 us (91%)
  waiting for transfers between devices  26.3 us (4%)
  starting transfers between devices  15.8 us (2%)
  local copies, waits for them, and re-layouts  6.73 us (1%)
    pallas_call x19, Pallas kernels, call(): pl.pallas_call(kernel, grid_spec=pltpu.PrefetchScalarGridSpec(num_scalar_...  353 us
    pallas_call x1, Pallas kernels, spread(): pl.pallas_call(spread_kernel, in_specs=[anywhere] + [whole] * 8, out_spec...  203 us
    pallas_call x1, Pallas kernels, reduce_all(): pl.pallas_call(reduce_kernel, out_shape=jax.ShapeDtypeStruct((ALL_ROWS, l...  30.3 us
  transfers between devices with their start and end apart: 18, of which 3 were waited for; matrix products, arithmetic and copies ran while one was open for 0% of the time, Pallas kernels for 48%

profile of v6, /device:TPU:0, one launch (start us, length us, event | category | flops | bytes accessed | tf_op | source)
XLA Modules:
  0.0 644.2 jit_solution(14076603428700331041)
XLA Ops:
  3.6 202.6 %spread.1 = (bf16[129,64,256]{2,1,0:T(8,128)(2,1)}, bf16[129,64,256]{2,1,0:T(8,128)(2,1)}, bf16[129,64,256]{2,1,0:T(8,128)(2,1)}, bf16[129,64,256]{2,1,0:T(8,128...) custom-call(bf16[128,256,128]{2,1,0:T(8,128)(2,1)} %bitcast.24, ...), custom_call_target="tpu_custom_call" | custom-call | tf_op jit(solution)/shard_map/spread/pallas_call | solution.py:1079
  210.5 12.4 %project.3 = (bf16[128,64,256]{2,1,0:T(8,128)(2,1)}, bf16[128,64,256]{2,1,0:T(8,128)(2,1)}) custom-call(bf16[129,64,256]{2,1,0:T(8,128)(2,1)} %get-tuple-element.141.acts_ref.code_ref.second.rest_0_.rest_1_.rest_3_.rest_4_, bf16[129,64,256]{2,1,0:T(8,128)(2,1)} %get-tuple-element.141.acts_ref.code_ref.second.rest_0_.rest_1_.rest_3_.rest_4_, ...), custom_call_target="tpu_custom_call" | custom-call | flops 15000 | bytes 1 | tf_op jit(solution)/shard_map/project/pallas_call | solution.py:289
  223.5 10.1 %triangle.4 = (f32[128,64,128]{2,1,0:T(8,128)}, bf16[128,64,128]{2,1,0:T(8,128)(2,1)}) custom-call(s32[3]{0:T(128)} %pad_add_fusion.ids, bf16[128,64,256]{2,1,0:T(8,128)(2,1)} %get-tuple-element.146.a0.refs_8_, bf16[128,64,256]{2,1,0:T(8,128)(2,1)} %get-tuple-element.147.a1.refs_12_, bf16[128,64,256]{2,1,0:T(8,128)(2,1)} %get-tuple-element.148.b0.refs_8_, ...), custom_call_target="tpu_custom_call" | custom-call | flops 14000 | bytes 1 | tf_op jit(solution)/shard_map/triangle/pallas_call | solution.py:289
  233.6 6.7 %turn.1.acts_ref.code_ref = bf16[129,256,128]{2,1,0:T(8,128)(2,1)} custom-call(bf16[129,64,256]{2,1,0:T(8,128)(2,1)} %get-tuple-element.150.first.rest_0_.rest_1_, bf16[129,64,256]{2,1,0:T(8,128)(2,1)} %get-tuple-element.141.acts_ref.code_ref.second.rest_0_.rest_1_.rest_3_.rest_4_), custom_call_target="tpu_custom_call" | custom-call | flops 12000 | bytes 1 | tf_op jit(solution)/shard_map/turn/pallas_call | solution.py:289
  240.4 23.9 %project_two.2 = (bf16[128,64,256]{2,1,0:T(8,128)(2,1)}, bf16[128,64,256]{2,1,0:T(8,128)(2,1)}, bf16[128,64,256]{2,1,0:T(8,128)(2,1)}, bf16[128,64,256]{2,1,0:T(8,128)(2,1)}) custom-call(bf16[129,64,256]{2,1,0:T(8,128)(2,1)} %get-tuple-element.167.acts0.code0, bf16[129,64,256]{2,1,0:T(8,128)(2,1)} %get-tuple-element.167.acts0.code0, ...), custom_call_target="tpu_custom_call" | custom-call | flops 30000 | bytes 1 | tf_op jit(solution)/shard_map/project_two/pallas_call | solution.py:289
  265.6 31.9 %pair.4 = (bf16[128,64,128]{2,1,0:T(8,128)(2,1)}, f32[1352,128]{1,0:T(8,128)}, f32[7,128,128]{2,1,0:T(8,128)}) custom-call(s32[3]{0:T(128)} %pad_add_fusion.ids, f32[128,64,128]{2,1,0:T(8,128)} %get-tuple-element.155.x_keep, bf16[128,64,128]{2,1,0:T(8,128)(2,1)} %copy-done.4, bf16[129,256,128]{2,1,0:T(8,128)(2,1)} %turn.1.acts_ref.code_ref, ...), custom_call_target="tpu_custom_call" | custom-call | flops 35000 | bytes 1 | tf_op jit(solution)/shard_map/pair/pallas_call | solution.py:289
  299.5 5.4 collective-permute-start.6
  304.9 12.5 %project.4 = (bf16[128,64,256]{2,1,0:T(8,128)(2,1)}, bf16[128,64,256]{2,1,0:T(8,128)(2,1)}) custom-call(bf16[129,64,256]{2,1,0:T(8,128)(2,1)} %collective-permute-done.3.acts_ref.code_ref, bf16[129,64,256]{2,1,0:T(8,128)(2,1)} %collective-permute-done.3.acts_ref.code_ref, bf16[512,128]{1,0:T(8,128)(2,1)} %get-tuple-element.142.w_ref, ...), custom_call_target="tpu_custom_call" | custom-call | flops 15000 | bytes 1 | tf_op jit(solution)/shard_map/project/pallas_call | solution.py:289
  317.4 10.1 %triangle.5 = (f32[128,64,128]{2,1,0:T(8,128)}, bf16[128,64,128]{2,1,0:T(8,128)(2,1)}) custom-call(s32[3]{0:T(128)} %pad_add_fusion.ids, bf16[128,64,256]{2,1,0:T(8,128)(2,1)} %get-tuple-element.146.a0.refs_8_, bf16[128,64,256]{2,1,0:T(8,128)(2,1)} %get-tuple-element.147.a1.refs_12_, bf16[128,64,256]{2,1,0:T(8,128)(2,1)} %get-tuple-element.173.b0.refs_9_, ...), custom_call_target="tpu_custom_call" | custom-call | flops 14000 | bytes 1 | tf_op jit(solution)/shard_map/triangle/pallas_call | solution.py:289
  327.5 12.5 %project.5 = (bf16[128,64,256]{2,1,0:T(8,128)(2,1)}, bf16[128,64,256]{2,1,0:T(8,128)(2,1)}) custom-call(bf16[129,64,256]{2,1,0:T(8,128)(2,1)} %collective-permute-done.2.acts_ref.code_ref, bf16[129,64,256]{2,1,0:T(8,128)(2,1)} %collective-permute-done.2.acts_ref.code_ref, bf16[512,128]{1,0:T(8,128)(2,1)} %get-tuple-element.142.w_ref, ...), custom_call_target="tpu_custom_call" | custom-call | flops 15000 | bytes 1 | tf_op jit(solution)/shard_map/project/pallas_call | solution.py:289
  340.0 10.6 %triangle.6 = (f32[128,64,128]{2,1,0:T(8,128)}, bf16[128,64,128]{2,1,0:T(8,128)(2,1)}) custom-call(s32[3]{0:T(128)} %pad_add_fusion.ids, bf16[128,64,256]{2,1,0:T(8,128)(2,1)} %get-tuple-element.146.a0.refs_8_, bf16[128,64,256]{2,1,0:T(8,128)(2,1)} %get-tuple-element.147.a1.refs_12_, bf16[128,64,256]{2,1,0:T(8,128)(2,1)} %get-tuple-element.178.b0.refs_10_, ...), custom_call_target="tpu_custom_call" | custom-call | flops 14000 | bytes 1 | tf_op jit(solution)/shard_map/triangle/pallas_call | solution.py:289
  351.1 32.0 %pair.5 = (bf16[128,64,128]{2,1,0:T(8,128)(2,1)}, f32[1352,128]{1,0:T(8,128)}, f32[7,128,128]{2,1,0:T(8,128)}) custom-call(s32[3]{0:T(128)} %pad_add_fusion.ids, f32[128,64,128]{2,1,0:T(8,128)} %get-tuple-element.181.x_keep, bf16[128,64,128]{2,1,0:T(8,128)(2,1)} %collective-permute-done.4.x_recv, bf16[129,256,128]{2,1,0:T(8,128)(2,1)} %turn.1.acts_ref.code_ref, ...), custom_call_target="tpu_custom_call" | custom-call | flops 35000 | bytes 1 | tf_op jit(solution)/shard_map/pair/pallas_call | solution.py:289
  384.5 32.1 %pair.6 = (bf16[128,64,128]{2,1,0:T(8,128)(2,1)}, f32[1352,128]{1,0:T(8,128)}, f32[7,128,128]{2,1,0:T(8,128)}) custom-call(s32[3]{0:T(128)} %pad_add_fusion.ids, f32[128,64,128]{2,1,0:T(8,128)} %get-tuple-element.186.x_keep, bf16[128,64,128]{2,1,0:T(8,128)(2,1)} %copy-done.5, bf16[129,256,128]{2,1,0:T(8,128)(2,1)} %turn.1.acts_ref.code_ref, ...), custom_call_target="tpu_custom_call" | custom-call | flops 35000 | bytes 1 | tf_op jit(solution)/shard_map/pair/pallas_call | solution.py:289
  417.2 23.8 %project_two.3 = (bf16[128,64,256]{2,1,0:T(8,128)(2,1)}, bf16[128,64,256]{2,1,0:T(8,128)(2,1)}, bf16[128,64,256]{2,1,0:T(8,128)(2,1)}, bf16[128,64,256]{2,1,0:T(8,128)(2,1)}) custom-call(bf16[129,64,256]{2,1,0:T(8,128)(2,1)} %collective-permute-done.1.acts0.code0, bf16[129,64,256]{2,1,0:T(8,128)(2,1)} %collective-permute-done.1.acts0.code0, ...), custom_call_target="tpu_custom_call" | custom-call | flops 30000 | bytes 1 | tf_op jit(solution)/shard_map/project_two/pallas_call | solution.py:289
  441.0 10.3 %triangle.7 = (f32[128,64,128]{2,1,0:T(8,128)}, bf16[128,64,128]{2,1,0:T(8,128)(2,1)}) custom-call(s32[3]{0:T(128)} %pad_add_fusion.ids, bf16[128,64,256]{2,1,0:T(8,128)(2,1)} %get-tuple-element.146.a0.refs_8_, bf16[128,64,256]{2,1,0:T(8,128)(2,1)} %get-tuple-element.147.a1.refs_12_, bf16[128,64,256]{2,1,0:T(8,128)(2,1)} %get-tuple-element.193.b0.refs_11_, ...), custom_call_target="tpu_custom_call" | custom-call | flops 14000 | bytes 1 | tf_op jit(solution)/shard_map/triangle/pallas_call | solution.py:289
  452.3 12.3 %collective-permute-done.8.refs_2_ = bf16[128,64,128]{2,1,0:T(8,128)(2,1)} collective-permute-done((bf16[128,64,128]{2,1,0:T(8,128)(2,1)}, bf16[128,64,128]{2,1,0:T(8,128)(2,1)}, u32[]{:S(2)}, u32[]{:S(2)}) %collective-permute-start.8) | collective-permute-done | bytes 2097184 | tf_op jit(solution)/shard_map/ppermute | solution.py:1186
  464.6 32.4 %pair.7 = (bf16[128,64,128]{2,1,0:T(8,128)(2,1)}, f32[1352,128]{1,0:T(8,128)}, f32[7,128,128]{2,1,0:T(8,128)}) custom-call(s32[3]{0:T(128)} %pad_add_fusion.ids, f32[128,64,128]{2,1,0:T(8,128)} %get-tuple-element.197.x_keep, bf16[128,64,128]{2,1,0:T(8,128)(2,1)} %collective-permute-done.9.x_recv, bf16[129,256,128]{2,1,0:T(8,128)(2,1)} %turn.1.acts_ref.code_ref, ...), custom_call_target="tpu_custom_call" | custom-call | flops 35000 | bytes 1 | tf_op jit(solution)/shard_map/pair/pallas_call | solution.py:289
  501.7 20.5 %left_back.1 = (bf16[128,64,256]{2,1,0:T(8,128)(2,1)}, bf16[128,64,256]{2,1,0:T(8,128)(2,1)}) custom-call(s32[3]{0:T(128)} %pad_add_fusion.ids, bf16[128,64,128]{2,1,0:T(8,128)(2,1)} %get-tuple-element.166.refs_0_, bf16[128,64,128]{2,1,0:T(8,128)(2,1)} %get-tuple-element.184.refs_1_, bf16[128,64,128]{2,1,0:T(8,128)(2,1)} %get-tuple-element.189.refs_2_, ...), custom_call_target="tpu_custom_call" | custom-call | flops 25000 | bytes 1 | tf_op jit(solution)/shard_map/left_back/pallas_call | solution.py:289
  522.2 12.8 %input_back.3 = (f32[272,128]{1,0:T(8,128)}, f32[256,128]{1,0:T(8,128)}, f32[256,128]{1,0:T(8,128)}) custom-call(bf16[512,128]{1,0:T(8,128)(2,1)} %get-tuple-element.142.w_ref, f32[6,128,128]{2,1,0:T(8,128)} %get-tuple-element.143.ln_ref, bf16[129,64,256]{2,1,0:T(8,128)(2,1)} %get-tuple-element.150.first.rest_0_.rest_1_, ...), custom_call_target="tpu_custom_call" | custom-call | flops 16000 | bytes 1 | tf_op jit(solution)/shard_map/input_back/pallas_call | solution.py:289
  535.1 11.3 %collective-permute-done.16.refs_3_ = bf16[128,64,128]{2,1,0:T(8,128)(2,1)} collective-permute-done((bf16[128,64,128]{2,1,0:T(8,128)(2,1)}, bf16[128,64,128]{2,1,0:T(8,128)(2,1)}, u32[]{:S(2)}, u32[]{:S(2)}) %collective-permute-start.16) | collective-permute-done | bytes 2097184 | tf_op jit(solution)/shard_map/ppermute | solution.py:1189
  549.1 13.4 %input_back.4 = (f32[272,128]{1,0:T(8,128)}, f32[256,128]{1,0:T(8,128)}, f32[256,128]{1,0:T(8,128)}) custom-call(bf16[512,128]{1,0:T(8,128)(2,1)} %get-tuple-element.142.w_ref, f32[6,128,128]{2,1,0:T(8,128)} %get-tuple-element.143.ln_ref, bf16[129,64,256]{2,1,0:T(8,128)(2,1)} %get-tuple-element.141.acts_ref.code_ref.second.rest_0_.rest_1_.rest_3_.rest_4_, ...), custom_call_target="tpu_custom_call" | custom-call | flops 16000 | bytes 1 | tf_op jit(solution)/shard_map/input_back/pallas_call | solution.py:289
  563.9 20.3 %right_back.1 = (bf16[128,64,256]{2,1,0:T(8,128)(2,1)}, bf16[128,64,256]{2,1,0:T(8,128)(2,1)}) custom-call(s32[3]{0:T(128)} %pad_add_fusion.ids, bf16[128,64,128]{2,1,0:T(8,128)(2,1)} %get-tuple-element.166.refs_0_, bf16[128,64,128]{2,1,0:T(8,128)(2,1)} %collective-permute-done.7.refs_1_, bf16[128,64,128]{2,1,0:T(8,128)(2,1)} %collective-permute-done.8.refs_2_, ...), custom_call_target="tpu_custom_call" | custom-call | flops 25000 | bytes 1 | tf_op jit(solution)/shard_map/right_back/pallas_call | solution.py:289
  584.2 24.4 %input_back.5 = (f32[272,128]{1,0:T(8,128)}, f32[256,128]{1,0:T(8,128)}, f32[256,128]{1,0:T(8,128)}) custom-call(bf16[512,128]{1,0:T(8,128)(2,1)} %get-tuple-element.142.w_ref, f32[6,128,128]{2,1,0:T(8,128)} %get-tuple-element.143.ln_ref, bf16[129,64,256]{2,1,0:T(8,128)(2,1)} %get-tuple-element.150.first.rest_0_.rest_1_, ...), custom_call_target="tpu_custom_call" | custom-call | flops 16000 | bytes 1 | tf_op jit(solution)/shard_map/input_back/pallas_call | solution.py:289
  608.6 30.3 %reduce_all.1.early_ref = f32[2048,128]{1,0:T(8,128)} custom-call(f32[1352,128]{1,0:T(8,128)} %scatter.4.pair_ref, f32[272,128]{1,0:T(8,128)} %get-tuple-element.208.left_ref, f32[272,128]{1,0:T(8,128)} %get-tuple-element.217.right_ref), custom_call_target="tpu_custom_call" | custom-call | tf_op jit(solution)/shard_map/reduce_all/pallas_call | solution.py:864
  (59 shorter events, 27.5 us)
Async XLA Ops:
  206.2 93.3 %collective-permute-start.2 = (bf16[129,64,256]{2,1,0:T(8,128)(2,1)}, bf16[129,64,256]{2,1,0:T(8,128)(2,1)}, u32[]{:S(2)}, u32[]{:S(2)}) collective-permute-start(bf16[129,64,256]{2,1,0:T(8,128)(2,1)} %get-tuple-element.141.acts_ref.code_ref.second.rest_0_.rest_1_.rest_3_.rest_4_), channel_id=1, source_target_pairs={{0,16},{8,24},{16,0},{24,8},{1,17},{9,25},{17,1},{25,9},{2,18},{10... | collective-permute-start | bytes 12681224 | tf_op jit(solution)/shard_map/ppermute | solution.py:1186
  206.3 98.6 %collective-permute-start.3 = (bf16[129,64,256]{2,1,0:T(8,128)(2,1)}, bf16[129,64,256]{2,1,0:T(8,128)(2,1)}, u32[]{:S(2)}, u32[]{:S(2)}) collective-permute-start(bf16[129,64,256]{2,1,0:T(8,128)(2,1)} %get-tuple-element.141.acts_ref.code_ref.second.rest_0_.rest_1_.rest_3_.rest_4_), channel_id=1, source_target_pairs={{0,8},{8,0},{16,24},{24,16},{1,9},{9,1},{17,25},{25,17},{2,10},{10... | collective-permute-start | bytes 12681224 | tf_op jit(solution)/shard_map/ppermute | solution.py:1183
  233.6 30.6 %collective-permute-start = (bf16[128,64,128]{2,1,0:T(8,128)(2,1)}, bf16[128,64,128]{2,1,0:T(8,128)(2,1)S(1)}, u32[]{:S(2)}, u32[]{:S(2)}) collective-permute-start(bf16[128,64,128]{2,1,0:T(8,128)(2,1)} %get-tuple-element.149), channel_id=1, source_target_pairs={{0,1},{1,0},{2,3},{3,2},{4,5},{5,4},{6,7},{7,6},{8,9},{9,8},{10,11... | collective-permute-start | bytes 6291464 | tf_op jit(solution)/shard_map/ppermute | solution.py:1192
  240.4 57.1 %slice-start = ((s8[4227072]{0:T(1024)(128)(4,1)}), s8[4194304]{0:T(1024)(128)(4,1)S(1)}, s32[]{:S(2)}) async-start(s8[4227072]{0:T(1024)(128)(4,1)} %bitcast.22), calls=%async_computation | async-start | bytes 8388608
  265.6 31.9 %slice-start.1 = ((s8[4227072]{0:T(1024)(128)(4,1)}), s8[32768]{0:T(1024)(128)(4,1)S(1)}, s32[]{:S(2)}) async-start(s8[4227072]{0:T(1024)(128)(4,1)} %bitcast.22), calls=%async_computation.1 | async-start | bytes 65536
  297.5 119.6 %collective-permute-start.1 = (bf16[129,64,256]{2,1,0:T(8,128)(2,1)S(1)}, bf16[129,64,256]{2,1,0:T(8,128)(2,1)}, u32[]{:S(2)}, u32[]{:S(2)}) collective-permute-start(bf16[129,64,256]{2,1,0:T(8,128)(2,1)S(1)} %bitcast.23), channel_id=1, source_target_pairs={{0,16},{8,24},{16,0},{24,8},{1,17},{9,25},{17,1},{25,9},{2,18},{10... | collective-permute-start | bytes 12681224 | tf_op jit(solution)/shard_map/ppermute | solution.py:1186
  299.5 117.6 %collective-permute-start.6 = (bf16[129,64,256]{2,1,0:T(8,128)(2,1)}, bf16[129,64,256]{2,1,0:T(8,128)(2,1)}, u32[]{:S(2)}, u32[]{:S(2)}) collective-permute-start(bf16[129,64,256]{2,1,0:T(8,128)(2,1)} %collective-permute-done.2.acts_ref.code_ref), channel_id=1, source_target_pairs={{0,8},{8,0},{16,24},{24,16},{1,9},{9,1},{17,25},{25,17},{2,10},{10... | collective-permute-start | bytes 12681224 | tf_op jit(solution)/shard_map/ppermute | solution.py:1183
  327.5 23.6 %collective-permute-start.4 = (bf16[128,64,128]{2,1,0:T(8,128)(2,1)}, bf16[128,64,128]{2,1,0:T(8,128)(2,1)}, u32[]{:S(2)}, u32[]{:S(2)}) collective-permute-start(bf16[128,64,128]{2,1,0:T(8,128)(2,1)} %get-tuple-element.174), channel_id=1, source_target_pairs={{0,1},{1,0},{2,3},{3,2},{4,5},{5,4},{6,7},{7,6},{8,9},{9,8},{10,11... | collective-permute-start | bytes 6291464 | tf_op jit(solution)/shard_map/ppermute | solution.py:1192
  350.6 32.5 %collective-permute-start.5 = (bf16[128,64,128]{2,1,0:T(8,128)(2,1)}, bf16[128,64,128]{2,1,0:T(8,128)(2,1)S(1)}, u32[]{:S(2)}, u32[]{:S(2)}) collective-permute-start(bf16[128,64,128]{2,1,0:T(8,128)(2,1)} %get-tuple-element.179), channel_id=1, source_target_pairs={{0,1},{1,0},{2,3},{3,2},{4,5},{5,4},{6,7},{7,6},{8,9},{9,8},{10,11... | collective-permute-start | bytes 6291464 | tf_op jit(solution)/shard_map/ppermute | solution.py:1192
  383.1 68.2 %collective-permute-start.7 = (bf16[128,64,128]{2,1,0:T(8,128)(2,1)}, bf16[128,64,128]{2,1,0:T(8,128)(2,1)}, u32[]{:S(2)}, u32[]{:S(2)}) collective-permute-start(bf16[128,64,128]{2,1,0:T(8,128)(2,1)} %get-tuple-element.184.refs_1_), channel_id=1, source_target_pairs={{0,8},{8,0},{16,24},{24,16},{1,9},{9,1},{17,25},{25,17},{2,10},{10... | collective-permute-start | bytes 6291464 | tf_op jit(solution)/shard_map/ppermute | solution.py:1183
  416.6 47.9 %collective-permute-start.8 = (bf16[128,64,128]{2,1,0:T(8,128)(2,1)}, bf16[128,64,128]{2,1,0:T(8,128)(2,1)}, u32[]{:S(2)}, u32[]{:S(2)}) collective-permute-start(bf16[128,64,128]{2,1,0:T(8,128)(2,1)} %get-tuple-element.189.refs_2_), channel_id=1, source_target_pairs={{0,16},{8,24},{16,0},{24,8},{1,17},{9,25},{17,1},{25,9},{2,18},{10... | collective-permute-start | bytes 6291464 | tf_op jit(solution)/shard_map/ppermute | solution.py:1186
  441.0 10.8 %copy-start = (bf16[128,64,128]{2,1,0:T(8,128)(2,1)S(1)}, bf16[128,64,128]{2,1,0:T(8,128)(2,1)}, u32[]{:S(2)}) copy-start(bf16[128,64,128]{2,1,0:T(8,128)(2,1)} %get-tuple-element.166.refs_0_) | copy-start | bytes 6291460
  451.3 13.3 %collective-permute-start.9 = (bf16[128,64,128]{2,1,0:T(8,128)(2,1)}, bf16[128,64,128]{2,1,0:T(8,128)(2,1)}, u32[]{:S(2)}, u32[]{:S(2)}) collective-permute-start(bf16[128,64,128]{2,1,0:T(8,128)(2,1)} %get-tuple-element.195), channel_id=1, source_target_pairs={{0,1},{1,0},{2,3},{3,2},{4,5},{5,4},{6,7},{7,6},{8,9},{9,8},{10,11... | collective-permute-start | bytes 6291464 | tf_op jit(solution)/shard_map/ppermute | solution.py:1192
  451.3 46.3 %collective-permute-start.10 = (bf16[128,64,128]{2,1,0:T(8,128)(2,1)}, bf16[128,64,128]{2,1,0:T(8,128)(2,1)S(1)}, u32[]{:S(2)}, u32[]{:S(2)}) collective-permute-start(bf16[128,64,128]{2,1,0:T(8,128)(2,1)} %collective-permute-done.7.refs_1_), channel_id=1, source_target_pairs={{0,1},{1,0},{2,3},{3,2},{4,5},{5,4},{6,7},{7,6},{8,9},{9,8},{10,11... | collective-permute-start | bytes 6291464 | tf_op jit(solution)/shard_map/ppermute | solution.py:1192
  451.8 47.2 %collective-permute-start.11 = (bf16[128,64,128]{2,1,0:T(8,128)(2,1)S(1)}, bf16[128,64,128]{2,1,0:T(8,128)(2,1)S(1)}, u32[]{:S(2)}, u32[]{:S(2)}) collective-permute-start(bf16[128,64,128]{2,1,0:T(8,128)(2,1)S(1)} %copy-done), channel_id=1, source_target_pairs={{0,1},{1,0},{2,3},{3,2},{4,5},{5,4},{6,7},{7,6},{8,9},{9,8},{10,11... | collective-permute-start | bytes 6291464 | tf_op jit(solution)/shard_map/ppermute | solution.py:1192
  451.8 47.2 %collective-permute-start.12 = (bf16[128,64,128]{2,1,0:T(8,128)(2,1)}, bf16[128,64,128]{2,1,0:T(8,128)(2,1)}, u32[]{:S(2)}, u32[]{:S(2)}) collective-permute-start(bf16[128,64,128]{2,1,0:T(8,128)(2,1)} %get-tuple-element.184.refs_1_), channel_id=1, source_target_pairs={{0,1},{1,0},{2,3},{3,2},{4,5},{5,4},{6,7},{7,6},{8,9},{9,8},{10,11... | collective-permute-start | bytes 6291464 | tf_op jit(solution)/shard_map/ppermute | solution.py:1192
  464.6 34.5 %collective-permute-start.13 = (bf16[128,64,128]{2,1,0:T(8,128)(2,1)}, bf16[128,64,128]{2,1,0:T(8,128)(2,1)}, u32[]{:S(2)}, u32[]{:S(2)}) collective-permute-start(bf16[128,64,128]{2,1,0:T(8,128)(2,1)} %get-tuple-element.189.refs_2_), channel_id=1, source_target_pairs={{0,1},{1,0},{2,3},{3,2},{4,5},{5,4},{6,7},{7,6},{8,9},{9,8},{10,11... | collective-permute-start | bytes 6291464 | tf_op jit(solution)/shard_map/ppermute | solution.py:1192
  497.0 4.7 collective-permute-start.14
  497.5 24.7 %copy-start.2 = (bf16[128,64,128]{2,1,0:T(8,128)(2,1)}, bf16[128,64,128]{2,1,0:T(8,128)(2,1)S(1)}, u32[]{:S(2)}) copy-start(bf16[128,64,128]{2,1,0:T(8,128)(2,1)S(1)} %collective-permute-done.10.refs_5_) | copy-start | bytes 6291460
  497.5 48.8 %collective-permute-start.16 = (bf16[128,64,128]{2,1,0:T(8,128)(2,1)}, bf16[128,64,128]{2,1,0:T(8,128)(2,1)}, u32[]{:S(2)}, u32[]{:S(2)}) collective-permute-start(bf16[128,64,128]{2,1,0:T(8,128)(2,1)} %get-tuple-element.201.refs_3_), channel_id=1, source_target_pairs={{0,24},{8,16},{16,8},{24,0},{1,25},{9,17},{17,9},{25,1},{2,26},{10... | collective-permute-start | bytes 6291464 | tf_op jit(solution)/shard_map/ppermute | solution.py:1189
  499.0 2.7 copy-start.1
  499.0 63.5 %collective-permute-start.15 = (bf16[128,64,128]{2,1,0:T(8,128)(2,1)}, bf16[128,64,128]{2,1,0:T(8,128)(2,1)}, u32[]{:S(2)}, u32[]{:S(2)}) collective-permute-start(bf16[128,64,128]{2,1,0:T(8,128)(2,1)} %collective-permute-done.8.refs_2_), channel_id=1, source_target_pairs={{0,1},{1,0},{2,3},{3,2},{4,5},{5,4},{6,7},{7,6},{8,9},{9,8},{10,11... | collective-permute-start | bytes 6291464 | tf_op jit(solution)/shard_map/ppermute | solution.py:1192
  522.2 24.2 %copy-start.6 = (s32[1,512]{1,0:T(1,128)S(1)}, s32[1,512]{1,0:T(1,128)}, u32[]{:S(2)}) copy-start(s32[1,512]{1,0:T(1,128)} %param.27) | copy-start | bytes 6148
  546.4 16.1 %collective-permute-start.17 = (bf16[128,64,128]{2,1,0:T(8,128)(2,1)}, bf16[128,64,128]{2,1,0:T(8,128)(2,1)S(1)}, u32[]{:S(2)}, u32[]{:S(2)}) collective-permute-start(bf16[128,64,128]{2,1,0:T(8,128)(2,1)} %collective-permute-done.16.refs_3_), channel_id=1, source_target_pairs={{0,1},{1,0},{2,3},{3,2},{4,5},{5,4},{6,7},{7,6},{8,9},{9,8},{10,11... | collective-permute-start | bytes 6291464 | tf_op jit(solution)/shard_map/ppermute | solution.py:1192
  (3 other events, 4.0 us)

commit v7 on v6

--- a/solution.py
+++ b/solution.py
@@ -652,11 +652,11 @@
 def turn(first, second):
     chans, half, lanes = first.shape
     lead = lambda i, *_: (i, 0, 0)
-    count = (chans + 1) // 2
+    count = next(n for n in (43, 16, 8, 4, 2, 1) if chans % n == 0)
     block = (count, half, lanes)
     return call(
         turn_kernel,
-        (2,),
+        (chans // count,),
         [],
         [(first, block, lead), (second, block, lead)],
         [((chans, lanes, 2 * half), BF16, (count, lanes, 2 * half), lead)],
@@ -804,7 +804,7 @@
     )
 
 
-def reduce_kernel(pair_ref, left_ref, right_ref, out_ref, full_s, core_s, crop_s, row_s, send, recv):
+def reduce_kernel(share_ref, pair_ref, left_ref, right_ref, out_ref, full_s, core_s, crop_s, row_s, send, recv):
     side, spot, level = lax.axis_index("col"), lax.axis_index("crop"), lax.axis_index("row")
     mesh_id = pl.DeviceIdType.MESH
     sibling = {"col": 1 - side}
@@ -834,6 +834,7 @@
         full_s[row : row + ref.shape[0]] = ref[...]
         row += ref.shape[0]
     full_s[row:] = jnp.zeros((full_s.shape[0] - row, full_s.shape[1]), F32)
+    full_s[BIAS_ROW : BIAS_ROW + 1] += share_ref[...]
     base = pl.multiple_of(side * half, 8)
     run([copy(full_s.at[pl.ds(pl.multiple_of((1 - side) * half, 8), half)], core_s, 0, sibling)])
     full_s[pl.ds(base, half)] += core_s[...]
@@ -859,8 +860,8 @@
 ALL_ROWS = 2048
 
 
-def reduce_all(*parts):
-    lanes = parts[0].shape[1]
+def reduce_all(share, *parts):
+    lanes = share.shape[1]
     return pl.pallas_call(
         reduce_kernel,
         out_shape=jax.ShapeDtypeStruct((ALL_ROWS, lanes), F32),
@@ -876,7 +877,7 @@
             collective_id=1, has_side_effects=True, vmem_limit_bytes=VMEM_LIMIT
         ),
         name="reduce_all",
-    )(*parts)
+    )(share, *parts)
 
 
 def flip(a, b):
@@ -1267,7 +1268,7 @@
         [right[q, 0] for q in range(4)],
         [right[q, 1] for q in range(4)],
     )
-    pair_sums = sums[0].at[LOSS_ROW - 1, 127].set(count * count / share_count)
+    share = jnp.where(jnp.arange(128) == 127, count * count / share_count, 0.0)[None]
     left_sum = []
     for h in range(2):
         left_sum = input_back([(acts[0, h], d_left[h])], 0, proj_w, ln_wide, left_sum, h == 1)
@@ -1282,7 +1283,7 @@
     )
     right_sum = input_back([(acts[0, h], d_right[h]) for h in range(2)], 1, proj_w, ln_wide, [], True)
     params = (w_in, w_out, w_t1, w_t2, w_dist, norm_params, dist_bias)
-    return update(reduce_all(pair_sums, left_sum[0], right_sum[0]), params, firsts, seconds)
+    return update(reduce_all(share, sums[0], left_sum[0], right_sum[0]), params, firsts, seconds)
 
 
 def solution(mesh):

time: 649 us -> 648 us (level)
  no operation moved by 1% of the time
where the time goes in v7:
time: 648 us; the launch traced here: 643 us
  Pallas kernels  593 us (92%)
  waiting for transfers between devices  25.6 us (4%)
  starting transfers between devices  13.8 us (2%)
    pallas_call x19, Pallas kernels, call(): pl.pallas_call(kernel, grid_spec=pltpu.PrefetchScalarGridSpec(num_scalar_...  355 us
    pallas_call x1, Pallas kernels, spread(): pl.pallas_call(spread_kernel, in_specs=[anywhere] + [whole] * 8, out_spec...  203 us
    pallas_call x1, Pallas kernels, reduce_all(): pl.pallas_call(reduce_kernel, out_shape=jax.ShapeDtypeStruct((ALL_ROWS, l...  30.3 us
  transfers between devices with their start and end apart: 18, of which 3 were waited for; matrix products, arithmetic and copies ran while one was open for 0% of the time, Pallas kernels for 48%

profile of v7, /device:TPU:0, one launch (start us, length us, event | category | flops | bytes accessed | tf_op | source)
XLA Modules:
  0.0 642.7 jit_solution(9098865230579574407)
XLA Ops:
  3.6 202.6 %spread.1 = (bf16[129,64,256]{2,1,0:T(8,128)(2,1)}, bf16[129,64,256]{2,1,0:T(8,128)(2,1)}, bf16[129,64,256]{2,1,0:T(8,128)(2,1)}, bf16[129,64,256]{2,1,0:T(8,128...) custom-call(bf16[128,256,128]{2,1,0:T(8,128)(2,1)} %bitcast.23, ...), custom_call_target="tpu_custom_call" | custom-call | tf_op jit(solution)/shard_map/spread/pallas_call | solution.py:1080
  210.5 12.4 %project.3 = (bf16[128,64,256]{2,1,0:T(8,128)(2,1)}, bf16[128,64,256]{2,1,0:T(8,128)(2,1)}) custom-call(bf16[129,64,256]{2,1,0:T(8,128)(2,1)} %get-tuple-element.129.acts_ref.code_ref.second.rest_0_.rest_1_.rest_3_.rest_4_, bf16[129,64,256]{2,1,0:T(8,128)(2,1)} %get-tuple-element.129.acts_ref.code_ref.second.rest_0_.rest_1_.rest_3_.rest_4_, ...), custom_call_target="tpu_custom_call" | custom-call | flops 15000 | bytes 1 | tf_op jit(solution)/shard_map/project/pallas_call | solution.py:289
  223.5 10.1 %triangle.4 = (f32[128,64,128]{2,1,0:T(8,128)}, bf16[128,64,128]{2,1,0:T(8,128)(2,1)}) custom-call(s32[3]{0:T(128)} %pad_add_fusion.ids, bf16[128,64,256]{2,1,0:T(8,128)(2,1)} %get-tuple-element.134.a0.refs_8_, bf16[128,64,256]{2,1,0:T(8,128)(2,1)} %get-tuple-element.135.a1.refs_12_, bf16[128,64,256]{2,1,0:T(8,128)(2,1)} %get-tuple-element.136.b0.refs_8_, ...), custom_call_target="tpu_custom_call" | custom-call | flops 14000 | bytes 1 | tf_op jit(solution)/shard_map/triangle/pallas_call | solution.py:289
  233.6 8.8 %turn.1.acts_ref.code_ref = bf16[129,256,128]{2,1,0:T(8,128)(2,1)} custom-call(bf16[129,64,256]{2,1,0:T(8,128)(2,1)} %get-tuple-element.138.first.rest_0_.rest_1_, bf16[129,64,256]{2,1,0:T(8,128)(2,1)} %get-tuple-element.129.acts_ref.code_ref.second.rest_0_.rest_1_.rest_3_.rest_4_), custom_call_target="tpu_custom_call" | custom-call | flops 12000 | bytes 1 | tf_op jit(solution)/shard_map/turn/pallas_call | solution.py:289
  242.4 23.9 %project_two.2 = (bf16[128,64,256]{2,1,0:T(8,128)(2,1)}, bf16[128,64,256]{2,1,0:T(8,128)(2,1)}, bf16[128,64,256]{2,1,0:T(8,128)(2,1)}, bf16[128,64,256]{2,1,0:T(8,128)(2,1)}) custom-call(bf16[129,64,256]{2,1,0:T(8,128)(2,1)} %get-tuple-element.155.acts0.code0, bf16[129,64,256]{2,1,0:T(8,128)(2,1)} %get-tuple-element.155.acts0.code0, ...), custom_call_target="tpu_custom_call" | custom-call | flops 30000 | bytes 1 | tf_op jit(solution)/shard_map/project_two/pallas_call | solution.py:289
  267.6 31.9 %pair.4 = (bf16[128,64,128]{2,1,0:T(8,128)(2,1)}, f32[1352,128]{1,0:T(8,128)}, f32[7,128,128]{2,1,0:T(8,128)}) custom-call(s32[3]{0:T(128)} %pad_add_fusion.ids, f32[128,64,128]{2,1,0:T(8,128)} %get-tuple-element.143.x_keep, bf16[128,64,128]{2,1,0:T(8,128)(2,1)} %copy-done.4, bf16[129,256,128]{2,1,0:T(8,128)(2,1)} %turn.1.acts_ref.code_ref, ...), custom_call_target="tpu_custom_call" | custom-call | flops 35000 | bytes 1 | tf_op jit(solution)/shard_map/pair/pallas_call | solution.py:289
  304.3 12.5 %project.4 = (bf16[128,64,256]{2,1,0:T(8,128)(2,1)}, bf16[128,64,256]{2,1,0:T(8,128)(2,1)}) custom-call(bf16[129,64,256]{2,1,0:T(8,128)(2,1)} %collective-permute-done.3.acts_ref.code_ref, bf16[129,64,256]{2,1,0:T(8,128)(2,1)} %collective-permute-done.3.acts_ref.code_ref, bf16[512,128]{1,0:T(8,128)(2,1)} %get-tuple-element.130.w_ref, ...), custom_call_target="tpu_custom_call" | custom-call | flops 15000 | bytes 1 | tf_op jit(solution)/shard_map/project/pallas_call | solution.py:289
  316.8 10.1 %triangle.5 = (f32[128,64,128]{2,1,0:T(8,128)}, bf16[128,64,128]{2,1,0:T(8,128)(2,1)}) custom-call(s32[3]{0:T(128)} %pad_add_fusion.ids, bf16[128,64,256]{2,1,0:T(8,128)(2,1)} %get-tuple-element.134.a0.refs_8_, bf16[128,64,256]{2,1,0:T(8,128)(2,1)} %get-tuple-element.135.a1.refs_12_, bf16[128,64,256]{2,1,0:T(8,128)(2,1)} %get-tuple-element.161.b0.refs_9_, ...), custom_call_target="tpu_custom_call" | custom-call | flops 14000 | bytes 1 | tf_op jit(solution)/shard_map/triangle/pallas_call | solution.py:289
  326.9 12.5 %project.5 = (bf16[128,64,256]{2,1,0:T(8,128)(2,1)}, bf16[128,64,256]{2,1,0:T(8,128)(2,1)}) custom-call(bf16[129,64,256]{2,1,0:T(8,128)(2,1)} %collective-permute-done.2.acts_ref.code_ref, bf16[129,64,256]{2,1,0:T(8,128)(2,1)} %collective-permute-done.2.acts_ref.code_ref, bf16[512,128]{1,0:T(8,128)(2,1)} %get-tuple-element.130.w_ref, ...), custom_call_target="tpu_custom_call" | custom-call | flops 15000 | bytes 1 | tf_op jit(solution)/shard_map/project/pallas_call | solution.py:289
  339.4 10.6 %triangle.6 = (f32[128,64,128]{2,1,0:T(8,128)}, bf16[128,64,128]{2,1,0:T(8,128)(2,1)}) custom-call(s32[3]{0:T(128)} %pad_add_fusion.ids, bf16[128,64,256]{2,1,0:T(8,128)(2,1)} %get-tuple-element.134.a0.refs_8_, bf16[128,64,256]{2,1,0:T(8,128)(2,1)} %get-tuple-element.135.a1.refs_12_, bf16[128,64,256]{2,1,0:T(8,128)(2,1)} %get-tuple-element.166.b0.refs_10_, ...), custom_call_target="tpu_custom_call" | custom-call | flops 14000 | bytes 1 | tf_op jit(solution)/shard_map/triangle/pallas_call | solution.py:289
  350.5 32.0 %pair.5 = (bf16[128,64,128]{2,1,0:T(8,128)(2,1)}, f32[1352,128]{1,0:T(8,128)}, f32[7,128,128]{2,1,0:T(8,128)}) custom-call(s32[3]{0:T(128)} %pad_add_fusion.ids, f32[128,64,128]{2,1,0:T(8,128)} %get-tuple-element.169.x_keep, bf16[128,64,128]{2,1,0:T(8,128)(2,1)} %collective-permute-done.4.x_recv, bf16[129,256,128]{2,1,0:T(8,128)(2,1)} %turn.1.acts_ref.code_ref, ...), custom_call_target="tpu_custom_call" | custom-call | flops 35000 | bytes 1 | tf_op jit(solution)/shard_map/pair/pallas_call | solution.py:289
  383.8 32.1 %pair.6 = (bf16[128,64,128]{2,1,0:T(8,128)(2,1)}, f32[1352,128]{1,0:T(8,128)}, f32[7,128,128]{2,1,0:T(8,128)}) custom-call(s32[3]{0:T(128)} %pad_add_fusion.ids, f32[128,64,128]{2,1,0:T(8,128)} %get-tuple-element.174.x_keep, bf16[128,64,128]{2,1,0:T(8,128)(2,1)} %copy-done.5, bf16[129,256,128]{2,1,0:T(8,128)(2,1)} %turn.1.acts_ref.code_ref, ...), custom_call_target="tpu_custom_call" | custom-call | flops 35000 | bytes 1 | tf_op jit(solution)/shard_map/pair/pallas_call | solution.py:289
  417.2 23.8 %project_two.3 = (bf16[128,64,256]{2,1,0:T(8,128)(2,1)}, bf16[128,64,256]{2,1,0:T(8,128)(2,1)}, bf16[128,64,256]{2,1,0:T(8,128)(2,1)}, bf16[128,64,256]{2,1,0:T(8,128)(2,1)}) custom-call(bf16[129,64,256]{2,1,0:T(8,128)(2,1)} %collective-permute-done.1.acts0.code0, bf16[129,64,256]{2,1,0:T(8,128)(2,1)} %collective-permute-done.1.acts0.code0, ...), custom_call_target="tpu_custom_call" | custom-call | flops 30000 | bytes 1 | tf_op jit(solution)/shard_map/project_two/pallas_call | solution.py:289
  441.0 10.3 %triangle.7 = (f32[128,64,128]{2,1,0:T(8,128)}, bf16[128,64,128]{2,1,0:T(8,128)(2,1)}) custom-call(s32[3]{0:T(128)} %pad_add_fusion.ids, bf16[128,64,256]{2,1,0:T(8,128)(2,1)} %get-tuple-element.134.a0.refs_8_, bf16[128,64,256]{2,1,0:T(8,128)(2,1)} %get-tuple-element.135.a1.refs_12_, bf16[128,64,256]{2,1,0:T(8,128)(2,1)} %get-tuple-element.181.b0.refs_11_, ...), custom_call_target="tpu_custom_call" | custom-call | flops 14000 | bytes 1 | tf_op jit(solution)/shard_map/triangle/pallas_call | solution.py:289
  452.3 11.6 %collective-permute-done.8.refs_2_ = bf16[128,64,128]{2,1,0:T(8,128)(2,1)} collective-permute-done((bf16[128,64,128]{2,1,0:T(8,128)(2,1)}, bf16[128,64,128]{2,1,0:T(8,128)(2,1)}, u32[]{:S(2)}, u32[]{:S(2)}) %collective-permute-start.8) | collective-permute-done | bytes 2097184 | tf_op jit(solution)/shard_map/ppermute | solution.py:1187
  463.9 32.4 %pair.7 = (bf16[128,64,128]{2,1,0:T(8,128)(2,1)}, f32[1352,128]{1,0:T(8,128)}, f32[7,128,128]{2,1,0:T(8,128)}) custom-call(s32[3]{0:T(128)} %pad_add_fusion.ids, f32[128,64,128]{2,1,0:T(8,128)} %get-tuple-element.185.x_keep, bf16[128,64,128]{2,1,0:T(8,128)(2,1)} %collective-permute-done.9.x_recv, bf16[129,256,128]{2,1,0:T(8,128)(2,1)} %turn.1.acts_ref.code_ref, ...), custom_call_target="tpu_custom_call" | custom-call | flops 35000 | bytes 1 | tf_op jit(solution)/shard_map/pair/pallas_call | solution.py:289
  501.0 20.5 %left_back.1 = (bf16[128,64,256]{2,1,0:T(8,128)(2,1)}, bf16[128,64,256]{2,1,0:T(8,128)(2,1)}) custom-call(s32[3]{0:T(128)} %pad_add_fusion.ids, bf16[128,64,128]{2,1,0:T(8,128)(2,1)} %get-tuple-element.154.refs_0_, bf16[128,64,128]{2,1,0:T(8,128)(2,1)} %get-tuple-element.172.refs_1_, bf16[128,64,128]{2,1,0:T(8,128)(2,1)} %get-tuple-element.177.refs_2_, ...), custom_call_target="tpu_custom_call" | custom-call | flops 25000 | bytes 1 | tf_op jit(solution)/shard_map/left_back/pallas_call | solution.py:289
  521.6 12.8 %input_back.3 = (f32[272,128]{1,0:T(8,128)}, f32[256,128]{1,0:T(8,128)}, f32[256,128]{1,0:T(8,128)}) custom-call(bf16[512,128]{1,0:T(8,128)(2,1)} %get-tuple-element.130.w_ref, f32[6,128,128]{2,1,0:T(8,128)} %get-tuple-element.131.ln_ref, bf16[129,64,256]{2,1,0:T(8,128)(2,1)} %get-tuple-element.138.first.rest_0_.rest_1_, ...), custom_call_target="tpu_custom_call" | custom-call | flops 16000 | bytes 1 | tf_op jit(solution)/shard_map/input_back/pallas_call | solution.py:289
  534.4 11.3 %collective-permute-done.16.refs_3_ = bf16[128,64,128]{2,1,0:T(8,128)(2,1)} collective-permute-done((bf16[128,64,128]{2,1,0:T(8,128)(2,1)}, bf16[128,64,128]{2,1,0:T(8,128)(2,1)}, u32[]{:S(2)}, u32[]{:S(2)}) %collective-permute-start.16) | collective-permute-done | bytes 2097184 | tf_op jit(solution)/shard_map/ppermute | solution.py:1190
  547.6 13.4 %input_back.4 = (f32[272,128]{1,0:T(8,128)}, f32[256,128]{1,0:T(8,128)}, f32[256,128]{1,0:T(8,128)}) custom-call(bf16[512,128]{1,0:T(8,128)(2,1)} %get-tuple-element.130.w_ref, f32[6,128,128]{2,1,0:T(8,128)} %get-tuple-element.131.ln_ref, bf16[129,64,256]{2,1,0:T(8,128)(2,1)} %get-tuple-element.129.acts_ref.code_ref.second.rest_0_.rest_1_.rest_3_.rest_4_, ...), custom_call_target="tpu_custom_call" | custom-call | flops 16000 | bytes 1 | tf_op jit(solution)/shard_map/input_back/pallas_call | solution.py:289
  562.4 20.3 %right_back.1 = (bf16[128,64,256]{2,1,0:T(8,128)(2,1)}, bf16[128,64,256]{2,1,0:T(8,128)(2,1)}) custom-call(s32[3]{0:T(128)} %pad_add_fusion.ids, bf16[128,64,128]{2,1,0:T(8,128)(2,1)} %get-tuple-element.154.refs_0_, bf16[128,64,128]{2,1,0:T(8,128)(2,1)} %collective-permute-done.7.refs_1_, bf16[128,64,128]{2,1,0:T(8,128)(2,1)} %collective-permute-done.8.refs_2_, ...), custom_call_target="tpu_custom_call" | custom-call | flops 25000 | bytes 1 | tf_op jit(solution)/shard_map/right_back/pallas_call | solution.py:289
  582.7 24.4 %input_back.5 = (f32[272,128]{1,0:T(8,128)}, f32[256,128]{1,0:T(8,128)}, f32[256,128]{1,0:T(8,128)}) custom-call(bf16[512,128]{1,0:T(8,128)(2,1)} %get-tuple-element.130.w_ref, f32[6,128,128]{2,1,0:T(8,128)} %get-tuple-element.131.ln_ref, bf16[129,64,256]{2,1,0:T(8,128)(2,1)} %get-tuple-element.138.first.rest_0_.rest_1_, ...), custom_call_target="tpu_custom_call" | custom-call | flops 16000 | bytes 1 | tf_op jit(solution)/shard_map/input_back/pallas_call | solution.py:289
  607.1 30.3 %reduce_all.1.early_ref = f32[2048,128]{1,0:T(8,128)} custom-call(f32[1,128]{1,0:T(1,128)} %compare_select_fusion.share_ref, f32[1352,128]{1,0:T(8,128)} %get-tuple-element.188.pair_ref, f32[272,128]{1,0:T(8,128)} %get-tuple-element.196.left_ref, f32[272,128]{1,0:T(8,128)} %get-tuple-element.205.right_ref), custom_call_target="tpu_custom_call" | custom-call | tf_op jit(solution)/shard_map/reduce_all/pallas_call | solution.py:865
  637.5 4.8 update.1
  (59 shorter events, 25.2 us)
Async XLA Ops:
  206.2 95.3 %collective-permute-start.2 = (bf16[129,64,256]{2,1,0:T(8,128)(2,1)}, bf16[129,64,256]{2,1,0:T(8,128)(2,1)}, u32[]{:S(2)}, u32[]{:S(2)}) collective-permute-start(bf16[129,64,256]{2,1,0:T(8,128)(2,1)} %get-tuple-element.129.acts_ref.code_ref.second.rest_0_.rest_1_.rest_3_.rest_4_), channel_id=1, source_target_pairs={{0,16},{8,24},{16,0},{24,8},{1,17},{9,25},{17,1},{25,9},{2,18},{10... | collective-permute-start | bytes 12681224 | tf_op jit(solution)/shard_map/ppermute | solution.py:1187
  206.3 98.0 %collective-permute-start.3 = (bf16[129,64,256]{2,1,0:T(8,128)(2,1)}, bf16[129,64,256]{2,1,0:T(8,128)(2,1)}, u32[]{:S(2)}, u32[]{:S(2)}) collective-permute-start(bf16[129,64,256]{2,1,0:T(8,128)(2,1)} %get-tuple-element.129.acts_ref.code_ref.second.rest_0_.rest_1_.rest_3_.rest_4_), channel_id=1, source_target_pairs={{0,8},{8,0},{16,24},{24,16},{1,9},{9,1},{17,25},{25,17},{2,10},{10... | collective-permute-start | bytes 12681224 | tf_op jit(solution)/shard_map/ppermute | solution.py:1184
  233.6 32.7 %collective-permute-start = (bf16[128,64,128]{2,1,0:T(8,128)(2,1)}, bf16[128,64,128]{2,1,0:T(8,128)(2,1)S(1)}, u32[]{:S(2)}, u32[]{:S(2)}) collective-permute-start(bf16[128,64,128]{2,1,0:T(8,128)(2,1)} %get-tuple-element.137), channel_id=1, source_target_pairs={{0,1},{1,0},{2,3},{3,2},{4,5},{5,4},{6,7},{7,6},{8,9},{9,8},{10,11... | collective-permute-start | bytes 6291464 | tf_op jit(solution)/shard_map/ppermute | solution.py:1193
  242.4 57.1 %slice-start = ((s8[4227072]{0:T(1024)(128)(4,1)}), s8[4194304]{0:T(1024)(128)(4,1)S(1)}, s32[]{:S(2)}) async-start(s8[4227072]{0:T(1024)(128)(4,1)} %bitcast.21), calls=%async_computation | async-start | bytes 8388608
  267.6 31.9 %slice-start.1 = ((s8[4227072]{0:T(1024)(128)(4,1)}), s8[32768]{0:T(1024)(128)(4,1)S(1)}, s32[]{:S(2)}) async-start(s8[4227072]{0:T(1024)(128)(4,1)} %bitcast.21), calls=%async_computation.1 | async-start | bytes 65536
  299.6 117.6 %collective-permute-start.1 = (bf16[129,64,256]{2,1,0:T(8,128)(2,1)S(1)}, bf16[129,64,256]{2,1,0:T(8,128)(2,1)}, u32[]{:S(2)}, u32[]{:S(2)}) collective-permute-start(bf16[129,64,256]{2,1,0:T(8,128)(2,1)S(1)} %bitcast.22), channel_id=1, source_target_pairs={{0,16},{8,24},{16,0},{24,8},{1,17},{9,25},{17,1},{25,9},{2,18},{10... | collective-permute-start | bytes 12681224 | tf_op jit(solution)/shard_map/ppermute | solution.py:1187
  301.6 115.6 %collective-permute-start.6 = (bf16[129,64,256]{2,1,0:T(8,128)(2,1)}, bf16[129,64,256]{2,1,0:T(8,128)(2,1)}, u32[]{:S(2)}, u32[]{:S(2)}) collective-permute-start(bf16[129,64,256]{2,1,0:T(8,128)(2,1)} %collective-permute-done.2.acts_ref.code_ref), channel_id=1, source_target_pairs={{0,8},{8,0},{16,24},{24,16},{1,9},{9,1},{17,25},{25,17},{2,10},{10... | collective-permute-start | bytes 12681224 | tf_op jit(solution)/shard_map/ppermute | solution.py:1184
  326.9 23.6 %collective-permute-start.4 = (bf16[128,64,128]{2,1,0:T(8,128)(2,1)}, bf16[128,64,128]{2,1,0:T(8,128)(2,1)}, u32[]{:S(2)}, u32[]{:S(2)}) collective-permute-start(bf16[128,64,128]{2,1,0:T(8,128)(2,1)} %get-tuple-element.162), channel_id=1, source_target_pairs={{0,1},{1,0},{2,3},{3,2},{4,5},{5,4},{6,7},{7,6},{8,9},{9,8},{10,11... | collective-permute-start | bytes 6291464 | tf_op jit(solution)/shard_map/ppermute | solution.py:1193
  350.0 32.5 %collective-permute-start.5 = (bf16[128,64,128]{2,1,0:T(8,128)(2,1)}, bf16[128,64,128]{2,1,0:T(8,128)(2,1)S(1)}, u32[]{:S(2)}, u32[]{:S(2)}) collective-permute-start(bf16[128,64,128]{2,1,0:T(8,128)(2,1)} %get-tuple-element.167), channel_id=1, source_target_pairs={{0,1},{1,0},{2,3},{3,2},{4,5},{5,4},{6,7},{7,6},{8,9},{9,8},{10,11... | collective-permute-start | bytes 6291464 | tf_op jit(solution)/shard_map/ppermute | solution.py:1193
  382.4 68.8 %collective-permute-start.7 = (bf16[128,64,128]{2,1,0:T(8,128)(2,1)}, bf16[128,64,128]{2,1,0:T(8,128)(2,1)}, u32[]{:S(2)}, u32[]{:S(2)}) collective-permute-start(bf16[128,64,128]{2,1,0:T(8,128)(2,1)} %get-tuple-element.172.refs_1_), channel_id=1, source_target_pairs={{0,8},{8,0},{16,24},{24,16},{1,9},{9,1},{17,25},{25,17},{2,10},{10... | collective-permute-start | bytes 6291464 | tf_op jit(solution)/shard_map/ppermute | solution.py:1184
  416.0 47.9 %collective-permute-start.8 = (bf16[128,64,128]{2,1,0:T(8,128)(2,1)}, bf16[128,64,128]{2,1,0:T(8,128)(2,1)}, u32[]{:S(2)}, u32[]{:S(2)}) collective-permute-start(bf16[128,64,128]{2,1,0:T(8,128)(2,1)} %get-tuple-element.177.refs_2_), channel_id=1, source_target_pairs={{0,16},{8,24},{16,0},{24,8},{1,17},{9,25},{17,1},{25,9},{2,18},{10... | collective-permute-start | bytes 6291464 | tf_op jit(solution)/shard_map/ppermute | solution.py:1187
  441.0 10.8 %copy-start = (bf16[128,64,128]{2,1,0:T(8,128)(2,1)S(1)}, bf16[128,64,128]{2,1,0:T(8,128)(2,1)}, u32[]{:S(2)}) copy-start(bf16[128,64,128]{2,1,0:T(8,128)(2,1)} %get-tuple-element.154.refs_0_) | copy-start | bytes 6291460
  451.3 12.7 %collective-permute-start.9 = (bf16[128,64,128]{2,1,0:T(8,128)(2,1)}, bf16[128,64,128]{2,1,0:T(8,128)(2,1)}, u32[]{:S(2)}, u32[]{:S(2)}) collective-permute-start(bf16[128,64,128]{2,1,0:T(8,128)(2,1)} %get-tuple-element.183), channel_id=1, source_target_pairs={{0,1},{1,0},{2,3},{3,2},{4,5},{5,4},{6,7},{7,6},{8,9},{9,8},{10,11... | collective-permute-start | bytes 6291464 | tf_op jit(solution)/shard_map/ppermute | solution.py:1193
  451.3 45.6 %collective-permute-start.10 = (bf16[128,64,128]{2,1,0:T(8,128)(2,1)}, bf16[128,64,128]{2,1,0:T(8,128)(2,1)S(1)}, u32[]{:S(2)}, u32[]{:S(2)}) collective-permute-start(bf16[128,64,128]{2,1,0:T(8,128)(2,1)} %collective-permute-done.7.refs_1_), channel_id=1, source_target_pairs={{0,1},{1,0},{2,3},{3,2},{4,5},{5,4},{6,7},{7,6},{8,9},{9,8},{10,11... | collective-permute-start | bytes 6291464 | tf_op jit(solution)/shard_map/ppermute | solution.py:1193
  451.8 46.6 %collective-permute-start.11 = (bf16[128,64,128]{2,1,0:T(8,128)(2,1)S(1)}, bf16[128,64,128]{2,1,0:T(8,128)(2,1)S(1)}, u32[]{:S(2)}, u32[]{:S(2)}) collective-permute-start(bf16[128,64,128]{2,1,0:T(8,128)(2,1)S(1)} %copy-done), channel_id=1, source_target_pairs={{0,1},{1,0},{2,3},{3,2},{4,5},{5,4},{6,7},{7,6},{8,9},{9,8},{10,11... | collective-permute-start | bytes 6291464 | tf_op jit(solution)/shard_map/ppermute | solution.py:1193
  451.8 46.5 %collective-permute-start.13 = (bf16[128,64,128]{2,1,0:T(8,128)(2,1)}, bf16[128,64,128]{2,1,0:T(8,128)(2,1)}, u32[]{:S(2)}, u32[]{:S(2)}) collective-permute-start(bf16[128,64,128]{2,1,0:T(8,128)(2,1)} %get-tuple-element.177.refs_2_), channel_id=1, source_target_pairs={{0,1},{1,0},{2,3},{3,2},{4,5},{5,4},{6,7},{7,6},{8,9},{9,8},{10,11... | collective-permute-start | bytes 6291464 | tf_op jit(solution)/shard_map/ppermute | solution.py:1193
  463.9 34.5 %collective-permute-start.12 = (bf16[128,64,128]{2,1,0:T(8,128)(2,1)}, bf16[128,64,128]{2,1,0:T(8,128)(2,1)}, u32[]{:S(2)}, u32[]{:S(2)}) collective-permute-start(bf16[128,64,128]{2,1,0:T(8,128)(2,1)} %get-tuple-element.172.refs_1_), channel_id=1, source_target_pairs={{0,1},{1,0},{2,3},{3,2},{4,5},{5,4},{6,7},{7,6},{8,9},{9,8},{10,11... | collective-permute-start | bytes 6291464 | tf_op jit(solution)/shard_map/ppermute | solution.py:1193
  496.3 4.7 collective-permute-start.14
  496.9 24.7 %copy-start.2 = (bf16[128,64,128]{2,1,0:T(8,128)(2,1)}, bf16[128,64,128]{2,1,0:T(8,128)(2,1)S(1)}, u32[]{:S(2)}) copy-start(bf16[128,64,128]{2,1,0:T(8,128)(2,1)S(1)} %collective-permute-done.10.refs_5_) | copy-start | bytes 6291460
  496.9 48.8 %collective-permute-start.16 = (bf16[128,64,128]{2,1,0:T(8,128)(2,1)}, bf16[128,64,128]{2,1,0:T(8,128)(2,1)}, u32[]{:S(2)}, u32[]{:S(2)}) collective-permute-start(bf16[128,64,128]{2,1,0:T(8,128)(2,1)} %get-tuple-element.189.refs_3_), channel_id=1, source_target_pairs={{0,24},{8,16},{16,8},{24,0},{1,25},{9,17},{17,9},{25,1},{2,26},{10... | collective-permute-start | bytes 6291464 | tf_op jit(solution)/shard_map/ppermute | solution.py:1190
  498.4 2.7 copy-start.1
  498.4 62.6 %collective-permute-start.15 = (bf16[128,64,128]{2,1,0:T(8,128)(2,1)}, bf16[128,64,128]{2,1,0:T(8,128)(2,1)}, u32[]{:S(2)}, u32[]{:S(2)}) collective-permute-start(bf16[128,64,128]{2,1,0:T(8,128)(2,1)} %collective-permute-done.8.refs_2_), channel_id=1, source_target_pairs={{0,1},{1,0},{2,3},{3,2},{4,5},{5,4},{6,7},{7,6},{8,9},{9,8},{10,11... | collective-permute-start | bytes 6291464 | tf_op jit(solution)/shard_map/ppermute | solution.py:1193
  521.6 24.2 %copy-start.6 = (s32[1,512]{1,0:T(1,128)S(1)}, s32[1,512]{1,0:T(1,128)}, u32[]{:S(2)}) copy-start(s32[1,512]{1,0:T(1,128)} %param.25) | copy-start | bytes 6148
  545.8 15.2 %collective-permute-start.17 = (bf16[128,64,128]{2,1,0:T(8,128)(2,1)}, bf16[128,64,128]{2,1,0:T(8,128)(2,1)S(1)}, u32[]{:S(2)}, u32[]{:S(2)}) collective-permute-start(bf16[128,64,128]{2,1,0:T(8,128)(2,1)} %collective-permute-done.16.refs_3_), channel_id=1, source_target_pairs={{0,1},{1,0},{2,3},{3,2},{4,5},{5,4},{6,7},{7,6},{8,9},{9,8},{10,11... | collective-permute-start | bytes 6291464 | tf_op jit(solution)/shard_map/ppermute | solution.py:1193
  (3 other events, 4.0 us)
